TPU v7x, 32 devices: a whole 2x2x4 slice. The times are simulated.
32 devices in a mesh: grp: 16 (over z, x, core), freq: 2 (over y).
Axes of the slice: x: 2, y: 2, z: 4, core: 2. Of those that a mesh axis runs over, the one named last changes fastest.
Arguments:
- spectra: bfloat16 [2, 4096, 1024], P('freq', 'grp'), may hold values from -3000 to 3000
- valid: int32 [4096, 512], P('grp'), may hold values 0 or 1
- station_index: int32 [16], replicated, may hold values from 0 to 4095, as said below
Outputs:
- cross: bfloat16 [2, 2, 4096, 4096], P('freq', None, 'grp')
- station_gather: float32 [16, 4096, 256], P(None, 'grp', 'freq')
Inputs may be any that keep to these rules, and one draw needn't show every extreme that they name: `station_index`: 16 distinct channel numbers.
All inputs are finite; a program needn't handle non-finite values. No bound on the sum of `valid` on one device may be relied on, other than what follows from the above.
Results may differ from a plain program's by a relative error of at most 0.0056.
Values may be sent and summed in bfloat16 or wider, within the bound.
No kernel may reach another device: no remote copies, remote signals or barrier semaphores. Data moves between devices by JAX's collectives and lax.ppermute only.
A program may use at most 128 MiB of HBM per device.

v0:
```python
import math

import jax
import jax.numpy as jnp
from jax import lax
from jax.sharding import PartitionSpec as P

LAGS = 256


def on_device(spectra, valid, station_index):
    bin_count, chan_count, double_width = spectra.shape
    window_count = double_width // 2
    group_index = lax.axis_index("grp")
    spectrum_f32 = spectra.astype(jnp.float32)
    real_part = spectrum_f32[..., :window_count]
    imag_part = spectrum_f32[..., window_count:]
    local_power = jnp.sum(real_part * real_part + imag_part * imag_part, axis=0)
    band_power = lax.psum(local_power, "freq")
    total_bins = bin_count * lax.axis_size("freq")
    factor = lax.rsqrt(band_power / total_bins + 1e-05) * valid.astype(jnp.float32)
    whitened = (spectrum_f32 * jnp.concatenate([factor, factor], axis=1)[None]).astype(jnp.bfloat16)
    swapped = jnp.concatenate([whitened[..., window_count:], -whitened[..., :window_count]], axis=2)
    stacked = jnp.concatenate([whitened, swapped], axis=1)
    scaling = 1.0 / math.sqrt(window_count)
    peer_rows = lax.all_gather(whitened, "grp", axis=1, tiled=True)
    product = jnp.einsum("bkw,bjw->bkj", stacked, peer_rows, preferred_element_type=jnp.float32)
    cross = (
        (product * scaling)
        .astype(jnp.bfloat16)
        .reshape(bin_count, 2, chan_count, peer_rows.shape[1])
    )
    station_count = station_index.shape[0]
    local_rel = station_index - group_index * chan_count
    selector = (local_rel[:, None] == jnp.arange(chan_count, dtype=jnp.int32)[None, :]).astype(
        jnp.bfloat16
    )
    picked = jnp.einsum("sc,bcw->bsw", selector, whitened, preferred_element_type=jnp.float32)
    station_rows = lax.psum(picked.astype(jnp.bfloat16), "grp")
    station_swapped = jnp.concatenate(
        [station_rows[..., window_count:], -station_rows[..., :window_count]], axis=2
    )
    station_left = jnp.concatenate([station_rows, station_swapped], axis=1)
    kernel = (
        jnp.einsum("bkw,bjw->bkj", station_left, whitened, preferred_element_type=jnp.float32)
        * scaling
    )
    kernel = kernel.reshape(bin_count, 2, station_count, chan_count)
    freq_index = lax.axis_index("freq")
    bin_values = (freq_index * bin_count + jnp.arange(bin_count, dtype=jnp.int32)).astype(
        jnp.float32
    ) + 1.0
    lag_values = jnp.arange(LAGS).astype(jnp.float32)
    phase = math.pi * bin_values[:, None] * lag_values[None, :] / LAGS
    lag_table = jnp.stack([jnp.cos(phase), -jnp.sin(phase)], axis=1)
    partial_lags = jnp.einsum(
        "frsc,frl->scl", kernel, lag_table, precision=lax.Precision.HIGHEST
    ) / math.sqrt(total_bins)
    station_gather = lax.psum_scatter(partial_lags, "freq", scatter_dimension=2, tiled=True)
    return (cross, station_gather)


def solution(mesh):
    placed = (P("freq", "grp", None), P("grp", None), P())
    return jax.shard_map(
        on_device,
        mesh=mesh,
        in_specs=placed,
        out_specs=(P("freq", None, "grp", None), P(None, "grp", "freq")),
        check_vma=False,
    )
```

profile of v0, /device:TPU:0, one launch (start us, length us, event | category | flops | bytes accessed | tf_op | source)
XLA Modules:
  0.0 183.0 jit_solution(14101456322627790743)
XLA Ops:
  7.2 0.0 copy-start.1
  7.2 0.0 copy-start.2
  7.2 0.0 all-reduce.2.cloned.1.call-start
  7.2 1.2 convert_element_type.43
  8.4 0.9 fusion.12
  9.3 0.0 all-reduce.2.cloned.1.call-update
  9.3 0.0 all-gather.2.cloned.1.call-start
  9.4 32.8 %all-reduce.2.cloned.1.call-done = f32[256,512]{1,0:T(8,128)} async-done(((f32[256,512]{1,0:T(8,128)}), f32[256,512]{1,0:T(8,128)}) %all-reduce.2.cloned.1.call-update) | async-done | bytes 524304 | tf_op jit(solution)/shard_map/psum | solution.py:19
  42.2 1.3 convert_multiply_fusion
  43.5 0.0 copy-done.1
  43.5 0.9 fusion.6
  44.5 0.0 all-gather.2.cloned.1.call-update
  44.5 0.0 reduce-scatter.2.cloned.1.call-start
  44.5 0.1 sine_negate_fusion
  44.6 0.0 copy-done.2
  44.6 1.3 fusion.4
  45.9 63.0 %psum.15 = bf16[1,16,1024]{2,1,0:T(8,128)(2,1)S(1)} all-reduce(bf16[1,16,1024]{2,1,0:T(8,128)(2,1)S(1)} %fusion.4), channel_id=1, replica_groups=mesh['grp'=16,'freq'=2] {'grp'}, use_global_device_ids=true, to_apply=%region_1.0 | all-reduce | flops 16384 | bytes 65536 | tf_op jit(solution)/shard_map/psum | solution.py:39
  108.9 1.3 convolution_multiply_fusion.1
  110.2 0.0 copy-start
  110.2 5.1 %convolution_multiply_fusion = f32[16,256,256]{2,1,0:T(8,128)} fusion(f32[2,16,256]{2,1,0:T(8,128)S(1)} %bitcast.34, f32[1,1,256]{2,1,0:T(1,128)S(1)} %get-tuple-element.6, f32[1,1,256]{2,1,0:T(1,128)S(1)} %get-tuple-element.7), kind=kOutput, calls=%fused_computation.3 | convolution fusion | flops 26214912 | bytes 4229120 | tf_op jit(solution)/shard_map/frsc,frl->scl/dot_general | solution.py:56
  115.3 0.0 reduce-scatter.2.cloned.1.call-update
  115.3 0.0 copy-done
  115.4 5.3 %all-gather.2.cloned.1.call-done = bf16[1,4096,1024]{2,1,0:T(8,128)(2,1)} async-done(((bf16[1,256,1024]{2,1,0:T(8,128)(2,1)}), bf16[1,4096,1024]{2,1,0:T(8,128)(2,1)}) %all-gather.2.cloned.1.call-update) | async-done | bytes 8388624 | tf_op jit(solution)/shard_map/all_gather | solution.py:26
  120.7 11.1 %multiply_convert_fusion = bf16[512,4096]{1,0:T(8,128)(2,1)} fusion(bf16[1,4096,1024]{2,1,0:T(8,128)(2,1)} %all-gather.2.cloned.1.call-done, bf16[1,256,512]{2,1,0:T(8,128)(2,1)S(1)} %get-tuple-element.3, bf16[1,256,512]{2,1,0:T(8,128)(2,1)S(1)} %get-tuple-element.2, bf16[1,256,1024]{2,1,0:T(8,128)(2,1)S(1)} %copy-done), kind=kOutput, calls=%fused_computation.2 | convolution fusion | flops 4302307328 | bytes 13631488 | tf_op jit(solution)/shard_map/bkw,bjw->bkj/dot_general | solution.py:27
  131.7 44.7 %reduce-scatter.2.cloned.1.call-done = f32[16,256,128]{2,1,0:T(8,128)} async-done(((f32[16,256,256]{2,1,0:T(8,128)}), f32[16,256,128]{2,1,0:T(8,128)}) %reduce-scatter.2.cloned.1.call-update) | async-done | bytes 2097168 | tf_op jit(solution)/shard_map/reduce_scatter | solution.py:59
  (3 shorter events, 0.0 us)
Async XLA Ops:
  7.2 36.4 %copy-start.1 = (bf16[1,256,1024]{2,1,0:T(8,128)(2,1)S(1)}, bf16[1,256,1024]{2,1,0:T(8,128)(2,1)}, u32[]{:S(2)}) copy-start(bf16[1,256,1024]{2,1,0:T(8,128)(2,1)} %param.3) | copy-start | bytes 1572868
  7.2 37.4 %copy-start.2 = (s32[16]{0:T(128)S(1)}, s32[16]{0:T(128)}, u32[]{:S(2)}) copy-start(s32[16]{0:T(128)} %param.5) | copy-start | bytes 196
  7.2 35.0 %all-reduce.2.cloned.1.call-start = ((), (), s32[]{:S(2)}) async-start(), calls=%async_computation.1 | async-start | bytes 1048576 | tf_op jit(solution)/shard_map/psum | solution.py:19
  9.3 111.3 %all-gather.2.cloned.1.call-start = ((), (), s32[]{:S(2)}) async-start(), calls=%async_computation.2 | async-start | bytes 8912896 | tf_op jit(solution)/shard_map/all_gather | solution.py:26
  44.5 132.0 %reduce-scatter.2.cloned.1.call-start = ((), (), s32[]{:S(2)}) async-start(), calls=%async_computation.3 | async-start | bytes 6291456 | tf_op jit(solution)/shard_map/reduce_scatter | solution.py:59
  110.2 5.2 %copy-start = (bf16[1,256,1024]{2,1,0:T(8,128)(2,1)S(1)}, bf16[1,256,1024]{2,1,0:T(8,128)(2,1)}, u32[]{:S(2)}) copy-start(bf16[1,256,1024]{2,1,0:T(8,128)(2,1)} %fusion.6) | copy-start | bytes 1572868
Sparse Core Ops, SparseCore 0:
  10.9 31.2 all-reduce.1
  45.2 75.4 all-gather.1
  123.6 52.7 reduce-scatter.1
where the time goes:
time: 183 us
  waiting for transfers between devices  82.9 us (45%)
  blocking collectives  63 us (34%)
  matrix products  18.7 us (10%)
  between operations  13.8 us (8%)
  other arithmetic  4.43 us (2%)
    psum x1, blocking collectives, on_device(): station_rows = lax.psum(picked.astype(jnp.bfloat16), 'grp')  63 us
    reduce_scatter x1, waiting for transfers between devices, on_device(): lax.psum_scatter(partial_lags, 'freq', scatter_dimension=2, tiled=True)  44.7 us
    psum x1, waiting for transfers between devices, on_device(): band_power = lax.psum(local_power, 'freq')  32.8 us
    dot_general x1, matrix products, on_device(): jnp.einsum('bkw,bjw->bkj', stacked, peer_rows, preferred_element_type=jnp...  11.1 us
    all_gather x1, waiting for transfers between devices, on_device(): peer_rows = lax.all_gather(whitened, 'grp', axis=1, tiled=True)  5.3 us
    dot_general x1, matrix products, on_device(): jnp.einsum('frsc,frl->scl', kernel, lag_table, precision=lax.Precision.HI...  5.11 us
  transfers between devices with their start and end apart: 3, of which 3 were waited for; matrix products, arithmetic and copies ran while one was open for 10% of the time, Pallas kernels for 0%

commit v1 on v0

v1 whole, which is shorter than its diff:
```python
import math

import jax
import jax.numpy as jnp
from jax import lax
from jax.experimental import pallas as pl
from jax.experimental.pallas import tpu as pltpu
from jax.sharding import PartitionSpec as P

LAGS = 256
ROWS_T = (((1,), (1,)), ((), ()))


def ring_pairs(group_size):
    chips = group_size // 2
    half = chips // 2

    def device(place, core):
        place %= chips
        z, x = (place, 0) if place < half else (chips - 1 - place, 1)
        return z * 4 + x * 2 + core

    pairs = []
    for place in range(chips):
        pairs.append((device(place, 0), device(place + 1, 0)))
        pairs.append((device(place, 1), device(place - 1, 1)))
    return pairs


def block_of(place, core, chips):
    place = lax.rem(place + chips, chips)
    half = chips // 2
    return jnp.where(place < half, place * 4, (chips - 1 - place) * 4 + 2) + core


def cross_kernel(scaling, first, where, left, one, two, *rest):
    out = rest[-3] if first else rest[1]
    held, sems = rest[-2:]
    copies = []
    for k, block in enumerate((one, two)):
        product = lax.dot_general(left[...], block[...], ROWS_T, preferred_element_type=jnp.float32)
        rows, width = block.shape[0], block.shape[0]
        held[k] = (product * scaling).astype(jnp.bfloat16).reshape(2, rows, width)
        start = pl.multiple_of(where[k] * width, width)
        copy = pltpu.make_async_copy(held.at[k], out.at[:, :, pl.ds(start, width)], sems.at[k])
        copy.start()
        copies.append(copy)
    for copy in copies:
        copy.wait()


def cross_blocks(left, one, two, where, cross, total, scaling):
    rows, depth = one.shape
    shape = jax.ShapeDtypeStruct((2, rows, total), jnp.bfloat16)
    first = cross is None
    vmem = pl.BlockSpec(memory_space=pltpu.VMEM)
    specs = [pl.BlockSpec(memory_space=pltpu.SMEM), vmem, vmem, vmem]
    args = [where, left, one, two]
    if not first:
        specs.append(pl.BlockSpec(memory_space=pl.ANY))
        args.append(cross)

    def body(*refs):
        cross_kernel(scaling, first, *refs)

    return pl.pallas_call(
        body,
        out_shape=shape,
        in_specs=specs,
        out_specs=pl.BlockSpec(memory_space=pl.ANY),
        scratch_shapes=[pltpu.VMEM((2, 2, rows, rows), jnp.bfloat16), pltpu.SemaphoreType.DMA((2,))],
        input_output_aliases={} if first else {4: 0},
        compiler_params=pltpu.CompilerParams(vmem_limit_bytes=16 * 2**20),
        cost_estimate=pl.CostEstimate(flops=4 * 2 * rows * rows * depth, bytes_accessed=4 * 2 * rows * depth, transcendentals=0),
    )(*args)


def make_on_device(group_size, freq_size):
    chips = group_size // 2
    ring = ring_pairs(group_size)

    def swap_by(bit):
        return [(g, g ^ bit) for g in range(group_size)]

    def from_freq(shift):
        return [(f, (f + shift) % freq_size) for f in range(freq_size)]

    def on_device(spectra, valid, station_index):
        bin_count, chan_count, double_width = spectra.shape
        assert bin_count == 1
        window_count = double_width // 2
        group_index = lax.axis_index("grp")
        freq_index = lax.axis_index("freq")
        core = lax.rem(group_index, 2)
        total_chans = chan_count * group_size
        total_bins = bin_count * freq_size
        scaling = 1.0 / math.sqrt(window_count)

        spectrum_f32 = spectra[0].astype(jnp.float32)
        real_part = spectrum_f32[:, :window_count]
        imag_part = spectrum_f32[:, window_count:]
        local_power = real_part * real_part + imag_part * imag_part
        sent_power = local_power.astype(jnp.bfloat16)
        band_power = local_power
        for shift in range(1, freq_size):
            band_power = band_power + lax.ppermute(sent_power, "freq", from_freq(shift)).astype(jnp.float32)
        factor = lax.rsqrt(band_power / total_bins + 1e-05) * valid.astype(jnp.float32)
        whitened = (spectrum_f32 * jnp.concatenate([factor, factor], axis=1)).astype(jnp.bfloat16)
        left = jnp.concatenate(
            [whitened, jnp.concatenate([whitened[:, window_count:], -whitened[:, :window_count]], axis=1)], axis=0
        )

        local_rel = station_index - group_index * chan_count
        selector = (local_rel[:, None] == jnp.arange(chan_count, dtype=jnp.int32)[None, :]).astype(jnp.bfloat16)
        stations = jnp.dot(selector, whitened, preferred_element_type=jnp.float32).astype(jnp.bfloat16)
        bit = 1
        while bit < group_size:
            stations = stations + lax.ppermute(stations, "grp", swap_by(bit))
            bit *= 2
        station_left = jnp.concatenate(
            [stations, jnp.concatenate([stations[:, window_count:], -stations[:, :window_count]], axis=1)], axis=0
        )
        kernel = lax.dot_general(station_left, whitened, ROWS_T, preferred_element_type=jnp.float32) * scaling
        station_count = station_index.shape[0]
        lags_here = LAGS // freq_size
        lag_values = (freq_index * lags_here + jnp.arange(lags_here, dtype=jnp.int32)).astype(jnp.float32)
        kernels, tables = [], []
        for shift in range(freq_size):
            got = kernel if shift == 0 else lax.ppermute(kernel, "freq", from_freq(shift))
            kernels.append(got.reshape(2, station_count, chan_count))
            bin_value = lax.rem(freq_index - shift + freq_size, freq_size).astype(jnp.float32) + 1.0
            phase = math.pi * bin_value * lag_values / LAGS
            tables.append(jnp.stack([jnp.cos(phase), -jnp.sin(phase)]))
        station_gather = jnp.einsum(
            "rsc,rl->scl",
            jnp.concatenate(kernels, axis=0),
            jnp.concatenate(tables, axis=0),
            precision=lax.Precision.HIGHEST,
        ) / math.sqrt(total_bins)

        half = chips // 2
        z, x = group_index // 4, lax.rem(group_index // 2, 2)
        place = jnp.where(x == 0, z, chips - 1 - z)
        sibling = lax.ppermute(whitened, "grp", swap_by(1))
        where = jnp.stack([group_index, group_index + 1 - 2 * core])
        cross = cross_blocks(left, whitened, sibling, where, None, total_chans, scaling)
        held = [whitened, sibling]
        step_sign = 1 - 2 * core
        for step in range(chips - 1):
            hop = step // 2 + 1
            got = lax.ppermute(held[step % 2], "grp", ring)
            held[step % 2] = got
            swapped = lax.ppermute(got, "grp", swap_by(1))
            kind = step % 2
            mine = block_of(place - hop * step_sign, core if kind == 0 else 1 - core, chips)
            other = block_of(place + hop * step_sign, 1 - core if kind == 0 else core, chips)
            cross = cross_blocks(left, got, swapped, jnp.stack([mine, other]), cross, total_chans, scaling)
        return (cross[None], station_gather)

    return on_device


def solution(mesh):
    placed = (P("freq", "grp", None), P("grp", None), P())
    return jax.shard_map(
        make_on_device(mesh.shape["grp"], mesh.shape["freq"]),
        mesh=mesh,
        in_specs=placed,
        out_specs=(P("freq", None, "grp", None), P(None, "grp", "freq")),
        check_vma=False,
    )
```

time: 183 us -> 86.9 us (0.47)
  blocking collectives: 63 us -> 0 us
  waiting for transfers between devices: 82.9 us -> 38.3 us
  starting transfers between devices: 0.12 us -> 22.3 us
  Pallas kernels: 0 us -> 17.3 us
  matrix products: 18.7 us -> 5.23 us
  between operations: 13.8 us -> 0.91 us
  other arithmetic: 4.43 us -> 2.55 us
    psum x1 -> x0, blocking collectives: 63 us -> none  [on_device(): station_rows = lax.psum(picked.astype(jnp.bfloat16), 'grp')]
    reduce_scatter x1 -> x0, waiting for transfers between devices: 44.7 us -> none  [on_device(): lax.psum_scatter(partial_lags, 'freq', scatter_dimension=2, tiled=True)]
    ppermute x0 -> x21, waiting for transfers between devices: none -> 38.3 us  [the longest x7 18.8 us: on_device(): got = lax.ppermute(held[step % 2], 'grp', ring)]
    psum x1 -> x0, waiting for transfers between devices: 32.8 us -> none  [on_device(): band_power = lax.psum(local_power, 'freq')]
    ppermute x0 -> x21, starting transfers between devices: none -> 22.3 us  [the longest x7 11.7 us: on_device(): got = lax.ppermute(held[step % 2], 'grp', ring)]
    pallas_call x0 -> x8, Pallas kernels: none -> 17.3 us  [cross_blocks(): pl.pallas_call(body, out_shape=shape, in_specs=specs, out_specs=pl.BlockS...]
    dot_general x4 -> x3, matrix products: 18.7 us -> 5.23 us  [the longest x1 4.76 us: on_device(): jnp.einsum('rsc,rl->scl', jnp.concatenate(kernels, axis=0), jnp.concatena...]
    all_gather x1 -> x0, waiting for transfers between devices: 5.3 us -> none  [on_device(): peer_rows = lax.all_gather(whitened, 'grp', axis=1, tiled=True)]
  transfers between devices with their start and end apart: 3 -> 21, of which waited for: 3 -> 10; matrix products, arithmetic and copies ran while one was open for 10% -> 7% of each run, Pallas kernels for 0% -> 18%
where the time goes in v1:
time: 86.9 us; the launch traced here: 86.7 us
  waiting for transfers between devices  38.3 us (44%)
  starting transfers between devices  22.3 us (26%)
  Pallas kernels  17.3 us (20%)
  matrix products  5.23 us (6%)
  other arithmetic  2.55 us (3%)
  between operations  0.91 us (1%)
    ppermute x7, waiting for transfers between devices, on_device(): got = lax.ppermute(held[step % 2], 'grp', ring)  18.8 us
    pallas_call x8, Pallas kernels, cross_blocks(): pl.pallas_call(body, out_shape=shape, in_specs=specs, out_specs=pl.BlockS...  17.3 us
    ppermute x7, starting transfers between devices, on_device(): got = lax.ppermute(held[step % 2], 'grp', ring)  11.7 us
    ppermute x4, waiting for transfers between devices, on_device(): stations = stations + lax.ppermute(stations, 'grp', swap_by(bit))  10.9 us
    ppermute x1, waiting for transfers between devices, on_device(): lax.ppermute(sent_power, 'freq', from_freq(shift)).astype(jnp.float32)  6.3 us
    ppermute x4, starting transfers between devices, on_device(): stations = stations + lax.ppermute(stations, 'grp', swap_by(bit))  4.82 us
    dot_general x1, matrix products, on_device(): jnp.einsum('rsc,rl->scl', jnp.concatenate(kernels, axis=0), jnp.concatena...  4.76 us
    ppermute x1, starting transfers between devices, on_device(): lax.ppermute(sent_power, 'freq', from_freq(shift)).astype(jnp.float32)  3.03 us
  transfers between devices with their start and end apart: 21, of which 10 were waited for; matrix products, arithmetic and copies ran while one was open for 7% of the time, Pallas kernels for 18%

profile of v1, /device:TPU:0, one launch (start us, length us, event | category | flops | bytes accessed | tf_op | source)
XLA Modules:
  0.0 86.7 jit_solution(9076398866465101913)
XLA Ops:
  0.6 1.2 %bitcast_convert_fusion = f32[256,1024]{1,0:T(8,128)S(1)} fusion(bf16[1,256,1024]{2,1,0:T(8,128)(2,1)} %param.3), kind=kLoop, calls=%fused_computation.9 | loop fusion | flops 262144 | bytes 1572864 | tf_op jit(solution)/shard_map/convert_element_type | solution.py:99
  2.0 3.0 %collective-permute-start = (bf16[256,512]{1,0:T(8,128)(2,1)S(1)}, bf16[256,512]{1,0:T(8,128)(2,1)S(1)}, u32[]{:S(2)}, u32[]{:S(2)}) collective-permute-start(bf16[256,512]{1,0:T(8,128)(2,1)S(1)} %fusion.2), channel_id=1, source_target_pairs={{0,1},{1,0},{2,3},{3,2},{4,5},{5,4},{6,7},{7,6},{8,9},{9,8},{10,11... | collective-permute-start | bytes 786440 | tf_op jit(solution)/shard_map/ppermute | solution.py:106
  5.0 6.3 %collective-permute-done = bf16[256,512]{1,0:T(8,128)(2,1)S(1)} collective-permute-done((bf16[256,512]{1,0:T(8,128)(2,1)S(1)}, bf16[256,512]{1,0:T(8,128)(2,1)S(1)}, u32[]{:S(2)}, u32[]{:S(2)}) %collective-permute-start) | collective-permute-done | bytes 262176 | tf_op jit(solution)/shard_map/ppermute | solution.py:106
  11.8 1.8 %collective-permute-start.1 = (bf16[256,1024]{1,0:T(8,128)(2,1)S(1)}, bf16[256,1024]{1,0:T(8,128)(2,1)S(1)}, u32[]{:S(2)}, u32[]{:S(2)}) collective-permute-start(bf16[256,1024]{1,0:T(8,128)(2,1)S(1)} %fusion.refs_2_), channel_id=1, source_target_pairs={{0,8},{2,6},{8,16},{10,2},{16,24},{18,10},{24,28},{26,18},{28,20},... | collective-permute-start | bytes 1572872 | tf_op jit(solution)/shard_map/ppermute | solution.py:151
  14.0 1.6 %collective-permute-start.7 = (bf16[256,1024]{1,0:T(8,128)(2,1)S(1)}, bf16[256,1024]{1,0:T(8,128)(2,1)S(1)}, u32[]{:S(2)}, u32[]{:S(2)}) collective-permute-start(bf16[256,1024]{1,0:T(8,128)(2,1)S(1)} %collective-permute-done.6.refs_3_), channel_id=1, source_target_pairs={{0,8},{2,6},{8,16},{10,2},{16,24},{18,10},{24,28},{26,18},{28,20},... | collective-permute-start | bytes 1572872 | tf_op jit(solution)/shard_map/ppermute | solution.py:151
  15.6 5.4 %collective-permute-done.1.refs_2_ = bf16[256,1024]{1,0:T(8,128)(2,1)S(1)} collective-permute-done((bf16[256,1024]{1,0:T(8,128)(2,1)S(1)}, bf16[256,1024]{1,0:T(8,128)(2,1)S(1)}, u32[]{:S(2)}, u32[]{:S(2)}) %collective-permute-start.1) | collective-permute-done | bytes 524320 | tf_op jit(solution)/shard_map/ppermute | solution.py:151
  21.0 1.8 %collective-permute-start.2 = (bf16[256,1024]{1,0:T(8,128)(2,1)S(1)}, bf16[256,1024]{1,0:T(8,128)(2,1)S(1)}, u32[]{:S(2)}, u32[]{:S(2)}) collective-permute-start(bf16[256,1024]{1,0:T(8,128)(2,1)S(1)} %collective-permute-done.1.refs_2_), channel_id=1, source_target_pairs={{0,8},{2,6},{8,16},{10,2},{16,24},{18,10},{24,28},{26,18},{28,20},... | collective-permute-start | bytes 1572872 | tf_op jit(solution)/shard_map/ppermute | solution.py:151
  23.1 1.1 %collective-permute-done.16 = bf16[16,1024]{1,0:T(8,128)(2,1)S(1)} collective-permute-done((bf16[16,1024]{1,0:T(8,128)(2,1)S(1)}, bf16[16,1024]{1,0:T(8,128)(2,1)S(1)}, u32[]{:S(2)}, u32[]{:S(2)}) %collective-permute-start.16) | collective-permute-done | bytes 32800 | tf_op jit(solution)/shard_map/ppermute | solution.py:118
  24.2 0.5 collective-permute-start.17
  24.8 1.8 %collective-permute-done.7.refs_2_ = bf16[256,1024]{1,0:T(8,128)(2,1)S(1)} collective-permute-done((bf16[256,1024]{1,0:T(8,128)(2,1)S(1)}, bf16[256,1024]{1,0:T(8,128)(2,1)S(1)}, u32[]{:S(2)}, u32[]{:S(2)}) %collective-permute-start.7) | collective-permute-done | bytes 524320 | tf_op jit(solution)/shard_map/ppermute | solution.py:151
  26.6 1.8 %collective-permute-start.8 = (bf16[256,1024]{1,0:T(8,128)(2,1)S(1)}, bf16[256,1024]{1,0:T(8,128)(2,1)}, u32[]{:S(2)}, u32[]{:S(2)}) collective-permute-start(bf16[256,1024]{1,0:T(8,128)(2,1)S(1)} %collective-permute-done.7.refs_2_), channel_id=1, source_target_pairs={{0,8},{2,6},{8,16},{10,2},{16,24},{18,10},{24,28},{26,18},{28,20},... | collective-permute-start | bytes 1572872 | tf_op jit(solution)/shard_map/ppermute | solution.py:151
  28.4 4.2 %collective-permute-done.2.refs_2_ = bf16[256,1024]{1,0:T(8,128)(2,1)S(1)} collective-permute-done((bf16[256,1024]{1,0:T(8,128)(2,1)S(1)}, bf16[256,1024]{1,0:T(8,128)(2,1)S(1)}, u32[]{:S(2)}, u32[]{:S(2)}) %collective-permute-start.2) | collective-permute-done | bytes 524320 | tf_op jit(solution)/shard_map/ppermute | solution.py:151
  32.6 1.4 %collective-permute-start.3 = (bf16[256,1024]{1,0:T(8,128)(2,1)S(1)}, bf16[256,1024]{1,0:T(8,128)(2,1)S(1)}, u32[]{:S(2)}, u32[]{:S(2)}) collective-permute-start(bf16[256,1024]{1,0:T(8,128)(2,1)S(1)} %collective-permute-done.2.refs_2_), channel_id=1, source_target_pairs={{0,8},{2,6},{8,16},{10,2},{16,24},{18,10},{24,28},{26,18},{28,20},... | collective-permute-start | bytes 1572872 | tf_op jit(solution)/shard_map/ppermute | solution.py:151
  34.1 1.6 %collective-permute-start.18 = (bf16[16,1024]{1,0:T(8,128)(2,1)S(1)}, bf16[16,1024]{1,0:T(8,128)(2,1)S(1)}, u32[]{:S(2)}, u32[]{:S(2)}) collective-permute-start(bf16[16,1024]{1,0:T(8,128)(2,1)S(1)} %add.226), channel_id=1, source_target_pairs={{0,8},{2,10},{4,12},{6,14},{8,0},{10,2},{12,4},{14,6},{16,24},{18,... | collective-permute-start | bytes 98312 | tf_op jit(solution)/shard_map/ppermute | solution.py:118
  35.8 7.6 %collective-permute-done.18 = bf16[16,1024]{1,0:T(8,128)(2,1)S(1)} collective-permute-done((bf16[16,1024]{1,0:T(8,128)(2,1)S(1)}, bf16[16,1024]{1,0:T(8,128)(2,1)S(1)}, u32[]{:S(2)}, u32[]{:S(2)}) %collective-permute-start.18) | collective-permute-done | bytes 32800 | tf_op jit(solution)/shard_map/ppermute | solution.py:118
  43.5 2.7 %collective-permute-start.19 = (bf16[16,1024]{1,0:T(8,128)(2,1)S(1)}, bf16[16,1024]{1,0:T(8,128)(2,1)S(1)}, u32[]{:S(2)}, u32[]{:S(2)}) collective-permute-start(bf16[16,1024]{1,0:T(8,128)(2,1)S(1)} %add.227), channel_id=1, source_target_pairs={{0,16},{2,18},{4,20},{6,22},{8,24},{10,26},{12,28},{14,30},{16,0},... | collective-permute-start | bytes 98312 | tf_op jit(solution)/shard_map/ppermute | solution.py:118
  46.2 2.1 %collective-permute-done.19 = bf16[16,1024]{1,0:T(8,128)(2,1)S(1)} collective-permute-done((bf16[16,1024]{1,0:T(8,128)(2,1)S(1)}, bf16[16,1024]{1,0:T(8,128)(2,1)S(1)}, u32[]{:S(2)}, u32[]{:S(2)}) %collective-permute-start.19) | collective-permute-done | bytes 32800 | tf_op jit(solution)/shard_map/ppermute | solution.py:118
  49.0 2.5 %collective-permute-start.9 = (bf16[256,1024]{1,0:T(8,128)(2,1)}, bf16[256,1024]{1,0:T(8,128)(2,1)S(1)}, u32[]{:S(2)}, u32[]{:S(2)}) collective-permute-start(bf16[256,1024]{1,0:T(8,128)(2,1)} %collective-permute-done.8.refs_2_), channel_id=1, source_target_pairs={{0,8},{2,6},{8,16},{10,2},{16,24},{18,10},{24,28},{26,18},{28,20},... | collective-permute-start | bytes 1572872 | tf_op jit(solution)/shard_map/ppermute | solution.py:151
  51.5 0.7 collective-permute-start.4
  52.4 1.6 %collective-permute-start.20 = (f32[32,256]{1,0:T(8,128)S(1)}, f32[32,256]{1,0:T(8,128)S(1)}, u32[]{:S(2)}, u32[]{:S(2)}) collective-permute-start(f32[32,256]{1,0:T(8,128)S(1)} %convolution_multiply_fusion.1), channel_id=1, source_target_pairs={{0,1},{1,0},{2,3},{3,2},{4,5},{5,4},{6,7},{7,6},{8,9},{9,8},{10,11... | collective-permute-start | bytes 98312 | tf_op jit(solution)/shard_map/ppermute | solution.py:129
  54.1 2.3 %collective-permute-done.20 = f32[32,256]{1,0:T(8,128)S(1)} collective-permute-done((f32[32,256]{1,0:T(8,128)S(1)}, f32[32,256]{1,0:T(8,128)S(1)}, u32[]{:S(2)}, u32[]{:S(2)}) %collective-permute-start.20) | collective-permute-done | bytes 32800 | tf_op jit(solution)/shard_map/ppermute | solution.py:129
  57.0 1.7 %collective-permute-done.9.refs_2_ = bf16[256,1024]{1,0:T(8,128)(2,1)S(1)} collective-permute-done((bf16[256,1024]{1,0:T(8,128)(2,1)}, bf16[256,1024]{1,0:T(8,128)(2,1)S(1)}, u32[]{:S(2)}, u32[]{:S(2)}) %collective-permute-start.9) | collective-permute-done | bytes 524320 | tf_op jit(solution)/shard_map/ppermute | solution.py:151
  58.7 5.6 %collective-permute-done.4.refs_2_ = bf16[256,1024]{1,0:T(8,128)(2,1)S(1)} collective-permute-done((bf16[256,1024]{1,0:T(8,128)(2,1)S(1)}, bf16[256,1024]{1,0:T(8,128)(2,1)S(1)}, u32[]{:S(2)}, u32[]{:S(2)}) %collective-permute-start.4) | collective-permute-done | bytes 524320 | tf_op jit(solution)/shard_map/ppermute | solution.py:151
  64.5 4.8 %convolution_multiply_fusion = f32[16,256,128]{2,1,0:T(8,128)} fusion(f32[2,16,256]{2,0,1:T(2,128)S(1)} %copy.13, f32[2,16,256]{2,0,1:T(2,128)S(1)} %copy.12, f32[1,128]{1,0:T(1,128)S(1)} %get-tuple-element.6, f32[1,128]{1,0:T(1,128)S(1)} %get-tuple-element.9, f32[1,128]{1,0:T(1,128)S(1)} %get-tuple-element.7, f32[1,128]{1,0:T(1,128)S(1)} %get-tuple-element.8), kind=kOutput, calls=%fused_computation | convolution fusion | flops 25708032 | bytes 2164736 | tf_op jit(solution)/shard_map/rsc,rl->scl/dot_general | solution.py:134
  69.3 2.1 %shard_map.50.refs_4_ = bf16[2,256,4096]{2,1,0:T(8,128)(2,1)} custom-call(s32[2]{0:T(128)S(1)} %pad_add_fusion.7.refs_0_, bf16[512,1024]{1,0:T(8,128)(2,1)S(1)} %maximum_maximum_fusion.refs_1_, bf16[256,1024]{1,0:T(8,128)(2,1)S(1)} %fusion.refs_2_, bf16[256,1024]{1,0:T(8,128)(2,1)S(1)} %collective-permute-done.6.refs_3_), custom_call_target="tpu_custom_call" | custom-call | flops 536870912 | bytes 2097152 | tf_op jit(solution)/shard_map/pallas_call | solution.py:66
  71.4 2.1 %shard_map.51.refs_4_ = bf16[2,256,4096]{2,1,0:T(8,128)(2,1)} custom-call(s32[2]{0:T(128)S(1)} %pad_add_fusion.6.refs_0_, bf16[512,1024]{1,0:T(8,128)(2,1)S(1)} %maximum_maximum_fusion.refs_1_, bf16[256,1024]{1,0:T(8,128)(2,1)S(1)} %collective-permute-done.1.refs_2_, ...), custom_call_target="tpu_custom_call", output_to_operand_aliasing={{}: (4, {})} | custom-call | flops 536870912 | bytes 2097152 | tf_op jit(solution)/shard_map/pallas_call | solution.py:66
  73.5 2.1 %shard_map.52.refs_4_ = bf16[2,256,4096]{2,1,0:T(8,128)(2,1)} custom-call(s32[2]{0:T(128)S(1)} %pad_add_fusion.5.refs_0_, bf16[512,1024]{1,0:T(8,128)(2,1)S(1)} %maximum_maximum_fusion.refs_1_, bf16[256,1024]{1,0:T(8,128)(2,1)S(1)} %collective-permute-done.7.refs_2_, ...), custom_call_target="tpu_custom_call", output_to_operand_aliasing={{}: (4, {})} | custom-call | flops 536870912 | bytes 2097152 | tf_op jit(solution)/shard_map/pallas_call | solution.py:66
  75.6 2.1 %shard_map.53.refs_4_ = bf16[2,256,4096]{2,1,0:T(8,128)(2,1)} custom-call(s32[2]{0:T(128)S(1)} %pad_add_fusion.4.refs_0_, bf16[512,1024]{1,0:T(8,128)(2,1)S(1)} %maximum_maximum_fusion.refs_1_, bf16[256,1024]{1,0:T(8,128)(2,1)S(1)} %collective-permute-done.2.refs_2_, ...), custom_call_target="tpu_custom_call", output_to_operand_aliasing={{}: (4, {})} | custom-call | flops 536870912 | bytes 2097152 | tf_op jit(solution)/shard_map/pallas_call | solution.py:66
  77.7 2.6 %shard_map.54.refs_4_ = bf16[2,256,4096]{2,1,0:T(8,128)(2,1)} custom-call(s32[2]{0:T(128)S(1)} %pad_add_fusion.3.refs_0_, bf16[512,1024]{1,0:T(8,128)(2,1)S(1)} %maximum_maximum_fusion.refs_1_, bf16[256,1024]{1,0:T(8,128)(2,1)} %collective-permute-done.8.refs_2_, ...), custom_call_target="tpu_custom_call", output_to_operand_aliasing={{}: (4, {})} | custom-call | flops 536870912 | bytes 2097152 | tf_op jit(solution)/shard_map/pallas_call | solution.py:66
  80.3 2.1 %shard_map.55.refs_4_ = bf16[2,256,4096]{2,1,0:T(8,128)(2,1)} custom-call(s32[2]{0:T(128)S(1)} %pad_add_fusion.2.refs_0_, bf16[512,1024]{1,0:T(8,128)(2,1)S(1)} %maximum_maximum_fusion.refs_1_, bf16[256,1024]{1,0:T(8,128)(2,1)S(1)} %collective-permute-done.3.refs_2_, ...), custom_call_target="tpu_custom_call", output_to_operand_aliasing={{}: (4, {})} | custom-call | flops 536870912 | bytes 2097152 | tf_op jit(solution)/shard_map/pallas_call | solution.py:66
  82.5 2.1 %shard_map.56.refs_4_ = bf16[2,256,4096]{2,1,0:T(8,128)(2,1)} custom-call(s32[2]{0:T(128)S(1)} %pad_add_fusion.1.refs_0_, bf16[512,1024]{1,0:T(8,128)(2,1)S(1)} %maximum_maximum_fusion.refs_1_, bf16[256,1024]{1,0:T(8,128)(2,1)S(1)} %collective-permute-done.9.refs_2_, ...), custom_call_target="tpu_custom_call", output_to_operand_aliasing={{}: (4, {})} | custom-call | flops 536870912 | bytes 2097152 | tf_op jit(solution)/shard_map/pallas_call | solution.py:66
  84.6 2.1 %shard_map.57 = bf16[2,256,4096]{2,1,0:T(8,128)(2,1)} custom-call(s32[2]{0:T(128)S(1)} %pad_add_fusion.refs_0_, bf16[512,1024]{1,0:T(8,128)(2,1)S(1)} %maximum_maximum_fusion.refs_1_, bf16[256,1024]{1,0:T(8,128)(2,1)S(1)} %collective-permute-done.4.refs_2_, bf16[256,1024]{1,0:T(8,128)(2,1)S(1)} %collective-permute-done.5.refs_3_, ...), custom_call_target="tpu_custom_call", output_to_operand_aliasing={{}: (4, {})} | custom-call | flops 536870912 | bytes 2097152 | tf_op jit(solution)/shard_map/pallas_call | solution.py:66
  (51 shorter events, 3.1 us)
Async XLA Ops:
  0.6 10.7 %copy-start.1 = (s32[256,512]{1,0:T(8,128)S(1)}, s32[256,512]{1,0:T(8,128)}, u32[]{:S(2)}) copy-start(s32[256,512]{1,0:T(8,128)} %param.4) | copy-start | bytes 1572868
  1.9 9.7 %copy-start = (bf16[1,256,1024]{2,1,0:T(8,128)(2,1)S(1)}, bf16[1,256,1024]{2,1,0:T(8,128)(2,1)}, u32[]{:S(2)}) copy-start(bf16[1,256,1024]{2,1,0:T(8,128)(2,1)} %param.3) | copy-start | bytes 1572868
  2.0 9.3 %collective-permute-start = (bf16[256,512]{1,0:T(8,128)(2,1)S(1)}, bf16[256,512]{1,0:T(8,128)(2,1)S(1)}, u32[]{:S(2)}, u32[]{:S(2)}) collective-permute-start(bf16[256,512]{1,0:T(8,128)(2,1)S(1)} %fusion.2), channel_id=1, source_target_pairs={{0,1},{1,0},{2,3},{3,2},{4,5},{5,4},{6,7},{7,6},{8,9},{9,8},{10,11... | collective-permute-start | bytes 786440 | tf_op jit(solution)/shard_map/ppermute | solution.py:106
  5.0 17.8 %copy-start.2 = (s32[16]{0:T(128)S(1)}, s32[16]{0:T(128)}, u32[]{:S(2)}) copy-start(s32[16]{0:T(128)} %param.5) | copy-start | bytes 196
  11.7 2.3 %collective-permute-start.6 = (bf16[256,1024]{1,0:T(8,128)(2,1)S(1)}, bf16[256,1024]{1,0:T(8,128)(2,1)S(1)}, u32[]{:S(2)}, u32[]{:S(2)}) collective-permute-start(bf16[256,1024]{1,0:T(8,128)(2,1)S(1)} %fusion.refs_2_), channel_id=1, source_target_pairs={{0,2},{2,0},{4,6},{6,4},{8,10},{10,8},{12,14},{14,12},{16,18},{18,... | collective-permute-start | bytes 1572872 | tf_op jit(solution)/shard_map/ppermute | solution.py:144
  11.8 9.2 %collective-permute-start.1 = (bf16[256,1024]{1,0:T(8,128)(2,1)S(1)}, bf16[256,1024]{1,0:T(8,128)(2,1)S(1)}, u32[]{:S(2)}, u32[]{:S(2)}) collective-permute-start(bf16[256,1024]{1,0:T(8,128)(2,1)S(1)} %fusion.refs_2_), channel_id=1, source_target_pairs={{0,8},{2,6},{8,16},{10,2},{16,24},{18,10},{24,28},{26,18},{28,20},... | collective-permute-start | bytes 1572872 | tf_op jit(solution)/shard_map/ppermute | solution.py:151
  14.0 12.6 %collective-permute-start.7 = (bf16[256,1024]{1,0:T(8,128)(2,1)S(1)}, bf16[256,1024]{1,0:T(8,128)(2,1)S(1)}, u32[]{:S(2)}, u32[]{:S(2)}) collective-permute-start(bf16[256,1024]{1,0:T(8,128)(2,1)S(1)} %collective-permute-done.6.refs_3_), channel_id=1, source_target_pairs={{0,8},{2,6},{8,16},{10,2},{16,24},{18,10},{24,28},{26,18},{28,20},... | collective-permute-start | bytes 1572872 | tf_op jit(solution)/shard_map/ppermute | solution.py:151
  21.0 11.6 %collective-permute-start.2 = (bf16[256,1024]{1,0:T(8,128)(2,1)S(1)}, bf16[256,1024]{1,0:T(8,128)(2,1)S(1)}, u32[]{:S(2)}, u32[]{:S(2)}) collective-permute-start(bf16[256,1024]{1,0:T(8,128)(2,1)S(1)} %collective-permute-done.1.refs_2_), channel_id=1, source_target_pairs={{0,8},{2,6},{8,16},{10,2},{16,24},{18,10},{24,28},{26,18},{28,20},... | collective-permute-start | bytes 1572872 | tf_op jit(solution)/shard_map/ppermute | solution.py:151
  23.0 1.2 %collective-permute-start.16 = (bf16[16,1024]{1,0:T(8,128)(2,1)S(1)}, bf16[16,1024]{1,0:T(8,128)(2,1)S(1)}, u32[]{:S(2)}, u32[]{:S(2)}) collective-permute-start(bf16[16,1024]{1,0:T(8,128)(2,1)S(1)} %convolution_convert_fusion), channel_id=1, source_target_pairs={{0,2},{2,0},{4,6},{6,4},{8,10},{10,8},{12,14},{14,12},{16,18},{18,... | collective-permute-start | bytes 98312 | tf_op jit(solution)/shard_map/ppermute | solution.py:118
  24.2 9.9 %collective-permute-start.17 = (bf16[16,1024]{1,0:T(8,128)(2,1)S(1)}, bf16[16,1024]{1,0:T(8,128)(2,1)S(1)}, u32[]{:S(2)}, u32[]{:S(2)}) collective-permute-start(bf16[16,1024]{1,0:T(8,128)(2,1)S(1)} %add.225), channel_id=1, source_target_pairs={{0,4},{2,6},{4,0},{6,2},{8,12},{10,14},{12,8},{14,10},{16,20},{18,... | collective-permute-start | bytes 98312 | tf_op jit(solution)/shard_map/ppermute | solution.py:118
  26.6 22.4 %collective-permute-start.8 = (bf16[256,1024]{1,0:T(8,128)(2,1)S(1)}, bf16[256,1024]{1,0:T(8,128)(2,1)}, u32[]{:S(2)}, u32[]{:S(2)}) collective-permute-start(bf16[256,1024]{1,0:T(8,128)(2,1)S(1)} %collective-permute-done.7.refs_2_), channel_id=1, source_target_pairs={{0,8},{2,6},{8,16},{10,2},{16,24},{18,10},{24,28},{26,18},{28,20},... | collective-permute-start | bytes 1572872 | tf_op jit(solution)/shard_map/ppermute | solution.py:151
  32.6 18.9 %collective-permute-start.3 = (bf16[256,1024]{1,0:T(8,128)(2,1)S(1)}, bf16[256,1024]{1,0:T(8,128)(2,1)S(1)}, u32[]{:S(2)}, u32[]{:S(2)}) collective-permute-start(bf16[256,1024]{1,0:T(8,128)(2,1)S(1)} %collective-permute-done.2.refs_2_), channel_id=1, source_target_pairs={{0,8},{2,6},{8,16},{10,2},{16,24},{18,10},{24,28},{26,18},{28,20},... | collective-permute-start | bytes 1572872 | tf_op jit(solution)/shard_map/ppermute | solution.py:151
  34.1 9.4 %collective-permute-start.18 = (bf16[16,1024]{1,0:T(8,128)(2,1)S(1)}, bf16[16,1024]{1,0:T(8,128)(2,1)S(1)}, u32[]{:S(2)}, u32[]{:S(2)}) collective-permute-start(bf16[16,1024]{1,0:T(8,128)(2,1)S(1)} %add.226), channel_id=1, source_target_pairs={{0,8},{2,10},{4,12},{6,14},{8,0},{10,2},{12,4},{14,6},{16,24},{18,... | collective-permute-start | bytes 98312 | tf_op jit(solution)/shard_map/ppermute | solution.py:118
  43.5 4.9 %collective-permute-start.19 = (bf16[16,1024]{1,0:T(8,128)(2,1)S(1)}, bf16[16,1024]{1,0:T(8,128)(2,1)S(1)}, u32[]{:S(2)}, u32[]{:S(2)}) collective-permute-start(bf16[16,1024]{1,0:T(8,128)(2,1)S(1)} %add.227), channel_id=1, source_target_pairs={{0,16},{2,18},{4,20},{6,22},{8,24},{10,26},{12,28},{14,30},{16,0},... | collective-permute-start | bytes 98312 | tf_op jit(solution)/shard_map/ppermute | solution.py:118
  48.4 8.0 %collective-permute-start.15 = (bf16[256,1024]{1,0:T(8,128)(2,1)S(1)}, bf16[256,1024]{1,0:T(8,128)(2,1)S(1)}, u32[]{:S(2)}, u32[]{:S(2)}) collective-permute-start(bf16[256,1024]{1,0:T(8,128)(2,1)S(1)} %collective-permute-done.1.refs_2_), channel_id=1, source_target_pairs={{0,2},{2,0},{4,6},{6,4},{8,10},{10,8},{12,14},{14,12},{16,18},{18,... | collective-permute-start | bytes 1572872 | tf_op jit(solution)/shard_map/ppermute | solution.py:153
  48.5 8.5 %collective-permute-start.14 = (bf16[256,1024]{1,0:T(8,128)(2,1)S(1)}, bf16[256,1024]{1,0:T(8,128)(2,1)S(1)}, u32[]{:S(2)}, u32[]{:S(2)}) collective-permute-start(bf16[256,1024]{1,0:T(8,128)(2,1)S(1)} %collective-permute-done.7.refs_2_), channel_id=1, source_target_pairs={{0,2},{2,0},{4,6},{6,4},{8,10},{10,8},{12,14},{14,12},{16,18},{18,... | collective-permute-start | bytes 1572872 | tf_op jit(solution)/shard_map/ppermute | solution.py:153
  49.0 9.8 %collective-permute-start.9 = (bf16[256,1024]{1,0:T(8,128)(2,1)}, bf16[256,1024]{1,0:T(8,128)(2,1)S(1)}, u32[]{:S(2)}, u32[]{:S(2)}) collective-permute-start(bf16[256,1024]{1,0:T(8,128)(2,1)} %collective-permute-done.8.refs_2_), channel_id=1, source_target_pairs={{0,8},{2,6},{8,16},{10,2},{16,24},{18,10},{24,28},{26,18},{28,20},... | collective-permute-start | bytes 1572872 | tf_op jit(solution)/shard_map/ppermute | solution.py:151
  51.5 12.9 %collective-permute-start.4 = (bf16[256,1024]{1,0:T(8,128)(2,1)S(1)}, bf16[256,1024]{1,0:T(8,128)(2,1)S(1)}, u32[]{:S(2)}, u32[]{:S(2)}) collective-permute-start(bf16[256,1024]{1,0:T(8,128)(2,1)S(1)} %collective-permute-done.3.refs_2_), channel_id=1, source_target_pairs={{0,8},{2,6},{8,16},{10,2},{16,24},{18,10},{24,28},{26,18},{28,20},... | collective-permute-start | bytes 1572872 | tf_op jit(solution)/shard_map/ppermute | solution.py:151
  52.4 4.0 %collective-permute-start.20 = (f32[32,256]{1,0:T(8,128)S(1)}, f32[32,256]{1,0:T(8,128)S(1)}, u32[]{:S(2)}, u32[]{:S(2)}) collective-permute-start(f32[32,256]{1,0:T(8,128)S(1)} %convolution_multiply_fusion.1), channel_id=1, source_target_pairs={{0,1},{1,0},{2,3},{3,2},{4,5},{5,4},{6,7},{7,6},{8,9},{9,8},{10,11... | collective-permute-start | bytes 98312 | tf_op jit(solution)/shard_map/ppermute | solution.py:129
  56.4 19.2 %collective-permute-start.13 = (bf16[256,1024]{1,0:T(8,128)(2,1)S(1)}, bf16[256,1024]{1,0:T(8,128)(2,1)S(1)}, u32[]{:S(2)}, u32[]{:S(2)}) collective-permute-start(bf16[256,1024]{1,0:T(8,128)(2,1)S(1)} %collective-permute-done.2.refs_2_), channel_id=1, source_target_pairs={{0,2},{2,0},{4,6},{6,4},{8,10},{10,8},{12,14},{14,12},{16,18},{18,... | collective-permute-start | bytes 1572872 | tf_op jit(solution)/shard_map/ppermute | solution.py:153
  56.4 21.3 %collective-permute-start.12 = (bf16[256,1024]{1,0:T(8,128)(2,1)}, bf16[256,1024]{1,0:T(8,128)(2,1)S(1)}, u32[]{:S(2)}, u32[]{:S(2)}) collective-permute-start(bf16[256,1024]{1,0:T(8,128)(2,1)} %collective-permute-done.8.refs_2_), channel_id=1, source_target_pairs={{0,2},{2,0},{4,6},{6,4},{8,10},{10,8},{12,14},{14,12},{16,18},{18,... | collective-permute-start | bytes 1572872 | tf_op jit(solution)/shard_map/ppermute | solution.py:153
  56.9 23.4 %collective-permute-start.11 = (bf16[256,1024]{1,0:T(8,128)(2,1)S(1)}, bf16[256,1024]{1,0:T(8,128)(2,1)S(1)}, u32[]{:S(2)}, u32[]{:S(2)}) collective-permute-start(bf16[256,1024]{1,0:T(8,128)(2,1)S(1)} %collective-permute-done.3.refs_2_), channel_id=1, source_target_pairs={{0,2},{2,0},{4,6},{6,4},{8,10},{10,8},{12,14},{14,12},{16,18},{18,... | collective-permute-start | bytes 1572872 | tf_op jit(solution)/shard_map/ppermute | solution.py:153
  58.7 23.7 %collective-permute-start.10 = (bf16[256,1024]{1,0:T(8,128)(2,1)S(1)}, bf16[256,1024]{1,0:T(8,128)(2,1)S(1)}, u32[]{:S(2)}, u32[]{:S(2)}) collective-permute-start(bf16[256,1024]{1,0:T(8,128)(2,1)S(1)} %collective-permute-done.9.refs_2_), channel_id=1, source_target_pairs={{0,2},{2,0},{4,6},{6,4},{8,10},{10,8},{12,14},{14,12},{16,18},{18,... | collective-permute-start | bytes 1572872 | tf_op jit(solution)/shard_map/ppermute | solution.py:153
  64.4 20.2 %collective-permute-start.5 = (bf16[256,1024]{1,0:T(8,128)(2,1)S(1)}, bf16[256,1024]{1,0:T(8,128)(2,1)S(1)}, u32[]{:S(2)}, u32[]{:S(2)}) collective-permute-start(bf16[256,1024]{1,0:T(8,128)(2,1)S(1)} %collective-permute-done.4.refs_2_), channel_id=1, source_target_pairs={{0,2},{2,0},{4,6},{6,4},{8,10},{10,8},{12,14},{14,12},{16,18},{18,... | collective-permute-start | bytes 1572872 | tf_op jit(solution)/shard_map/ppermute | solution.py:153

commit v2 on v0

v2 whole, which is shorter than its diff:
```python
import functools
import math

import jax
import jax.numpy as jnp
from jax import lax
from jax.experimental import pallas as pl
from jax.experimental.pallas import tpu as pltpu
from jax.sharding import PartitionSpec as P

LAGS = 256
ROWS_T = (((1,), (1,)), ((), ()))


def device_of(place, core, chips):
    place %= chips
    z, x = (place, 0) if place < chips // 2 else (chips - 1 - place, 1)
    return z * 4 + x * 2 + core


def place_of(device, chips):
    z, x = device // 4, device // 2 % 2
    return z if x == 0 else chips - 1 - z


def ring_pairs(group_size):
    chips = group_size // 2
    return [
        (device, device_of(place_of(device, chips) + 1 - 2 * (device % 2), device % 2, chips)) for device in range(group_size)
    ]


def block_of(place, core, chips):
    place = lax.rem(place + chips, chips)
    half = chips // 2
    return jnp.where(place < half, place * 4, (chips - 1 - place) * 4 + 2) + core


def own_block():
    return [lax.axis_index("grp")]


def sibling_block():
    group_index = lax.axis_index("grp")
    return [group_index + 1 - 2 * lax.rem(group_index, 2)]


def ring_blocks(step, chips):
    group_index = lax.axis_index("grp")
    core = lax.rem(group_index, 2)
    z, x = group_index // 4, lax.rem(group_index // 2, 2)
    place = jnp.where(x == 0, z, chips - 1 - z)
    back = (step // 2 + 1) * (1 - 2 * core)
    kept = core if step % 2 == 0 else 1 - core
    return [block_of(place - back, kept, chips), block_of(place + back, 1 - kept, chips)]


def cost(microseconds):
    return pl.CostEstimate(flops=int(microseconds * 1.15e9), bytes_accessed=0, transcendentals=0)


def split(values):
    terms = []
    for _ in range(3):
        term = lax.reduce_precision(values, 8, 7)
        terms.append(term.astype(jnp.bfloat16))
        values = values - term
    return terms


def band_powers(raw, chunks):
    rows, width = raw.shape[0], raw.shape[1] // 2

    def body(raw_ref, raw_out, *power_outs):
        for k, power_out in enumerate(power_outs):
            part = raw_ref[k * rows // chunks : (k + 1) * rows // chunks, :].astype(jnp.float32)
            power_out[...] = (part[:, :width] * part[:, :width] + part[:, width:] * part[:, width:]).astype(jnp.bfloat16)
        raw_out[...] = raw_ref[...]

    vmem = pl.BlockSpec(memory_space=pltpu.VMEM)
    return pl.pallas_call(
        body,
        out_shape=[jax.ShapeDtypeStruct(raw.shape, jnp.bfloat16)]
        + [jax.ShapeDtypeStruct((rows // chunks, width), jnp.bfloat16)] * chunks,
        in_specs=[vmem],
        out_specs=[vmem] * (1 + chunks),
        compiler_params=pltpu.CompilerParams(vmem_limit_bytes=8 * 2**20),
        cost_estimate=cost(0.1),
    )(raw)


def prepare(valid, station_index, after):
    rows, width = valid.shape
    stations = station_index.shape[0]

    def body(index_ref, valid_ref, _, valid_out, numbers_out, valid_held, index_held, sems):
        copies = [
            pltpu.make_async_copy(valid_ref, valid_held, sems.at[0]),
            pltpu.make_async_copy(index_ref, index_held, sems.at[1]),
        ]
        for copy in copies:
            copy.start()
        copies[1].wait()
        place = lax.broadcasted_iota(jnp.int32, (stations, rows), 0)
        numbers = jnp.zeros((stations, rows), jnp.int32)
        for k in range(stations):
            numbers = jnp.where(place == k, index_held[k], numbers)
        numbers_out[...] = numbers
        copies[0].wait()
        valid_out[...] = valid_held[...].astype(jnp.bfloat16)

    vmem, anywhere = pl.BlockSpec(memory_space=pltpu.VMEM), pl.BlockSpec(memory_space=pl.ANY)
    return pl.pallas_call(
        body,
        out_shape=[jax.ShapeDtypeStruct(valid.shape, jnp.bfloat16), jax.ShapeDtypeStruct((stations, rows), jnp.int32)],
        in_specs=[anywhere] * 3,
        out_specs=[vmem] * 2,
        scratch_shapes=[
            pltpu.VMEM(valid.shape, jnp.int32),
            pltpu.SMEM(station_index.shape, jnp.int32),
            pltpu.SemaphoreType.DMA((2,)),
        ],
        compiler_params=pltpu.CompilerParams(vmem_limit_bytes=8 * 2**20),
        cost_estimate=cost(0.3),
    )(station_index, valid, after)


def whiten(raw, valid, received, chunk, chunks, total_bins):
    rows, width = raw.shape[0] // chunks, raw.shape[1] // 2

    def body(raw_ref, valid_ref, *refs):
        part = raw_ref[...].astype(jnp.float32)
        real, imag = part[:, :width], part[:, width:]
        power = real * real + imag * imag
        for ref in refs[:-1]:
            power = power + ref[...].astype(jnp.float32)
        factor = lax.rsqrt(power / total_bins + 1e-05) * valid_ref[...].astype(jnp.float32)
        refs[-1][:, :width] = (real * factor).astype(jnp.bfloat16)
        refs[-1][:, width:] = (imag * factor).astype(jnp.bfloat16)

    vmem = pl.BlockSpec(memory_space=pltpu.VMEM)
    return pl.pallas_call(
        body,
        grid=(1,),
        out_shape=jax.ShapeDtypeStruct((rows, 2 * width), jnp.bfloat16),
        in_specs=[pl.BlockSpec((rows, 2 * width), lambda i: (chunk, 0)), pl.BlockSpec((rows, width), lambda i: (chunk, 0))]
        + [vmem] * len(received),
        out_specs=pl.BlockSpec((rows, 2 * width), lambda i: (0, 0)),
        compiler_params=pltpu.CompilerParams(vmem_limit_bytes=8 * 2**20),
        cost_estimate=cost(0.15),
    )(raw, valid, *received)


def cross_blocks(left, blocks, places, cross, total, scaling, numbers=None, stations=None, microseconds=0.0):
    rows, depth = blocks[0].shape
    count = len(blocks)
    vmem, anywhere = pl.BlockSpec(memory_space=pltpu.VMEM), pl.BlockSpec(memory_space=pl.ANY)
    operands = [left, *blocks]
    specs = [vmem] * len(operands)
    for more in (numbers, stations):
        if more is not None:
            operands.append(more)
            specs.append(vmem)
    aliases = {}
    if cross is not None:
        aliases = {len(operands): 0}
        operands.append(cross)
        specs.append(anywhere)
    shapes, out_specs = [jax.ShapeDtypeStruct((2, rows, total), jnp.bfloat16)], [anywhere]
    if numbers is not None:
        shapes.append(jax.ShapeDtypeStruct((numbers.shape[0], depth), jnp.bfloat16))
        out_specs.append(vmem)

    def body(left_ref, *refs):
        held, sems = refs[-2:]
        out_ref = refs[len(operands) - 1]
        copies, picked = [], None
        for k, place in enumerate(places()):
            product = lax.dot_general(left_ref[...], refs[k][...], ROWS_T, preferred_element_type=jnp.float32)
            held[k] = (product * scaling).astype(jnp.bfloat16).reshape(2, rows, rows)
            start = pl.multiple_of(place * rows, rows)
            copies.append(pltpu.make_async_copy(held.at[k], out_ref.at[:, :, pl.ds(start, rows)], sems.at[k]))
            copies[k].start()
            if numbers is not None:
                wanted = refs[count][...] - start
                selector = (wanted == lax.broadcasted_iota(jnp.int32, wanted.shape, 1)).astype(jnp.bfloat16)
                found = jnp.dot(selector, refs[k][...], preferred_element_type=jnp.float32)
                picked = found if picked is None else picked + found
        if numbers is not None:
            if stations is not None:
                picked = picked + refs[count + 1][...].astype(jnp.float32)
            refs[len(operands)][...] = picked.astype(jnp.bfloat16)
        for copy in copies:
            copy.wait()

    out = pl.pallas_call(
        body,
        out_shape=shapes,
        in_specs=specs,
        out_specs=out_specs,
        scratch_shapes=[pltpu.VMEM((count, 2, rows, rows), jnp.bfloat16), pltpu.SemaphoreType.DMA((count,))],
        input_output_aliases=aliases,
        compiler_params=pltpu.CompilerParams(vmem_limit_bytes=8 * 2**20),
        cost_estimate=cost(microseconds),
    )(*operands)
    return out if numbers is not None else out[0]


def make_on_device(group_size, freq_size):
    chips = group_size // 2
    ring = ring_pairs(group_size)

    def swap_by(bit):
        return [(g, g ^ bit) for g in range(group_size)]

    def swap(block, pieces=2):
        rows = block.shape[0] // pieces
        got = [lax.ppermute(block[k * rows : (k + 1) * rows], "grp", swap_by(1)) for k in range(pieces)]
        return got[0] if pieces == 1 else jnp.concatenate(got, axis=0)

    def from_freq(shift):
        return [(f, (f + shift) % freq_size) for f in range(freq_size)]

    def on_device(spectra, valid, station_index):
        bin_count, chan_count, double_width = spectra.shape
        assert bin_count == 1
        window_count = double_width // 2
        freq_index = lax.axis_index("freq")
        total_chans = chan_count * group_size
        total_bins = bin_count * freq_size
        scaling = 1.0 / math.sqrt(window_count)

        def to_kernel(stations, whitened):
            station_left = jnp.concatenate(
                [stations, jnp.concatenate([stations[:, window_count:], -stations[:, :window_count]], axis=1)], axis=0
            )
            kernel = lax.dot_general(station_left, whitened, ROWS_T, preferred_element_type=jnp.float32) * scaling
            kernels = [kernel]
            for shift in range(1, freq_size):
                kernels.append(lax.ppermute(kernel, "freq", from_freq(shift)))
            return kernels

        def to_lags(kernels):
            lags_here = LAGS // freq_size
            lag_values = (freq_index * lags_here + jnp.arange(lags_here, dtype=jnp.int32)).astype(jnp.float32)
            tables = []
            for shift in range(freq_size):
                bin_value = lax.rem(freq_index - shift + freq_size, freq_size).astype(jnp.float32) + 1.0
                phase = math.pi * bin_value * lag_values / LAGS
                tables += [jnp.cos(phase), -jnp.sin(phase)]
            table = jnp.stack(tables) / math.sqrt(total_bins)
            kernels = jnp.concatenate(kernels, axis=0).reshape(2 * freq_size, station_index.shape[0], chan_count)
            parts, table_parts = split(kernels), split(table)
            pairs = [(0, 0), (0, 1), (1, 0), (0, 2), (1, 1), (2, 0)]
            return jnp.einsum(
                "rsc,rl->scl",
                jnp.concatenate([parts[i] for i, _ in pairs], axis=0),
                jnp.concatenate([table_parts[j] for _, j in pairs], axis=0),
                preferred_element_type=jnp.float32,
            )

        chunks = 2
        raw, *powers = band_powers(spectra[0], chunks)
        valid, numbers = prepare(valid, station_index, raw)
        received = [[lax.ppermute(power, "freq", from_freq(shift)) for shift in range(1, freq_size)] for power in powers]

        parts = [whiten(raw, valid, received[0], 0, chunks, total_bins)]
        flying_parts = [lax.ppermute(parts[0], "grp", ring)]
        second, _ = lax.optimization_barrier((received[1], parts[0]))
        parts.append(whiten(raw, valid, second, 1, chunks, total_bins))
        flying_parts.append(lax.ppermute(parts[1], "grp", ring))
        whitened = jnp.concatenate(parts, axis=0)
        swapped = swap(whitened)
        flying = [None, lax.ppermute(swapped, "grp", ring)]
        left = jnp.concatenate(
            [whitened, jnp.concatenate([whitened[:, window_count:], -whitened[:, :window_count]], axis=1)], axis=0
        )
        later, flying_parts = lax.optimization_barrier((whitened, flying_parts))
        flying[0] = jnp.concatenate(flying_parts, axis=0)
        cross, stations = cross_blocks(left, [later], own_block, None, total_chans, scaling, numbers, None, 4.0)

        steps = chips - 1
        waiting, places = [], sibling_block
        for step in range(steps):
            arrived, cross, stations, swapped = lax.optimization_barrier((flying[step], cross, stations, swapped))
            if step + 2 < steps:
                flying.append(lax.ppermute(arrived, "grp", ring))
            next_swapped = swap(arrived)
            if step + 1 < steps:
                cross, stations = cross_blocks(left, [*waiting, swapped], places, cross, total_chans, scaling, numbers, stations)
            waiting, swapped, places = [arrived], next_swapped, functools.partial(ring_blocks, step, chips)
            if step + 2 == steps:
                cross, stations = cross_blocks(left, [*waiting, swapped], places, cross, total_chans, scaling, numbers, stations)
        cross, stations = cross_blocks(left, waiting, lambda: places()[:1], cross, total_chans, scaling, numbers, stations)
        cross, stations = cross_blocks(left, [swapped], lambda: places()[1:], cross, total_chans, scaling, numbers, stations)
        station_gather = to_lags(to_kernel(stations, whitened))
        return (cross[None], station_gather)

    return on_device


def solution(mesh):
    placed = (P("freq", "grp", None), P("grp", None), P())
    return jax.shard_map(
        make_on_device(mesh.shape["grp"], mesh.shape["freq"]),
        mesh=mesh,
        in_specs=placed,
        out_specs=(P("freq", None, "grp", None), P(None, "grp", "freq")),
        check_vma=False,
    )
```

time: 183 us -> 67.6 us (0.37)
  blocking collectives: 63 us -> 0 us
  waiting for transfers between devices: 82.9 us -> 21.7 us
  starting transfers between devices: 0.12 us -> 23.4 us
  matrix products: 18.7 us -> 2.05 us
  Pallas kernels: 0 us -> 15.3 us
  between operations: 13.8 us -> 1.12 us
  other arithmetic: 4.43 us -> 0.64 us
  local copies, waits for them, and re-layouts: 0.01 us -> 3.14 us
    psum x1 -> x0, blocking collectives: 63 us -> none  [on_device(): station_rows = lax.psum(picked.astype(jnp.bfloat16), 'grp')]
    reduce_scatter x1 -> x0, waiting for transfers between devices: 44.7 us -> none  [on_device(): lax.psum_scatter(partial_lags, 'freq', scatter_dimension=2, tiled=True)]
    psum x1 -> x0, waiting for transfers between devices: 32.8 us -> none  [on_device(): band_power = lax.psum(local_power, 'freq')]
    ppermute x0 -> x27, starting transfers between devices: none -> 23.4 us  [the longest x5 8.76 us: on_device(): flying.append(lax.ppermute(arrived, 'grp', ring))]
    ppermute x0 -> x27, waiting for transfers between devices: none -> 21.7 us  [the longest x5 8.14 us: on_device(): flying.append(lax.ppermute(arrived, 'grp', ring))]
    dot_general x4 -> x2, matrix products: 18.7 us -> 2.05 us  [the longest x1 1.8 us: to_lags(): jnp.einsum('rsc,rl->scl', jnp.concatenate([parts[i] for i, _ in pairs], a...]
    pallas_call x0 -> x14, Pallas kernels: none -> 15.3 us  [the longest x10 14.3 us: cross_blocks(): pl.pallas_call(body, out_shape=shapes, in_specs=specs, out_specs=out_spec...]
    all_gather x1 -> x0, waiting for transfers between devices: 5.3 us -> none  [on_device(): peer_rows = lax.all_gather(whitened, 'grp', axis=1, tiled=True)]
  transfers between devices with their start and end apart: 3 -> 27, of which waited for: 3 -> 11; matrix products, arithmetic and copies ran while one was open for 10% -> 1% of each run, Pallas kernels for 0% -> 20%
where the time goes in v2:
time: 67.6 us; the launch traced here: 67.4 us
  starting transfers between devices  23.4 us (35%)
  waiting for transfers between devices  21.7 us (32%)
  Pallas kernels  15.3 us (23%)
  local copies, waits for them, and re-layouts  3.14 us (5%)
  matrix products  2.05 us (3%)
  between operations  1.12 us (2%)
    pallas_call x10, Pallas kernels, cross_blocks(): pl.pallas_call(body, out_shape=shapes, in_specs=specs, out_specs=out_spec...  14.3 us
    ppermute x5, starting transfers between devices, on_device(): flying.append(lax.ppermute(arrived, 'grp', ring))  8.76 us
    ppermute x5, waiting for transfers between devices, on_device(): flying.append(lax.ppermute(arrived, 'grp', ring))  8.14 us
    ppermute x16, starting transfers between devices, swap(): lax.ppermute(block[k * rows:(k + 1) * rows], 'grp', swap_by(1))  4.49 us
    ppermute x2, waiting for transfers between devices, on_device(): lax.ppermute(power, 'freq', from_freq(shift))  3.75 us
    ppermute x2, starting transfers between devices, on_device(): lax.ppermute(power, 'freq', from_freq(shift))  3.11 us
    ppermute x1, waiting for transfers between devices, on_device(): flying_parts = [lax.ppermute(parts[0], 'grp', ring)]  2.81 us
    unnamed x8, local copies, waits for them, and re-layouts  2.77 us
  transfers between devices with their start and end apart: 27, of which 11 were waited for; matrix products, arithmetic and copies ran while one was open for 1% of the time, Pallas kernels for 20%

profile of v2, /device:TPU:0, one launch (start us, length us, event | category | flops | bytes accessed | tf_op | source)
XLA Modules:
  0.0 67.4 jit_solution(15918627398549958981)
XLA Ops:
  1.8 3.0 %collective-permute-start = (bf16[128,512]{1,0:T(8,128)(2,1)S(1)}, bf16[128,512]{1,0:T(8,128)(2,1)S(1)}, u32[]{:S(2)}, u32[]{:S(2)}) collective-permute-start(bf16[128,512]{1,0:T(8,128)(2,1)S(1)} %get-tuple-element.60), channel_id=1, source_target_pairs={{0,1},{1,0},{2,3},{3,2},{4,5},{5,4},{6,7},{7,6},{8,9},{9,8},{10,11... | collective-permute-start | bytes 393224 | tf_op jit(solution)/shard_map/ppermute | solution.py:265
  7.2 1.9 %collective-permute-done.refs_0_ = bf16[128,512]{1,0:T(8,128)(2,1)S(1)} collective-permute-done((bf16[128,512]{1,0:T(8,128)(2,1)S(1)}, bf16[128,512]{1,0:T(8,128)(2,1)S(1)}, u32[]{:S(2)}, u32[]{:S(2)}) %collective-permute-start) | collective-permute-done | bytes 131104 | tf_op jit(solution)/shard_map/ppermute | solution.py:265
  9.3 1.8 %collective-permute-done.1.refs_0_ = bf16[128,512]{1,0:T(8,128)(2,1)S(1)} collective-permute-done((bf16[128,512]{1,0:T(8,128)(2,1)S(1)}, bf16[128,512]{1,0:T(8,128)(2,1)S(1)}, u32[]{:S(2)}, u32[]{:S(2)}) %collective-permute-start.1) | collective-permute-done | bytes 131104 | tf_op jit(solution)/shard_map/ppermute | solution.py:265
  11.3 1.8 %collective-permute-start.3 = (bf16[128,1024]{1,0:T(8,128)(2,1)S(1)}, bf16[128,1024]{1,0:T(8,128)(2,1)S(1)}, u32[]{:S(2)}, u32[]{:S(2)}) collective-permute-start(bf16[128,1024]{1,0:T(8,128)(2,1)S(1)} %shard_map.53), channel_id=1, source_target_pairs={{0,8},{2,6},{4,0},{6,14},{8,16},{10,2},{12,4},{14,22},{16,24},{18,... | collective-permute-start | bytes 786440 | tf_op jit(solution)/shard_map/ppermute | solution.py:271
  13.2 1.6 %collective-permute-start.2 = (bf16[128,1024]{1,0:T(8,128)(2,1)S(1)}, bf16[128,1024]{1,0:T(8,128)(2,1)S(1)}, u32[]{:S(2)}, u32[]{:S(2)}) collective-permute-start(bf16[128,1024]{1,0:T(8,128)(2,1)S(1)} %shard_map.52), channel_id=1, source_target_pairs={{0,8},{2,6},{4,0},{6,14},{8,16},{10,2},{12,4},{14,22},{16,24},{18,... | collective-permute-start | bytes 786440 | tf_op jit(solution)/shard_map/ppermute | solution.py:268
  15.4 2.3 %collective-permute-done.3 = bf16[128,1024]{1,0:T(8,128)(2,1)S(1)} collective-permute-done((bf16[128,1024]{1,0:T(8,128)(2,1)S(1)}, bf16[128,1024]{1,0:T(8,128)(2,1)S(1)}, u32[]{:S(2)}, u32[]{:S(2)}) %collective-permute-start.3) | collective-permute-done | bytes 262176 | tf_op jit(solution)/shard_map/ppermute | solution.py:271
  17.7 2.8 %collective-permute-done.2 = bf16[128,1024]{1,0:T(8,128)(2,1)S(1)} collective-permute-done((bf16[128,1024]{1,0:T(8,128)(2,1)S(1)}, bf16[128,1024]{1,0:T(8,128)(2,1)S(1)}, u32[]{:S(2)}, u32[]{:S(2)}) %collective-permute-start.2) | collective-permute-done | bytes 262176 | tf_op jit(solution)/shard_map/ppermute | solution.py:268
  20.6 1.8 %collective-permute-start.7 = (bf16[256,1024]{1,0:T(8,128)(2,1)S(1)}, bf16[256,1024]{1,0:T(8,128)(2,1)S(1)}, u32[]{:S(2)}, u32[]{:S(2)}) collective-permute-start(bf16[256,1024]{1,0:T(8,128)(2,1)S(1)} %constant_dynamic-update-slice_fusion.refs_0_), channel_id=1, source_target_pairs={{0,8},{2,6},{4,0},{6,14},{8,16},{10,2},{12,4},{14,22},{16,24},{18,... | collective-permute-start | bytes 1572872 | tf_op jit(solution)/shard_map/ppermute | solution.py:274
  22.5 1.2 %shard_map.54 = (bf16[2,256,4096]{2,1,0:T(8,128)(2,1)}, bf16[16,1024]{1,0:T(8,128)(2,1)S(1)}) custom-call(bf16[512,1024]{1,0:T(8,128)(2,1)S(1)} %maximum_maximum_fusion.left_ref, bf16[256,1024]{1,0:T(8,128)(2,1)S(1)} %pad_maximum_fusion.refs_0_, s32[16,256]{1,0:T(8,128)S(1)} %get-tuple-element.66.refs_1_.refs_2_), custom_call_target="tpu_custom_call" | custom-call | flops 4600000000 | tf_op jit(solution)/shard_map/pallas_call | solution.py:196
  24.4 1.6 %collective-permute-start.6 = (bf16[256,1024]{1,0:T(8,128)(2,1)S(1)}, bf16[256,1024]{1,0:T(8,128)(2,1)S(1)}, u32[]{:S(2)}, u32[]{:S(2)}) collective-permute-start(bf16[256,1024]{1,0:T(8,128)(2,1)S(1)} %pad_maximum_fusion.1.refs_0_), channel_id=1, source_target_pairs={{0,8},{2,6},{4,0},{6,14},{8,16},{10,2},{12,4},{14,22},{16,24},{18,... | collective-permute-start | bytes 1572872 | tf_op jit(solution)/shard_map/ppermute | solution.py:287
  26.0 1.2 %shard_map.55 = (bf16[2,256,4096]{2,1,0:T(8,128)(2,1)}, bf16[16,1024]{1,0:T(8,128)(2,1)S(1)}) custom-call(bf16[512,1024]{1,0:T(8,128)(2,1)S(1)} %maximum_maximum_fusion.left_ref, bf16[256,1024]{1,0:T(8,128)(2,1)S(1)} %constant_dynamic-update-slice_fusion.refs_0_, s32[16,256]{1,0:T(8,128)S(1)} %get-tuple-element.66.refs_1_.refs_2_, ...), custom_call_target="tpu_custom_call", output_to_operand_aliasing={{0}: (4, {})} | custom-call | tf_op jit(solution)/shard_map/pallas_call | solution.py:196
  27.3 2.6 %collective-permute-done.7.refs_0_ = bf16[256,1024]{1,0:T(8,128)(2,1)S(1)} collective-permute-done((bf16[256,1024]{1,0:T(8,128)(2,1)S(1)}, bf16[256,1024]{1,0:T(8,128)(2,1)S(1)}, u32[]{:S(2)}, u32[]{:S(2)}) %collective-permute-start.7) | collective-permute-done | bytes 524320 | tf_op jit(solution)/shard_map/ppermute | solution.py:274
  30.5 1.8 %collective-permute-start.13 = (bf16[256,1024]{1,0:T(8,128)(2,1)S(1)}, bf16[256,1024]{1,0:T(8,128)(2,1)S(1)}, u32[]{:S(2)}, u32[]{:S(2)}) collective-permute-start(bf16[256,1024]{1,0:T(8,128)(2,1)S(1)} %collective-permute-done.7.refs_0_), channel_id=1, source_target_pairs={{0,8},{2,6},{4,0},{6,14},{8,16},{10,2},{12,4},{14,22},{16,24},{18,... | collective-permute-start | bytes 1572872 | tf_op jit(solution)/shard_map/ppermute | solution.py:287
  32.3 1.5 %shard_map.56 = (bf16[2,256,4096]{2,1,0:T(8,128)(2,1)}, bf16[16,1024]{1,0:T(8,128)(2,1)S(1)}) custom-call(bf16[512,1024]{1,0:T(8,128)(2,1)S(1)} %maximum_maximum_fusion.left_ref, bf16[256,1024]{1,0:T(8,128)(2,1)S(1)} %pad_maximum_fusion.1.refs_0_, bf16[256,1024]{1,0:T(8,128)(2,1)S(1)} %pad_maximum_fusion.2.refs_1_, ...), custom_call_target="tpu_custom_call", output_to_operand_aliasing={{0}: (5, {})} | custom-call | tf_op jit(solution)/shard_map/pallas_call | solution.py:196
  33.9 1.6 %collective-permute-done.6.refs_0_ = bf16[256,1024]{1,0:T(8,128)(2,1)S(1)} collective-permute-done((bf16[256,1024]{1,0:T(8,128)(2,1)S(1)}, bf16[256,1024]{1,0:T(8,128)(2,1)S(1)}, u32[]{:S(2)}, u32[]{:S(2)}) %collective-permute-start.6) | collective-permute-done | bytes 524320 | tf_op jit(solution)/shard_map/ppermute | solution.py:287
  36.1 1.8 %collective-permute-start.12 = (bf16[256,1024]{1,0:T(8,128)(2,1)S(1)}, bf16[256,1024]{1,0:T(8,128)(2,1)S(1)}, u32[]{:S(2)}, u32[]{:S(2)}) collective-permute-start(bf16[256,1024]{1,0:T(8,128)(2,1)S(1)} %collective-permute-done.6.refs_0_), channel_id=1, source_target_pairs={{0,8},{2,6},{4,0},{6,14},{8,16},{10,2},{12,4},{14,22},{16,24},{18,... | collective-permute-start | bytes 1572872 | tf_op jit(solution)/shard_map/ppermute | solution.py:287
  37.9 1.6 %shard_map.57 = (bf16[2,256,4096]{2,1,0:T(8,128)(2,1)}, bf16[16,1024]{1,0:T(8,128)(2,1)S(1)}) custom-call(bf16[512,1024]{1,0:T(8,128)(2,1)S(1)} %maximum_maximum_fusion.left_ref, bf16[256,1024]{1,0:T(8,128)(2,1)S(1)} %collective-permute-done.7.refs_0_, bf16[256,1024]{1,0:T(8,128)(2,1)S(1)} %pad_maximum_fusion.3.refs_1_, ...), custom_call_target="tpu_custom_call", output_to_operand_aliasing={{0}: (5, {})} | custom-call | tf_op jit(solution)/shard_map/pallas_call | solution.py:196
  39.5 1.6 %collective-permute-done.13.refs_0_ = bf16[256,1024]{1,0:T(8,128)(2,1)S(1)} collective-permute-done((bf16[256,1024]{1,0:T(8,128)(2,1)S(1)}, bf16[256,1024]{1,0:T(8,128)(2,1)S(1)}, u32[]{:S(2)}, u32[]{:S(2)}) %collective-permute-start.13) | collective-permute-done | bytes 524320 | tf_op jit(solution)/shard_map/ppermute | solution.py:287
  41.7 1.8 %collective-permute-start.19 = (bf16[256,1024]{1,0:T(8,128)(2,1)S(1)}, bf16[256,1024]{1,0:T(8,128)(2,1)S(1)}, u32[]{:S(2)}, u32[]{:S(2)}) collective-permute-start(bf16[256,1024]{1,0:T(8,128)(2,1)S(1)} %collective-permute-done.13.refs_0_), channel_id=1, source_target_pairs={{0,8},{2,6},{4,0},{6,14},{8,16},{10,2},{12,4},{14,22},{16,24},{18,... | collective-permute-start | bytes 1572872 | tf_op jit(solution)/shard_map/ppermute | solution.py:287
  43.5 1.5 %shard_map.58 = (bf16[2,256,4096]{2,1,0:T(8,128)(2,1)}, bf16[16,1024]{1,0:T(8,128)(2,1)S(1)}) custom-call(bf16[512,1024]{1,0:T(8,128)(2,1)S(1)} %maximum_maximum_fusion.left_ref, bf16[256,1024]{1,0:T(8,128)(2,1)S(1)} %collective-permute-done.6.refs_0_, bf16[256,1024]{1,0:T(8,128)(2,1)S(1)} %pad_maximum_fusion.4.refs_1_, ...), custom_call_target="tpu_custom_call", output_to_operand_aliasing={{0}: (5, {})} | custom-call | tf_op jit(solution)/shard_map/pallas_call | solution.py:196
  45.1 1.6 %collective-permute-done.12.refs_0_ = bf16[256,1024]{1,0:T(8,128)(2,1)S(1)} collective-permute-done((bf16[256,1024]{1,0:T(8,128)(2,1)S(1)}, bf16[256,1024]{1,0:T(8,128)(2,1)S(1)}, u32[]{:S(2)}, u32[]{:S(2)}) %collective-permute-start.12) | collective-permute-done | bytes 524320 | tf_op jit(solution)/shard_map/ppermute | solution.py:287
  47.3 1.8 %collective-permute-start.18 = (bf16[256,1024]{1,0:T(8,128)(2,1)S(1)}, bf16[256,1024]{1,0:T(8,128)(2,1)S(1)}, u32[]{:S(2)}, u32[]{:S(2)}) collective-permute-start(bf16[256,1024]{1,0:T(8,128)(2,1)S(1)} %collective-permute-done.12.refs_0_), channel_id=1, source_target_pairs={{0,8},{2,6},{4,0},{6,14},{8,16},{10,2},{12,4},{14,22},{16,24},{18,... | collective-permute-start | bytes 1572872 | tf_op jit(solution)/shard_map/ppermute | solution.py:287
  49.1 1.5 %shard_map.59 = (bf16[2,256,4096]{2,1,0:T(8,128)(2,1)}, bf16[16,1024]{1,0:T(8,128)(2,1)S(1)}) custom-call(bf16[512,1024]{1,0:T(8,128)(2,1)S(1)} %maximum_maximum_fusion.left_ref, bf16[256,1024]{1,0:T(8,128)(2,1)S(1)} %collective-permute-done.13.refs_0_, bf16[256,1024]{1,0:T(8,128)(2,1)S(1)} %pad_maximum_fusion.5.refs_1_, ...), custom_call_target="tpu_custom_call", output_to_operand_aliasing={{0}: (5, {})} | custom-call | tf_op jit(solution)/shard_map/pallas_call | solution.py:196
  50.7 1.6 %collective-permute-done.19.refs_0_ = bf16[256,1024]{1,0:T(8,128)(2,1)S(1)} collective-permute-done((bf16[256,1024]{1,0:T(8,128)(2,1)S(1)}, bf16[256,1024]{1,0:T(8,128)(2,1)S(1)}, u32[]{:S(2)}, u32[]{:S(2)}) %collective-permute-start.19) | collective-permute-done | bytes 524320 | tf_op jit(solution)/shard_map/ppermute | solution.py:287
  52.9 1.5 %shard_map.60 = (bf16[2,256,4096]{2,1,0:T(8,128)(2,1)}, bf16[16,1024]{1,0:T(8,128)(2,1)S(1)}) custom-call(bf16[512,1024]{1,0:T(8,128)(2,1)S(1)} %maximum_maximum_fusion.left_ref, bf16[256,1024]{1,0:T(8,128)(2,1)S(1)} %collective-permute-done.12.refs_0_, bf16[256,1024]{1,0:T(8,128)(2,1)S(1)} %pad_maximum_fusion.6.refs_1_, ...), custom_call_target="tpu_custom_call", output_to_operand_aliasing={{0}: (5, {})} | custom-call | tf_op jit(solution)/shard_map/pallas_call | solution.py:196
  54.6 1.6 %shard_map.61 = (bf16[2,256,4096]{2,1,0:T(8,128)(2,1)}, bf16[16,1024]{1,0:T(8,128)(2,1)S(1)}) custom-call(bf16[512,1024]{1,0:T(8,128)(2,1)S(1)} %maximum_maximum_fusion.left_ref, bf16[256,1024]{1,0:T(8,128)(2,1)S(1)} %collective-permute-done.19.refs_0_, ...), custom_call_target="tpu_custom_call", output_to_operand_aliasing={{0}: (5, {})} | custom-call | tf_op jit(solution)/shard_map/pallas_call | solution.py:196
  56.1 1.8 %collective-permute-done.18.refs_0_ = bf16[256,1024]{1,0:T(8,128)(2,1)S(1)} collective-permute-done((bf16[256,1024]{1,0:T(8,128)(2,1)S(1)}, bf16[256,1024]{1,0:T(8,128)(2,1)S(1)}, u32[]{:S(2)}, u32[]{:S(2)}) %collective-permute-start.18) | collective-permute-done | bytes 524320 | tf_op jit(solution)/shard_map/ppermute | solution.py:287
  58.7 1.3 %shard_map.62 = (bf16[2,256,4096]{2,1,0:T(8,128)(2,1)}, bf16[16,1024]{1,0:T(8,128)(2,1)S(1)}) custom-call(bf16[512,1024]{1,0:T(8,128)(2,1)S(1)} %maximum_maximum_fusion.left_ref, bf16[256,1024]{1,0:T(8,128)(2,1)S(1)} %collective-permute-done.18.refs_0_, s32[16,256]{1,0:T(8,128)S(1)} %get-tuple-element.66.refs_1_.refs_2_, ...), custom_call_target="tpu_custom_call", output_to_operand_aliasing={{0}: (4, {})} | custom-call | tf_op jit(solution)/shard_map/pallas_call | solution.py:196
  60.0 1.2 %shard_map.63 = (bf16[2,256,4096]{2,1,0:T(8,128)(2,1)}, bf16[16,1024]{1,0:T(8,128)(2,1)S(1)}) custom-call(bf16[512,1024]{1,0:T(8,128)(2,1)S(1)} %maximum_maximum_fusion.left_ref, bf16[256,1024]{1,0:T(8,128)(2,1)S(1)} %pad_maximum_fusion.7.refs_0_, s32[16,256]{1,0:T(8,128)S(1)} %get-tuple-element.66.refs_1_.refs_2_, ...), custom_call_target="tpu_custom_call", output_to_operand_aliasing={{0}: (4, {})} | custom-call | tf_op jit(solution)/shard_map/pallas_call | solution.py:196
  61.5 1.8 %collective-permute-start.26 = (f32[32,256]{1,0:T(8,128)S(1)}, f32[32,256]{1,0:T(8,128)S(1)}, u32[]{:S(2)}, u32[]{:S(2)}) collective-permute-start(f32[32,256]{1,0:T(8,128)S(1)} %convolution_multiply_fusion), channel_id=1, source_target_pairs={{0,1},{1,0},{2,3},{3,2},{4,5},{5,4},{6,7},{7,6},{8,9},{9,8},{10,11... | collective-permute-start | bytes 98312 | tf_op jit(solution)/shard_map/ppermute | solution.py:240
  63.4 2.1 %collective-permute-done.26 = f32[32,256]{1,0:T(8,128)S(1)} collective-permute-done((f32[32,256]{1,0:T(8,128)S(1)}, f32[32,256]{1,0:T(8,128)S(1)}, u32[]{:S(2)}, u32[]{:S(2)}) %collective-permute-start.26) | collective-permute-done | bytes 32800 | tf_op jit(solution)/shard_map/ppermute | solution.py:240
  65.6 1.8 %fusion.3 = f32[16,256,128]{2,1,0:T(8,128)} fusion(bf16[24,16,256]{2,1,0:T(8,128)(2,1)S(1)} %fusion.12, bf16[24,128]{1,0:T(8,128)(2,1)S(1)} %concatenate.68), kind=kOutput, calls=%fused_computation.17 | convolution fusion | flops 25165824 | bytes 2299904 | tf_op jit(solution)/shard_map/rsc,rl->scl/dot_general | solution.py:255
  (77 shorter events, 9.6 us)
Async XLA Ops:
  0.6 1.0 %copy-start = (bf16[1,256,1024]{2,1,0:T(8,128)(2,1)S(1)}, bf16[1,256,1024]{2,1,0:T(8,128)(2,1)}, u32[]{:S(2)}) copy-start(bf16[1,256,1024]{2,1,0:T(8,128)(2,1)} %param.3) | copy-start | bytes 1572868
  1.8 7.4 %collective-permute-start = (bf16[128,512]{1,0:T(8,128)(2,1)S(1)}, bf16[128,512]{1,0:T(8,128)(2,1)S(1)}, u32[]{:S(2)}, u32[]{:S(2)}) collective-permute-start(bf16[128,512]{1,0:T(8,128)(2,1)S(1)} %get-tuple-element.60), channel_id=1, source_target_pairs={{0,1},{1,0},{2,3},{3,2},{4,5},{5,4},{6,7},{7,6},{8,9},{9,8},{10,11... | collective-permute-start | bytes 393224 | tf_op jit(solution)/shard_map/ppermute | solution.py:265
  4.8 6.3 %collective-permute-start.1 = (bf16[128,512]{1,0:T(8,128)(2,1)S(1)}, bf16[128,512]{1,0:T(8,128)(2,1)S(1)}, u32[]{:S(2)}, u32[]{:S(2)}) collective-permute-start(bf16[128,512]{1,0:T(8,128)(2,1)S(1)} %get-tuple-element.61), channel_id=1, source_target_pairs={{0,1},{1,0},{2,3},{3,2},{4,5},{5,4},{6,7},{7,6},{8,9},{9,8},{10,11... | collective-permute-start | bytes 393224 | tf_op jit(solution)/shard_map/ppermute | solution.py:265
  4.9 1.0 %copy-start.1 = (s32[256,512]{1,0:T(8,128)S(1)}, s32[256,512]{1,0:T(8,128)}, u32[]{:S(2)}) copy-start(s32[256,512]{1,0:T(8,128)} %valid_ref.1) | copy-start | bytes 1572868
  5.9 0.7 copy-start.2
  11.3 6.4 %collective-permute-start.3 = (bf16[128,1024]{1,0:T(8,128)(2,1)S(1)}, bf16[128,1024]{1,0:T(8,128)(2,1)S(1)}, u32[]{:S(2)}, u32[]{:S(2)}) collective-permute-start(bf16[128,1024]{1,0:T(8,128)(2,1)S(1)} %shard_map.53), channel_id=1, source_target_pairs={{0,8},{2,6},{4,0},{6,14},{8,16},{10,2},{12,4},{14,22},{16,24},{18,... | collective-permute-start | bytes 786440 | tf_op jit(solution)/shard_map/ppermute | solution.py:271
  13.2 7.4 %collective-permute-start.2 = (bf16[128,1024]{1,0:T(8,128)(2,1)S(1)}, bf16[128,1024]{1,0:T(8,128)(2,1)S(1)}, u32[]{:S(2)}, u32[]{:S(2)}) collective-permute-start(bf16[128,1024]{1,0:T(8,128)(2,1)S(1)} %shard_map.52), channel_id=1, source_target_pairs={{0,8},{2,6},{4,0},{6,14},{8,16},{10,2},{12,4},{14,22},{16,24},{18,... | collective-permute-start | bytes 786440 | tf_op jit(solution)/shard_map/ppermute | solution.py:268
  14.7 5.8 %collective-permute-start.5 = (bf16[128,1024]{1,0:T(8,128)(2,1)S(1)}, bf16[128,1024]{1,0:T(8,128)(2,1)S(1)}, u32[]{:S(2)}, u32[]{:S(2)}) collective-permute-start(bf16[128,1024]{1,0:T(8,128)(2,1)S(1)} %shard_map.53), channel_id=1, source_target_pairs={{0,2},{2,0},{4,6},{6,4},{8,10},{10,8},{12,14},{14,12},{16,18},{18,... | collective-permute-start | bytes 786440 | tf_op jit(solution)/shard_map/ppermute | solution.py:218
  14.8 5.8 %collective-permute-start.4 = (bf16[128,1024]{1,0:T(8,128)(2,1)S(1)}, bf16[128,1024]{1,0:T(8,128)(2,1)S(1)}, u32[]{:S(2)}, u32[]{:S(2)}) collective-permute-start(bf16[128,1024]{1,0:T(8,128)(2,1)S(1)} %shard_map.52), channel_id=1, source_target_pairs={{0,2},{2,0},{4,6},{6,4},{8,10},{10,8},{12,14},{14,12},{16,18},{18,... | collective-permute-start | bytes 786440 | tf_op jit(solution)/shard_map/ppermute | solution.py:218
  20.6 9.2 %collective-permute-start.7 = (bf16[256,1024]{1,0:T(8,128)(2,1)S(1)}, bf16[256,1024]{1,0:T(8,128)(2,1)S(1)}, u32[]{:S(2)}, u32[]{:S(2)}) collective-permute-start(bf16[256,1024]{1,0:T(8,128)(2,1)S(1)} %constant_dynamic-update-slice_fusion.refs_0_), channel_id=1, source_target_pairs={{0,8},{2,6},{4,0},{6,14},{8,16},{10,2},{12,4},{14,22},{16,24},{18,... | collective-permute-start | bytes 1572872 | tf_op jit(solution)/shard_map/ppermute | solution.py:274
  23.8 3.4 %collective-permute-start.8 = (bf16[128,1024]{1,0:T(8,128)(2,1)S(1)}, bf16[128,1024]{1,0:T(8,128)(2,1)S(1)}, u32[]{:S(2)}, u32[]{:S(2)}) collective-permute-start(bf16[128,1024]{1,0:T(8,128)(2,1)S(1)} %get-tuple-element.126), channel_id=1, source_target_pairs={{0,2},{2,0},{4,6},{6,4},{8,10},{10,8},{12,14},{14,12},{16,18},{18,... | collective-permute-start | bytes 786440 | tf_op jit(solution)/shard_map/ppermute | solution.py:218
  23.9 3.3 %collective-permute-start.9 = (bf16[128,1024]{1,0:T(8,128)(2,1)S(1)}, bf16[128,1024]{1,0:T(8,128)(2,1)S(1)}, u32[]{:S(2)}, u32[]{:S(2)}) collective-permute-start(bf16[128,1024]{1,0:T(8,128)(2,1)S(1)} %get-tuple-element.127), channel_id=1, source_target_pairs={{0,2},{2,0},{4,6},{6,4},{8,10},{10,8},{12,14},{14,12},{16,18},{18,... | collective-permute-start | bytes 786440 | tf_op jit(solution)/shard_map/ppermute | solution.py:218
  24.4 11.1 %collective-permute-start.6 = (bf16[256,1024]{1,0:T(8,128)(2,1)S(1)}, bf16[256,1024]{1,0:T(8,128)(2,1)S(1)}, u32[]{:S(2)}, u32[]{:S(2)}) collective-permute-start(bf16[256,1024]{1,0:T(8,128)(2,1)S(1)} %pad_maximum_fusion.1.refs_0_), channel_id=1, source_target_pairs={{0,8},{2,6},{4,0},{6,14},{8,16},{10,2},{12,4},{14,22},{16,24},{18,... | collective-permute-start | bytes 1572872 | tf_op jit(solution)/shard_map/ppermute | solution.py:287
  29.9 3.9 %collective-permute-start.10 = (bf16[128,1024]{1,0:T(8,128)(2,1)S(1)}, bf16[128,1024]{1,0:T(8,128)(2,1)S(1)}, u32[]{:S(2)}, u32[]{:S(2)}) collective-permute-start(bf16[128,1024]{1,0:T(8,128)(2,1)S(1)} %get-tuple-element.124), channel_id=1, source_target_pairs={{0,2},{2,0},{4,6},{6,4},{8,10},{10,8},{12,14},{14,12},{16,18},{18,... | collective-permute-start | bytes 786440 | tf_op jit(solution)/shard_map/ppermute | solution.py:218
  30.0 3.9 %collective-permute-start.11 = (bf16[128,1024]{1,0:T(8,128)(2,1)S(1)}, bf16[128,1024]{1,0:T(8,128)(2,1)S(1)}, u32[]{:S(2)}, u32[]{:S(2)}) collective-permute-start(bf16[128,1024]{1,0:T(8,128)(2,1)S(1)} %get-tuple-element.125), channel_id=1, source_target_pairs={{0,2},{2,0},{4,6},{6,4},{8,10},{10,8},{12,14},{14,12},{16,18},{18,... | collective-permute-start | bytes 786440 | tf_op jit(solution)/shard_map/ppermute | solution.py:218
  30.5 10.6 %collective-permute-start.13 = (bf16[256,1024]{1,0:T(8,128)(2,1)S(1)}, bf16[256,1024]{1,0:T(8,128)(2,1)S(1)}, u32[]{:S(2)}, u32[]{:S(2)}) collective-permute-start(bf16[256,1024]{1,0:T(8,128)(2,1)S(1)} %collective-permute-done.7.refs_0_), channel_id=1, source_target_pairs={{0,8},{2,6},{4,0},{6,14},{8,16},{10,2},{12,4},{14,22},{16,24},{18,... | collective-permute-start | bytes 1572872 | tf_op jit(solution)/shard_map/ppermute | solution.py:287
  35.5 3.9 %collective-permute-start.14 = (bf16[128,1024]{1,0:T(8,128)(2,1)S(1)}, bf16[128,1024]{1,0:T(8,128)(2,1)S(1)}, u32[]{:S(2)}, u32[]{:S(2)}) collective-permute-start(bf16[128,1024]{1,0:T(8,128)(2,1)S(1)} %get-tuple-element.122), channel_id=1, source_target_pairs={{0,2},{2,0},{4,6},{6,4},{8,10},{10,8},{12,14},{14,12},{16,18},{18,... | collective-permute-start | bytes 786440 | tf_op jit(solution)/shard_map/ppermute | solution.py:218
  35.6 3.9 %collective-permute-start.15 = (bf16[128,1024]{1,0:T(8,128)(2,1)S(1)}, bf16[128,1024]{1,0:T(8,128)(2,1)S(1)}, u32[]{:S(2)}, u32[]{:S(2)}) collective-permute-start(bf16[128,1024]{1,0:T(8,128)(2,1)S(1)} %get-tuple-element.123), channel_id=1, source_target_pairs={{0,2},{2,0},{4,6},{6,4},{8,10},{10,8},{12,14},{14,12},{16,18},{18,... | collective-permute-start | bytes 786440 | tf_op jit(solution)/shard_map/ppermute | solution.py:218
  36.1 10.6 %collective-permute-start.12 = (bf16[256,1024]{1,0:T(8,128)(2,1)S(1)}, bf16[256,1024]{1,0:T(8,128)(2,1)S(1)}, u32[]{:S(2)}, u32[]{:S(2)}) collective-permute-start(bf16[256,1024]{1,0:T(8,128)(2,1)S(1)} %collective-permute-done.6.refs_0_), channel_id=1, source_target_pairs={{0,8},{2,6},{4,0},{6,14},{8,16},{10,2},{12,4},{14,22},{16,24},{18,... | collective-permute-start | bytes 1572872 | tf_op jit(solution)/shard_map/ppermute | solution.py:287
  41.1 3.9 %collective-permute-start.16 = (bf16[128,1024]{1,0:T(8,128)(2,1)S(1)}, bf16[128,1024]{1,0:T(8,128)(2,1)S(1)}, u32[]{:S(2)}, u32[]{:S(2)}) collective-permute-start(bf16[128,1024]{1,0:T(8,128)(2,1)S(1)} %get-tuple-element.120), channel_id=1, source_target_pairs={{0,2},{2,0},{4,6},{6,4},{8,10},{10,8},{12,14},{14,12},{16,18},{18,... | collective-permute-start | bytes 786440 | tf_op jit(solution)/shard_map/ppermute | solution.py:218
  41.2 3.9 %collective-permute-start.17 = (bf16[128,1024]{1,0:T(8,128)(2,1)S(1)}, bf16[128,1024]{1,0:T(8,128)(2,1)S(1)}, u32[]{:S(2)}, u32[]{:S(2)}) collective-permute-start(bf16[128,1024]{1,0:T(8,128)(2,1)S(1)} %get-tuple-element.121), channel_id=1, source_target_pairs={{0,2},{2,0},{4,6},{6,4},{8,10},{10,8},{12,14},{14,12},{16,18},{18,... | collective-permute-start | bytes 786440 | tf_op jit(solution)/shard_map/ppermute | solution.py:218
  41.7 10.6 %collective-permute-start.19 = (bf16[256,1024]{1,0:T(8,128)(2,1)S(1)}, bf16[256,1024]{1,0:T(8,128)(2,1)S(1)}, u32[]{:S(2)}, u32[]{:S(2)}) collective-permute-start(bf16[256,1024]{1,0:T(8,128)(2,1)S(1)} %collective-permute-done.13.refs_0_), channel_id=1, source_target_pairs={{0,8},{2,6},{4,0},{6,14},{8,16},{10,2},{12,4},{14,22},{16,24},{18,... | collective-permute-start | bytes 1572872 | tf_op jit(solution)/shard_map/ppermute | solution.py:287
  46.7 3.9 %collective-permute-start.20 = (bf16[128,1024]{1,0:T(8,128)(2,1)S(1)}, bf16[128,1024]{1,0:T(8,128)(2,1)S(1)}, u32[]{:S(2)}, u32[]{:S(2)}) collective-permute-start(bf16[128,1024]{1,0:T(8,128)(2,1)S(1)} %get-tuple-element.118), channel_id=1, source_target_pairs={{0,2},{2,0},{4,6},{6,4},{8,10},{10,8},{12,14},{14,12},{16,18},{18,... | collective-permute-start | bytes 786440 | tf_op jit(solution)/shard_map/ppermute | solution.py:218
  46.8 3.9 %collective-permute-start.21 = (bf16[128,1024]{1,0:T(8,128)(2,1)S(1)}, bf16[128,1024]{1,0:T(8,128)(2,1)S(1)}, u32[]{:S(2)}, u32[]{:S(2)}) collective-permute-start(bf16[128,1024]{1,0:T(8,128)(2,1)S(1)} %get-tuple-element.119), channel_id=1, source_target_pairs={{0,2},{2,0},{4,6},{6,4},{8,10},{10,8},{12,14},{14,12},{16,18},{18,... | collective-permute-start | bytes 786440 | tf_op jit(solution)/shard_map/ppermute | solution.py:218
  47.3 10.6 %collective-permute-start.18 = (bf16[256,1024]{1,0:T(8,128)(2,1)S(1)}, bf16[256,1024]{1,0:T(8,128)(2,1)S(1)}, u32[]{:S(2)}, u32[]{:S(2)}) collective-permute-start(bf16[256,1024]{1,0:T(8,128)(2,1)S(1)} %collective-permute-done.12.refs_0_), channel_id=1, source_target_pairs={{0,8},{2,6},{4,0},{6,14},{8,16},{10,2},{12,4},{14,22},{16,24},{18,... | collective-permute-start | bytes 1572872 | tf_op jit(solution)/shard_map/ppermute | solution.py:287
  52.4 2.1 %collective-permute-start.22 = (bf16[128,1024]{1,0:T(8,128)(2,1)S(1)}, bf16[128,1024]{1,0:T(8,128)(2,1)S(1)}, u32[]{:S(2)}, u32[]{:S(2)}) collective-permute-start(bf16[128,1024]{1,0:T(8,128)(2,1)S(1)} %get-tuple-element.117), channel_id=1, source_target_pairs={{0,2},{2,0},{4,6},{6,4},{8,10},{10,8},{12,14},{14,12},{16,18},{18,... | collective-permute-start | bytes 786440 | tf_op jit(solution)/shard_map/ppermute | solution.py:218
  52.4 2.1 %collective-permute-start.23 = (bf16[128,1024]{1,0:T(8,128)(2,1)S(1)}, bf16[128,1024]{1,0:T(8,128)(2,1)S(1)}, u32[]{:S(2)}, u32[]{:S(2)}) collective-permute-start(bf16[128,1024]{1,0:T(8,128)(2,1)S(1)} %get-tuple-element.116), channel_id=1, source_target_pairs={{0,2},{2,0},{4,6},{6,4},{8,10},{10,8},{12,14},{14,12},{16,18},{18,... | collective-permute-start | bytes 786440 | tf_op jit(solution)/shard_map/ppermute | solution.py:218
  58.0 2.0 %collective-permute-start.24 = (bf16[128,1024]{1,0:T(8,128)(2,1)S(1)}, bf16[128,1024]{1,0:T(8,128)(2,1)S(1)}, u32[]{:S(2)}, u32[]{:S(2)}) collective-permute-start(bf16[128,1024]{1,0:T(8,128)(2,1)S(1)} %get-tuple-element.114), channel_id=1, source_target_pairs={{0,2},{2,0},{4,6},{6,4},{8,10},{10,8},{12,14},{14,12},{16,18},{18,... | collective-permute-start | bytes 786440 | tf_op jit(solution)/shard_map/ppermute | solution.py:218
  58.1 1.9 %collective-permute-start.25 = (bf16[128,1024]{1,0:T(8,128)(2,1)S(1)}, bf16[128,1024]{1,0:T(8,128)(2,1)S(1)}, u32[]{:S(2)}, u32[]{:S(2)}) collective-permute-start(bf16[128,1024]{1,0:T(8,128)(2,1)S(1)} %get-tuple-element.115), channel_id=1, source_target_pairs={{0,2},{2,0},{4,6},{6,4},{8,10},{10,8},{12,14},{14,12},{16,18},{18,... | collective-permute-start | bytes 786440 | tf_op jit(solution)/shard_map/ppermute | solution.py:218
  61.5 4.0 %collective-permute-start.26 = (f32[32,256]{1,0:T(8,128)S(1)}, f32[32,256]{1,0:T(8,128)S(1)}, u32[]{:S(2)}, u32[]{:S(2)}) collective-permute-start(f32[32,256]{1,0:T(8,128)S(1)} %convolution_multiply_fusion), channel_id=1, source_target_pairs={{0,1},{1,0},{2,3},{3,2},{4,5},{5,4},{6,7},{7,6},{8,9},{9,8},{10,11... | collective-permute-start | bytes 98312 | tf_op jit(solution)/shard_map/ppermute | solution.py:240

commit v3 on v2

--- a/solution.py
+++ b/solution.py
@@ -36,13 +36,9 @@
     return jnp.where(place < half, place * 4, (chips - 1 - place) * 4 + 2) + core
 
 
-def own_block():
-    return [lax.axis_index("grp")]
-
-
-def sibling_block():
+def own_blocks():
     group_index = lax.axis_index("grp")
-    return [group_index + 1 - 2 * lax.rem(group_index, 2)]
+    return [group_index, group_index + 1 - 2 * lax.rem(group_index, 2)]
 
 
 def ring_blocks(step, chips):
@@ -84,7 +80,7 @@
         + [jax.ShapeDtypeStruct((rows // chunks, width), jnp.bfloat16)] * chunks,
         in_specs=[vmem],
         out_specs=[vmem] * (1 + chunks),
-        compiler_params=pltpu.CompilerParams(vmem_limit_bytes=8 * 2**20),
+        compiler_params=pltpu.CompilerParams(vmem_limit_bytes=6 * 2**20),
         cost_estimate=cost(0.1),
     )(raw)
 
@@ -120,7 +116,7 @@
             pltpu.SMEM(station_index.shape, jnp.int32),
             pltpu.SemaphoreType.DMA((2,)),
         ],
-        compiler_params=pltpu.CompilerParams(vmem_limit_bytes=8 * 2**20),
+        compiler_params=pltpu.CompilerParams(vmem_limit_bytes=6 * 2**20),
         cost_estimate=cost(0.3),
     )(station_index, valid, after)
 
@@ -146,16 +142,38 @@
         in_specs=[pl.BlockSpec((rows, 2 * width), lambda i: (chunk, 0)), pl.BlockSpec((rows, width), lambda i: (chunk, 0))]
         + [vmem] * len(received),
         out_specs=pl.BlockSpec((rows, 2 * width), lambda i: (0, 0)),
-        compiler_params=pltpu.CompilerParams(vmem_limit_bytes=8 * 2**20),
-        cost_estimate=cost(0.15),
+        compiler_params=pltpu.CompilerParams(vmem_limit_bytes=6 * 2**20),
+        cost_estimate=cost(0.7),
     )(raw, valid, *received)
 
 
+def select(numbers, first):
+    wanted = numbers - first
+    return (wanted == lax.broadcasted_iota(jnp.int32, wanted.shape, 1)).astype(jnp.bfloat16)
+
+
+def pick(block, numbers, places):
+    def body(block_ref, numbers_ref, out_ref):
+        selector = select(numbers_ref[...], places()[0] * block_ref.shape[0])
+        out_ref[...] = jnp.dot(selector, block_ref[...], preferred_element_type=jnp.float32).astype(jnp.bfloat16)
+
+    vmem = pl.BlockSpec(memory_space=pltpu.VMEM)
+    return pl.pallas_call(
+        body,
+        out_shape=jax.ShapeDtypeStruct((numbers.shape[0], block.shape[1]), jnp.bfloat16),
+        in_specs=[vmem, vmem],
+        out_specs=vmem,
+        compiler_params=pltpu.CompilerParams(vmem_limit_bytes=6 * 2**20),
+        cost_estimate=cost(0.1),
+    )(block, numbers)
+
+
 def cross_blocks(left, blocks, places, cross, total, scaling, numbers=None, stations=None, microseconds=0.0):
-    rows, depth = blocks[0].shape
-    count = len(blocks)
+    rows, depth = left.shape[0] // 2, left.shape[1]
+    pieces = [len(block) for block in blocks]
+    count = sum(pieces)
     vmem, anywhere = pl.BlockSpec(memory_space=pltpu.VMEM), pl.BlockSpec(memory_space=pl.ANY)
-    operands = [left, *blocks]
+    operands = [left, *(piece for block in blocks for piece in block)]
     specs = [vmem] * len(operands)
     for more in (numbers, stations):
         if more is not None:
@@ -176,15 +194,15 @@
         out_ref = refs[len(operands) - 1]
         copies, picked = [], None
         for k, place in enumerate(places()):
-            product = lax.dot_general(left_ref[...], refs[k][...], ROWS_T, preferred_element_type=jnp.float32)
+            first = sum(pieces[:k])
+            block = jnp.concatenate([ref[...] for ref in refs[first : first + pieces[k]]], axis=0)
+            product = lax.dot_general(left_ref[...], block, ROWS_T, preferred_element_type=jnp.float32)
             held[k] = (product * scaling).astype(jnp.bfloat16).reshape(2, rows, rows)
             start = pl.multiple_of(place * rows, rows)
             copies.append(pltpu.make_async_copy(held.at[k], out_ref.at[:, :, pl.ds(start, rows)], sems.at[k]))
             copies[k].start()
             if numbers is not None:
-                wanted = refs[count][...] - start
-                selector = (wanted == lax.broadcasted_iota(jnp.int32, wanted.shape, 1)).astype(jnp.bfloat16)
-                found = jnp.dot(selector, refs[k][...], preferred_element_type=jnp.float32)
+                found = jnp.dot(select(refs[count][...], start), block, preferred_element_type=jnp.float32)
                 picked = found if picked is None else picked + found
         if numbers is not None:
             if stations is not None:
@@ -198,14 +216,38 @@
         out_shape=shapes,
         in_specs=specs,
         out_specs=out_specs,
-        scratch_shapes=[pltpu.VMEM((count, 2, rows, rows), jnp.bfloat16), pltpu.SemaphoreType.DMA((count,))],
+        scratch_shapes=[
+            pltpu.VMEM((len(blocks), 2, rows, rows), jnp.bfloat16),
+            pltpu.SemaphoreType.DMA((len(blocks),)),
+        ],
         input_output_aliases=aliases,
-        compiler_params=pltpu.CompilerParams(vmem_limit_bytes=8 * 2**20),
+        compiler_params=pltpu.CompilerParams(vmem_limit_bytes=6 * 2**20),
         cost_estimate=cost(microseconds),
     )(*operands)
     return out if numbers is not None else out[0]
 
 
+def station_kernel(parts, left, scaling):
+    rows, width = left.shape[0] // 2, left.shape[1] // 2
+    stations = parts[0].shape[0]
+
+    def body(left_ref, *refs):
+        found = sum(ref[...].astype(jnp.float32) for ref in refs[:-1])
+        turned = jnp.concatenate([found[:, width:], -found[:, :width]], axis=1)
+        both = jnp.concatenate([found, turned], axis=0).astype(jnp.bfloat16)
+        refs[-1][...] = lax.dot_general(both, left_ref[:rows, :], ROWS_T, preferred_element_type=jnp.float32) * scaling
+
+    vmem = pl.BlockSpec(memory_space=pltpu.VMEM)
+    return pl.pallas_call(
+        body,
+        out_shape=jax.ShapeDtypeStruct((2 * stations, rows), jnp.float32),
+        in_specs=[vmem] * (1 + len(parts)),
+        out_specs=vmem,
+        compiler_params=pltpu.CompilerParams(vmem_limit_bytes=6 * 2**20),
+        cost_estimate=cost(0.2),
+    )(left, *parts)
+
+
 def make_on_device(group_size, freq_size):
     chips = group_size // 2
     ring = ring_pairs(group_size)
@@ -213,10 +255,12 @@
     def swap_by(bit):
         return [(g, g ^ bit) for g in range(group_size)]
 
-    def swap(block, pieces=2):
+    def swap_pieces(block, pieces):
         rows = block.shape[0] // pieces
-        got = [lax.ppermute(block[k * rows : (k + 1) * rows], "grp", swap_by(1)) for k in range(pieces)]
-        return got[0] if pieces == 1 else jnp.concatenate(got, axis=0)
+        return [lax.ppermute(block[k * rows : (k + 1) * rows], "grp", swap_by(1)) for k in range(pieces)]
+
+    def swap(block):
+        return swap_pieces(block, 2)
 
     def from_freq(shift):
         return [(f, (f + shift) % freq_size) for f in range(freq_size)]
@@ -230,15 +274,9 @@
         total_bins = bin_count * freq_size
         scaling = 1.0 / math.sqrt(window_count)
 
-        def to_kernel(stations, whitened):
-            station_left = jnp.concatenate(
-                [stations, jnp.concatenate([stations[:, window_count:], -stations[:, :window_count]], axis=1)], axis=0
-            )
-            kernel = lax.dot_general(station_left, whitened, ROWS_T, preferred_element_type=jnp.float32) * scaling
-            kernels = [kernel]
-            for shift in range(1, freq_size):
-                kernels.append(lax.ppermute(kernel, "freq", from_freq(shift)))
-            return kernels
+        def to_kernel(stations):
+            kernel = station_kernel(stations, left, scaling)
+            return [kernel] + [lax.ppermute(kernel, "freq", from_freq(shift)) for shift in range(1, freq_size)]
 
         def to_lags(kernels):
             lags_here = LAGS // freq_size
@@ -266,34 +304,40 @@
 
         parts = [whiten(raw, valid, received[0], 0, chunks, total_bins)]
         flying_parts = [lax.ppermute(parts[0], "grp", ring)]
+        swapped = swap_pieces(parts[0], 2)
         second, _ = lax.optimization_barrier((received[1], parts[0]))
         parts.append(whiten(raw, valid, second, 1, chunks, total_bins))
-        flying_parts.append(lax.ppermute(parts[1], "grp", ring))
+        second, swapped[0] = lax.optimization_barrier((parts[1], swapped[0]))
+        flying_parts.append(lax.ppermute(second, "grp", ring))
+        swapped += swap_pieces(parts[1], 2)
         whitened = jnp.concatenate(parts, axis=0)
-        swapped = swap(whitened)
-        flying = [None, lax.ppermute(swapped, "grp", ring)]
+        flying = [None, lax.ppermute(jnp.concatenate(swapped, axis=0), "grp", ring)]
         left = jnp.concatenate(
             [whitened, jnp.concatenate([whitened[:, window_count:], -whitened[:, :window_count]], axis=1)], axis=0
         )
-        later, flying_parts = lax.optimization_barrier((whitened, flying_parts))
+        later, flying_parts[0] = lax.optimization_barrier((whitened, flying_parts[0]))
+        cross, stations = cross_blocks(
+            left, [[later], swapped], own_blocks, None, total_chans, scaling, numbers, None, 4.0
+        )
         flying[0] = jnp.concatenate(flying_parts, axis=0)
-        cross, stations = cross_blocks(left, [later], own_block, None, total_chans, scaling, numbers, None, 4.0)
 
         steps = chips - 1
-        waiting, places = [], sibling_block
+        waiting = []
         for step in range(steps):
             arrived, cross, stations, swapped = lax.optimization_barrier((flying[step], cross, stations, swapped))
             if step + 2 < steps:
                 flying.append(lax.ppermute(arrived, "grp", ring))
             next_swapped = swap(arrived)
-            if step + 1 < steps:
-                cross, stations = cross_blocks(left, [*waiting, swapped], places, cross, total_chans, scaling, numbers, stations)
+            if waiting and step + 1 < steps:
+                cross, stations = cross_blocks(left, [waiting, swapped], places, cross, total_chans, scaling, numbers, stations)
             waiting, swapped, places = [arrived], next_swapped, functools.partial(ring_blocks, step, chips)
             if step + 2 == steps:
-                cross, stations = cross_blocks(left, [*waiting, swapped], places, cross, total_chans, scaling, numbers, stations)
-        cross, stations = cross_blocks(left, waiting, lambda: places()[:1], cross, total_chans, scaling, numbers, stations)
-        cross, stations = cross_blocks(left, [swapped], lambda: places()[1:], cross, total_chans, scaling, numbers, stations)
-        station_gather = to_lags(to_kernel(stations, whitened))
+                cross, stations = cross_blocks(left, [waiting, swapped], places, cross, total_chans, scaling, numbers, stations)
+        found = pick(waiting[0], numbers, places)
+        kernels = to_kernel([stations, found, lax.ppermute(found, "grp", swap_by(1))])
+        cross = cross_blocks(left, [waiting, swapped], places, cross, total_chans, scaling)
+        kernels, cross = lax.optimization_barrier((kernels, cross))
+        station_gather = to_lags(kernels)
         return (cross[None], station_gather)
 
     return on_device

time: 67.6 us -> 61.6 us (0.911)
  waiting for transfers between devices: 21.7 us -> 16.4 us
  local copies, waits for them, and re-layouts: 3.14 us -> 3.88 us
    ppermute x1, waiting for transfers between devices: 2.81 us -> 0.01 us  [on_device(): flying_parts = [lax.ppermute(parts[0], 'grp', ring)]]
    ppermute x2, waiting for transfers between devices: 3.75 us -> 1.91 us  [on_device(): lax.ppermute(power, 'freq', from_freq(shift))]
    pallas_call x10 -> x8, Pallas kernels: 14.3 us -> 13.3 us  [cross_blocks(): pl.pallas_call(body, out_shape=shapes, in_specs=specs, out_specs=out_spec...]
    ppermute x5, starting transfers between devices: 8.76 us -> 7.88 us  [on_device(): flying.append(lax.ppermute(arrived, 'grp', ring))]
    slice x7 -> x9, local copies, waits for them, and re-layouts: 0.24 us -> 1.07 us  [swap_pieces(): block[k * rows:(k + 1) * rows]]
    ppermute x5, waiting for transfers between devices: 8.14 us -> 7.45 us  [on_device(): flying.append(lax.ppermute(arrived, 'grp', ring))]
    ppermute x19 -> x22, starting transfers between devices: 9.99 us -> 9.92 us  [the longest x18 5 us: swap_pieces(): lax.ppermute(block[k * rows:(k + 1) * rows], 'grp', swap_by(1))]
    unnamed x8 -> x6, local copies, waits for them, and re-layouts: 2.77 us -> 2.73 us
  transfers between devices with their start and end apart: 27 -> 30, of which waited for: 11 -> 11; matrix products, arithmetic and copies ran while one was open for 1% -> 2% of each run, Pallas kernels for 20% -> 24%
where the time goes in v3:
time: 61.6 us; the launch traced here: 61.4 us
  starting transfers between devices  23.1 us (38%)
  waiting for transfers between devices  16.4 us (27%)
  Pallas kernels  14.8 us (24%)
  local copies, waits for them, and re-layouts  3.88 us (6%)
  matrix products  1.8 us (3%)
  between operations  0.99 us (2%)
    pallas_call x8, Pallas kernels, cross_blocks(): pl.pallas_call(body, out_shape=shapes, in_specs=specs, out_specs=out_spec...  13.3 us
    ppermute x5, starting transfers between devices, on_device(): flying.append(lax.ppermute(arrived, 'grp', ring))  7.88 us
    ppermute x5, waiting for transfers between devices, on_device(): flying.append(lax.ppermute(arrived, 'grp', ring))  7.45 us
    ppermute x18, starting transfers between devices, swap_pieces(): lax.ppermute(block[k * rows:(k + 1) * rows], 'grp', swap_by(1))  5 us
    ppermute x1, waiting for transfers between devices, on_device(): flying = [None, lax.ppermute(jnp.concatenate(swapped, axis=0), 'grp', ring)]  3.37 us
    ppermute x2, starting transfers between devices, on_device(): lax.ppermute(power, 'freq', from_freq(shift))  3.11 us
    unnamed x6, local copies, waits for them, and re-layouts  2.73 us
    ppermute x1, starting transfers between devices, on_device(): flying_parts = [lax.ppermute(parts[0], 'grp', ring)]  2.17 us
  transfers between devices with their start and end apart: 30, of which 11 were waited for; matrix products, arithmetic and copies ran while one was open for 2% of the time, Pallas kernels for 24%

profile of v3, /device:TPU:0, one launch (start us, length us, event | category | flops | bytes accessed | tf_op | source)
XLA Modules:
  0.0 61.4 jit_solution(6102986891638013304)
XLA Ops:
  0.6 1.0 %copy-done = bf16[1,256,1024]{2,1,0:T(8,128)(2,1)S(1)} copy-done((bf16[1,256,1024]{2,1,0:T(8,128)(2,1)S(1)}, bf16[1,256,1024]{2,1,0:T(8,128)(2,1)}, u32[]{:S(2)}) %copy-start) | copy-done | bytes 524312
  1.8 3.0 %collective-permute-start = (bf16[128,512]{1,0:T(8,128)(2,1)S(1)}, bf16[128,512]{1,0:T(8,128)(2,1)S(1)}, u32[]{:S(2)}, u32[]{:S(2)}) collective-permute-start(bf16[128,512]{1,0:T(8,128)(2,1)S(1)} %get-tuple-element.62), channel_id=1, source_target_pairs={{0,1},{1,0},{2,3},{3,2},{4,5},{5,4},{6,7},{7,6},{8,9},{9,8},{10,11... | collective-permute-start | bytes 393224 | tf_op jit(solution)/shard_map/ppermute | solution.py:303
  4.9 1.0 %copy-done.1 = s32[256,512]{1,0:T(8,128)S(1)} copy-done((s32[256,512]{1,0:T(8,128)S(1)}, s32[256,512]{1,0:T(8,128)}, u32[]{:S(2)}) %copy-start.1) | copy-done | bytes 524312
  5.9 0.7 %copy-done.2 = s32[16]{0:T(128)S(1)} copy-done((s32[16]{0:T(128)S(1)}, s32[16]{0:T(128)}, u32[]{:S(2)}) %copy-start.2) | copy-done | bytes 88
  7.2 1.9 %collective-permute-done.refs_0_ = bf16[128,512]{1,0:T(8,128)(2,1)S(1)} collective-permute-done((bf16[128,512]{1,0:T(8,128)(2,1)S(1)}, bf16[128,512]{1,0:T(8,128)(2,1)S(1)}, u32[]{:S(2)}, u32[]{:S(2)}) %collective-permute-start) | collective-permute-done | bytes 131104 | tf_op jit(solution)/shard_map/ppermute | solution.py:303
  9.3 2.2 %collective-permute-start.2 = (bf16[128,1024]{1,0:T(8,128)(2,1)S(1)}, bf16[128,1024]{1,0:T(8,128)(2,1)S(1)}, u32[]{:S(2)}, u32[]{:S(2)}) collective-permute-start(bf16[128,1024]{1,0:T(8,128)(2,1)S(1)} %shard_map.52), channel_id=1, source_target_pairs={{0,8},{2,6},{4,0},{6,14},{8,16},{10,2},{12,4},{14,22},{16,24},{18,... | collective-permute-start | bytes 786440 | tf_op jit(solution)/shard_map/ppermute | solution.py:306
  13.1 1.6 %collective-permute-start.4 = (bf16[128,1024]{1,0:T(8,128)(2,1)S(1)}, bf16[128,1024]{1,0:T(8,128)(2,1)S(1)}, u32[]{:S(2)}, u32[]{:S(2)}) collective-permute-start(bf16[128,1024]{1,0:T(8,128)(2,1)S(1)} %shard_map.53), channel_id=1, source_target_pairs={{0,8},{2,6},{4,0},{6,14},{8,16},{10,2},{12,4},{14,22},{16,24},{18,... | collective-permute-start | bytes 786440 | tf_op jit(solution)/shard_map/ppermute | solution.py:311
  14.8 1.6 %collective-permute-start.9 = (bf16[256,1024]{1,0:T(8,128)(2,1)S(1)}, bf16[256,1024]{1,0:T(8,128)(2,1)S(1)}, u32[]{:S(2)}, u32[]{:S(2)}) collective-permute-start(bf16[256,1024]{1,0:T(8,128)(2,1)S(1)} %pad_maximum_fusion.2), channel_id=1, source_target_pairs={{0,8},{2,6},{4,0},{6,14},{8,16},{10,2},{12,4},{14,22},{16,24},{18,... | collective-permute-start | bytes 1572872 | tf_op jit(solution)/shard_map/ppermute | solution.py:314
  16.4 1.5 %shard_map.54 = (bf16[2,256,4096]{2,1,0:T(8,128)(2,1)}, bf16[16,1024]{1,0:T(8,128)(2,1)S(1)}) custom-call(bf16[512,1024]{1,0:T(8,128)(2,1)S(1)} %maximum_maximum_fusion.left_ref, bf16[256,1024]{1,0:T(8,128)(2,1)S(1)} %pad_maximum_fusion.refs_0_, bf16[64,1024]{1,0:T(8,128)(2,1)S(1)} %collective-permute-done.3.refs_1_, ...), custom_call_target="tpu_custom_call" | custom-call | flops 4600000000 | tf_op jit(solution)/shard_map/pallas_call | solution.py:214
  17.9 1.5 %collective-permute-done.4 = bf16[128,1024]{1,0:T(8,128)(2,1)S(1)} collective-permute-done((bf16[128,1024]{1,0:T(8,128)(2,1)S(1)}, bf16[128,1024]{1,0:T(8,128)(2,1)S(1)}, u32[]{:S(2)}, u32[]{:S(2)}) %collective-permute-start.4) | collective-permute-done | bytes 262176 | tf_op jit(solution)/shard_map/ppermute | solution.py:311
  20.2 1.6 %collective-permute-start.8 = (bf16[256,1024]{1,0:T(8,128)(2,1)S(1)}, bf16[256,1024]{1,0:T(8,128)(2,1)S(1)}, u32[]{:S(2)}, u32[]{:S(2)}) collective-permute-start(bf16[256,1024]{1,0:T(8,128)(2,1)S(1)} %pad_maximum_fusion.1.refs_0_), channel_id=1, source_target_pairs={{0,8},{2,6},{4,0},{6,14},{8,16},{10,2},{12,4},{14,22},{16,24},{18,... | collective-permute-start | bytes 1572872 | tf_op jit(solution)/shard_map/ppermute | solution.py:329
  21.7 3.4 %collective-permute-done.9.refs_0_ = bf16[256,1024]{1,0:T(8,128)(2,1)S(1)} collective-permute-done((bf16[256,1024]{1,0:T(8,128)(2,1)S(1)}, bf16[256,1024]{1,0:T(8,128)(2,1)S(1)}, u32[]{:S(2)}, u32[]{:S(2)}) %collective-permute-start.9) | collective-permute-done | bytes 524320 | tf_op jit(solution)/shard_map/ppermute | solution.py:314
  25.7 1.6 %collective-permute-start.15 = (bf16[256,1024]{1,0:T(8,128)(2,1)S(1)}, bf16[256,1024]{1,0:T(8,128)(2,1)S(1)}, u32[]{:S(2)}, u32[]{:S(2)}) collective-permute-start(bf16[256,1024]{1,0:T(8,128)(2,1)S(1)} %collective-permute-done.9.refs_0_), channel_id=1, source_target_pairs={{0,8},{2,6},{4,0},{6,14},{8,16},{10,2},{12,4},{14,22},{16,24},{18,... | collective-permute-start | bytes 1572872 | tf_op jit(solution)/shard_map/ppermute | solution.py:329
  27.3 1.5 %shard_map.55 = (bf16[2,256,4096]{2,1,0:T(8,128)(2,1)}, bf16[16,1024]{1,0:T(8,128)(2,1)S(1)}) custom-call(bf16[512,1024]{1,0:T(8,128)(2,1)S(1)} %maximum_maximum_fusion.left_ref, bf16[256,1024]{1,0:T(8,128)(2,1)S(1)} %pad_maximum_fusion.1.refs_0_, bf16[128,1024]{1,0:T(8,128)(2,1)S(1)} %collective-permute-done.10.refs_1_, ...), custom_call_target="tpu_custom_call", output_to_operand_aliasing={{0}: (6, {})} | custom-call | tf_op jit(solution)/shard_map/pallas_call | solution.py:214
  28.9 1.8 %collective-permute-done.8.refs_0_ = bf16[256,1024]{1,0:T(8,128)(2,1)S(1)} collective-permute-done((bf16[256,1024]{1,0:T(8,128)(2,1)S(1)}, bf16[256,1024]{1,0:T(8,128)(2,1)S(1)}, u32[]{:S(2)}, u32[]{:S(2)}) %collective-permute-start.8) | collective-permute-done | bytes 524320 | tf_op jit(solution)/shard_map/ppermute | solution.py:329
  31.3 1.6 %collective-permute-start.14 = (bf16[256,1024]{1,0:T(8,128)(2,1)S(1)}, bf16[256,1024]{1,0:T(8,128)(2,1)S(1)}, u32[]{:S(2)}, u32[]{:S(2)}) collective-permute-start(bf16[256,1024]{1,0:T(8,128)(2,1)S(1)} %collective-permute-done.8.refs_0_), channel_id=1, source_target_pairs={{0,8},{2,6},{4,0},{6,14},{8,16},{10,2},{12,4},{14,22},{16,24},{18,... | collective-permute-start | bytes 1572872 | tf_op jit(solution)/shard_map/ppermute | solution.py:329
  32.9 1.5 %shard_map.56 = (bf16[2,256,4096]{2,1,0:T(8,128)(2,1)}, bf16[16,1024]{1,0:T(8,128)(2,1)S(1)}) custom-call(bf16[512,1024]{1,0:T(8,128)(2,1)S(1)} %maximum_maximum_fusion.left_ref, bf16[256,1024]{1,0:T(8,128)(2,1)S(1)} %collective-permute-done.9.refs_0_, bf16[128,1024]{1,0:T(8,128)(2,1)S(1)} %collective-permute-done.12.refs_1_, ...), custom_call_target="tpu_custom_call", output_to_operand_aliasing={{0}: (6, {})} | custom-call | tf_op jit(solution)/shard_map/pallas_call | solution.py:214
  34.5 1.8 %collective-permute-done.15.refs_0_ = bf16[256,1024]{1,0:T(8,128)(2,1)S(1)} collective-permute-done((bf16[256,1024]{1,0:T(8,128)(2,1)S(1)}, bf16[256,1024]{1,0:T(8,128)(2,1)S(1)}, u32[]{:S(2)}, u32[]{:S(2)}) %collective-permute-start.15) | collective-permute-done | bytes 524320 | tf_op jit(solution)/shard_map/ppermute | solution.py:329
  37.0 1.6 %collective-permute-start.21 = (bf16[256,1024]{1,0:T(8,128)(2,1)S(1)}, bf16[256,1024]{1,0:T(8,128)(2,1)S(1)}, u32[]{:S(2)}, u32[]{:S(2)}) collective-permute-start(bf16[256,1024]{1,0:T(8,128)(2,1)S(1)} %collective-permute-done.15.refs_0_), channel_id=1, source_target_pairs={{0,8},{2,6},{4,0},{6,14},{8,16},{10,2},{12,4},{14,22},{16,24},{18,... | collective-permute-start | bytes 1572872 | tf_op jit(solution)/shard_map/ppermute | solution.py:329
  38.5 1.5 %shard_map.57 = (bf16[2,256,4096]{2,1,0:T(8,128)(2,1)}, bf16[16,1024]{1,0:T(8,128)(2,1)S(1)}) custom-call(bf16[512,1024]{1,0:T(8,128)(2,1)S(1)} %maximum_maximum_fusion.left_ref, bf16[256,1024]{1,0:T(8,128)(2,1)S(1)} %collective-permute-done.8.refs_0_, bf16[128,1024]{1,0:T(8,128)(2,1)S(1)} %collective-permute-done.16.refs_1_, ...), custom_call_target="tpu_custom_call", output_to_operand_aliasing={{0}: (6, {})} | custom-call | tf_op jit(solution)/shard_map/pallas_call | solution.py:214
  40.1 1.9 %collective-permute-done.14.refs_0_ = bf16[256,1024]{1,0:T(8,128)(2,1)S(1)} collective-permute-done((bf16[256,1024]{1,0:T(8,128)(2,1)S(1)}, bf16[256,1024]{1,0:T(8,128)(2,1)S(1)}, u32[]{:S(2)}, u32[]{:S(2)}) %collective-permute-start.14) | collective-permute-done | bytes 524320 | tf_op jit(solution)/shard_map/ppermute | solution.py:329
  42.6 1.6 %collective-permute-start.20 = (bf16[256,1024]{1,0:T(8,128)(2,1)S(1)}, bf16[256,1024]{1,0:T(8,128)(2,1)S(1)}, u32[]{:S(2)}, u32[]{:S(2)}) collective-permute-start(bf16[256,1024]{1,0:T(8,128)(2,1)S(1)} %collective-permute-done.14.refs_0_), channel_id=1, source_target_pairs={{0,8},{2,6},{4,0},{6,14},{8,16},{10,2},{12,4},{14,22},{16,24},{18,... | collective-permute-start | bytes 1572872 | tf_op jit(solution)/shard_map/ppermute | solution.py:329
  44.2 1.5 %shard_map.58 = (bf16[2,256,4096]{2,1,0:T(8,128)(2,1)}, bf16[16,1024]{1,0:T(8,128)(2,1)S(1)}) custom-call(bf16[512,1024]{1,0:T(8,128)(2,1)S(1)} %maximum_maximum_fusion.left_ref, bf16[256,1024]{1,0:T(8,128)(2,1)S(1)} %collective-permute-done.15.refs_0_, bf16[128,1024]{1,0:T(8,128)(2,1)S(1)} %collective-permute-done.18.refs_1_, ...), custom_call_target="tpu_custom_call", output_to_operand_aliasing={{0}: (6, {})} | custom-call | tf_op jit(solution)/shard_map/pallas_call | solution.py:214
  45.7 1.8 %collective-permute-done.21.refs_0_ = bf16[256,1024]{1,0:T(8,128)(2,1)S(1)} collective-permute-done((bf16[256,1024]{1,0:T(8,128)(2,1)S(1)}, bf16[256,1024]{1,0:T(8,128)(2,1)S(1)}, u32[]{:S(2)}, u32[]{:S(2)}) %collective-permute-start.21) | collective-permute-done | bytes 524320 | tf_op jit(solution)/shard_map/ppermute | solution.py:329
  47.6 0.8 %fusion.14 = (bf16[128,1024]{1,0:T(8,128)(2,1)}, bf16[128,1024]{1,0:T(8,128)(2,1)}) fusion(bf16[256,1024]{1,0:T(8,128)(2,1)S(1)} %collective-permute-done.21.refs_0_), kind=kLoop, calls=%fused_computation.42 | loop fusion | bytes 1048576 | tf_op jit(solution)/shard_map/slice | solution.py:260
  48.9 1.6 %shard_map.59 = (bf16[2,256,4096]{2,1,0:T(8,128)(2,1)}, bf16[16,1024]{1,0:T(8,128)(2,1)S(1)}) custom-call(bf16[512,1024]{1,0:T(8,128)(2,1)S(1)} %maximum_maximum_fusion.left_ref, bf16[256,1024]{1,0:T(8,128)(2,1)S(1)} %collective-permute-done.14.refs_0_, bf16[128,1024]{1,0:T(8,128)(2,1)S(1)} %collective-permute-done.22.refs_1_, ...), custom_call_target="tpu_custom_call", output_to_operand_aliasing={{0}: (6, {})} | custom-call | tf_op jit(solution)/shard_map/pallas_call | solution.py:214
  50.7 2.5 %shard_map.60 = (bf16[2,256,4096]{2,1,0:T(8,128)(2,1)}, bf16[16,1024]{1,0:T(8,128)(2,1)S(1)}) custom-call(bf16[512,1024]{1,0:T(8,128)(2,1)S(1)} %maximum_maximum_fusion.left_ref, bf16[256,1024]{1,0:T(8,128)(2,1)S(1)} %collective-permute-done.21.refs_0_, bf16[128,1024]{1,0:T(8,128)(2,1)S(1)} %collective-permute-done.24.refs_1_, ...), custom_call_target="tpu_custom_call", output_to_operand_aliasing={{0}: (6, {})} | custom-call | tf_op jit(solution)/shard_map/pallas_call | solution.py:214
  54.2 1.0 %collective-permute-done.26.refs_2_ = bf16[16,1024]{1,0:T(8,128)(2,1)S(1)} collective-permute-done((bf16[16,1024]{1,0:T(8,128)(2,1)S(1)}, bf16[16,1024]{1,0:T(8,128)(2,1)S(1)}, u32[]{:S(2)}, u32[]{:S(2)}) %collective-permute-start.26) | collective-permute-done | bytes 32800 | tf_op jit(solution)/shard_map/ppermute | solution.py:337
  55.5 1.6 %collective-permute-start.27 = (f32[32,256]{1,0:T(8,128)S(1)}, f32[32,256]{1,0:T(8,128)S(1)}, u32[]{:S(2)}, u32[]{:S(2)}) collective-permute-start(f32[32,256]{1,0:T(8,128)S(1)} %shard_map.62), channel_id=1, source_target_pairs={{0,1},{1,0},{2,3},{3,2},{4,5},{5,4},{6,7},{7,6},{8,9},{9,8},{10,11... | collective-permute-start | bytes 98312 | tf_op jit(solution)/shard_map/ppermute | solution.py:279
  57.2 1.5 %shard_map.63 = bf16[2,256,4096]{2,1,0:T(8,128)(2,1)} custom-call(bf16[512,1024]{1,0:T(8,128)(2,1)S(1)} %maximum_maximum_fusion.left_ref, bf16[256,1024]{1,0:T(8,128)(2,1)S(1)} %collective-permute-done.20.block_ref.refs_0_, bf16[128,1024]{1,0:T(8,128)(2,1)S(1)} %collective-permute-done.28.refs_1_, ...), custom_call_target="tpu_custom_call", output_to_operand_aliasing={{}: (4, {})} | custom-call | tf_op jit(solution)/shard_map/pallas_call | solution.py:214
  58.8 0.7 %collective-permute-done.27 = f32[32,256]{1,0:T(8,128)S(1)} collective-permute-done((f32[32,256]{1,0:T(8,128)S(1)}, f32[32,256]{1,0:T(8,128)S(1)}, u32[]{:S(2)}, u32[]{:S(2)}) %collective-permute-start.27) | collective-permute-done | bytes 32800 | tf_op jit(solution)/shard_map/ppermute | solution.py:279
  59.6 1.8 %fusion.3 = f32[16,256,128]{2,1,0:T(8,128)} fusion(bf16[24,16,256]{2,1,0:T(8,128)(2,1)S(1)} %fusion.7, bf16[24,128]{1,0:T(8,128)(2,1)S(1)} %concatenate.32), kind=kOutput, calls=%fused_computation.11 | convolution fusion | flops 25165824 | bytes 2299904 | tf_op jit(solution)/shard_map/rsc,rl->scl/dot_general | solution.py:293
  (74 shorter events, 7.8 us)
Async XLA Ops:
  0.6 1.0 %copy-start = (bf16[1,256,1024]{2,1,0:T(8,128)(2,1)S(1)}, bf16[1,256,1024]{2,1,0:T(8,128)(2,1)}, u32[]{:S(2)}) copy-start(bf16[1,256,1024]{2,1,0:T(8,128)(2,1)} %param.3) | copy-start | bytes 1572868
  1.8 7.4 %collective-permute-start = (bf16[128,512]{1,0:T(8,128)(2,1)S(1)}, bf16[128,512]{1,0:T(8,128)(2,1)S(1)}, u32[]{:S(2)}, u32[]{:S(2)}) collective-permute-start(bf16[128,512]{1,0:T(8,128)(2,1)S(1)} %get-tuple-element.62), channel_id=1, source_target_pairs={{0,1},{1,0},{2,3},{3,2},{4,5},{5,4},{6,7},{7,6},{8,9},{9,8},{10,11... | collective-permute-start | bytes 393224 | tf_op jit(solution)/shard_map/ppermute | solution.py:303
  4.8 6.7 %collective-permute-start.1 = (bf16[128,512]{1,0:T(8,128)(2,1)S(1)}, bf16[128,512]{1,0:T(8,128)(2,1)S(1)}, u32[]{:S(2)}, u32[]{:S(2)}) collective-permute-start(bf16[128,512]{1,0:T(8,128)(2,1)S(1)} %get-tuple-element.63), channel_id=1, source_target_pairs={{0,1},{1,0},{2,3},{3,2},{4,5},{5,4},{6,7},{7,6},{8,9},{9,8},{10,11... | collective-permute-start | bytes 393224 | tf_op jit(solution)/shard_map/ppermute | solution.py:303
  4.9 1.0 %copy-start.1 = (s32[256,512]{1,0:T(8,128)S(1)}, s32[256,512]{1,0:T(8,128)}, u32[]{:S(2)}) copy-start(s32[256,512]{1,0:T(8,128)} %valid_ref.1) | copy-start | bytes 1572868
  9.3 7.1 %collective-permute-start.2 = (bf16[128,1024]{1,0:T(8,128)(2,1)S(1)}, bf16[128,1024]{1,0:T(8,128)(2,1)S(1)}, u32[]{:S(2)}, u32[]{:S(2)}) collective-permute-start(bf16[128,1024]{1,0:T(8,128)(2,1)S(1)} %shard_map.52), channel_id=1, source_target_pairs={{0,8},{2,6},{4,0},{6,14},{8,16},{10,2},{12,4},{14,22},{16,24},{18,... | collective-permute-start | bytes 786440 | tf_op jit(solution)/shard_map/ppermute | solution.py:306
  11.7 1.4 %collective-permute-start.3 = (bf16[64,1024]{1,0:T(8,128)(2,1)S(1)}, bf16[64,1024]{1,0:T(8,128)(2,1)S(1)}, u32[]{:S(2)}, u32[]{:S(2)}) collective-permute-start(bf16[64,1024]{1,0:T(8,128)(2,1)S(1)} %get-tuple-element.137), channel_id=1, source_target_pairs={{0,2},{2,0},{4,6},{6,4},{8,10},{10,8},{12,14},{14,12},{16,18},{18,... | collective-permute-start | bytes 393224 | tf_op jit(solution)/shard_map/ppermute | solution.py:260
  11.8 2.9 %collective-permute-start.6 = (bf16[64,1024]{1,0:T(8,128)(2,1)S(1)}, bf16[64,1024]{1,0:T(8,128)(2,1)S(1)}, u32[]{:S(2)}, u32[]{:S(2)}) collective-permute-start(bf16[64,1024]{1,0:T(8,128)(2,1)S(1)} %get-tuple-element.135), channel_id=1, source_target_pairs={{0,2},{2,0},{4,6},{6,4},{8,10},{10,8},{12,14},{14,12},{16,18},{18,... | collective-permute-start | bytes 393224 | tf_op jit(solution)/shard_map/ppermute | solution.py:260
  12.3 2.4 %collective-permute-start.7 = (bf16[64,1024]{1,0:T(8,128)(2,1)S(1)}, bf16[64,1024]{1,0:T(8,128)(2,1)S(1)}, u32[]{:S(2)}, u32[]{:S(2)}) collective-permute-start(bf16[64,1024]{1,0:T(8,128)(2,1)S(1)} %get-tuple-element.134), channel_id=1, source_target_pairs={{0,2},{2,0},{4,6},{6,4},{8,10},{10,8},{12,14},{14,12},{16,18},{18,... | collective-permute-start | bytes 393224 | tf_op jit(solution)/shard_map/ppermute | solution.py:260
  12.4 2.3 %collective-permute-start.5 = (bf16[64,1024]{1,0:T(8,128)(2,1)S(1)}, bf16[64,1024]{1,0:T(8,128)(2,1)S(1)}, u32[]{:S(2)}, u32[]{:S(2)}) collective-permute-start(bf16[64,1024]{1,0:T(8,128)(2,1)S(1)} %get-tuple-element.136), channel_id=1, source_target_pairs={{0,2},{2,0},{4,6},{6,4},{8,10},{10,8},{12,14},{14,12},{16,18},{18,... | collective-permute-start | bytes 393224 | tf_op jit(solution)/shard_map/ppermute | solution.py:260
  13.1 6.4 %collective-permute-start.4 = (bf16[128,1024]{1,0:T(8,128)(2,1)S(1)}, bf16[128,1024]{1,0:T(8,128)(2,1)S(1)}, u32[]{:S(2)}, u32[]{:S(2)}) collective-permute-start(bf16[128,1024]{1,0:T(8,128)(2,1)S(1)} %shard_map.53), channel_id=1, source_target_pairs={{0,8},{2,6},{4,0},{6,14},{8,16},{10,2},{12,4},{14,22},{16,24},{18,... | collective-permute-start | bytes 786440 | tf_op jit(solution)/shard_map/ppermute | solution.py:311
  14.8 10.4 %collective-permute-start.9 = (bf16[256,1024]{1,0:T(8,128)(2,1)S(1)}, bf16[256,1024]{1,0:T(8,128)(2,1)S(1)}, u32[]{:S(2)}, u32[]{:S(2)}) collective-permute-start(bf16[256,1024]{1,0:T(8,128)(2,1)S(1)} %pad_maximum_fusion.2), channel_id=1, source_target_pairs={{0,8},{2,6},{4,0},{6,14},{8,16},{10,2},{12,4},{14,22},{16,24},{18,... | collective-permute-start | bytes 1572872 | tf_op jit(solution)/shard_map/ppermute | solution.py:314
  19.6 2.2 %collective-permute-start.10 = (bf16[128,1024]{1,0:T(8,128)(2,1)S(1)}, bf16[128,1024]{1,0:T(8,128)(2,1)S(1)}, u32[]{:S(2)}, u32[]{:S(2)}) collective-permute-start(bf16[128,1024]{1,0:T(8,128)(2,1)S(1)} %get-tuple-element.131), channel_id=1, source_target_pairs={{0,2},{2,0},{4,6},{6,4},{8,10},{10,8},{12,14},{14,12},{16,18},{18,... | collective-permute-start | bytes 786440 | tf_op jit(solution)/shard_map/ppermute | solution.py:260
  19.7 2.1 %collective-permute-start.11 = (bf16[128,1024]{1,0:T(8,128)(2,1)S(1)}, bf16[128,1024]{1,0:T(8,128)(2,1)S(1)}, u32[]{:S(2)}, u32[]{:S(2)}) collective-permute-start(bf16[128,1024]{1,0:T(8,128)(2,1)S(1)} %get-tuple-element.130), channel_id=1, source_target_pairs={{0,2},{2,0},{4,6},{6,4},{8,10},{10,8},{12,14},{14,12},{16,18},{18,... | collective-permute-start | bytes 786440 | tf_op jit(solution)/shard_map/ppermute | solution.py:260
  20.2 10.6 %collective-permute-start.8 = (bf16[256,1024]{1,0:T(8,128)(2,1)S(1)}, bf16[256,1024]{1,0:T(8,128)(2,1)S(1)}, u32[]{:S(2)}, u32[]{:S(2)}) collective-permute-start(bf16[256,1024]{1,0:T(8,128)(2,1)S(1)} %pad_maximum_fusion.1.refs_0_), channel_id=1, source_target_pairs={{0,8},{2,6},{4,0},{6,14},{8,16},{10,2},{12,4},{14,22},{16,24},{18,... | collective-permute-start | bytes 1572872 | tf_op jit(solution)/shard_map/ppermute | solution.py:329
  25.2 3.7 %collective-permute-start.12 = (bf16[128,1024]{1,0:T(8,128)(2,1)S(1)}, bf16[128,1024]{1,0:T(8,128)(2,1)S(1)}, u32[]{:S(2)}, u32[]{:S(2)}) collective-permute-start(bf16[128,1024]{1,0:T(8,128)(2,1)S(1)} %get-tuple-element.129), channel_id=1, source_target_pairs={{0,2},{2,0},{4,6},{6,4},{8,10},{10,8},{12,14},{14,12},{16,18},{18,... | collective-permute-start | bytes 786440 | tf_op jit(solution)/shard_map/ppermute | solution.py:260
  25.2 3.6 %collective-permute-start.13 = (bf16[128,1024]{1,0:T(8,128)(2,1)S(1)}, bf16[128,1024]{1,0:T(8,128)(2,1)S(1)}, u32[]{:S(2)}, u32[]{:S(2)}) collective-permute-start(bf16[128,1024]{1,0:T(8,128)(2,1)S(1)} %get-tuple-element.128), channel_id=1, source_target_pairs={{0,2},{2,0},{4,6},{6,4},{8,10},{10,8},{12,14},{14,12},{16,18},{18,... | collective-permute-start | bytes 786440 | tf_op jit(solution)/shard_map/ppermute | solution.py:260
  25.7 10.6 %collective-permute-start.15 = (bf16[256,1024]{1,0:T(8,128)(2,1)S(1)}, bf16[256,1024]{1,0:T(8,128)(2,1)S(1)}, u32[]{:S(2)}, u32[]{:S(2)}) collective-permute-start(bf16[256,1024]{1,0:T(8,128)(2,1)S(1)} %collective-permute-done.9.refs_0_), channel_id=1, source_target_pairs={{0,8},{2,6},{4,0},{6,14},{8,16},{10,2},{12,4},{14,22},{16,24},{18,... | collective-permute-start | bytes 1572872 | tf_op jit(solution)/shard_map/ppermute | solution.py:329
  30.8 3.7 %collective-permute-start.16 = (bf16[128,1024]{1,0:T(8,128)(2,1)S(1)}, bf16[128,1024]{1,0:T(8,128)(2,1)S(1)}, u32[]{:S(2)}, u32[]{:S(2)}) collective-permute-start(bf16[128,1024]{1,0:T(8,128)(2,1)S(1)} %get-tuple-element.127), channel_id=1, source_target_pairs={{0,2},{2,0},{4,6},{6,4},{8,10},{10,8},{12,14},{14,12},{16,18},{18,... | collective-permute-start | bytes 786440 | tf_op jit(solution)/shard_map/ppermute | solution.py:260
  30.9 3.6 %collective-permute-start.17 = (bf16[128,1024]{1,0:T(8,128)(2,1)S(1)}, bf16[128,1024]{1,0:T(8,128)(2,1)S(1)}, u32[]{:S(2)}, u32[]{:S(2)}) collective-permute-start(bf16[128,1024]{1,0:T(8,128)(2,1)S(1)} %get-tuple-element.126), channel_id=1, source_target_pairs={{0,2},{2,0},{4,6},{6,4},{8,10},{10,8},{12,14},{14,12},{16,18},{18,... | collective-permute-start | bytes 786440 | tf_op jit(solution)/shard_map/ppermute | solution.py:260
  31.3 10.6 %collective-permute-start.14 = (bf16[256,1024]{1,0:T(8,128)(2,1)S(1)}, bf16[256,1024]{1,0:T(8,128)(2,1)S(1)}, u32[]{:S(2)}, u32[]{:S(2)}) collective-permute-start(bf16[256,1024]{1,0:T(8,128)(2,1)S(1)} %collective-permute-done.8.refs_0_), channel_id=1, source_target_pairs={{0,8},{2,6},{4,0},{6,14},{8,16},{10,2},{12,4},{14,22},{16,24},{18,... | collective-permute-start | bytes 1572872 | tf_op jit(solution)/shard_map/ppermute | solution.py:329
  36.4 5.6 %collective-permute-start.18 = (bf16[128,1024]{1,0:T(8,128)(2,1)S(1)}, bf16[128,1024]{1,0:T(8,128)(2,1)S(1)}, u32[]{:S(2)}, u32[]{:S(2)}) collective-permute-start(bf16[128,1024]{1,0:T(8,128)(2,1)S(1)} %get-tuple-element.125), channel_id=1, source_target_pairs={{0,2},{2,0},{4,6},{6,4},{8,10},{10,8},{12,14},{14,12},{16,18},{18,... | collective-permute-start | bytes 786440 | tf_op jit(solution)/shard_map/ppermute | solution.py:260
  36.5 5.5 %collective-permute-start.19 = (bf16[128,1024]{1,0:T(8,128)(2,1)S(1)}, bf16[128,1024]{1,0:T(8,128)(2,1)S(1)}, u32[]{:S(2)}, u32[]{:S(2)}) collective-permute-start(bf16[128,1024]{1,0:T(8,128)(2,1)S(1)} %get-tuple-element.124), channel_id=1, source_target_pairs={{0,2},{2,0},{4,6},{6,4},{8,10},{10,8},{12,14},{14,12},{16,18},{18,... | collective-permute-start | bytes 786440 | tf_op jit(solution)/shard_map/ppermute | solution.py:260
  37.0 10.6 %collective-permute-start.21 = (bf16[256,1024]{1,0:T(8,128)(2,1)S(1)}, bf16[256,1024]{1,0:T(8,128)(2,1)S(1)}, u32[]{:S(2)}, u32[]{:S(2)}) collective-permute-start(bf16[256,1024]{1,0:T(8,128)(2,1)S(1)} %collective-permute-done.15.refs_0_), channel_id=1, source_target_pairs={{0,8},{2,6},{4,0},{6,14},{8,16},{10,2},{12,4},{14,22},{16,24},{18,... | collective-permute-start | bytes 1572872 | tf_op jit(solution)/shard_map/ppermute | solution.py:329
  42.0 3.7 %collective-permute-start.22 = (bf16[128,1024]{1,0:T(8,128)(2,1)S(1)}, bf16[128,1024]{1,0:T(8,128)(2,1)S(1)}, u32[]{:S(2)}, u32[]{:S(2)}) collective-permute-start(bf16[128,1024]{1,0:T(8,128)(2,1)S(1)} %get-tuple-element.123), channel_id=1, source_target_pairs={{0,2},{2,0},{4,6},{6,4},{8,10},{10,8},{12,14},{14,12},{16,18},{18,... | collective-permute-start | bytes 786440 | tf_op jit(solution)/shard_map/ppermute | solution.py:260
  42.1 3.6 %collective-permute-start.23 = (bf16[128,1024]{1,0:T(8,128)(2,1)S(1)}, bf16[128,1024]{1,0:T(8,128)(2,1)S(1)}, u32[]{:S(2)}, u32[]{:S(2)}) collective-permute-start(bf16[128,1024]{1,0:T(8,128)(2,1)S(1)} %get-tuple-element.122), channel_id=1, source_target_pairs={{0,2},{2,0},{4,6},{6,4},{8,10},{10,8},{12,14},{14,12},{16,18},{18,... | collective-permute-start | bytes 786440 | tf_op jit(solution)/shard_map/ppermute | solution.py:260
  42.6 10.6 %collective-permute-start.20 = (bf16[256,1024]{1,0:T(8,128)(2,1)S(1)}, bf16[256,1024]{1,0:T(8,128)(2,1)S(1)}, u32[]{:S(2)}, u32[]{:S(2)}) collective-permute-start(bf16[256,1024]{1,0:T(8,128)(2,1)S(1)} %collective-permute-done.14.refs_0_), channel_id=1, source_target_pairs={{0,8},{2,6},{4,0},{6,14},{8,16},{10,2},{12,4},{14,22},{16,24},{18,... | collective-permute-start | bytes 1572872 | tf_op jit(solution)/shard_map/ppermute | solution.py:329
  48.4 2.1 %collective-permute-start.24 = (bf16[128,1024]{1,0:T(8,128)(2,1)}, bf16[128,1024]{1,0:T(8,128)(2,1)S(1)}, u32[]{:S(2)}, u32[]{:S(2)}) collective-permute-start(bf16[128,1024]{1,0:T(8,128)(2,1)} %get-tuple-element.121), channel_id=1, source_target_pairs={{0,2},{2,0},{4,6},{6,4},{8,10},{10,8},{12,14},{14,12},{16,18},{18,... | collective-permute-start | bytes 786440 | tf_op jit(solution)/shard_map/ppermute | solution.py:260
  48.4 2.2 %collective-permute-start.25 = (bf16[128,1024]{1,0:T(8,128)(2,1)}, bf16[128,1024]{1,0:T(8,128)(2,1)}, u32[]{:S(2)}, u32[]{:S(2)}) collective-permute-start(bf16[128,1024]{1,0:T(8,128)(2,1)} %get-tuple-element.120), channel_id=1, source_target_pairs={{0,2},{2,0},{4,6},{6,4},{8,10},{10,8},{12,14},{14,12},{16,18},{18,... | collective-permute-start | bytes 786440 | tf_op jit(solution)/shard_map/ppermute | solution.py:260
  53.2 4.0 %collective-permute-start.28 = (bf16[128,1024]{1,0:T(8,128)(2,1)S(1)}, bf16[128,1024]{1,0:T(8,128)(2,1)S(1)}, u32[]{:S(2)}, u32[]{:S(2)}) collective-permute-start(bf16[128,1024]{1,0:T(8,128)(2,1)S(1)} %get-tuple-element.119), channel_id=1, source_target_pairs={{0,2},{2,0},{4,6},{6,4},{8,10},{10,8},{12,14},{14,12},{16,18},{18,... | collective-permute-start | bytes 786440 | tf_op jit(solution)/shard_map/ppermute | solution.py:260
  53.4 3.8 %collective-permute-start.29 = (bf16[128,1024]{1,0:T(8,128)(2,1)S(1)}, bf16[128,1024]{1,0:T(8,128)(2,1)S(1)}, u32[]{:S(2)}, u32[]{:S(2)}) collective-permute-start(bf16[128,1024]{1,0:T(8,128)(2,1)S(1)} %get-tuple-element.118), channel_id=1, source_target_pairs={{0,2},{2,0},{4,6},{6,4},{8,10},{10,8},{12,14},{14,12},{16,18},{18,... | collective-permute-start | bytes 786440 | tf_op jit(solution)/shard_map/ppermute | solution.py:260
  54.0 1.2 %collective-permute-start.26 = (bf16[16,1024]{1,0:T(8,128)(2,1)S(1)}, bf16[16,1024]{1,0:T(8,128)(2,1)S(1)}, u32[]{:S(2)}, u32[]{:S(2)}) collective-permute-start(bf16[16,1024]{1,0:T(8,128)(2,1)S(1)} %shard_map.61.refs_1_), channel_id=1, source_target_pairs={{0,2},{2,0},{4,6},{6,4},{8,10},{10,8},{12,14},{14,12},{16,18},{18,... | collective-permute-start | bytes 98312 | tf_op jit(solution)/shard_map/ppermute | solution.py:337
  55.5 4.0 %collective-permute-start.27 = (f32[32,256]{1,0:T(8,128)S(1)}, f32[32,256]{1,0:T(8,128)S(1)}, u32[]{:S(2)}, u32[]{:S(2)}) collective-permute-start(f32[32,256]{1,0:T(8,128)S(1)} %shard_map.62), channel_id=1, source_target_pairs={{0,1},{1,0},{2,3},{3,2},{4,5},{5,4},{6,7},{7,6},{8,9},{9,8},{10,11... | collective-permute-start | bytes 98312 | tf_op jit(solution)/shard_map/ppermute | solution.py:279
  (1 other events, 0.7 us)

commit v4 on v3

--- a/solution.py
+++ b/solution.py
@@ -53,15 +53,6 @@
 
 def cost(microseconds):
     return pl.CostEstimate(flops=int(microseconds * 1.15e9), bytes_accessed=0, transcendentals=0)
-
-
-def split(values):
-    terms = []
-    for _ in range(3):
-        term = lax.reduce_precision(values, 8, 7)
-        terms.append(term.astype(jnp.bfloat16))
-        values = values - term
-    return terms
 
 
 def band_powers(raw, chunks):
@@ -248,9 +239,60 @@
     )(left, *parts)
 
 
+def spread(table, stations):
+    parts, lags = table.shape
+    high = lax.reduce_precision(table, 8, 7)
+    low = table - high
+    same = jnp.eye(stations, dtype=jnp.float32)[None, :, :, None]
+
+    def blocks(values):
+        return (values[:, None, None, :] * same).reshape(parts * stations, stations * lags).astype(jnp.bfloat16)
+
+    return jnp.concatenate([blocks(high), blocks(low), blocks(high)], axis=0)
+
+
+def lag_sums(kernels, table):
+    rows = kernels[0].shape[1]
+    stations = kernels[0].shape[0] // 2
+    lags = table.shape[1] // stations
+    groups = 4
+    each = stations // groups
+
+    def body(table_ref, *refs):
+        out_ref, held, sems = refs[-3:]
+        parts = jnp.concatenate([ref[...] for ref in refs[:-3]], axis=0)
+        high = parts.astype(jnp.bfloat16).astype(jnp.float32)
+        columns = jnp.concatenate([high, high, parts - high], axis=0).T.astype(jnp.bfloat16)
+        copies = []
+        for group in range(groups):
+            part = slice(group * each * lags, (group + 1) * each * lags)
+            sums = jnp.dot(columns, table_ref[:, part], preferred_element_type=jnp.float32)
+            for k in range(each):
+                held[group * each + k] = sums[:, k * lags : (k + 1) * lags]
+            part = pl.ds(group * each, each)
+            copies.append(pltpu.make_async_copy(held.at[part], out_ref.at[part], sems.at[group]))
+            copies[group].start()
+        for copy in copies:
+            copy.wait()
+
+    vmem = pl.BlockSpec(memory_space=pltpu.VMEM)
+    return pl.pallas_call(
+        body,
+        out_shape=jax.ShapeDtypeStruct((stations, rows, lags), jnp.float32),
+        in_specs=[vmem] * (1 + len(kernels)),
+        out_specs=pl.BlockSpec(memory_space=pl.ANY),
+        scratch_shapes=[pltpu.VMEM((stations, rows, lags), jnp.float32), pltpu.SemaphoreType.DMA((groups,))],
+        compiler_params=pltpu.CompilerParams(vmem_limit_bytes=8 * 2**20),
+        cost_estimate=cost(8.0),
+    )(table, *kernels)
+
+
 def make_on_device(group_size, freq_size):
     chips = group_size // 2
     ring = ring_pairs(group_size)
+    across = [
+        (device, device_of(place_of(device, chips) - 1 + 2 * (device % 2), 1 - device % 2, chips)) for device in range(group_size)
+    ]
 
     def swap_by(bit):
         return [(g, g ^ bit) for g in range(group_size)]
@@ -274,28 +316,15 @@
         total_bins = bin_count * freq_size
         scaling = 1.0 / math.sqrt(window_count)
 
-        def to_kernel(stations):
-            kernel = station_kernel(stations, left, scaling)
-            return [kernel] + [lax.ppermute(kernel, "freq", from_freq(shift)) for shift in range(1, freq_size)]
-
-        def to_lags(kernels):
-            lags_here = LAGS // freq_size
-            lag_values = (freq_index * lags_here + jnp.arange(lags_here, dtype=jnp.int32)).astype(jnp.float32)
-            tables = []
-            for shift in range(freq_size):
-                bin_value = lax.rem(freq_index - shift + freq_size, freq_size).astype(jnp.float32) + 1.0
-                phase = math.pi * bin_value * lag_values / LAGS
-                tables += [jnp.cos(phase), -jnp.sin(phase)]
-            table = jnp.stack(tables) / math.sqrt(total_bins)
-            kernels = jnp.concatenate(kernels, axis=0).reshape(2 * freq_size, station_index.shape[0], chan_count)
-            parts, table_parts = split(kernels), split(table)
-            pairs = [(0, 0), (0, 1), (1, 0), (0, 2), (1, 1), (2, 0)]
-            return jnp.einsum(
-                "rsc,rl->scl",
-                jnp.concatenate([parts[i] for i, _ in pairs], axis=0),
-                jnp.concatenate([table_parts[j] for _, j in pairs], axis=0),
-                preferred_element_type=jnp.float32,
-            )
+        station_count = station_index.shape[0]
+        lags_here = LAGS // freq_size
+        lag_values = (freq_index * lags_here + jnp.arange(lags_here, dtype=jnp.int32)).astype(jnp.float32)
+        tables = []
+        for shift in range(freq_size):
+            bin_value = lax.rem(freq_index - shift + freq_size, freq_size).astype(jnp.float32) + 1.0
+            phase = math.pi * bin_value * lag_values / LAGS
+            tables += [jnp.cos(phase), -jnp.sin(phase)]
+        table = spread(jnp.stack(tables) / math.sqrt(total_bins), station_count)
 
         chunks = 2
         raw, *powers = band_powers(spectra[0], chunks)
@@ -322,22 +351,30 @@
         flying[0] = jnp.concatenate(flying_parts, axis=0)
 
         steps = chips - 1
-        waiting = []
+        waiting, ahead, kernels = [], [], []
         for step in range(steps):
-            arrived, cross, stations, swapped = lax.optimization_barrier((flying[step], cross, stations, swapped))
+            arrived, cross, stations, swapped, ahead, kernels = lax.optimization_barrier(
+                (flying[step], cross, stations, swapped, ahead, kernels)
+            )
             if step + 2 < steps:
                 flying.append(lax.ppermute(arrived, "grp", ring))
+            if step + 3 == steps:
+                found = pick(arrived, numbers, functools.partial(ring_blocks, step, chips))
+                ahead = [lax.ppermute(lax.ppermute(found, "grp", swap_by(1)), "grp", across)]
+            if step == 2:
+                table, cross = lax.optimization_barrier((table, cross))
+            if step + 2 == steps:
+                ahead.append(lax.ppermute(ahead[0], "grp", swap_by(1)))
             next_swapped = swap(arrived)
             if waiting and step + 1 < steps:
                 cross, stations = cross_blocks(left, [waiting, swapped], places, cross, total_chans, scaling, numbers, stations)
             waiting, swapped, places = [arrived], next_swapped, functools.partial(ring_blocks, step, chips)
             if step + 2 == steps:
                 cross, stations = cross_blocks(left, [waiting, swapped], places, cross, total_chans, scaling, numbers, stations)
-        found = pick(waiting[0], numbers, places)
-        kernels = to_kernel([stations, found, lax.ppermute(found, "grp", swap_by(1))])
+                kernels = [station_kernel([stations, *ahead], left, scaling)]
+                others = [lax.ppermute(kernels[0], "freq", from_freq(shift)) for shift in range(1, freq_size)]
+        station_gather = lag_sums(kernels + others, table)
         cross = cross_blocks(left, [waiting, swapped], places, cross, total_chans, scaling)
-        kernels, cross = lax.optimization_barrier((kernels, cross))
-        station_gather = to_lags(kernels)
         return (cross[None], station_gather)
 
     return on_device

time: 61.6 us -> 60.1 us (0.976)
  matrix products: 1.8 us -> 0 us
  waiting for transfers between devices: 16.4 us -> 15.5 us
  Pallas kernels: 14.8 us -> 15.5 us
    dot_general x1 -> x0, matrix products: 1.8 us -> none  [to_lags(): jnp.einsum('rsc,rl->scl', jnp.concatenate([parts[i] for i, _ in pairs], a...]
    pallas_call x0 -> x1, Pallas kernels: none -> 1.63 us  [lag_sums(): pl.pallas_call(body, out_shape=jax.ShapeDtypeStruct((stations, rows, lags...]
    ppermute x5, waiting for transfers between devices: 7.45 us -> 5.82 us  [on_device(): flying.append(lax.ppermute(arrived, 'grp', ring))]
    ppermute x1 -> x3, starting transfers between devices: 1.59 us -> 2.76 us  [the longest x1 1.59 us: on_device(): lax.ppermute(kernels[0], 'freq', from_freq(shift))]
    pallas_call x8, Pallas kernels: 13.3 us -> 12.4 us  [cross_blocks(): pl.pallas_call(body, out_shape=shapes, in_specs=specs, out_specs=out_spec...]
    ppermute x1 -> x3, waiting for transfers between devices: 0.73 us -> 1.51 us  [the longest x1 1.08 us: on_device(): lax.ppermute(kernels[0], 'freq', from_freq(shift))]
    ppermute x5, starting transfers between devices: 7.88 us -> 7.14 us  [on_device(): flying.append(lax.ppermute(arrived, 'grp', ring))]
    ppermute x1, waiting for transfers between devices: 3.37 us -> 2.64 us  [on_device(): flying = [None, lax.ppermute(jnp.concatenate(swapped, axis=0), 'grp', ring)]]
  transfers between devices with their start and end apart: 30 -> 32, of which waited for: 11 -> 12; matrix products, arithmetic and copies ran while one was open for 2% -> 3% of each run, Pallas kernels for 24% -> 23%
where the time goes in v4:
time: 60.1 us; the launch traced here: 59.9 us
  starting transfers between devices  23.5 us (39%)
  Pallas kernels  15.5 us (26%)
  waiting for transfers between devices  15.5 us (26%)
  local copies, waits for them, and re-layouts  3.86 us (6%)
  between operations  1 us (2%)
  other arithmetic  0.63 us (1%)
    pallas_call x8, Pallas kernels, cross_blocks(): pl.pallas_call(body, out_shape=shapes, in_specs=specs, out_specs=out_spec...  12.4 us
    ppermute x5, starting transfers between devices, on_device(): flying.append(lax.ppermute(arrived, 'grp', ring))  7.14 us
    ppermute x5, waiting for transfers between devices, on_device(): flying.append(lax.ppermute(arrived, 'grp', ring))  5.82 us
    ppermute x18, starting transfers between devices, swap_pieces(): lax.ppermute(block[k * rows:(k + 1) * rows], 'grp', swap_by(1))  5 us
    ppermute x2, starting transfers between devices, on_device(): lax.ppermute(power, 'freq', from_freq(shift))  3.11 us
    unnamed x8, local copies, waits for them, and re-layouts  2.87 us
    ppermute x1, waiting for transfers between devices, on_device(): flying = [None, lax.ppermute(jnp.concatenate(swapped, axis=0), 'grp', ring)]  2.64 us
    ppermute x1, starting transfers between devices, on_device(): flying_parts = [lax.ppermute(parts[0], 'grp', ring)]  2.17 us
  transfers between devices with their start and end apart: 32, of which 12 were waited for; matrix products, arithmetic and copies ran while one was open for 3% of the time, Pallas kernels for 23%

profile of v4, /device:TPU:0, one launch (start us, length us, event | category | flops | bytes accessed | tf_op | source)
XLA Modules:
  0.0 59.9 jit_solution(450257614935426529)
XLA Ops:
  0.6 1.0 %copy-done = bf16[1,256,1024]{2,1,0:T(8,128)(2,1)S(1)} copy-done((bf16[1,256,1024]{2,1,0:T(8,128)(2,1)S(1)}, bf16[1,256,1024]{2,1,0:T(8,128)(2,1)}, u32[]{:S(2)}) %copy-start) | copy-done | bytes 524312
  1.8 3.0 %collective-permute-start = (bf16[128,512]{1,0:T(8,128)(2,1)S(1)}, bf16[128,512]{1,0:T(8,128)(2,1)S(1)}, u32[]{:S(2)}, u32[]{:S(2)}) collective-permute-start(bf16[128,512]{1,0:T(8,128)(2,1)S(1)} %get-tuple-element.62), channel_id=1, source_target_pairs={{0,1},{1,0},{2,3},{3,2},{4,5},{5,4},{6,7},{7,6},{8,9},{9,8},{10,11... | collective-permute-start | bytes 393224 | tf_op jit(solution)/shard_map/ppermute | solution.py:332
  4.9 1.0 %copy-done.1 = s32[256,512]{1,0:T(8,128)S(1)} copy-done((s32[256,512]{1,0:T(8,128)S(1)}, s32[256,512]{1,0:T(8,128)}, u32[]{:S(2)}) %copy-start.1) | copy-done | bytes 524312
  7.2 1.9 %collective-permute-done.refs_0_ = bf16[128,512]{1,0:T(8,128)(2,1)S(1)} collective-permute-done((bf16[128,512]{1,0:T(8,128)(2,1)S(1)}, bf16[128,512]{1,0:T(8,128)(2,1)S(1)}, u32[]{:S(2)}, u32[]{:S(2)}) %collective-permute-start) | collective-permute-done | bytes 131104 | tf_op jit(solution)/shard_map/ppermute | solution.py:332
  9.3 2.2 %collective-permute-start.2 = (bf16[128,1024]{1,0:T(8,128)(2,1)S(1)}, bf16[128,1024]{1,0:T(8,128)(2,1)S(1)}, u32[]{:S(2)}, u32[]{:S(2)}) collective-permute-start(bf16[128,1024]{1,0:T(8,128)(2,1)S(1)} %shard_map.52), channel_id=1, source_target_pairs={{0,8},{2,6},{4,0},{6,14},{8,16},{10,2},{12,4},{14,22},{16,24},{18,... | collective-permute-start | bytes 786440 | tf_op jit(solution)/shard_map/ppermute | solution.py:335
  13.0 0.9 %collective-permute-done.3.refs_1_ = bf16[64,1024]{1,0:T(8,128)(2,1)S(1)} collective-permute-done((bf16[64,1024]{1,0:T(8,128)(2,1)S(1)}, bf16[64,1024]{1,0:T(8,128)(2,1)S(1)}, u32[]{:S(2)}, u32[]{:S(2)}) %collective-permute-start.3) | collective-permute-done | bytes 131104 | tf_op jit(solution)/shard_map/ppermute | solution.py:302
  13.8 1.6 %collective-permute-start.4 = (bf16[128,1024]{1,0:T(8,128)(2,1)S(1)}, bf16[128,1024]{1,0:T(8,128)(2,1)S(1)}, u32[]{:S(2)}, u32[]{:S(2)}) collective-permute-start(bf16[128,1024]{1,0:T(8,128)(2,1)S(1)} %shard_map.53), channel_id=1, source_target_pairs={{0,8},{2,6},{4,0},{6,14},{8,16},{10,2},{12,4},{14,22},{16,24},{18,... | collective-permute-start | bytes 786440 | tf_op jit(solution)/shard_map/ppermute | solution.py:340
  15.5 1.6 %collective-permute-start.9 = (bf16[256,1024]{1,0:T(8,128)(2,1)S(1)}, bf16[256,1024]{1,0:T(8,128)(2,1)S(1)}, u32[]{:S(2)}, u32[]{:S(2)}) collective-permute-start(bf16[256,1024]{1,0:T(8,128)(2,1)S(1)} %pad_maximum_fusion.3), channel_id=1, source_target_pairs={{0,8},{2,6},{4,0},{6,14},{8,16},{10,2},{12,4},{14,22},{16,24},{18,... | collective-permute-start | bytes 1572872 | tf_op jit(solution)/shard_map/ppermute | solution.py:343
  17.1 1.6 %shard_map.54 = (bf16[2,256,4096]{2,1,0:T(8,128)(2,1)}, bf16[16,1024]{1,0:T(8,128)(2,1)S(1)}) custom-call(bf16[512,1024]{1,0:T(8,128)(2,1)S(1)} %maximum_maximum_fusion.left_ref, bf16[256,1024]{1,0:T(8,128)(2,1)S(1)} %pad_maximum_fusion.1.refs_0_, bf16[64,1024]{1,0:T(8,128)(2,1)S(1)} %collective-permute-done.3.refs_1_, ...), custom_call_target="tpu_custom_call" | custom-call | flops 4600000000 | tf_op jit(solution)/shard_map/pallas_call | solution.py:205
  18.7 1.5 %collective-permute-done.4 = bf16[128,1024]{1,0:T(8,128)(2,1)S(1)} collective-permute-done((bf16[128,1024]{1,0:T(8,128)(2,1)S(1)}, bf16[128,1024]{1,0:T(8,128)(2,1)S(1)}, u32[]{:S(2)}, u32[]{:S(2)}) %collective-permute-start.4) | collective-permute-done | bytes 262176 | tf_op jit(solution)/shard_map/ppermute | solution.py:340
  20.2 0.7 %fusion.13 = (bf16[128,1024]{1,0:T(8,128)(2,1)}, bf16[128,1024]{1,0:T(8,128)(2,1)S(1)}) fusion(bf16[256,1024]{1,0:T(8,128)(2,1)S(1)} %pad_maximum_fusion.2.refs_0_), kind=kLoop, calls=%fused_computation.34 | loop fusion | bytes 1048576 | tf_op jit(solution)/shard_map/slice | solution.py:302
  21.5 1.6 %collective-permute-start.8 = (bf16[256,1024]{1,0:T(8,128)(2,1)S(1)}, bf16[256,1024]{1,0:T(8,128)(2,1)S(1)}, u32[]{:S(2)}, u32[]{:S(2)}) collective-permute-start(bf16[256,1024]{1,0:T(8,128)(2,1)S(1)} %pad_maximum_fusion.2.refs_0_), channel_id=1, source_target_pairs={{0,8},{2,6},{4,0},{6,14},{8,16},{10,2},{12,4},{14,22},{16,24},{18,... | collective-permute-start | bytes 1572872 | tf_op jit(solution)/shard_map/ppermute | solution.py:360
  23.2 2.6 %collective-permute-done.9.refs_0_ = bf16[256,1024]{1,0:T(8,128)(2,1)S(1)} collective-permute-done((bf16[256,1024]{1,0:T(8,128)(2,1)S(1)}, bf16[256,1024]{1,0:T(8,128)(2,1)S(1)}, u32[]{:S(2)}, u32[]{:S(2)}) %collective-permute-start.9) | collective-permute-done | bytes 524320 | tf_op jit(solution)/shard_map/ppermute | solution.py:343
  26.5 1.6 %collective-permute-start.15 = (bf16[256,1024]{1,0:T(8,128)(2,1)S(1)}, bf16[256,1024]{1,0:T(8,128)(2,1)S(1)}, u32[]{:S(2)}, u32[]{:S(2)}) collective-permute-start(bf16[256,1024]{1,0:T(8,128)(2,1)S(1)} %collective-permute-done.9.refs_0_), channel_id=1, source_target_pairs={{0,8},{2,6},{4,0},{6,14},{8,16},{10,2},{12,4},{14,22},{16,24},{18,... | collective-permute-start | bytes 1572872 | tf_op jit(solution)/shard_map/ppermute | solution.py:360
  28.2 1.5 %shard_map.55 = (bf16[2,256,4096]{2,1,0:T(8,128)(2,1)}, bf16[16,1024]{1,0:T(8,128)(2,1)S(1)}) custom-call(bf16[512,1024]{1,0:T(8,128)(2,1)S(1)} %maximum_maximum_fusion.left_ref, bf16[256,1024]{1,0:T(8,128)(2,1)S(1)} %pad_maximum_fusion.2.refs_0_, bf16[128,1024]{1,0:T(8,128)(2,1)S(1)} %collective-permute-done.10.refs_1_, ...), custom_call_target="tpu_custom_call", output_to_operand_aliasing={{0}: (6, {})} | custom-call | tf_op jit(solution)/shard_map/pallas_call | solution.py:205
  29.7 1.7 %collective-permute-done.8.refs_0_ = bf16[256,1024]{1,0:T(8,128)(2,1)S(1)} collective-permute-done((bf16[256,1024]{1,0:T(8,128)(2,1)S(1)}, bf16[256,1024]{1,0:T(8,128)(2,1)S(1)}, u32[]{:S(2)}, u32[]{:S(2)}) %collective-permute-start.8) | collective-permute-done | bytes 524320 | tf_op jit(solution)/shard_map/ppermute | solution.py:360
  32.4 1.6 %collective-permute-start.14 = (bf16[256,1024]{1,0:T(8,128)(2,1)S(1)}, bf16[256,1024]{1,0:T(8,128)(2,1)S(1)}, u32[]{:S(2)}, u32[]{:S(2)}) collective-permute-start(bf16[256,1024]{1,0:T(8,128)(2,1)S(1)} %collective-permute-done.8.refs_0_), channel_id=1, source_target_pairs={{0,8},{2,6},{4,0},{6,14},{8,16},{10,2},{12,4},{14,22},{16,24},{18,... | collective-permute-start | bytes 1572872 | tf_op jit(solution)/shard_map/ppermute | solution.py:360
  34.1 1.6 %shard_map.56 = (bf16[2,256,4096]{2,1,0:T(8,128)(2,1)}, bf16[16,1024]{1,0:T(8,128)(2,1)S(1)}) custom-call(bf16[512,1024]{1,0:T(8,128)(2,1)S(1)} %maximum_maximum_fusion.left_ref, bf16[256,1024]{1,0:T(8,128)(2,1)S(1)} %collective-permute-done.9.refs_0_, bf16[128,1024]{1,0:T(8,128)(2,1)S(1)} %collective-permute-done.12.refs_1_, ...), custom_call_target="tpu_custom_call", output_to_operand_aliasing={{0}: (6, {})} | custom-call | tf_op jit(solution)/shard_map/pallas_call | solution.py:205
  35.6 1.4 %collective-permute-done.15.refs_0_ = bf16[256,1024]{1,0:T(8,128)(2,1)S(1)} collective-permute-done((bf16[256,1024]{1,0:T(8,128)(2,1)S(1)}, bf16[256,1024]{1,0:T(8,128)(2,1)S(1)}, u32[]{:S(2)}, u32[]{:S(2)}) %collective-permute-start.15) | collective-permute-done | bytes 524320 | tf_op jit(solution)/shard_map/ppermute | solution.py:360
  37.7 1.6 %collective-permute-start.21 = (bf16[256,1024]{1,0:T(8,128)(2,1)S(1)}, bf16[256,1024]{1,0:T(8,128)(2,1)S(1)}, u32[]{:S(2)}, u32[]{:S(2)}) collective-permute-start(bf16[256,1024]{1,0:T(8,128)(2,1)S(1)} %collective-permute-done.15.refs_0_), channel_id=1, source_target_pairs={{0,8},{2,6},{4,0},{6,14},{8,16},{10,2},{12,4},{14,22},{16,24},{18,... | collective-permute-start | bytes 1572872 | tf_op jit(solution)/shard_map/ppermute | solution.py:360
  39.2 1.5 %shard_map.57 = (bf16[2,256,4096]{2,1,0:T(8,128)(2,1)}, bf16[16,1024]{1,0:T(8,128)(2,1)S(1)}) custom-call(bf16[512,1024]{1,0:T(8,128)(2,1)S(1)} %maximum_maximum_fusion.left_ref, bf16[256,1024]{1,0:T(8,128)(2,1)S(1)} %collective-permute-done.8.refs_0_, bf16[128,1024]{1,0:T(8,128)(2,1)S(1)} %collective-permute-done.16.refs_1_, ...), custom_call_target="tpu_custom_call", output_to_operand_aliasing={{0}: (6, {})} | custom-call | tf_op jit(solution)/shard_map/pallas_call | solution.py:205
  40.8 1.9 %collective-permute-done.14.block_ref.refs_0_ = bf16[256,1024]{1,0:T(8,128)(2,1)S(1)} collective-permute-done((bf16[256,1024]{1,0:T(8,128)(2,1)S(1)}, bf16[256,1024]{1,0:T(8,128)(2,1)S(1)}, u32[]{:S(2)}, u32[]{:S(2)}) %collective-permute-start.14) | collective-permute-done | bytes 524320 | tf_op jit(solution)/shard_map/ppermute | solution.py:360
  43.6 1.2 %collective-permute-done.24 = bf16[16,1024]{1,0:T(8,128)(2,1)S(1)} collective-permute-done((bf16[16,1024]{1,0:T(8,128)(2,1)S(1)}, bf16[16,1024]{1,0:T(8,128)(2,1)S(1)}, u32[]{:S(2)}, u32[]{:S(2)}) %collective-permute-start.24) | collective-permute-done | bytes 32800 | tf_op jit(solution)/shard_map/ppermute | solution.py:363
  44.7 1.1 %collective-permute-start.25 = (bf16[16,1024]{1,0:T(8,128)(2,1)S(1)}, bf16[16,1024]{1,0:T(8,128)(2,1)S(1)}, u32[]{:S(2)}, u32[]{:S(2)}) collective-permute-start(bf16[16,1024]{1,0:T(8,128)(2,1)S(1)} %collective-permute-done.24), channel_id=1, source_target_pairs={{0,6},{2,8},{4,14},{6,0},{8,2},{10,16},{12,22},{14,4},{16,10},{18,... | collective-permute-start | bytes 98312 | tf_op jit(solution)/shard_map/ppermute | solution.py:363
  46.5 1.5 %shard_map.58 = (bf16[2,256,4096]{2,1,0:T(8,128)(2,1)}, bf16[16,1024]{1,0:T(8,128)(2,1)S(1)}) custom-call(bf16[512,1024]{1,0:T(8,128)(2,1)S(1)} %maximum_maximum_fusion.left_ref, bf16[256,1024]{1,0:T(8,128)(2,1)S(1)} %collective-permute-done.15.refs_0_, bf16[128,1024]{1,0:T(8,128)(2,1)S(1)} %collective-permute-done.18.refs_1_, ...), custom_call_target="tpu_custom_call", output_to_operand_aliasing={{0}: (6, {})} | custom-call | tf_op jit(solution)/shard_map/pallas_call | solution.py:205
  49.3 1.5 %shard_map.60 = (bf16[2,256,4096]{2,1,0:T(8,128)(2,1)}, bf16[16,1024]{1,0:T(8,128)(2,1)S(1)}) custom-call(bf16[512,1024]{1,0:T(8,128)(2,1)S(1)} %maximum_maximum_fusion.left_ref, bf16[256,1024]{1,0:T(8,128)(2,1)S(1)} %collective-permute-done.14.block_ref.refs_0_, ...), custom_call_target="tpu_custom_call", output_to_operand_aliasing={{0}: (6, {})} | custom-call | tf_op jit(solution)/shard_map/pallas_call | solution.py:205
  50.9 1.6 %shard_map.61 = (bf16[2,256,4096]{2,1,0:T(8,128)(2,1)}, bf16[16,1024]{1,0:T(8,128)(2,1)S(1)}) custom-call(bf16[512,1024]{1,0:T(8,128)(2,1)S(1)} %maximum_maximum_fusion.left_ref, bf16[256,1024]{1,0:T(8,128)(2,1)S(1)} %collective-permute-done.21.refs_0_, bf16[128,1024]{1,0:T(8,128)(2,1)S(1)} %collective-permute-done.26.refs_1_, ...), custom_call_target="tpu_custom_call", output_to_operand_aliasing={{0}: (6, {})} | custom-call | tf_op jit(solution)/shard_map/pallas_call | solution.py:205
  52.7 1.6 %collective-permute-start.31 = (f32[32,256]{1,0:T(8,128)S(1)}, f32[32,256]{1,0:T(8,128)S(1)}, u32[]{:S(2)}, u32[]{:S(2)}) collective-permute-start(f32[32,256]{1,0:T(8,128)S(1)} %shard_map.62.refs_0_), channel_id=1, source_target_pairs={{0,1},{1,0},{2,3},{3,2},{4,5},{5,4},{6,7},{7,6},{8,9},{9,8},{10,11... | collective-permute-start | bytes 98312 | tf_op jit(solution)/shard_map/ppermute | solution.py:375
  54.3 0.7 %collective-permute-done.20.refs_0_ = bf16[256,1024]{1,0:T(8,128)(2,1)S(1)} collective-permute-done((bf16[256,1024]{1,0:T(8,128)(2,1)S(1)}, bf16[256,1024]{1,0:T(8,128)(2,1)S(1)}, u32[]{:S(2)}, u32[]{:S(2)}) %collective-permute-start.20) | collective-permute-done | bytes 524320 | tf_op jit(solution)/shard_map/ppermute | solution.py:360
  55.6 1.1 %collective-permute-done.31.refs_1_ = f32[32,256]{1,0:T(8,128)S(1)} collective-permute-done((f32[32,256]{1,0:T(8,128)S(1)}, f32[32,256]{1,0:T(8,128)S(1)}, u32[]{:S(2)}, u32[]{:S(2)}) %collective-permute-start.31) | collective-permute-done | bytes 32800 | tf_op jit(solution)/shard_map/ppermute | solution.py:375
  56.7 1.6 %shard_map.64 = f32[16,256,128]{2,1,0:T(8,128)} custom-call(bf16[192,2048]{1,0:T(8,128)(2,1)S(1)} %pad_maximum_fusion.table_ref, f32[32,256]{1,0:T(8,128)S(1)} %shard_map.62.refs_0_, f32[32,256]{1,0:T(8,128)S(1)} %collective-permute-done.31.refs_1_), custom_call_target="tpu_custom_call" | custom-call | flops 9200000000 | tf_op jit(solution)/shard_map/pallas_call | solution.py:279
  58.4 1.6 %shard_map.63 = bf16[2,256,4096]{2,1,0:T(8,128)(2,1)} custom-call(bf16[512,1024]{1,0:T(8,128)(2,1)S(1)} %maximum_maximum_fusion.left_ref, bf16[256,1024]{1,0:T(8,128)(2,1)S(1)} %collective-permute-done.20.refs_0_, bf16[128,1024]{1,0:T(8,128)(2,1)S(1)} %collective-permute-done.29.refs_1_, ...), custom_call_target="tpu_custom_call", output_to_operand_aliasing={{}: (4, {})} | custom-call | tf_op jit(solution)/shard_map/pallas_call | solution.py:205
  (75 shorter events, 9.6 us)
Async XLA Ops:
  1.8 7.4 %collective-permute-start = (bf16[128,512]{1,0:T(8,128)(2,1)S(1)}, bf16[128,512]{1,0:T(8,128)(2,1)S(1)}, u32[]{:S(2)}, u32[]{:S(2)}) collective-permute-start(bf16[128,512]{1,0:T(8,128)(2,1)S(1)} %get-tuple-element.62), channel_id=1, source_target_pairs={{0,1},{1,0},{2,3},{3,2},{4,5},{5,4},{6,7},{7,6},{8,9},{9,8},{10,11... | collective-permute-start | bytes 393224 | tf_op jit(solution)/shard_map/ppermute | solution.py:332
  4.8 6.7 %collective-permute-start.1 = (bf16[128,512]{1,0:T(8,128)(2,1)S(1)}, bf16[128,512]{1,0:T(8,128)(2,1)S(1)}, u32[]{:S(2)}, u32[]{:S(2)}) collective-permute-start(bf16[128,512]{1,0:T(8,128)(2,1)S(1)} %get-tuple-element.63), channel_id=1, source_target_pairs={{0,1},{1,0},{2,3},{3,2},{4,5},{5,4},{6,7},{7,6},{8,9},{9,8},{10,11... | collective-permute-start | bytes 393224 | tf_op jit(solution)/shard_map/ppermute | solution.py:332
  9.3 7.8 %collective-permute-start.2 = (bf16[128,1024]{1,0:T(8,128)(2,1)S(1)}, bf16[128,1024]{1,0:T(8,128)(2,1)S(1)}, u32[]{:S(2)}, u32[]{:S(2)}) collective-permute-start(bf16[128,1024]{1,0:T(8,128)(2,1)S(1)} %shard_map.52), channel_id=1, source_target_pairs={{0,8},{2,6},{4,0},{6,14},{8,16},{10,2},{12,4},{14,22},{16,24},{18,... | collective-permute-start | bytes 786440 | tf_op jit(solution)/shard_map/ppermute | solution.py:335
  11.7 3.7 %collective-permute-start.7 = (bf16[64,1024]{1,0:T(8,128)(2,1)S(1)}, bf16[64,1024]{1,0:T(8,128)(2,1)S(1)}, u32[]{:S(2)}, u32[]{:S(2)}) collective-permute-start(bf16[64,1024]{1,0:T(8,128)(2,1)S(1)} %get-tuple-element.134), channel_id=1, source_target_pairs={{0,2},{2,0},{4,6},{6,4},{8,10},{10,8},{12,14},{14,12},{16,18},{18,... | collective-permute-start | bytes 393224 | tf_op jit(solution)/shard_map/ppermute | solution.py:302
  11.8 3.6 %collective-permute-start.6 = (bf16[64,1024]{1,0:T(8,128)(2,1)S(1)}, bf16[64,1024]{1,0:T(8,128)(2,1)S(1)}, u32[]{:S(2)}, u32[]{:S(2)}) collective-permute-start(bf16[64,1024]{1,0:T(8,128)(2,1)S(1)} %get-tuple-element.135), channel_id=1, source_target_pairs={{0,2},{2,0},{4,6},{6,4},{8,10},{10,8},{12,14},{14,12},{16,18},{18,... | collective-permute-start | bytes 393224 | tf_op jit(solution)/shard_map/ppermute | solution.py:302
  12.3 3.1 %collective-permute-start.5 = (bf16[64,1024]{1,0:T(8,128)(2,1)S(1)}, bf16[64,1024]{1,0:T(8,128)(2,1)S(1)}, u32[]{:S(2)}, u32[]{:S(2)}) collective-permute-start(bf16[64,1024]{1,0:T(8,128)(2,1)S(1)} %get-tuple-element.136), channel_id=1, source_target_pairs={{0,2},{2,0},{4,6},{6,4},{8,10},{10,8},{12,14},{14,12},{16,18},{18,... | collective-permute-start | bytes 393224 | tf_op jit(solution)/shard_map/ppermute | solution.py:302
  12.4 1.5 %collective-permute-start.3 = (bf16[64,1024]{1,0:T(8,128)(2,1)S(1)}, bf16[64,1024]{1,0:T(8,128)(2,1)S(1)}, u32[]{:S(2)}, u32[]{:S(2)}) collective-permute-start(bf16[64,1024]{1,0:T(8,128)(2,1)S(1)} %get-tuple-element.137), channel_id=1, source_target_pairs={{0,2},{2,0},{4,6},{6,4},{8,10},{10,8},{12,14},{14,12},{16,18},{18,... | collective-permute-start | bytes 393224 | tf_op jit(solution)/shard_map/ppermute | solution.py:302
  13.8 6.4 %collective-permute-start.4 = (bf16[128,1024]{1,0:T(8,128)(2,1)S(1)}, bf16[128,1024]{1,0:T(8,128)(2,1)S(1)}, u32[]{:S(2)}, u32[]{:S(2)}) collective-permute-start(bf16[128,1024]{1,0:T(8,128)(2,1)S(1)} %shard_map.53), channel_id=1, source_target_pairs={{0,8},{2,6},{4,0},{6,14},{8,16},{10,2},{12,4},{14,22},{16,24},{18,... | collective-permute-start | bytes 786440 | tf_op jit(solution)/shard_map/ppermute | solution.py:340
  15.5 10.4 %collective-permute-start.9 = (bf16[256,1024]{1,0:T(8,128)(2,1)S(1)}, bf16[256,1024]{1,0:T(8,128)(2,1)S(1)}, u32[]{:S(2)}, u32[]{:S(2)}) collective-permute-start(bf16[256,1024]{1,0:T(8,128)(2,1)S(1)} %pad_maximum_fusion.3), channel_id=1, source_target_pairs={{0,8},{2,6},{4,0},{6,14},{8,16},{10,2},{12,4},{14,22},{16,24},{18,... | collective-permute-start | bytes 1572872 | tf_op jit(solution)/shard_map/ppermute | solution.py:343
  21.0 4.8 %collective-permute-start.11 = (bf16[128,1024]{1,0:T(8,128)(2,1)}, bf16[128,1024]{1,0:T(8,128)(2,1)S(1)}, u32[]{:S(2)}, u32[]{:S(2)}) collective-permute-start(bf16[128,1024]{1,0:T(8,128)(2,1)} %get-tuple-element.130), channel_id=1, source_target_pairs={{0,2},{2,0},{4,6},{6,4},{8,10},{10,8},{12,14},{14,12},{16,18},{18,... | collective-permute-start | bytes 786440 | tf_op jit(solution)/shard_map/ppermute | solution.py:302
  21.0 4.8 %collective-permute-start.10 = (bf16[128,1024]{1,0:T(8,128)(2,1)S(1)}, bf16[128,1024]{1,0:T(8,128)(2,1)S(1)}, u32[]{:S(2)}, u32[]{:S(2)}) collective-permute-start(bf16[128,1024]{1,0:T(8,128)(2,1)S(1)} %get-tuple-element.131), channel_id=1, source_target_pairs={{0,2},{2,0},{4,6},{6,4},{8,10},{10,8},{12,14},{14,12},{16,18},{18,... | collective-permute-start | bytes 786440 | tf_op jit(solution)/shard_map/ppermute | solution.py:302
  21.5 9.9 %collective-permute-start.8 = (bf16[256,1024]{1,0:T(8,128)(2,1)S(1)}, bf16[256,1024]{1,0:T(8,128)(2,1)S(1)}, u32[]{:S(2)}, u32[]{:S(2)}) collective-permute-start(bf16[256,1024]{1,0:T(8,128)(2,1)S(1)} %pad_maximum_fusion.2.refs_0_), channel_id=1, source_target_pairs={{0,8},{2,6},{4,0},{6,14},{8,16},{10,2},{12,4},{14,22},{16,24},{18,... | collective-permute-start | bytes 1572872 | tf_op jit(solution)/shard_map/ppermute | solution.py:360
  25.9 3.9 %collective-permute-start.13 = (bf16[128,1024]{1,0:T(8,128)(2,1)S(1)}, bf16[128,1024]{1,0:T(8,128)(2,1)S(1)}, u32[]{:S(2)}, u32[]{:S(2)}) collective-permute-start(bf16[128,1024]{1,0:T(8,128)(2,1)S(1)} %get-tuple-element.128), channel_id=1, source_target_pairs={{0,2},{2,0},{4,6},{6,4},{8,10},{10,8},{12,14},{14,12},{16,18},{18,... | collective-permute-start | bytes 786440 | tf_op jit(solution)/shard_map/ppermute | solution.py:302
  25.9 3.8 %collective-permute-start.12 = (bf16[128,1024]{1,0:T(8,128)(2,1)S(1)}, bf16[128,1024]{1,0:T(8,128)(2,1)S(1)}, u32[]{:S(2)}, u32[]{:S(2)}) collective-permute-start(bf16[128,1024]{1,0:T(8,128)(2,1)S(1)} %get-tuple-element.129), channel_id=1, source_target_pairs={{0,2},{2,0},{4,6},{6,4},{8,10},{10,8},{12,14},{14,12},{16,18},{18,... | collective-permute-start | bytes 786440 | tf_op jit(solution)/shard_map/ppermute | solution.py:302
  26.5 10.5 %collective-permute-start.15 = (bf16[256,1024]{1,0:T(8,128)(2,1)S(1)}, bf16[256,1024]{1,0:T(8,128)(2,1)S(1)}, u32[]{:S(2)}, u32[]{:S(2)}) collective-permute-start(bf16[256,1024]{1,0:T(8,128)(2,1)S(1)} %collective-permute-done.9.refs_0_), channel_id=1, source_target_pairs={{0,8},{2,6},{4,0},{6,14},{8,16},{10,2},{12,4},{14,22},{16,24},{18,... | collective-permute-start | bytes 1572872 | tf_op jit(solution)/shard_map/ppermute | solution.py:360
  31.5 5.6 %collective-permute-start.17 = (bf16[128,1024]{1,0:T(8,128)(2,1)S(1)}, bf16[128,1024]{1,0:T(8,128)(2,1)S(1)}, u32[]{:S(2)}, u32[]{:S(2)}) collective-permute-start(bf16[128,1024]{1,0:T(8,128)(2,1)S(1)} %get-tuple-element.126), channel_id=1, source_target_pairs={{0,2},{2,0},{4,6},{6,4},{8,10},{10,8},{12,14},{14,12},{16,18},{18,... | collective-permute-start | bytes 786440 | tf_op jit(solution)/shard_map/ppermute | solution.py:302
  31.5 5.5 %collective-permute-start.16 = (bf16[128,1024]{1,0:T(8,128)(2,1)S(1)}, bf16[128,1024]{1,0:T(8,128)(2,1)S(1)}, u32[]{:S(2)}, u32[]{:S(2)}) collective-permute-start(bf16[128,1024]{1,0:T(8,128)(2,1)S(1)} %get-tuple-element.127), channel_id=1, source_target_pairs={{0,2},{2,0},{4,6},{6,4},{8,10},{10,8},{12,14},{14,12},{16,18},{18,... | collective-permute-start | bytes 786440 | tf_op jit(solution)/shard_map/ppermute | solution.py:302
  32.4 10.3 %collective-permute-start.14 = (bf16[256,1024]{1,0:T(8,128)(2,1)S(1)}, bf16[256,1024]{1,0:T(8,128)(2,1)S(1)}, u32[]{:S(2)}, u32[]{:S(2)}) collective-permute-start(bf16[256,1024]{1,0:T(8,128)(2,1)S(1)} %collective-permute-done.8.refs_0_), channel_id=1, source_target_pairs={{0,8},{2,6},{4,0},{6,14},{8,16},{10,2},{12,4},{14,22},{16,24},{18,... | collective-permute-start | bytes 1572872 | tf_op jit(solution)/shard_map/ppermute | solution.py:360
  37.1 5.6 %collective-permute-start.19 = (bf16[128,1024]{1,0:T(8,128)(2,1)S(1)}, bf16[128,1024]{1,0:T(8,128)(2,1)S(1)}, u32[]{:S(2)}, u32[]{:S(2)}) collective-permute-start(bf16[128,1024]{1,0:T(8,128)(2,1)S(1)} %get-tuple-element.124), channel_id=1, source_target_pairs={{0,2},{2,0},{4,6},{6,4},{8,10},{10,8},{12,14},{14,12},{16,18},{18,... | collective-permute-start | bytes 786440 | tf_op jit(solution)/shard_map/ppermute | solution.py:302
  37.2 5.5 %collective-permute-start.18 = (bf16[128,1024]{1,0:T(8,128)(2,1)S(1)}, bf16[128,1024]{1,0:T(8,128)(2,1)S(1)}, u32[]{:S(2)}, u32[]{:S(2)}) collective-permute-start(bf16[128,1024]{1,0:T(8,128)(2,1)S(1)} %get-tuple-element.125), channel_id=1, source_target_pairs={{0,2},{2,0},{4,6},{6,4},{8,10},{10,8},{12,14},{14,12},{16,18},{18,... | collective-permute-start | bytes 786440 | tf_op jit(solution)/shard_map/ppermute | solution.py:302
  37.7 11.0 %collective-permute-start.21 = (bf16[256,1024]{1,0:T(8,128)(2,1)S(1)}, bf16[256,1024]{1,0:T(8,128)(2,1)S(1)}, u32[]{:S(2)}, u32[]{:S(2)}) collective-permute-start(bf16[256,1024]{1,0:T(8,128)(2,1)S(1)} %collective-permute-done.15.refs_0_), channel_id=1, source_target_pairs={{0,8},{2,6},{4,0},{6,14},{8,16},{10,2},{12,4},{14,22},{16,24},{18,... | collective-permute-start | bytes 1572872 | tf_op jit(solution)/shard_map/ppermute | solution.py:360
  42.7 5.9 %collective-permute-start.23 = (bf16[128,1024]{1,0:T(8,128)(2,1)S(1)}, bf16[128,1024]{1,0:T(8,128)(2,1)S(1)}, u32[]{:S(2)}, u32[]{:S(2)}) collective-permute-start(bf16[128,1024]{1,0:T(8,128)(2,1)S(1)} %get-tuple-element.122), channel_id=1, source_target_pairs={{0,2},{2,0},{4,6},{6,4},{8,10},{10,8},{12,14},{14,12},{16,18},{18,... | collective-permute-start | bytes 786440 | tf_op jit(solution)/shard_map/ppermute | solution.py:302
  42.8 5.8 %collective-permute-start.22 = (bf16[128,1024]{1,0:T(8,128)(2,1)S(1)}, bf16[128,1024]{1,0:T(8,128)(2,1)S(1)}, u32[]{:S(2)}, u32[]{:S(2)}) collective-permute-start(bf16[128,1024]{1,0:T(8,128)(2,1)S(1)} %get-tuple-element.123), channel_id=1, source_target_pairs={{0,2},{2,0},{4,6},{6,4},{8,10},{10,8},{12,14},{14,12},{16,18},{18,... | collective-permute-start | bytes 786440 | tf_op jit(solution)/shard_map/ppermute | solution.py:302
  43.5 1.3 %collective-permute-start.24 = (bf16[16,1024]{1,0:T(8,128)(2,1)S(1)}, bf16[16,1024]{1,0:T(8,128)(2,1)S(1)}, u32[]{:S(2)}, u32[]{:S(2)}) collective-permute-start(bf16[16,1024]{1,0:T(8,128)(2,1)S(1)} %shard_map.59), channel_id=1, source_target_pairs={{0,2},{2,0},{4,6},{6,4},{8,10},{10,8},{12,14},{14,12},{16,18},{18,... | collective-permute-start | bytes 98312 | tf_op jit(solution)/shard_map/ppermute | solution.py:363
  44.7 3.8 %collective-permute-start.25 = (bf16[16,1024]{1,0:T(8,128)(2,1)S(1)}, bf16[16,1024]{1,0:T(8,128)(2,1)S(1)}, u32[]{:S(2)}, u32[]{:S(2)}) collective-permute-start(bf16[16,1024]{1,0:T(8,128)(2,1)S(1)} %collective-permute-done.24), channel_id=1, source_target_pairs={{0,6},{2,8},{4,14},{6,0},{8,2},{10,16},{12,22},{14,4},{16,10},{18,... | collective-permute-start | bytes 98312 | tf_op jit(solution)/shard_map/ppermute | solution.py:363
  45.8 9.2 %collective-permute-start.20 = (bf16[256,1024]{1,0:T(8,128)(2,1)S(1)}, bf16[256,1024]{1,0:T(8,128)(2,1)S(1)}, u32[]{:S(2)}, u32[]{:S(2)}) collective-permute-start(bf16[256,1024]{1,0:T(8,128)(2,1)S(1)} %collective-permute-done.14.block_ref.refs_0_), channel_id=1, source_target_pairs={{0,8},{2,6},{4,0},{6,14},{8,16},{10,2},{12,4},{14,22},{16,24},{18,... | collective-permute-start | bytes 1572872 | tf_op jit(solution)/shard_map/ppermute | solution.py:360
  48.7 2.2 %collective-permute-start.27 = (bf16[128,1024]{1,0:T(8,128)(2,1)S(1)}, bf16[128,1024]{1,0:T(8,128)(2,1)S(1)}, u32[]{:S(2)}, u32[]{:S(2)}) collective-permute-start(bf16[128,1024]{1,0:T(8,128)(2,1)S(1)} %get-tuple-element.120), channel_id=1, source_target_pairs={{0,2},{2,0},{4,6},{6,4},{8,10},{10,8},{12,14},{14,12},{16,18},{18,... | collective-permute-start | bytes 786440 | tf_op jit(solution)/shard_map/ppermute | solution.py:302
  48.8 2.1 %collective-permute-start.26 = (bf16[128,1024]{1,0:T(8,128)(2,1)S(1)}, bf16[128,1024]{1,0:T(8,128)(2,1)S(1)}, u32[]{:S(2)}, u32[]{:S(2)}) collective-permute-start(bf16[128,1024]{1,0:T(8,128)(2,1)S(1)} %get-tuple-element.121), channel_id=1, source_target_pairs={{0,2},{2,0},{4,6},{6,4},{8,10},{10,8},{12,14},{14,12},{16,18},{18,... | collective-permute-start | bytes 786440 | tf_op jit(solution)/shard_map/ppermute | solution.py:302
  49.3 3.2 %collective-permute-start.28 = (bf16[16,1024]{1,0:T(8,128)(2,1)S(1)}, bf16[16,1024]{1,0:T(8,128)(2,1)S(1)}, u32[]{:S(2)}, u32[]{:S(2)}) collective-permute-start(bf16[16,1024]{1,0:T(8,128)(2,1)S(1)} %collective-permute-done.25.refs_1_), channel_id=1, source_target_pairs={{0,2},{2,0},{4,6},{6,4},{8,10},{10,8},{12,14},{14,12},{16,18},{18,... | collective-permute-start | bytes 98312 | tf_op jit(solution)/shard_map/ppermute | solution.py:367
  52.7 4.0 %collective-permute-start.31 = (f32[32,256]{1,0:T(8,128)S(1)}, f32[32,256]{1,0:T(8,128)S(1)}, u32[]{:S(2)}, u32[]{:S(2)}) collective-permute-start(f32[32,256]{1,0:T(8,128)S(1)} %shard_map.62.refs_0_), channel_id=1, source_target_pairs={{0,1},{1,0},{2,3},{3,2},{4,5},{5,4},{6,7},{7,6},{8,9},{9,8},{10,11... | collective-permute-start | bytes 98312 | tf_op jit(solution)/shard_map/ppermute | solution.py:375
  55.0 3.3 %collective-permute-start.30 = (bf16[128,1024]{1,0:T(8,128)(2,1)S(1)}, bf16[128,1024]{1,0:T(8,128)(2,1)S(1)}, u32[]{:S(2)}, u32[]{:S(2)}) collective-permute-start(bf16[128,1024]{1,0:T(8,128)(2,1)S(1)} %get-tuple-element.118), channel_id=1, source_target_pairs={{0,2},{2,0},{4,6},{6,4},{8,10},{10,8},{12,14},{14,12},{16,18},{18,... | collective-permute-start | bytes 786440 | tf_op jit(solution)/shard_map/ppermute | solution.py:302
  55.1 3.2 %collective-permute-start.29 = (bf16[128,1024]{1,0:T(8,128)(2,1)S(1)}, bf16[128,1024]{1,0:T(8,128)(2,1)S(1)}, u32[]{:S(2)}, u32[]{:S(2)}) collective-permute-start(bf16[128,1024]{1,0:T(8,128)(2,1)S(1)} %get-tuple-element.119), channel_id=1, source_target_pairs={{0,2},{2,0},{4,6},{6,4},{8,10},{10,8},{12,14},{14,12},{16,18},{18,... | collective-permute-start | bytes 786440 | tf_op jit(solution)/shard_map/ppermute | solution.py:302
  (3 other events, 2.7 us)

commit v5 on v4

--- a/solution.py
+++ b/solution.py
@@ -55,22 +55,20 @@
     return pl.CostEstimate(flops=int(microseconds * 1.15e9), bytes_accessed=0, transcendentals=0)
 
 
-def band_powers(raw, chunks):
+def band_power(raw):
     rows, width = raw.shape[0], raw.shape[1] // 2
 
-    def body(raw_ref, raw_out, *power_outs):
-        for k, power_out in enumerate(power_outs):
-            part = raw_ref[k * rows // chunks : (k + 1) * rows // chunks, :].astype(jnp.float32)
-            power_out[...] = (part[:, :width] * part[:, :width] + part[:, width:] * part[:, width:]).astype(jnp.bfloat16)
+    def body(raw_ref, raw_out, power_out):
+        part = raw_ref[...].astype(jnp.float32)
+        power_out[...] = (part[:, :width] * part[:, :width] + part[:, width:] * part[:, width:]).astype(jnp.bfloat16)
         raw_out[...] = raw_ref[...]
 
     vmem = pl.BlockSpec(memory_space=pltpu.VMEM)
     return pl.pallas_call(
         body,
-        out_shape=[jax.ShapeDtypeStruct(raw.shape, jnp.bfloat16)]
-        + [jax.ShapeDtypeStruct((rows // chunks, width), jnp.bfloat16)] * chunks,
+        out_shape=[jax.ShapeDtypeStruct(raw.shape, jnp.bfloat16), jax.ShapeDtypeStruct((rows, width), jnp.bfloat16)],
         in_specs=[vmem],
-        out_specs=[vmem] * (1 + chunks),
+        out_specs=[vmem, vmem],
         compiler_params=pltpu.CompilerParams(vmem_limit_bytes=6 * 2**20),
         cost_estimate=cost(0.1),
     )(raw)
@@ -112,30 +110,50 @@
     )(station_index, valid, after)
 
 
-def whiten(raw, valid, received, chunk, chunks, total_bins):
-    rows, width = raw.shape[0] // chunks, raw.shape[1] // 2
+def whiten_rows(raw, others, total_bins):
+    part = raw.astype(jnp.float32)
+    width = part.shape[1] // 2
+    real, imag = part[:, :width], part[:, width:]
+    power = real * real + imag * imag + others
+    factor = jnp.where(others < 0.0, 0.0, lax.rsqrt(power / total_bins + 1e-05))
+    return (real * factor).astype(jnp.bfloat16), (imag * factor).astype(jnp.bfloat16)
+
+
+def whiten_own(raw, valid, received, total_bins):
+    rows, width = valid.shape
 
     def body(raw_ref, valid_ref, *refs):
-        part = raw_ref[...].astype(jnp.float32)
-        real, imag = part[:, :width], part[:, width:]
-        power = real * real + imag * imag
-        for ref in refs[:-1]:
-            power = power + ref[...].astype(jnp.float32)
-        factor = lax.rsqrt(power / total_bins + 1e-05) * valid_ref[...].astype(jnp.float32)
-        refs[-1][:, :width] = (real * factor).astype(jnp.bfloat16)
-        refs[-1][:, width:] = (imag * factor).astype(jnp.bfloat16)
-
-    vmem = pl.BlockSpec(memory_space=pltpu.VMEM)
-    return pl.pallas_call(
-        body,
-        grid=(1,),
-        out_shape=jax.ShapeDtypeStruct((rows, 2 * width), jnp.bfloat16),
-        in_specs=[pl.BlockSpec((rows, 2 * width), lambda i: (chunk, 0)), pl.BlockSpec((rows, width), lambda i: (chunk, 0))]
-        + [vmem] * len(received),
-        out_specs=pl.BlockSpec((rows, 2 * width), lambda i: (0, 0)),
-        compiler_params=pltpu.CompilerParams(vmem_limit_bytes=6 * 2**20),
-        cost_estimate=cost(0.7),
+        others = sum(ref[...].astype(jnp.float32) for ref in refs[:-2])
+        others = jnp.where(valid_ref[...].astype(jnp.float32) > 0.0, others, -1.0).astype(jnp.bfloat16)
+        refs[-1][...] = others
+        refs[-2][:, :width], refs[-2][:, width:] = whiten_rows(raw_ref[...], others.astype(jnp.float32), total_bins)
+
+    vmem = pl.BlockSpec(memory_space=pltpu.VMEM)
+    return pl.pallas_call(
+        body,
+        out_shape=[jax.ShapeDtypeStruct(raw.shape, jnp.bfloat16), jax.ShapeDtypeStruct((rows, width), jnp.bfloat16)],
+        in_specs=[vmem] * (2 + len(received)),
+        out_specs=[vmem, vmem],
+        compiler_params=pltpu.CompilerParams(vmem_limit_bytes=6 * 2**20),
+        cost_estimate=cost(0.2),
     )(raw, valid, *received)
+
+
+def whiten_passed(raw, others, total_bins):
+    width = others.shape[1]
+
+    def body(raw_ref, others_ref, out_ref):
+        out_ref[:, :width], out_ref[:, width:] = whiten_rows(raw_ref[...], others_ref[...].astype(jnp.float32), total_bins)
+
+    vmem = pl.BlockSpec(memory_space=pltpu.VMEM)
+    return pl.pallas_call(
+        body,
+        out_shape=jax.ShapeDtypeStruct(raw.shape, jnp.bfloat16),
+        in_specs=[vmem, vmem],
+        out_specs=vmem,
+        compiler_params=pltpu.CompilerParams(vmem_limit_bytes=6 * 2**20),
+        cost_estimate=cost(0.2),
+    )(raw, others)
 
 
 def select(numbers, first):
@@ -326,29 +344,21 @@
             tables += [jnp.cos(phase), -jnp.sin(phase)]
         table = spread(jnp.stack(tables) / math.sqrt(total_bins), station_count)
 
-        chunks = 2
-        raw, *powers = band_powers(spectra[0], chunks)
+        raw, power = band_power(spectra[0])
         valid, numbers = prepare(valid, station_index, raw)
-        received = [[lax.ppermute(power, "freq", from_freq(shift)) for shift in range(1, freq_size)] for power in powers]
-
-        parts = [whiten(raw, valid, received[0], 0, chunks, total_bins)]
-        flying_parts = [lax.ppermute(parts[0], "grp", ring)]
-        swapped = swap_pieces(parts[0], 2)
-        second, _ = lax.optimization_barrier((received[1], parts[0]))
-        parts.append(whiten(raw, valid, second, 1, chunks, total_bins))
-        second, swapped[0] = lax.optimization_barrier((parts[1], swapped[0]))
-        flying_parts.append(lax.ppermute(second, "grp", ring))
-        swapped += swap_pieces(parts[1], 2)
-        whitened = jnp.concatenate(parts, axis=0)
+        received = [lax.ppermute(power, "freq", from_freq(shift)) for shift in range(1, freq_size)]
+        raw_flying = lax.ppermute(raw, "grp", ring)
+        whitened, others = whiten_own(raw, valid, received, total_bins)
+        others_flying = lax.ppermute(others, "grp", ring)
+        swapped = swap(whitened)
         flying = [None, lax.ppermute(jnp.concatenate(swapped, axis=0), "grp", ring)]
         left = jnp.concatenate(
             [whitened, jnp.concatenate([whitened[:, window_count:], -whitened[:, :window_count]], axis=1)], axis=0
         )
-        later, flying_parts[0] = lax.optimization_barrier((whitened, flying_parts[0]))
         cross, stations = cross_blocks(
-            left, [[later], swapped], own_blocks, None, total_chans, scaling, numbers, None, 4.0
+            left, [[whitened], swapped], own_blocks, None, total_chans, scaling, numbers, None, 4.0
         )
-        flying[0] = jnp.concatenate(flying_parts, axis=0)
+        flying[0] = whiten_passed(raw_flying, others_flying, total_bins)
 
         steps = chips - 1
         waiting, ahead, kernels = [], [], []

time: 60.1 us -> 58.9 us (0.980)
  starting transfers between devices: 23.5 us -> 22.6 us
    ppermute x2, waiting for transfers between devices: 1.54 us -> 0.01 us  [the longest x1 0.01 us: on_device(): others_flying = lax.ppermute(others, 'grp', ring)]
    ppermute x1, starting transfers between devices: 1.09 us -> 0.36 us  [on_device(): lax.ppermute(lax.ppermute(found, 'grp', swap_by(1)), 'grp', across)]
    ppermute x5, starting transfers between devices: 7.14 us -> 7.87 us  [on_device(): flying.append(lax.ppermute(arrived, 'grp', ring))]
    ppermute x1, waiting for transfers between devices: 1.08 us -> 1.78 us  [on_device(): lax.ppermute(kernels[0], 'freq', from_freq(shift))]
    ppermute x5, waiting for transfers between devices: 5.82 us -> 5.13 us  [on_device(): flying.append(lax.ppermute(arrived, 'grp', ring))]
    ppermute x18 -> x16, starting transfers between devices: 5 us -> 4.49 us  [swap_pieces(): lax.ppermute(block[k * rows:(k + 1) * rows], 'grp', swap_by(1))]
    ppermute x2 -> x1, waiting for transfers between devices: 1.91 us -> 2.39 us  [on_device(): lax.ppermute(power, 'freq', from_freq(shift))]
    ppermute x18 -> x16, waiting for transfers between devices: 0.91 us -> 1.28 us  [swap_pieces(): lax.ppermute(block[k * rows:(k + 1) * rows], 'grp', swap_by(1))]
  transfers between devices with their start and end apart: 32 -> 29, of which waited for: 12 -> 11; matrix products, arithmetic and copies ran while one was open for 3% -> 3% of each run, Pallas kernels for 23% -> 24%
where the time goes in v5:
time: 58.9 us; the launch traced here: 58.7 us
  starting transfers between devices  22.6 us (38%)
  Pallas kernels  15.8 us (27%)
  waiting for transfers between devices  15 us (25%)
  local copies, waits for them, and re-layouts  3.85 us (7%)
  between operations  0.96 us (2%)
    pallas_call x8, Pallas kernels, cross_blocks(): pl.pallas_call(body, out_shape=shapes, in_specs=specs, out_specs=out_spec...  12.4 us
    ppermute x5, starting transfers between devices, on_device(): flying.append(lax.ppermute(arrived, 'grp', ring))  7.87 us
    ppermute x5, waiting for transfers between devices, on_device(): flying.append(lax.ppermute(arrived, 'grp', ring))  5.13 us
    ppermute x16, starting transfers between devices, swap_pieces(): lax.ppermute(block[k * rows:(k + 1) * rows], 'grp', swap_by(1))  4.49 us
    ppermute x1, starting transfers between devices, on_device(): lax.ppermute(power, 'freq', from_freq(shift))  3.03 us
    unnamed x8, local copies, waits for them, and re-layouts  2.87 us
    ppermute x1, waiting for transfers between devices, on_device(): flying = [None, lax.ppermute(jnp.concatenate(swapped, axis=0), 'grp', ring)]  2.77 us
    ppermute x1, waiting for transfers between devices, on_device(): lax.ppermute(power, 'freq', from_freq(shift))  2.39 us
  transfers between devices with their start and end apart: 29, of which 11 were waited for; matrix products, arithmetic and copies ran while one was open for 3% of the time, Pallas kernels for 24%

profile of v5, /device:TPU:0, one launch (start us, length us, event | category | flops | bytes accessed | tf_op | source)
XLA Modules:
  0.0 58.7 jit_solution(11948757474777044069)
XLA Ops:
  0.6 1.0 %copy-done = bf16[1,256,1024]{2,1,0:T(8,128)(2,1)S(1)} copy-done((bf16[1,256,1024]{2,1,0:T(8,128)(2,1)S(1)}, bf16[1,256,1024]{2,1,0:T(8,128)(2,1)}, u32[]{:S(2)}) %copy-start) | copy-done | bytes 524312
  1.8 3.0 %collective-permute-start = (bf16[256,512]{1,0:T(8,128)(2,1)S(1)}, bf16[256,512]{1,0:T(8,128)(2,1)S(1)}, u32[]{:S(2)}, u32[]{:S(2)}) collective-permute-start(bf16[256,512]{1,0:T(8,128)(2,1)S(1)} %get-tuple-element.58), channel_id=1, source_target_pairs={{0,1},{1,0},{2,3},{3,2},{4,5},{5,4},{6,7},{7,6},{8,9},{9,8},{10,11... | collective-permute-start | bytes 786440 | tf_op jit(solution)/shard_map/ppermute | solution.py:349
  4.8 1.6 %collective-permute-start.1 = (bf16[256,1024]{1,0:T(8,128)(2,1)S(1)}, bf16[256,1024]{1,0:T(8,128)(2,1)S(1)}, u32[]{:S(2)}, u32[]{:S(2)}) collective-permute-start(bf16[256,1024]{1,0:T(8,128)(2,1)S(1)} %get-tuple-element.56._.raw_ref), channel_id=1, source_target_pairs={{0,8},{2,6},{4,0},{6,14},{8,16},{10,2},{12,4},{14,22},{16,24},{18,... | collective-permute-start | bytes 1572872 | tf_op jit(solution)/shard_map/ppermute | solution.py:350
  6.4 1.0 %copy-done.1 = s32[256,512]{1,0:T(8,128)S(1)} copy-done((s32[256,512]{1,0:T(8,128)S(1)}, s32[256,512]{1,0:T(8,128)}, u32[]{:S(2)}) %copy-start.1) | copy-done | bytes 524312
  7.4 0.7 %copy-done.2 = s32[16]{0:T(128)S(1)} copy-done((s32[16]{0:T(128)S(1)}, s32[16]{0:T(128)}, u32[]{:S(2)}) %copy-start.2) | copy-done | bytes 88
  8.1 0.6 %shard_map.51 = (bf16[256,512]{1,0:T(8,128)(2,1)S(1)}, s32[16,256]{1,0:T(8,128)S(1)}) custom-call(s32[16]{0:T(128)S(1)} %copy-done.2, s32[256,512]{1,0:T(8,128)S(1)} %copy-done.1, bf16[256,1024]{1,0:T(8,128)(2,1)S(1)} %get-tuple-element.56._.raw_ref), custom_call_target="tpu_custom_call" | custom-call | flops 345000000 | tf_op jit(solution)/shard_map/pallas_call | solution.py:98
  8.7 2.4 %collective-permute-done.refs_0_ = bf16[256,512]{1,0:T(8,128)(2,1)S(1)} collective-permute-done((bf16[256,512]{1,0:T(8,128)(2,1)S(1)}, bf16[256,512]{1,0:T(8,128)(2,1)S(1)}, u32[]{:S(2)}, u32[]{:S(2)}) %collective-permute-start) | collective-permute-done | bytes 262176 | tf_op jit(solution)/shard_map/ppermute | solution.py:349
  11.5 1.8 %collective-permute-start.2 = (bf16[256,512]{1,0:T(8,128)(2,1)S(1)}, bf16[256,512]{1,0:T(8,128)(2,1)S(1)}, u32[]{:S(2)}, u32[]{:S(2)}) collective-permute-start(bf16[256,512]{1,0:T(8,128)(2,1)S(1)} %get-tuple-element.60), channel_id=1, source_target_pairs={{0,8},{2,6},{4,0},{6,14},{8,16},{10,2},{12,4},{14,22},{16,24},{18,... | collective-permute-start | bytes 786440 | tf_op jit(solution)/shard_map/ppermute | solution.py:352
  14.1 0.9 %collective-permute-done.4.refs_2_ = bf16[128,1024]{1,0:T(8,128)(2,1)S(1)} collective-permute-done((bf16[128,1024]{1,0:T(8,128)(2,1)S(1)}, bf16[128,1024]{1,0:T(8,128)(2,1)S(1)}, u32[]{:S(2)}, u32[]{:S(2)}) %collective-permute-start.4) | collective-permute-done | bytes 262176 | tf_op jit(solution)/shard_map/ppermute | solution.py:320
  15.4 1.6 %collective-permute-start.6 = (bf16[256,1024]{1,0:T(8,128)(2,1)S(1)}, bf16[256,1024]{1,0:T(8,128)(2,1)S(1)}, u32[]{:S(2)}, u32[]{:S(2)}) collective-permute-start(bf16[256,1024]{1,0:T(8,128)(2,1)S(1)} %pad_maximum_fusion.1), channel_id=1, source_target_pairs={{0,8},{2,6},{4,0},{6,14},{8,16},{10,2},{12,4},{14,22},{16,24},{18,... | collective-permute-start | bytes 1572872 | tf_op jit(solution)/shard_map/ppermute | solution.py:354
  17.0 1.6 %shard_map.54 = (bf16[2,256,4096]{2,1,0:T(8,128)(2,1)}, bf16[16,1024]{1,0:T(8,128)(2,1)S(1)}) custom-call(bf16[512,1024]{1,0:T(8,128)(2,1)S(1)} %maximum_maximum_fusion.left_ref, bf16[256,1024]{1,0:T(8,128)(2,1)S(1)} %get-tuple-element.59.refs_0_, bf16[128,1024]{1,0:T(8,128)(2,1)S(1)} %collective-permute-done.3.refs_1_, ...), custom_call_target="tpu_custom_call" | custom-call | flops 4600000000 | tf_op jit(solution)/shard_map/pallas_call | solution.py:223
  18.9 0.7 %fusion.10 = (bf16[128,1024]{1,0:T(8,128)(2,1)}, bf16[128,1024]{1,0:T(8,128)(2,1)S(1)}) fusion(bf16[256,1024]{1,0:T(8,128)(2,1)S(1)} %shard_map.53.refs_0_), kind=kLoop, calls=%fused_computation.26 | loop fusion | bytes 1048576 | tf_op jit(solution)/shard_map/slice | solution.py:320
  20.2 1.6 %collective-permute-start.5 = (bf16[256,1024]{1,0:T(8,128)(2,1)S(1)}, bf16[256,1024]{1,0:T(8,128)(2,1)S(1)}, u32[]{:S(2)}, u32[]{:S(2)}) collective-permute-start(bf16[256,1024]{1,0:T(8,128)(2,1)S(1)} %shard_map.53.refs_0_), channel_id=1, source_target_pairs={{0,8},{2,6},{4,0},{6,14},{8,16},{10,2},{12,4},{14,22},{16,24},{18,... | collective-permute-start | bytes 1572872 | tf_op jit(solution)/shard_map/ppermute | solution.py:370
  21.8 2.8 %collective-permute-done.6.refs_0_ = bf16[256,1024]{1,0:T(8,128)(2,1)S(1)} collective-permute-done((bf16[256,1024]{1,0:T(8,128)(2,1)S(1)}, bf16[256,1024]{1,0:T(8,128)(2,1)S(1)}, u32[]{:S(2)}, u32[]{:S(2)}) %collective-permute-start.6) | collective-permute-done | bytes 524320 | tf_op jit(solution)/shard_map/ppermute | solution.py:354
  25.3 1.6 %collective-permute-start.12 = (bf16[256,1024]{1,0:T(8,128)(2,1)S(1)}, bf16[256,1024]{1,0:T(8,128)(2,1)S(1)}, u32[]{:S(2)}, u32[]{:S(2)}) collective-permute-start(bf16[256,1024]{1,0:T(8,128)(2,1)S(1)} %collective-permute-done.6.refs_0_), channel_id=1, source_target_pairs={{0,8},{2,6},{4,0},{6,14},{8,16},{10,2},{12,4},{14,22},{16,24},{18,... | collective-permute-start | bytes 1572872 | tf_op jit(solution)/shard_map/ppermute | solution.py:370
  26.9 1.5 %shard_map.55 = (bf16[2,256,4096]{2,1,0:T(8,128)(2,1)}, bf16[16,1024]{1,0:T(8,128)(2,1)S(1)}) custom-call(bf16[512,1024]{1,0:T(8,128)(2,1)S(1)} %maximum_maximum_fusion.left_ref, bf16[256,1024]{1,0:T(8,128)(2,1)S(1)} %shard_map.53.refs_0_, bf16[128,1024]{1,0:T(8,128)(2,1)S(1)} %collective-permute-done.7.refs_1_, ...), custom_call_target="tpu_custom_call", output_to_operand_aliasing={{0}: (6, {})} | custom-call | tf_op jit(solution)/shard_map/pallas_call | solution.py:223
  28.5 1.7 %collective-permute-done.5.refs_0_ = bf16[256,1024]{1,0:T(8,128)(2,1)S(1)} collective-permute-done((bf16[256,1024]{1,0:T(8,128)(2,1)S(1)}, bf16[256,1024]{1,0:T(8,128)(2,1)S(1)}, u32[]{:S(2)}, u32[]{:S(2)}) %collective-permute-start.5) | collective-permute-done | bytes 524320 | tf_op jit(solution)/shard_map/ppermute | solution.py:370
  31.1 1.6 %collective-permute-start.11 = (bf16[256,1024]{1,0:T(8,128)(2,1)S(1)}, bf16[256,1024]{1,0:T(8,128)(2,1)S(1)}, u32[]{:S(2)}, u32[]{:S(2)}) collective-permute-start(bf16[256,1024]{1,0:T(8,128)(2,1)S(1)} %collective-permute-done.5.refs_0_), channel_id=1, source_target_pairs={{0,8},{2,6},{4,0},{6,14},{8,16},{10,2},{12,4},{14,22},{16,24},{18,... | collective-permute-start | bytes 1572872 | tf_op jit(solution)/shard_map/ppermute | solution.py:370
  32.9 1.6 %shard_map.56 = (bf16[2,256,4096]{2,1,0:T(8,128)(2,1)}, bf16[16,1024]{1,0:T(8,128)(2,1)S(1)}) custom-call(bf16[512,1024]{1,0:T(8,128)(2,1)S(1)} %maximum_maximum_fusion.left_ref, bf16[256,1024]{1,0:T(8,128)(2,1)S(1)} %collective-permute-done.6.refs_0_, bf16[128,1024]{1,0:T(8,128)(2,1)S(1)} %collective-permute-done.9.refs_1_, ...), custom_call_target="tpu_custom_call", output_to_operand_aliasing={{0}: (6, {})} | custom-call | tf_op jit(solution)/shard_map/pallas_call | solution.py:223
  34.4 1.4 %collective-permute-done.12.refs_0_ = bf16[256,1024]{1,0:T(8,128)(2,1)S(1)} collective-permute-done((bf16[256,1024]{1,0:T(8,128)(2,1)S(1)}, bf16[256,1024]{1,0:T(8,128)(2,1)S(1)}, u32[]{:S(2)}, u32[]{:S(2)}) %collective-permute-start.12) | collective-permute-done | bytes 524320 | tf_op jit(solution)/shard_map/ppermute | solution.py:370
  36.5 1.6 %collective-permute-start.18 = (bf16[256,1024]{1,0:T(8,128)(2,1)S(1)}, bf16[256,1024]{1,0:T(8,128)(2,1)S(1)}, u32[]{:S(2)}, u32[]{:S(2)}) collective-permute-start(bf16[256,1024]{1,0:T(8,128)(2,1)S(1)} %collective-permute-done.12.refs_0_), channel_id=1, source_target_pairs={{0,8},{2,6},{4,0},{6,14},{8,16},{10,2},{12,4},{14,22},{16,24},{18,... | collective-permute-start | bytes 1572872 | tf_op jit(solution)/shard_map/ppermute | solution.py:370
  38.0 1.5 %shard_map.57 = (bf16[2,256,4096]{2,1,0:T(8,128)(2,1)}, bf16[16,1024]{1,0:T(8,128)(2,1)S(1)}) custom-call(bf16[512,1024]{1,0:T(8,128)(2,1)S(1)} %maximum_maximum_fusion.left_ref, bf16[256,1024]{1,0:T(8,128)(2,1)S(1)} %collective-permute-done.5.refs_0_, bf16[128,1024]{1,0:T(8,128)(2,1)S(1)} %collective-permute-done.13.refs_1_, ...), custom_call_target="tpu_custom_call", output_to_operand_aliasing={{0}: (6, {})} | custom-call | tf_op jit(solution)/shard_map/pallas_call | solution.py:223
  39.6 1.8 %collective-permute-done.11.block_ref.refs_0_ = bf16[256,1024]{1,0:T(8,128)(2,1)S(1)} collective-permute-done((bf16[256,1024]{1,0:T(8,128)(2,1)S(1)}, bf16[256,1024]{1,0:T(8,128)(2,1)S(1)}, u32[]{:S(2)}, u32[]{:S(2)}) %collective-permute-start.11) | collective-permute-done | bytes 524320 | tf_op jit(solution)/shard_map/ppermute | solution.py:370
  42.3 1.2 %collective-permute-done.21 = bf16[16,1024]{1,0:T(8,128)(2,1)S(1)} collective-permute-done((bf16[16,1024]{1,0:T(8,128)(2,1)S(1)}, bf16[16,1024]{1,0:T(8,128)(2,1)S(1)}, u32[]{:S(2)}, u32[]{:S(2)}) %collective-permute-start.21) | collective-permute-done | bytes 32800 | tf_op jit(solution)/shard_map/ppermute | solution.py:373
  43.9 1.4 %collective-permute-start.17 = (bf16[256,1024]{1,0:T(8,128)(2,1)S(1)}, bf16[256,1024]{1,0:T(8,128)(2,1)S(1)}, u32[]{:S(2)}, u32[]{:S(2)}) collective-permute-start(bf16[256,1024]{1,0:T(8,128)(2,1)S(1)} %collective-permute-done.11.block_ref.refs_0_), channel_id=1, source_target_pairs={{0,8},{2,6},{4,0},{6,14},{8,16},{10,2},{12,4},{14,22},{16,24},{18,... | collective-permute-start | bytes 1572872 | tf_op jit(solution)/shard_map/ppermute | solution.py:370
  45.3 1.5 %shard_map.58 = (bf16[2,256,4096]{2,1,0:T(8,128)(2,1)}, bf16[16,1024]{1,0:T(8,128)(2,1)S(1)}) custom-call(bf16[512,1024]{1,0:T(8,128)(2,1)S(1)} %maximum_maximum_fusion.left_ref, bf16[256,1024]{1,0:T(8,128)(2,1)S(1)} %collective-permute-done.12.refs_0_, bf16[128,1024]{1,0:T(8,128)(2,1)S(1)} %collective-permute-done.15.refs_1_, ...), custom_call_target="tpu_custom_call", output_to_operand_aliasing={{0}: (6, {})} | custom-call | tf_op jit(solution)/shard_map/pallas_call | solution.py:223
  48.1 1.5 %shard_map.60 = (bf16[2,256,4096]{2,1,0:T(8,128)(2,1)}, bf16[16,1024]{1,0:T(8,128)(2,1)S(1)}) custom-call(bf16[512,1024]{1,0:T(8,128)(2,1)S(1)} %maximum_maximum_fusion.left_ref, bf16[256,1024]{1,0:T(8,128)(2,1)S(1)} %collective-permute-done.11.block_ref.refs_0_, ...), custom_call_target="tpu_custom_call", output_to_operand_aliasing={{0}: (6, {})} | custom-call | tf_op jit(solution)/shard_map/pallas_call | solution.py:223
  49.7 1.6 %shard_map.61 = (bf16[2,256,4096]{2,1,0:T(8,128)(2,1)}, bf16[16,1024]{1,0:T(8,128)(2,1)S(1)}) custom-call(bf16[512,1024]{1,0:T(8,128)(2,1)S(1)} %maximum_maximum_fusion.left_ref, bf16[256,1024]{1,0:T(8,128)(2,1)S(1)} %collective-permute-done.18.refs_0_, bf16[128,1024]{1,0:T(8,128)(2,1)S(1)} %collective-permute-done.23.refs_1_, ...), custom_call_target="tpu_custom_call", output_to_operand_aliasing={{0}: (6, {})} | custom-call | tf_op jit(solution)/shard_map/pallas_call | solution.py:223
  51.5 1.6 %collective-permute-start.28 = (f32[32,256]{1,0:T(8,128)S(1)}, f32[32,256]{1,0:T(8,128)S(1)}, u32[]{:S(2)}, u32[]{:S(2)}) collective-permute-start(f32[32,256]{1,0:T(8,128)S(1)} %shard_map.62.refs_0_), channel_id=1, source_target_pairs={{0,1},{1,0},{2,3},{3,2},{4,5},{5,4},{6,7},{7,6},{8,9},{9,8},{10,11... | collective-permute-start | bytes 98312 | tf_op jit(solution)/shard_map/ppermute | solution.py:385
  53.7 1.8 %collective-permute-done.28.refs_1_ = f32[32,256]{1,0:T(8,128)S(1)} collective-permute-done((f32[32,256]{1,0:T(8,128)S(1)}, f32[32,256]{1,0:T(8,128)S(1)}, u32[]{:S(2)}, u32[]{:S(2)}) %collective-permute-start.28) | collective-permute-done | bytes 32800 | tf_op jit(solution)/shard_map/ppermute | solution.py:385
  55.5 1.6 %shard_map.64 = f32[16,256,128]{2,1,0:T(8,128)} custom-call(bf16[192,2048]{1,0:T(8,128)(2,1)S(1)} %pad_maximum_fusion.table_ref, f32[32,256]{1,0:T(8,128)S(1)} %shard_map.62.refs_0_, f32[32,256]{1,0:T(8,128)S(1)} %collective-permute-done.28.refs_1_), custom_call_target="tpu_custom_call" | custom-call | flops 9200000000 | tf_op jit(solution)/shard_map/pallas_call | solution.py:297
  57.1 1.6 %shard_map.63 = bf16[2,256,4096]{2,1,0:T(8,128)(2,1)} custom-call(bf16[512,1024]{1,0:T(8,128)(2,1)S(1)} %maximum_maximum_fusion.left_ref, bf16[256,1024]{1,0:T(8,128)(2,1)S(1)} %collective-permute-done.17.refs_0_, bf16[128,1024]{1,0:T(8,128)(2,1)S(1)} %collective-permute-done.26.refs_1_, ...), custom_call_target="tpu_custom_call", output_to_operand_aliasing={{}: (4, {})} | custom-call | tf_op jit(solution)/shard_map/pallas_call | solution.py:223
  (66 shorter events, 8.1 us)
Async XLA Ops:
  0.6 1.0 %copy-start = (bf16[1,256,1024]{2,1,0:T(8,128)(2,1)S(1)}, bf16[1,256,1024]{2,1,0:T(8,128)(2,1)}, u32[]{:S(2)}) copy-start(bf16[1,256,1024]{2,1,0:T(8,128)(2,1)} %param.3) | copy-start | bytes 1572868
  1.8 9.3 %collective-permute-start = (bf16[256,512]{1,0:T(8,128)(2,1)S(1)}, bf16[256,512]{1,0:T(8,128)(2,1)S(1)}, u32[]{:S(2)}, u32[]{:S(2)}) collective-permute-start(bf16[256,512]{1,0:T(8,128)(2,1)S(1)} %get-tuple-element.58), channel_id=1, source_target_pairs={{0,1},{1,0},{2,3},{3,2},{4,5},{5,4},{6,7},{7,6},{8,9},{9,8},{10,11... | collective-permute-start | bytes 786440 | tf_op jit(solution)/shard_map/ppermute | solution.py:349
  4.8 13.8 %collective-permute-start.1 = (bf16[256,1024]{1,0:T(8,128)(2,1)S(1)}, bf16[256,1024]{1,0:T(8,128)(2,1)S(1)}, u32[]{:S(2)}, u32[]{:S(2)}) collective-permute-start(bf16[256,1024]{1,0:T(8,128)(2,1)S(1)} %get-tuple-element.56._.raw_ref), channel_id=1, source_target_pairs={{0,8},{2,6},{4,0},{6,14},{8,16},{10,2},{12,4},{14,22},{16,24},{18,... | collective-permute-start | bytes 1572872 | tf_op jit(solution)/shard_map/ppermute | solution.py:350
  6.4 1.0 %copy-start.1 = (s32[256,512]{1,0:T(8,128)S(1)}, s32[256,512]{1,0:T(8,128)}, u32[]{:S(2)}) copy-start(s32[256,512]{1,0:T(8,128)} %valid_ref.1) | copy-start | bytes 1572868
  7.4 0.7 %copy-start.2 = (s32[16]{0:T(128)S(1)}, s32[16]{0:T(128)}, u32[]{:S(2)}) copy-start(s32[16]{0:T(128)} %index_ref.1) | copy-start | bytes 196
  11.5 7.1 %collective-permute-start.2 = (bf16[256,512]{1,0:T(8,128)(2,1)S(1)}, bf16[256,512]{1,0:T(8,128)(2,1)S(1)}, u32[]{:S(2)}, u32[]{:S(2)}) collective-permute-start(bf16[256,512]{1,0:T(8,128)(2,1)S(1)} %get-tuple-element.60), channel_id=1, source_target_pairs={{0,8},{2,6},{4,0},{6,14},{8,16},{10,2},{12,4},{14,22},{16,24},{18,... | collective-permute-start | bytes 786440 | tf_op jit(solution)/shard_map/ppermute | solution.py:352
  13.3 1.6 %collective-permute-start.4 = (bf16[128,1024]{1,0:T(8,128)(2,1)S(1)}, bf16[128,1024]{1,0:T(8,128)(2,1)S(1)}, u32[]{:S(2)}, u32[]{:S(2)}) collective-permute-start(bf16[128,1024]{1,0:T(8,128)(2,1)S(1)} %get-tuple-element.124), channel_id=1, source_target_pairs={{0,2},{2,0},{4,6},{6,4},{8,10},{10,8},{12,14},{14,12},{16,18},{18,... | collective-permute-start | bytes 786440 | tf_op jit(solution)/shard_map/ppermute | solution.py:320
  13.4 1.9 %collective-permute-start.3 = (bf16[128,1024]{1,0:T(8,128)(2,1)S(1)}, bf16[128,1024]{1,0:T(8,128)(2,1)S(1)}, u32[]{:S(2)}, u32[]{:S(2)}) collective-permute-start(bf16[128,1024]{1,0:T(8,128)(2,1)S(1)} %get-tuple-element.125), channel_id=1, source_target_pairs={{0,2},{2,0},{4,6},{6,4},{8,10},{10,8},{12,14},{14,12},{16,18},{18,... | collective-permute-start | bytes 786440 | tf_op jit(solution)/shard_map/ppermute | solution.py:320
  15.4 9.2 %collective-permute-start.6 = (bf16[256,1024]{1,0:T(8,128)(2,1)S(1)}, bf16[256,1024]{1,0:T(8,128)(2,1)S(1)}, u32[]{:S(2)}, u32[]{:S(2)}) collective-permute-start(bf16[256,1024]{1,0:T(8,128)(2,1)S(1)} %pad_maximum_fusion.1), channel_id=1, source_target_pairs={{0,8},{2,6},{4,0},{6,14},{8,16},{10,2},{12,4},{14,22},{16,24},{18,... | collective-permute-start | bytes 1572872 | tf_op jit(solution)/shard_map/ppermute | solution.py:354
  19.6 2.2 %collective-permute-start.8 = (bf16[128,1024]{1,0:T(8,128)(2,1)}, bf16[128,1024]{1,0:T(8,128)(2,1)S(1)}, u32[]{:S(2)}, u32[]{:S(2)}) collective-permute-start(bf16[128,1024]{1,0:T(8,128)(2,1)} %get-tuple-element.122), channel_id=1, source_target_pairs={{0,2},{2,0},{4,6},{6,4},{8,10},{10,8},{12,14},{14,12},{16,18},{18,... | collective-permute-start | bytes 786440 | tf_op jit(solution)/shard_map/ppermute | solution.py:320
  19.6 2.2 %collective-permute-start.7 = (bf16[128,1024]{1,0:T(8,128)(2,1)S(1)}, bf16[128,1024]{1,0:T(8,128)(2,1)S(1)}, u32[]{:S(2)}, u32[]{:S(2)}) collective-permute-start(bf16[128,1024]{1,0:T(8,128)(2,1)S(1)} %get-tuple-element.123), channel_id=1, source_target_pairs={{0,2},{2,0},{4,6},{6,4},{8,10},{10,8},{12,14},{14,12},{16,18},{18,... | collective-permute-start | bytes 786440 | tf_op jit(solution)/shard_map/ppermute | solution.py:320
  20.2 10.0 %collective-permute-start.5 = (bf16[256,1024]{1,0:T(8,128)(2,1)S(1)}, bf16[256,1024]{1,0:T(8,128)(2,1)S(1)}, u32[]{:S(2)}, u32[]{:S(2)}) collective-permute-start(bf16[256,1024]{1,0:T(8,128)(2,1)S(1)} %shard_map.53.refs_0_), channel_id=1, source_target_pairs={{0,8},{2,6},{4,0},{6,14},{8,16},{10,2},{12,4},{14,22},{16,24},{18,... | collective-permute-start | bytes 1572872 | tf_op jit(solution)/shard_map/ppermute | solution.py:370
  24.6 5.6 %collective-permute-start.10 = (bf16[128,1024]{1,0:T(8,128)(2,1)S(1)}, bf16[128,1024]{1,0:T(8,128)(2,1)S(1)}, u32[]{:S(2)}, u32[]{:S(2)}) collective-permute-start(bf16[128,1024]{1,0:T(8,128)(2,1)S(1)} %get-tuple-element.120), channel_id=1, source_target_pairs={{0,2},{2,0},{4,6},{6,4},{8,10},{10,8},{12,14},{14,12},{16,18},{18,... | collective-permute-start | bytes 786440 | tf_op jit(solution)/shard_map/ppermute | solution.py:320
  24.7 5.5 %collective-permute-start.9 = (bf16[128,1024]{1,0:T(8,128)(2,1)S(1)}, bf16[128,1024]{1,0:T(8,128)(2,1)S(1)}, u32[]{:S(2)}, u32[]{:S(2)}) collective-permute-start(bf16[128,1024]{1,0:T(8,128)(2,1)S(1)} %get-tuple-element.121), channel_id=1, source_target_pairs={{0,2},{2,0},{4,6},{6,4},{8,10},{10,8},{12,14},{14,12},{16,18},{18,... | collective-permute-start | bytes 786440 | tf_op jit(solution)/shard_map/ppermute | solution.py:320
  25.3 10.5 %collective-permute-start.12 = (bf16[256,1024]{1,0:T(8,128)(2,1)S(1)}, bf16[256,1024]{1,0:T(8,128)(2,1)S(1)}, u32[]{:S(2)}, u32[]{:S(2)}) collective-permute-start(bf16[256,1024]{1,0:T(8,128)(2,1)S(1)} %collective-permute-done.6.refs_0_), channel_id=1, source_target_pairs={{0,8},{2,6},{4,0},{6,14},{8,16},{10,2},{12,4},{14,22},{16,24},{18,... | collective-permute-start | bytes 1572872 | tf_op jit(solution)/shard_map/ppermute | solution.py:370
  30.3 5.6 %collective-permute-start.14 = (bf16[128,1024]{1,0:T(8,128)(2,1)S(1)}, bf16[128,1024]{1,0:T(8,128)(2,1)S(1)}, u32[]{:S(2)}, u32[]{:S(2)}) collective-permute-start(bf16[128,1024]{1,0:T(8,128)(2,1)S(1)} %get-tuple-element.118), channel_id=1, source_target_pairs={{0,2},{2,0},{4,6},{6,4},{8,10},{10,8},{12,14},{14,12},{16,18},{18,... | collective-permute-start | bytes 786440 | tf_op jit(solution)/shard_map/ppermute | solution.py:320
  30.3 5.5 %collective-permute-start.13 = (bf16[128,1024]{1,0:T(8,128)(2,1)S(1)}, bf16[128,1024]{1,0:T(8,128)(2,1)S(1)}, u32[]{:S(2)}, u32[]{:S(2)}) collective-permute-start(bf16[128,1024]{1,0:T(8,128)(2,1)S(1)} %get-tuple-element.119), channel_id=1, source_target_pairs={{0,2},{2,0},{4,6},{6,4},{8,10},{10,8},{12,14},{14,12},{16,18},{18,... | collective-permute-start | bytes 786440 | tf_op jit(solution)/shard_map/ppermute | solution.py:320
  31.1 10.3 %collective-permute-start.11 = (bf16[256,1024]{1,0:T(8,128)(2,1)S(1)}, bf16[256,1024]{1,0:T(8,128)(2,1)S(1)}, u32[]{:S(2)}, u32[]{:S(2)}) collective-permute-start(bf16[256,1024]{1,0:T(8,128)(2,1)S(1)} %collective-permute-done.5.refs_0_), channel_id=1, source_target_pairs={{0,8},{2,6},{4,0},{6,14},{8,16},{10,2},{12,4},{14,22},{16,24},{18,... | collective-permute-start | bytes 1572872 | tf_op jit(solution)/shard_map/ppermute | solution.py:370
  35.9 3.7 %collective-permute-start.16 = (bf16[128,1024]{1,0:T(8,128)(2,1)S(1)}, bf16[128,1024]{1,0:T(8,128)(2,1)S(1)}, u32[]{:S(2)}, u32[]{:S(2)}) collective-permute-start(bf16[128,1024]{1,0:T(8,128)(2,1)S(1)} %get-tuple-element.116), channel_id=1, source_target_pairs={{0,2},{2,0},{4,6},{6,4},{8,10},{10,8},{12,14},{14,12},{16,18},{18,... | collective-permute-start | bytes 786440 | tf_op jit(solution)/shard_map/ppermute | solution.py:320
  36.0 3.6 %collective-permute-start.15 = (bf16[128,1024]{1,0:T(8,128)(2,1)S(1)}, bf16[128,1024]{1,0:T(8,128)(2,1)S(1)}, u32[]{:S(2)}, u32[]{:S(2)}) collective-permute-start(bf16[128,1024]{1,0:T(8,128)(2,1)S(1)} %get-tuple-element.117), channel_id=1, source_target_pairs={{0,2},{2,0},{4,6},{6,4},{8,10},{10,8},{12,14},{14,12},{16,18},{18,... | collective-permute-start | bytes 786440 | tf_op jit(solution)/shard_map/ppermute | solution.py:320
  36.5 11.0 %collective-permute-start.18 = (bf16[256,1024]{1,0:T(8,128)(2,1)S(1)}, bf16[256,1024]{1,0:T(8,128)(2,1)S(1)}, u32[]{:S(2)}, u32[]{:S(2)}) collective-permute-start(bf16[256,1024]{1,0:T(8,128)(2,1)S(1)} %collective-permute-done.12.refs_0_), channel_id=1, source_target_pairs={{0,8},{2,6},{4,0},{6,14},{8,16},{10,2},{12,4},{14,22},{16,24},{18,... | collective-permute-start | bytes 1572872 | tf_op jit(solution)/shard_map/ppermute | solution.py:370
  41.5 5.9 %collective-permute-start.20 = (bf16[128,1024]{1,0:T(8,128)(2,1)S(1)}, bf16[128,1024]{1,0:T(8,128)(2,1)S(1)}, u32[]{:S(2)}, u32[]{:S(2)}) collective-permute-start(bf16[128,1024]{1,0:T(8,128)(2,1)S(1)} %get-tuple-element.114), channel_id=1, source_target_pairs={{0,2},{2,0},{4,6},{6,4},{8,10},{10,8},{12,14},{14,12},{16,18},{18,... | collective-permute-start | bytes 786440 | tf_op jit(solution)/shard_map/ppermute | solution.py:320
  41.6 5.9 %collective-permute-start.19 = (bf16[128,1024]{1,0:T(8,128)(2,1)S(1)}, bf16[128,1024]{1,0:T(8,128)(2,1)S(1)}, u32[]{:S(2)}, u32[]{:S(2)}) collective-permute-start(bf16[128,1024]{1,0:T(8,128)(2,1)S(1)} %get-tuple-element.115), channel_id=1, source_target_pairs={{0,2},{2,0},{4,6},{6,4},{8,10},{10,8},{12,14},{14,12},{16,18},{18,... | collective-permute-start | bytes 786440 | tf_op jit(solution)/shard_map/ppermute | solution.py:320
  42.2 1.3 %collective-permute-start.21 = (bf16[16,1024]{1,0:T(8,128)(2,1)S(1)}, bf16[16,1024]{1,0:T(8,128)(2,1)S(1)}, u32[]{:S(2)}, u32[]{:S(2)}) collective-permute-start(bf16[16,1024]{1,0:T(8,128)(2,1)S(1)} %shard_map.59), channel_id=1, source_target_pairs={{0,2},{2,0},{4,6},{6,4},{8,10},{10,8},{12,14},{14,12},{16,18},{18,... | collective-permute-start | bytes 98312 | tf_op jit(solution)/shard_map/ppermute | solution.py:373
  43.5 3.8 %collective-permute-start.22 = (bf16[16,1024]{1,0:T(8,128)(2,1)S(1)}, bf16[16,1024]{1,0:T(8,128)(2,1)S(1)}, u32[]{:S(2)}, u32[]{:S(2)}) collective-permute-start(bf16[16,1024]{1,0:T(8,128)(2,1)S(1)} %collective-permute-done.21), channel_id=1, source_target_pairs={{0,6},{2,8},{4,14},{6,0},{8,2},{10,16},{12,22},{14,4},{16,10},{18,... | collective-permute-start | bytes 98312 | tf_op jit(solution)/shard_map/ppermute | solution.py:373
  43.9 9.2 %collective-permute-start.17 = (bf16[256,1024]{1,0:T(8,128)(2,1)S(1)}, bf16[256,1024]{1,0:T(8,128)(2,1)S(1)}, u32[]{:S(2)}, u32[]{:S(2)}) collective-permute-start(bf16[256,1024]{1,0:T(8,128)(2,1)S(1)} %collective-permute-done.11.block_ref.refs_0_), channel_id=1, source_target_pairs={{0,8},{2,6},{4,0},{6,14},{8,16},{10,2},{12,4},{14,22},{16,24},{18,... | collective-permute-start | bytes 1572872 | tf_op jit(solution)/shard_map/ppermute | solution.py:370
  47.5 2.2 %collective-permute-start.24 = (bf16[128,1024]{1,0:T(8,128)(2,1)S(1)}, bf16[128,1024]{1,0:T(8,128)(2,1)S(1)}, u32[]{:S(2)}, u32[]{:S(2)}) collective-permute-start(bf16[128,1024]{1,0:T(8,128)(2,1)S(1)} %get-tuple-element.112), channel_id=1, source_target_pairs={{0,2},{2,0},{4,6},{6,4},{8,10},{10,8},{12,14},{14,12},{16,18},{18,... | collective-permute-start | bytes 786440 | tf_op jit(solution)/shard_map/ppermute | solution.py:320
  47.5 2.1 %collective-permute-start.23 = (bf16[128,1024]{1,0:T(8,128)(2,1)S(1)}, bf16[128,1024]{1,0:T(8,128)(2,1)S(1)}, u32[]{:S(2)}, u32[]{:S(2)}) collective-permute-start(bf16[128,1024]{1,0:T(8,128)(2,1)S(1)} %get-tuple-element.113), channel_id=1, source_target_pairs={{0,2},{2,0},{4,6},{6,4},{8,10},{10,8},{12,14},{14,12},{16,18},{18,... | collective-permute-start | bytes 786440 | tf_op jit(solution)/shard_map/ppermute | solution.py:320
  48.0 3.2 %collective-permute-start.25 = (bf16[16,1024]{1,0:T(8,128)(2,1)S(1)}, bf16[16,1024]{1,0:T(8,128)(2,1)S(1)}, u32[]{:S(2)}, u32[]{:S(2)}) collective-permute-start(bf16[16,1024]{1,0:T(8,128)(2,1)S(1)} %collective-permute-done.22.refs_1_), channel_id=1, source_target_pairs={{0,2},{2,0},{4,6},{6,4},{8,10},{10,8},{12,14},{14,12},{16,18},{18,... | collective-permute-start | bytes 98312 | tf_op jit(solution)/shard_map/ppermute | solution.py:377
  51.5 4.0 %collective-permute-start.28 = (f32[32,256]{1,0:T(8,128)S(1)}, f32[32,256]{1,0:T(8,128)S(1)}, u32[]{:S(2)}, u32[]{:S(2)}) collective-permute-start(f32[32,256]{1,0:T(8,128)S(1)} %shard_map.62.refs_0_), channel_id=1, source_target_pairs={{0,1},{1,0},{2,3},{3,2},{4,5},{5,4},{6,7},{7,6},{8,9},{9,8},{10,11... | collective-permute-start | bytes 98312 | tf_op jit(solution)/shard_map/ppermute | solution.py:385
  53.1 4.0 %collective-permute-start.27 = (bf16[128,1024]{1,0:T(8,128)(2,1)S(1)}, bf16[128,1024]{1,0:T(8,128)(2,1)S(1)}, u32[]{:S(2)}, u32[]{:S(2)}) collective-permute-start(bf16[128,1024]{1,0:T(8,128)(2,1)S(1)} %get-tuple-element.110), channel_id=1, source_target_pairs={{0,2},{2,0},{4,6},{6,4},{8,10},{10,8},{12,14},{14,12},{16,18},{18,... | collective-permute-start | bytes 786440 | tf_op jit(solution)/shard_map/ppermute | solution.py:320
  53.4 3.8 %collective-permute-start.26 = (bf16[128,1024]{1,0:T(8,128)(2,1)S(1)}, bf16[128,1024]{1,0:T(8,128)(2,1)S(1)}, u32[]{:S(2)}, u32[]{:S(2)}) collective-permute-start(bf16[128,1024]{1,0:T(8,128)(2,1)S(1)} %get-tuple-element.111), channel_id=1, source_target_pairs={{0,2},{2,0},{4,6},{6,4},{8,10},{10,8},{12,14},{14,12},{16,18},{18,... | collective-permute-start | bytes 786440 | tf_op jit(solution)/shard_map/ppermute | solution.py:320

commit v6 on v5

--- a/solution.py
+++ b/solution.py
@@ -161,20 +161,28 @@
     return (wanted == lax.broadcasted_iota(jnp.int32, wanted.shape, 1)).astype(jnp.bfloat16)
 
 
-def pick(block, numbers, places):
-    def body(block_ref, numbers_ref, out_ref):
-        selector = select(numbers_ref[...], places()[0] * block_ref.shape[0])
-        out_ref[...] = jnp.dot(selector, block_ref[...], preferred_element_type=jnp.float32).astype(jnp.bfloat16)
-
-    vmem = pl.BlockSpec(memory_space=pltpu.VMEM)
-    return pl.pallas_call(
-        body,
-        out_shape=jax.ShapeDtypeStruct((numbers.shape[0], block.shape[1]), jnp.bfloat16),
-        in_specs=[vmem, vmem],
+def pick(blocks, numbers, places):
+    rows, depth = sum(piece.shape[0] for piece in blocks[0]), blocks[0][0].shape[1]
+    pieces = [len(block) for block in blocks]
+
+    def body(numbers_ref, *refs):
+        picked = None
+        for k, place in enumerate(places()[: len(blocks)]):
+            first = sum(pieces[:k])
+            block = jnp.concatenate([ref[...] for ref in refs[first : first + pieces[k]]], axis=0)
+            found = jnp.dot(select(numbers_ref[...], place * rows), block, preferred_element_type=jnp.float32)
+            picked = found if picked is None else picked + found
+        refs[-1][...] = picked.astype(jnp.bfloat16)
+
+    vmem = pl.BlockSpec(memory_space=pltpu.VMEM)
+    return pl.pallas_call(
+        body,
+        out_shape=jax.ShapeDtypeStruct((numbers.shape[0], depth), jnp.bfloat16),
+        in_specs=[vmem] * (1 + sum(pieces)),
         out_specs=vmem,
         compiler_params=pltpu.CompilerParams(vmem_limit_bytes=6 * 2**20),
         cost_estimate=cost(0.1),
-    )(block, numbers)
+    )(numbers, *(piece for block in blocks for piece in block))
 
 
 def cross_blocks(left, blocks, places, cross, total, scaling, numbers=None, stations=None, microseconds=0.0):
@@ -369,7 +377,7 @@
             if step + 2 < steps:
                 flying.append(lax.ppermute(arrived, "grp", ring))
             if step + 3 == steps:
-                found = pick(arrived, numbers, functools.partial(ring_blocks, step, chips))
+                found = pick([[arrived]], numbers, functools.partial(ring_blocks, step, chips))
                 ahead = [lax.ppermute(lax.ppermute(found, "grp", swap_by(1)), "grp", across)]
             if step == 2:
                 table, cross = lax.optimization_barrier((table, cross))
@@ -380,9 +388,11 @@
                 cross, stations = cross_blocks(left, [waiting, swapped], places, cross, total_chans, scaling, numbers, stations)
             waiting, swapped, places = [arrived], next_swapped, functools.partial(ring_blocks, step, chips)
             if step + 2 == steps:
-                cross, stations = cross_blocks(left, [waiting, swapped], places, cross, total_chans, scaling, numbers, stations)
-                kernels = [station_kernel([stations, *ahead], left, scaling)]
+                found = pick([waiting, swapped], numbers, places)
+                kernels = [station_kernel([stations, found, *ahead], left, scaling)]
                 others = [lax.ppermute(kernels[0], "freq", from_freq(shift)) for shift in range(1, freq_size)]
+                cross, kernels = lax.optimization_barrier((cross, kernels))
+                cross = cross_blocks(left, [waiting, swapped], places, cross, total_chans, scaling)
         station_gather = lag_sums(kernels + others, table)
         cross = cross_blocks(left, [waiting, swapped], places, cross, total_chans, scaling)
         return (cross[None], station_gather)

time: 58.9 us -> 57.6 us (0.978)
  waiting for transfers between devices: 15 us -> 13.4 us
    ppermute x1, waiting for transfers between devices: 1.78 us -> 0.21 us  [on_device(): lax.ppermute(kernels[0], 'freq', from_freq(shift))]
  transfers between devices with their start and end apart: 29 -> 29, of which waited for: 11 -> 11; matrix products, arithmetic and copies ran while one was open for 3% -> 3% of each run, Pallas kernels for 24% -> 25%
where the time goes in v6:
time: 57.6 us; the launch traced here: 57.4 us
  starting transfers between devices  22.6 us (39%)
  Pallas kernels  16.1 us (28%)
  waiting for transfers between devices  13.4 us (23%)
  local copies, waits for them, and re-layouts  3.85 us (7%)
  between operations  0.97 us (2%)
    pallas_call x8, Pallas kernels, cross_blocks(): pl.pallas_call(body, out_shape=shapes, in_specs=specs, out_specs=out_spec...  12.4 us
    ppermute x5, starting transfers between devices, on_device(): flying.append(lax.ppermute(arrived, 'grp', ring))  7.87 us
    ppermute x5, waiting for transfers between devices, on_device(): flying.append(lax.ppermute(arrived, 'grp', ring))  5.13 us
    ppermute x16, starting transfers between devices, swap_pieces(): lax.ppermute(block[k * rows:(k + 1) * rows], 'grp', swap_by(1))  4.49 us
    ppermute x1, starting transfers between devices, on_device(): lax.ppermute(power, 'freq', from_freq(shift))  3.03 us
    unnamed x8, local copies, waits for them, and re-layouts  2.87 us
    ppermute x1, waiting for transfers between devices, on_device(): flying = [None, lax.ppermute(jnp.concatenate(swapped, axis=0), 'grp', ring)]  2.77 us
    ppermute x1, waiting for transfers between devices, on_device(): lax.ppermute(power, 'freq', from_freq(shift))  2.39 us
  transfers between devices with their start and end apart: 29, of which 11 were waited for; matrix products, arithmetic and copies ran while one was open for 3% of the time, Pallas kernels for 25%

profile of v6, /device:TPU:0, one launch (start us, length us, event | category | flops | bytes accessed | tf_op | source)
XLA Modules:
  0.0 57.4 jit_solution(5848280041853732912)
XLA Ops:
  0.6 1.0 %copy-done = bf16[1,256,1024]{2,1,0:T(8,128)(2,1)S(1)} copy-done((bf16[1,256,1024]{2,1,0:T(8,128)(2,1)S(1)}, bf16[1,256,1024]{2,1,0:T(8,128)(2,1)}, u32[]{:S(2)}) %copy-start) | copy-done | bytes 524312
  1.8 3.0 %collective-permute-start = (bf16[256,512]{1,0:T(8,128)(2,1)S(1)}, bf16[256,512]{1,0:T(8,128)(2,1)S(1)}, u32[]{:S(2)}, u32[]{:S(2)}) collective-permute-start(bf16[256,512]{1,0:T(8,128)(2,1)S(1)} %get-tuple-element.58), channel_id=1, source_target_pairs={{0,1},{1,0},{2,3},{3,2},{4,5},{5,4},{6,7},{7,6},{8,9},{9,8},{10,11... | collective-permute-start | bytes 786440 | tf_op jit(solution)/shard_map/ppermute | solution.py:357
  4.8 1.6 %collective-permute-start.1 = (bf16[256,1024]{1,0:T(8,128)(2,1)S(1)}, bf16[256,1024]{1,0:T(8,128)(2,1)S(1)}, u32[]{:S(2)}, u32[]{:S(2)}) collective-permute-start(bf16[256,1024]{1,0:T(8,128)(2,1)S(1)} %get-tuple-element.56._.raw_ref), channel_id=1, source_target_pairs={{0,8},{2,6},{4,0},{6,14},{8,16},{10,2},{12,4},{14,22},{16,24},{18,... | collective-permute-start | bytes 1572872 | tf_op jit(solution)/shard_map/ppermute | solution.py:358
  6.4 1.0 %copy-done.1 = s32[256,512]{1,0:T(8,128)S(1)} copy-done((s32[256,512]{1,0:T(8,128)S(1)}, s32[256,512]{1,0:T(8,128)}, u32[]{:S(2)}) %copy-start.1) | copy-done | bytes 524312
  7.4 0.7 %copy-done.2 = s32[16]{0:T(128)S(1)} copy-done((s32[16]{0:T(128)S(1)}, s32[16]{0:T(128)}, u32[]{:S(2)}) %copy-start.2) | copy-done | bytes 88
  8.1 0.6 %shard_map.51 = (bf16[256,512]{1,0:T(8,128)(2,1)S(1)}, s32[16,256]{1,0:T(8,128)S(1)}) custom-call(s32[16]{0:T(128)S(1)} %copy-done.2, s32[256,512]{1,0:T(8,128)S(1)} %copy-done.1, bf16[256,1024]{1,0:T(8,128)(2,1)S(1)} %get-tuple-element.56._.raw_ref), custom_call_target="tpu_custom_call" | custom-call | flops 345000000 | tf_op jit(solution)/shard_map/pallas_call | solution.py:98
  8.7 2.4 %collective-permute-done.refs_0_ = bf16[256,512]{1,0:T(8,128)(2,1)S(1)} collective-permute-done((bf16[256,512]{1,0:T(8,128)(2,1)S(1)}, bf16[256,512]{1,0:T(8,128)(2,1)S(1)}, u32[]{:S(2)}, u32[]{:S(2)}) %collective-permute-start) | collective-permute-done | bytes 262176 | tf_op jit(solution)/shard_map/ppermute | solution.py:357
  11.5 1.8 %collective-permute-start.2 = (bf16[256,512]{1,0:T(8,128)(2,1)S(1)}, bf16[256,512]{1,0:T(8,128)(2,1)S(1)}, u32[]{:S(2)}, u32[]{:S(2)}) collective-permute-start(bf16[256,512]{1,0:T(8,128)(2,1)S(1)} %get-tuple-element.60), channel_id=1, source_target_pairs={{0,8},{2,6},{4,0},{6,14},{8,16},{10,2},{12,4},{14,22},{16,24},{18,... | collective-permute-start | bytes 786440 | tf_op jit(solution)/shard_map/ppermute | solution.py:360
  14.1 0.9 %collective-permute-done.4.refs_2_ = bf16[128,1024]{1,0:T(8,128)(2,1)S(1)} collective-permute-done((bf16[128,1024]{1,0:T(8,128)(2,1)S(1)}, bf16[128,1024]{1,0:T(8,128)(2,1)S(1)}, u32[]{:S(2)}, u32[]{:S(2)}) %collective-permute-start.4) | collective-permute-done | bytes 262176 | tf_op jit(solution)/shard_map/ppermute | solution.py:328
  15.4 1.6 %collective-permute-start.6 = (bf16[256,1024]{1,0:T(8,128)(2,1)S(1)}, bf16[256,1024]{1,0:T(8,128)(2,1)S(1)}, u32[]{:S(2)}, u32[]{:S(2)}) collective-permute-start(bf16[256,1024]{1,0:T(8,128)(2,1)S(1)} %pad_maximum_fusion.1), channel_id=1, source_target_pairs={{0,8},{2,6},{4,0},{6,14},{8,16},{10,2},{12,4},{14,22},{16,24},{18,... | collective-permute-start | bytes 1572872 | tf_op jit(solution)/shard_map/ppermute | solution.py:362
  17.0 1.6 %shard_map.54 = (bf16[2,256,4096]{2,1,0:T(8,128)(2,1)}, bf16[16,1024]{1,0:T(8,128)(2,1)S(1)}) custom-call(bf16[512,1024]{1,0:T(8,128)(2,1)S(1)} %maximum_maximum_fusion.left_ref, bf16[256,1024]{1,0:T(8,128)(2,1)S(1)} %get-tuple-element.59.refs_0_, bf16[128,1024]{1,0:T(8,128)(2,1)S(1)} %collective-permute-done.3.refs_1_, ...), custom_call_target="tpu_custom_call" | custom-call | flops 4600000000 | tf_op jit(solution)/shard_map/pallas_call | solution.py:231
  18.9 0.7 %fusion.10 = (bf16[128,1024]{1,0:T(8,128)(2,1)}, bf16[128,1024]{1,0:T(8,128)(2,1)S(1)}) fusion(bf16[256,1024]{1,0:T(8,128)(2,1)S(1)} %shard_map.53.refs_0_), kind=kLoop, calls=%fused_computation.26 | loop fusion | bytes 1048576 | tf_op jit(solution)/shard_map/slice | solution.py:328
  19.6 0.5 collective-permute-start.7
  20.2 1.6 %collective-permute-start.5 = (bf16[256,1024]{1,0:T(8,128)(2,1)S(1)}, bf16[256,1024]{1,0:T(8,128)(2,1)S(1)}, u32[]{:S(2)}, u32[]{:S(2)}) collective-permute-start(bf16[256,1024]{1,0:T(8,128)(2,1)S(1)} %shard_map.53.refs_0_), channel_id=1, source_target_pairs={{0,8},{2,6},{4,0},{6,14},{8,16},{10,2},{12,4},{14,22},{16,24},{18,... | collective-permute-start | bytes 1572872 | tf_op jit(solution)/shard_map/ppermute | solution.py:378
  21.8 2.8 %collective-permute-done.6.refs_0_ = bf16[256,1024]{1,0:T(8,128)(2,1)S(1)} collective-permute-done((bf16[256,1024]{1,0:T(8,128)(2,1)S(1)}, bf16[256,1024]{1,0:T(8,128)(2,1)S(1)}, u32[]{:S(2)}, u32[]{:S(2)}) %collective-permute-start.6) | collective-permute-done | bytes 524320 | tf_op jit(solution)/shard_map/ppermute | solution.py:362
  25.3 1.6 %collective-permute-start.12 = (bf16[256,1024]{1,0:T(8,128)(2,1)S(1)}, bf16[256,1024]{1,0:T(8,128)(2,1)S(1)}, u32[]{:S(2)}, u32[]{:S(2)}) collective-permute-start(bf16[256,1024]{1,0:T(8,128)(2,1)S(1)} %collective-permute-done.6.refs_0_), channel_id=1, source_target_pairs={{0,8},{2,6},{4,0},{6,14},{8,16},{10,2},{12,4},{14,22},{16,24},{18,... | collective-permute-start | bytes 1572872 | tf_op jit(solution)/shard_map/ppermute | solution.py:378
  26.9 1.5 %shard_map.55 = (bf16[2,256,4096]{2,1,0:T(8,128)(2,1)}, bf16[16,1024]{1,0:T(8,128)(2,1)S(1)}) custom-call(bf16[512,1024]{1,0:T(8,128)(2,1)S(1)} %maximum_maximum_fusion.left_ref, bf16[256,1024]{1,0:T(8,128)(2,1)S(1)} %shard_map.53.refs_0_, bf16[128,1024]{1,0:T(8,128)(2,1)S(1)} %collective-permute-done.7.refs_1_, ...), custom_call_target="tpu_custom_call", output_to_operand_aliasing={{0}: (6, {})} | custom-call | tf_op jit(solution)/shard_map/pallas_call | solution.py:231
  28.5 1.7 %collective-permute-done.5.refs_0_ = bf16[256,1024]{1,0:T(8,128)(2,1)S(1)} collective-permute-done((bf16[256,1024]{1,0:T(8,128)(2,1)S(1)}, bf16[256,1024]{1,0:T(8,128)(2,1)S(1)}, u32[]{:S(2)}, u32[]{:S(2)}) %collective-permute-start.5) | collective-permute-done | bytes 524320 | tf_op jit(solution)/shard_map/ppermute | solution.py:378
  31.1 1.6 %collective-permute-start.11 = (bf16[256,1024]{1,0:T(8,128)(2,1)S(1)}, bf16[256,1024]{1,0:T(8,128)(2,1)S(1)}, u32[]{:S(2)}, u32[]{:S(2)}) collective-permute-start(bf16[256,1024]{1,0:T(8,128)(2,1)S(1)} %collective-permute-done.5.refs_0_), channel_id=1, source_target_pairs={{0,8},{2,6},{4,0},{6,14},{8,16},{10,2},{12,4},{14,22},{16,24},{18,... | collective-permute-start | bytes 1572872 | tf_op jit(solution)/shard_map/ppermute | solution.py:378
  32.9 1.6 %shard_map.56 = (bf16[2,256,4096]{2,1,0:T(8,128)(2,1)}, bf16[16,1024]{1,0:T(8,128)(2,1)S(1)}) custom-call(bf16[512,1024]{1,0:T(8,128)(2,1)S(1)} %maximum_maximum_fusion.left_ref, bf16[256,1024]{1,0:T(8,128)(2,1)S(1)} %collective-permute-done.6.refs_0_, bf16[128,1024]{1,0:T(8,128)(2,1)S(1)} %collective-permute-done.9.refs_1_, ...), custom_call_target="tpu_custom_call", output_to_operand_aliasing={{0}: (6, {})} | custom-call | tf_op jit(solution)/shard_map/pallas_call | solution.py:231
  34.4 1.4 %collective-permute-done.12.refs_0_ = bf16[256,1024]{1,0:T(8,128)(2,1)S(1)} collective-permute-done((bf16[256,1024]{1,0:T(8,128)(2,1)S(1)}, bf16[256,1024]{1,0:T(8,128)(2,1)S(1)}, u32[]{:S(2)}, u32[]{:S(2)}) %collective-permute-start.12) | collective-permute-done | bytes 524320 | tf_op jit(solution)/shard_map/ppermute | solution.py:378
  36.5 1.6 %collective-permute-start.18 = (bf16[256,1024]{1,0:T(8,128)(2,1)S(1)}, bf16[256,1024]{1,0:T(8,128)(2,1)S(1)}, u32[]{:S(2)}, u32[]{:S(2)}) collective-permute-start(bf16[256,1024]{1,0:T(8,128)(2,1)S(1)} %collective-permute-done.12.refs_0_), channel_id=1, source_target_pairs={{0,8},{2,6},{4,0},{6,14},{8,16},{10,2},{12,4},{14,22},{16,24},{18,... | collective-permute-start | bytes 1572872 | tf_op jit(solution)/shard_map/ppermute | solution.py:378
  38.0 1.5 %shard_map.57 = (bf16[2,256,4096]{2,1,0:T(8,128)(2,1)}, bf16[16,1024]{1,0:T(8,128)(2,1)S(1)}) custom-call(bf16[512,1024]{1,0:T(8,128)(2,1)S(1)} %maximum_maximum_fusion.left_ref, bf16[256,1024]{1,0:T(8,128)(2,1)S(1)} %collective-permute-done.5.refs_0_, bf16[128,1024]{1,0:T(8,128)(2,1)S(1)} %collective-permute-done.13.refs_1_, ...), custom_call_target="tpu_custom_call", output_to_operand_aliasing={{0}: (6, {})} | custom-call | tf_op jit(solution)/shard_map/pallas_call | solution.py:231
  39.6 1.8 %collective-permute-done.11.refs_0_ = bf16[256,1024]{1,0:T(8,128)(2,1)S(1)} collective-permute-done((bf16[256,1024]{1,0:T(8,128)(2,1)S(1)}, bf16[256,1024]{1,0:T(8,128)(2,1)S(1)}, u32[]{:S(2)}, u32[]{:S(2)}) %collective-permute-start.11) | collective-permute-done | bytes 524320 | tf_op jit(solution)/shard_map/ppermute | solution.py:378
  42.3 1.2 %collective-permute-done.21 = bf16[16,1024]{1,0:T(8,128)(2,1)S(1)} collective-permute-done((bf16[16,1024]{1,0:T(8,128)(2,1)S(1)}, bf16[16,1024]{1,0:T(8,128)(2,1)S(1)}, u32[]{:S(2)}, u32[]{:S(2)}) %collective-permute-start.21) | collective-permute-done | bytes 32800 | tf_op jit(solution)/shard_map/ppermute | solution.py:381
  43.9 1.4 %collective-permute-start.17 = (bf16[256,1024]{1,0:T(8,128)(2,1)S(1)}, bf16[256,1024]{1,0:T(8,128)(2,1)S(1)}, u32[]{:S(2)}, u32[]{:S(2)}) collective-permute-start(bf16[256,1024]{1,0:T(8,128)(2,1)S(1)} %collective-permute-done.11.refs_0_), channel_id=1, source_target_pairs={{0,8},{2,6},{4,0},{6,14},{8,16},{10,2},{12,4},{14,22},{16,24},{18,... | collective-permute-start | bytes 1572872 | tf_op jit(solution)/shard_map/ppermute | solution.py:378
  45.3 1.5 %shard_map.58 = (bf16[2,256,4096]{2,1,0:T(8,128)(2,1)}, bf16[16,1024]{1,0:T(8,128)(2,1)S(1)}) custom-call(bf16[512,1024]{1,0:T(8,128)(2,1)S(1)} %maximum_maximum_fusion.left_ref, bf16[256,1024]{1,0:T(8,128)(2,1)S(1)} %collective-permute-done.12.refs_0_, bf16[128,1024]{1,0:T(8,128)(2,1)S(1)} %collective-permute-done.15.refs_1_, ...), custom_call_target="tpu_custom_call", output_to_operand_aliasing={{0}: (6, {})} | custom-call | tf_op jit(solution)/shard_map/pallas_call | solution.py:231
  48.1 1.5 %shard_map.60 = (bf16[2,256,4096]{2,1,0:T(8,128)(2,1)}, bf16[16,1024]{1,0:T(8,128)(2,1)S(1)}) custom-call(bf16[512,1024]{1,0:T(8,128)(2,1)S(1)} %maximum_maximum_fusion.left_ref, bf16[256,1024]{1,0:T(8,128)(2,1)S(1)} %collective-permute-done.11.refs_0_, bf16[128,1024]{1,0:T(8,128)(2,1)S(1)} %collective-permute-done.19.refs_1_, ...), custom_call_target="tpu_custom_call", output_to_operand_aliasing={{0}: (6, {})} | custom-call | tf_op jit(solution)/shard_map/pallas_call | solution.py:231
  50.2 1.6 %collective-permute-start.28 = (f32[32,256]{1,0:T(8,128)S(1)}, f32[32,256]{1,0:T(8,128)S(1)}, u32[]{:S(2)}, u32[]{:S(2)}) collective-permute-start(f32[32,256]{1,0:T(8,128)S(1)} %shard_map.62.refs_0_), channel_id=1, source_target_pairs={{0,1},{1,0},{2,3},{3,2},{4,5},{5,4},{6,7},{7,6},{8,9},{9,8},{10,11... | collective-permute-start | bytes 98312 | tf_op jit(solution)/shard_map/ppermute | solution.py:393
  51.8 1.6 %shard_map.63.refs_3_ = bf16[2,256,4096]{2,1,0:T(8,128)(2,1)} custom-call(bf16[512,1024]{1,0:T(8,128)(2,1)S(1)} %maximum_maximum_fusion.left_ref, bf16[256,1024]{1,0:T(8,128)(2,1)S(1)} %collective-permute-done.18.refs_0_, bf16[128,1024]{1,0:T(8,128)(2,1)S(1)} %collective-permute-done.23.refs_1_, ...), custom_call_target="tpu_custom_call", output_to_operand_aliasing={{}: (4, {})} | custom-call | tf_op jit(solution)/shard_map/pallas_call | solution.py:231
  54.2 1.6 %shard_map.65 = f32[16,256,128]{2,1,0:T(8,128)} custom-call(bf16[192,2048]{1,0:T(8,128)(2,1)S(1)} %pad_maximum_fusion.table_ref, f32[32,256]{1,0:T(8,128)S(1)} %shard_map.62.refs_0_, f32[32,256]{1,0:T(8,128)S(1)} %collective-permute-done.28.refs_1_), custom_call_target="tpu_custom_call" | custom-call | flops 9200000000 | tf_op jit(solution)/shard_map/pallas_call | solution.py:305
  55.8 1.6 %shard_map.64 = bf16[2,256,4096]{2,1,0:T(8,128)(2,1)} custom-call(bf16[512,1024]{1,0:T(8,128)(2,1)S(1)} %maximum_maximum_fusion.left_ref, bf16[256,1024]{1,0:T(8,128)(2,1)S(1)} %collective-permute-done.17.refs_0_, bf16[128,1024]{1,0:T(8,128)(2,1)S(1)} %collective-permute-done.26.refs_1_, ...), custom_call_target="tpu_custom_call", output_to_operand_aliasing={{}: (4, {})} | custom-call | tf_op jit(solution)/shard_map/pallas_call | solution.py:231
  (67 shorter events, 8.0 us)
Async XLA Ops:
  0.6 1.0 %copy-start = (bf16[1,256,1024]{2,1,0:T(8,128)(2,1)S(1)}, bf16[1,256,1024]{2,1,0:T(8,128)(2,1)}, u32[]{:S(2)}) copy-start(bf16[1,256,1024]{2,1,0:T(8,128)(2,1)} %param.3) | copy-start | bytes 1572868
  1.8 9.3 %collective-permute-start = (bf16[256,512]{1,0:T(8,128)(2,1)S(1)}, bf16[256,512]{1,0:T(8,128)(2,1)S(1)}, u32[]{:S(2)}, u32[]{:S(2)}) collective-permute-start(bf16[256,512]{1,0:T(8,128)(2,1)S(1)} %get-tuple-element.58), channel_id=1, source_target_pairs={{0,1},{1,0},{2,3},{3,2},{4,5},{5,4},{6,7},{7,6},{8,9},{9,8},{10,11... | collective-permute-start | bytes 786440 | tf_op jit(solution)/shard_map/ppermute | solution.py:357
  4.8 13.8 %collective-permute-start.1 = (bf16[256,1024]{1,0:T(8,128)(2,1)S(1)}, bf16[256,1024]{1,0:T(8,128)(2,1)S(1)}, u32[]{:S(2)}, u32[]{:S(2)}) collective-permute-start(bf16[256,1024]{1,0:T(8,128)(2,1)S(1)} %get-tuple-element.56._.raw_ref), channel_id=1, source_target_pairs={{0,8},{2,6},{4,0},{6,14},{8,16},{10,2},{12,4},{14,22},{16,24},{18,... | collective-permute-start | bytes 1572872 | tf_op jit(solution)/shard_map/ppermute | solution.py:358
  6.4 1.0 %copy-start.1 = (s32[256,512]{1,0:T(8,128)S(1)}, s32[256,512]{1,0:T(8,128)}, u32[]{:S(2)}) copy-start(s32[256,512]{1,0:T(8,128)} %valid_ref.1) | copy-start | bytes 1572868
  7.4 0.7 %copy-start.2 = (s32[16]{0:T(128)S(1)}, s32[16]{0:T(128)}, u32[]{:S(2)}) copy-start(s32[16]{0:T(128)} %index_ref.1) | copy-start | bytes 196
  11.5 7.1 %collective-permute-start.2 = (bf16[256,512]{1,0:T(8,128)(2,1)S(1)}, bf16[256,512]{1,0:T(8,128)(2,1)S(1)}, u32[]{:S(2)}, u32[]{:S(2)}) collective-permute-start(bf16[256,512]{1,0:T(8,128)(2,1)S(1)} %get-tuple-element.60), channel_id=1, source_target_pairs={{0,8},{2,6},{4,0},{6,14},{8,16},{10,2},{12,4},{14,22},{16,24},{18,... | collective-permute-start | bytes 786440 | tf_op jit(solution)/shard_map/ppermute | solution.py:360
  13.3 1.6 %collective-permute-start.4 = (bf16[128,1024]{1,0:T(8,128)(2,1)S(1)}, bf16[128,1024]{1,0:T(8,128)(2,1)S(1)}, u32[]{:S(2)}, u32[]{:S(2)}) collective-permute-start(bf16[128,1024]{1,0:T(8,128)(2,1)S(1)} %get-tuple-element.124), channel_id=1, source_target_pairs={{0,2},{2,0},{4,6},{6,4},{8,10},{10,8},{12,14},{14,12},{16,18},{18,... | collective-permute-start | bytes 786440 | tf_op jit(solution)/shard_map/ppermute | solution.py:328
  13.4 1.9 %collective-permute-start.3 = (bf16[128,1024]{1,0:T(8,128)(2,1)S(1)}, bf16[128,1024]{1,0:T(8,128)(2,1)S(1)}, u32[]{:S(2)}, u32[]{:S(2)}) collective-permute-start(bf16[128,1024]{1,0:T(8,128)(2,1)S(1)} %get-tuple-element.125), channel_id=1, source_target_pairs={{0,2},{2,0},{4,6},{6,4},{8,10},{10,8},{12,14},{14,12},{16,18},{18,... | collective-permute-start | bytes 786440 | tf_op jit(solution)/shard_map/ppermute | solution.py:328
  15.4 9.2 %collective-permute-start.6 = (bf16[256,1024]{1,0:T(8,128)(2,1)S(1)}, bf16[256,1024]{1,0:T(8,128)(2,1)S(1)}, u32[]{:S(2)}, u32[]{:S(2)}) collective-permute-start(bf16[256,1024]{1,0:T(8,128)(2,1)S(1)} %pad_maximum_fusion.1), channel_id=1, source_target_pairs={{0,8},{2,6},{4,0},{6,14},{8,16},{10,2},{12,4},{14,22},{16,24},{18,... | collective-permute-start | bytes 1572872 | tf_op jit(solution)/shard_map/ppermute | solution.py:362
  19.6 2.2 %collective-permute-start.8 = (bf16[128,1024]{1,0:T(8,128)(2,1)}, bf16[128,1024]{1,0:T(8,128)(2,1)S(1)}, u32[]{:S(2)}, u32[]{:S(2)}) collective-permute-start(bf16[128,1024]{1,0:T(8,128)(2,1)} %get-tuple-element.122), channel_id=1, source_target_pairs={{0,2},{2,0},{4,6},{6,4},{8,10},{10,8},{12,14},{14,12},{16,18},{18,... | collective-permute-start | bytes 786440 | tf_op jit(solution)/shard_map/ppermute | solution.py:328
  19.6 2.2 %collective-permute-start.7 = (bf16[128,1024]{1,0:T(8,128)(2,1)S(1)}, bf16[128,1024]{1,0:T(8,128)(2,1)S(1)}, u32[]{:S(2)}, u32[]{:S(2)}) collective-permute-start(bf16[128,1024]{1,0:T(8,128)(2,1)S(1)} %get-tuple-element.123), channel_id=1, source_target_pairs={{0,2},{2,0},{4,6},{6,4},{8,10},{10,8},{12,14},{14,12},{16,18},{18,... | collective-permute-start | bytes 786440 | tf_op jit(solution)/shard_map/ppermute | solution.py:328
  20.2 10.0 %collective-permute-start.5 = (bf16[256,1024]{1,0:T(8,128)(2,1)S(1)}, bf16[256,1024]{1,0:T(8,128)(2,1)S(1)}, u32[]{:S(2)}, u32[]{:S(2)}) collective-permute-start(bf16[256,1024]{1,0:T(8,128)(2,1)S(1)} %shard_map.53.refs_0_), channel_id=1, source_target_pairs={{0,8},{2,6},{4,0},{6,14},{8,16},{10,2},{12,4},{14,22},{16,24},{18,... | collective-permute-start | bytes 1572872 | tf_op jit(solution)/shard_map/ppermute | solution.py:378
  24.6 5.6 %collective-permute-start.10 = (bf16[128,1024]{1,0:T(8,128)(2,1)S(1)}, bf16[128,1024]{1,0:T(8,128)(2,1)S(1)}, u32[]{:S(2)}, u32[]{:S(2)}) collective-permute-start(bf16[128,1024]{1,0:T(8,128)(2,1)S(1)} %get-tuple-element.120), channel_id=1, source_target_pairs={{0,2},{2,0},{4,6},{6,4},{8,10},{10,8},{12,14},{14,12},{16,18},{18,... | collective-permute-start | bytes 786440 | tf_op jit(solution)/shard_map/ppermute | solution.py:328
  24.7 5.5 %collective-permute-start.9 = (bf16[128,1024]{1,0:T(8,128)(2,1)S(1)}, bf16[128,1024]{1,0:T(8,128)(2,1)S(1)}, u32[]{:S(2)}, u32[]{:S(2)}) collective-permute-start(bf16[128,1024]{1,0:T(8,128)(2,1)S(1)} %get-tuple-element.121), channel_id=1, source_target_pairs={{0,2},{2,0},{4,6},{6,4},{8,10},{10,8},{12,14},{14,12},{16,18},{18,... | collective-permute-start | bytes 786440 | tf_op jit(solution)/shard_map/ppermute | solution.py:328
  25.3 10.5 %collective-permute-start.12 = (bf16[256,1024]{1,0:T(8,128)(2,1)S(1)}, bf16[256,1024]{1,0:T(8,128)(2,1)S(1)}, u32[]{:S(2)}, u32[]{:S(2)}) collective-permute-start(bf16[256,1024]{1,0:T(8,128)(2,1)S(1)} %collective-permute-done.6.refs_0_), channel_id=1, source_target_pairs={{0,8},{2,6},{4,0},{6,14},{8,16},{10,2},{12,4},{14,22},{16,24},{18,... | collective-permute-start | bytes 1572872 | tf_op jit(solution)/shard_map/ppermute | solution.py:378
  30.3 5.6 %collective-permute-start.14 = (bf16[128,1024]{1,0:T(8,128)(2,1)S(1)}, bf16[128,1024]{1,0:T(8,128)(2,1)S(1)}, u32[]{:S(2)}, u32[]{:S(2)}) collective-permute-start(bf16[128,1024]{1,0:T(8,128)(2,1)S(1)} %get-tuple-element.118), channel_id=1, source_target_pairs={{0,2},{2,0},{4,6},{6,4},{8,10},{10,8},{12,14},{14,12},{16,18},{18,... | collective-permute-start | bytes 786440 | tf_op jit(solution)/shard_map/ppermute | solution.py:328
  30.3 5.5 %collective-permute-start.13 = (bf16[128,1024]{1,0:T(8,128)(2,1)S(1)}, bf16[128,1024]{1,0:T(8,128)(2,1)S(1)}, u32[]{:S(2)}, u32[]{:S(2)}) collective-permute-start(bf16[128,1024]{1,0:T(8,128)(2,1)S(1)} %get-tuple-element.119), channel_id=1, source_target_pairs={{0,2},{2,0},{4,6},{6,4},{8,10},{10,8},{12,14},{14,12},{16,18},{18,... | collective-permute-start | bytes 786440 | tf_op jit(solution)/shard_map/ppermute | solution.py:328
  31.1 10.3 %collective-permute-start.11 = (bf16[256,1024]{1,0:T(8,128)(2,1)S(1)}, bf16[256,1024]{1,0:T(8,128)(2,1)S(1)}, u32[]{:S(2)}, u32[]{:S(2)}) collective-permute-start(bf16[256,1024]{1,0:T(8,128)(2,1)S(1)} %collective-permute-done.5.refs_0_), channel_id=1, source_target_pairs={{0,8},{2,6},{4,0},{6,14},{8,16},{10,2},{12,4},{14,22},{16,24},{18,... | collective-permute-start | bytes 1572872 | tf_op jit(solution)/shard_map/ppermute | solution.py:378
  35.9 3.7 %collective-permute-start.16 = (bf16[128,1024]{1,0:T(8,128)(2,1)S(1)}, bf16[128,1024]{1,0:T(8,128)(2,1)S(1)}, u32[]{:S(2)}, u32[]{:S(2)}) collective-permute-start(bf16[128,1024]{1,0:T(8,128)(2,1)S(1)} %get-tuple-element.116), channel_id=1, source_target_pairs={{0,2},{2,0},{4,6},{6,4},{8,10},{10,8},{12,14},{14,12},{16,18},{18,... | collective-permute-start | bytes 786440 | tf_op jit(solution)/shard_map/ppermute | solution.py:328
  36.0 3.6 %collective-permute-start.15 = (bf16[128,1024]{1,0:T(8,128)(2,1)S(1)}, bf16[128,1024]{1,0:T(8,128)(2,1)S(1)}, u32[]{:S(2)}, u32[]{:S(2)}) collective-permute-start(bf16[128,1024]{1,0:T(8,128)(2,1)S(1)} %get-tuple-element.117), channel_id=1, source_target_pairs={{0,2},{2,0},{4,6},{6,4},{8,10},{10,8},{12,14},{14,12},{16,18},{18,... | collective-permute-start | bytes 786440 | tf_op jit(solution)/shard_map/ppermute | solution.py:328
  36.5 11.0 %collective-permute-start.18 = (bf16[256,1024]{1,0:T(8,128)(2,1)S(1)}, bf16[256,1024]{1,0:T(8,128)(2,1)S(1)}, u32[]{:S(2)}, u32[]{:S(2)}) collective-permute-start(bf16[256,1024]{1,0:T(8,128)(2,1)S(1)} %collective-permute-done.12.refs_0_), channel_id=1, source_target_pairs={{0,8},{2,6},{4,0},{6,14},{8,16},{10,2},{12,4},{14,22},{16,24},{18,... | collective-permute-start | bytes 1572872 | tf_op jit(solution)/shard_map/ppermute | solution.py:378
  41.5 5.9 %collective-permute-start.20 = (bf16[128,1024]{1,0:T(8,128)(2,1)S(1)}, bf16[128,1024]{1,0:T(8,128)(2,1)S(1)}, u32[]{:S(2)}, u32[]{:S(2)}) collective-permute-start(bf16[128,1024]{1,0:T(8,128)(2,1)S(1)} %get-tuple-element.114), channel_id=1, source_target_pairs={{0,2},{2,0},{4,6},{6,4},{8,10},{10,8},{12,14},{14,12},{16,18},{18,... | collective-permute-start | bytes 786440 | tf_op jit(solution)/shard_map/ppermute | solution.py:328
  41.6 5.9 %collective-permute-start.19 = (bf16[128,1024]{1,0:T(8,128)(2,1)S(1)}, bf16[128,1024]{1,0:T(8,128)(2,1)S(1)}, u32[]{:S(2)}, u32[]{:S(2)}) collective-permute-start(bf16[128,1024]{1,0:T(8,128)(2,1)S(1)} %get-tuple-element.115), channel_id=1, source_target_pairs={{0,2},{2,0},{4,6},{6,4},{8,10},{10,8},{12,14},{14,12},{16,18},{18,... | collective-permute-start | bytes 786440 | tf_op jit(solution)/shard_map/ppermute | solution.py:328
  42.2 1.3 %collective-permute-start.21 = (bf16[16,1024]{1,0:T(8,128)(2,1)S(1)}, bf16[16,1024]{1,0:T(8,128)(2,1)S(1)}, u32[]{:S(2)}, u32[]{:S(2)}) collective-permute-start(bf16[16,1024]{1,0:T(8,128)(2,1)S(1)} %shard_map.59), channel_id=1, source_target_pairs={{0,2},{2,0},{4,6},{6,4},{8,10},{10,8},{12,14},{14,12},{16,18},{18,... | collective-permute-start | bytes 98312 | tf_op jit(solution)/shard_map/ppermute | solution.py:381
  43.5 3.8 %collective-permute-start.22 = (bf16[16,1024]{1,0:T(8,128)(2,1)S(1)}, bf16[16,1024]{1,0:T(8,128)(2,1)S(1)}, u32[]{:S(2)}, u32[]{:S(2)}) collective-permute-start(bf16[16,1024]{1,0:T(8,128)(2,1)S(1)} %collective-permute-done.21), channel_id=1, source_target_pairs={{0,6},{2,8},{4,14},{6,0},{8,2},{10,16},{12,22},{14,4},{16,10},{18,... | collective-permute-start | bytes 98312 | tf_op jit(solution)/shard_map/ppermute | solution.py:381
  43.9 9.5 %collective-permute-start.17 = (bf16[256,1024]{1,0:T(8,128)(2,1)S(1)}, bf16[256,1024]{1,0:T(8,128)(2,1)S(1)}, u32[]{:S(2)}, u32[]{:S(2)}) collective-permute-start(bf16[256,1024]{1,0:T(8,128)(2,1)S(1)} %collective-permute-done.11.refs_0_), channel_id=1, source_target_pairs={{0,8},{2,6},{4,0},{6,14},{8,16},{10,2},{12,4},{14,22},{16,24},{18,... | collective-permute-start | bytes 1572872 | tf_op jit(solution)/shard_map/ppermute | solution.py:378
  47.5 2.2 %collective-permute-start.24 = (bf16[128,1024]{1,0:T(8,128)(2,1)S(1)}, bf16[128,1024]{1,0:T(8,128)(2,1)S(1)}, u32[]{:S(2)}, u32[]{:S(2)}) collective-permute-start(bf16[128,1024]{1,0:T(8,128)(2,1)S(1)} %get-tuple-element.112), channel_id=1, source_target_pairs={{0,2},{2,0},{4,6},{6,4},{8,10},{10,8},{12,14},{14,12},{16,18},{18,... | collective-permute-start | bytes 786440 | tf_op jit(solution)/shard_map/ppermute | solution.py:328
  47.5 2.1 %collective-permute-start.23 = (bf16[128,1024]{1,0:T(8,128)(2,1)S(1)}, bf16[128,1024]{1,0:T(8,128)(2,1)S(1)}, u32[]{:S(2)}, u32[]{:S(2)}) collective-permute-start(bf16[128,1024]{1,0:T(8,128)(2,1)S(1)} %get-tuple-element.113), channel_id=1, source_target_pairs={{0,2},{2,0},{4,6},{6,4},{8,10},{10,8},{12,14},{14,12},{16,18},{18,... | collective-permute-start | bytes 786440 | tf_op jit(solution)/shard_map/ppermute | solution.py:328
  48.0 1.9 %collective-permute-start.25 = (bf16[16,1024]{1,0:T(8,128)(2,1)S(1)}, bf16[16,1024]{1,0:T(8,128)(2,1)S(1)}, u32[]{:S(2)}, u32[]{:S(2)}) collective-permute-start(bf16[16,1024]{1,0:T(8,128)(2,1)S(1)} %collective-permute-done.22.refs_2_), channel_id=1, source_target_pairs={{0,2},{2,0},{4,6},{6,4},{8,10},{10,8},{12,14},{14,12},{16,18},{18,... | collective-permute-start | bytes 98312 | tf_op jit(solution)/shard_map/ppermute | solution.py:385
  50.2 4.0 %collective-permute-start.28 = (f32[32,256]{1,0:T(8,128)S(1)}, f32[32,256]{1,0:T(8,128)S(1)}, u32[]{:S(2)}, u32[]{:S(2)}) collective-permute-start(f32[32,256]{1,0:T(8,128)S(1)} %shard_map.62.refs_0_), channel_id=1, source_target_pairs={{0,1},{1,0},{2,3},{3,2},{4,5},{5,4},{6,7},{7,6},{8,9},{9,8},{10,11... | collective-permute-start | bytes 98312 | tf_op jit(solution)/shard_map/ppermute | solution.py:393
  53.4 2.4 %collective-permute-start.27 = (bf16[128,1024]{1,0:T(8,128)(2,1)S(1)}, bf16[128,1024]{1,0:T(8,128)(2,1)S(1)}, u32[]{:S(2)}, u32[]{:S(2)}) collective-permute-start(bf16[128,1024]{1,0:T(8,128)(2,1)S(1)} %get-tuple-element.110), channel_id=1, source_target_pairs={{0,2},{2,0},{4,6},{6,4},{8,10},{10,8},{12,14},{14,12},{16,18},{18,... | collective-permute-start | bytes 786440 | tf_op jit(solution)/shard_map/ppermute | solution.py:328
  53.6 2.2 %collective-permute-start.26 = (bf16[128,1024]{1,0:T(8,128)(2,1)S(1)}, bf16[128,1024]{1,0:T(8,128)(2,1)S(1)}, u32[]{:S(2)}, u32[]{:S(2)}) collective-permute-start(bf16[128,1024]{1,0:T(8,128)(2,1)S(1)} %get-tuple-element.111), channel_id=1, source_target_pairs={{0,2},{2,0},{4,6},{6,4},{8,10},{10,8},{12,14},{14,12},{16,18},{18,... | collective-permute-start | bytes 786440 | tf_op jit(solution)/shard_map/ppermute | solution.py:328

commit v7 on v6

--- a/solution.py
+++ b/solution.py
@@ -363,13 +363,11 @@
         left = jnp.concatenate(
             [whitened, jnp.concatenate([whitened[:, window_count:], -whitened[:, :window_count]], axis=1)], axis=0
         )
-        cross, stations = cross_blocks(
-            left, [[whitened], swapped], own_blocks, None, total_chans, scaling, numbers, None, 4.0
-        )
         flying[0] = whiten_passed(raw_flying, others_flying, total_bins)
 
         steps = chips - 1
         waiting, ahead, kernels = [], [], []
+        cross = stations = None
         for step in range(steps):
             arrived, cross, stations, swapped, ahead, kernels = lax.optimization_barrier(
                 (flying[step], cross, stations, swapped, ahead, kernels)
@@ -384,7 +382,11 @@
             if step + 2 == steps:
                 ahead.append(lax.ppermute(ahead[0], "grp", swap_by(1)))
             next_swapped = swap(arrived)
-            if waiting and step + 1 < steps:
+            if step == 0:
+                cross, stations = cross_blocks(
+                    left, [[whitened], swapped], own_blocks, None, total_chans, scaling, numbers, None, 4.0
+                )
+            elif step + 1 < steps:
                 cross, stations = cross_blocks(left, [waiting, swapped], places, cross, total_chans, scaling, numbers, stations)
             waiting, swapped, places = [arrived], next_swapped, functools.partial(ring_blocks, step, chips)
             if step + 2 == steps:

time: 57.6 us -> 57.6 us (level)
  local copies, waits for them, and re-layouts: 3.85 us -> 3.15 us
    ppermute x1, waiting for transfers between devices: 0.01 us -> 0.89 us  [on_device(): others_flying = lax.ppermute(others, 'grp', ring)]
    slice x8, local copies, waits for them, and re-layouts: 0.98 us -> 0.28 us  [swap_pieces(): block[k * rows:(k + 1) * rows]]
  transfers between devices with their start and end apart: 29 -> 29, of which waited for: 11 -> 12; matrix products, arithmetic and copies ran while one was open for 3% -> 2% of each run, Pallas kernels for 25% -> 25%
where the time goes in v7:
time: 57.6 us; the launch traced here: 57.4 us
  starting transfers between devices  22.8 us (40%)
  Pallas kernels  16.1 us (28%)
  waiting for transfers between devices  13.9 us (24%)
  local copies, waits for them, and re-layouts  3.15 us (5%)
  between operations  0.96 us (2%)
    pallas_call x8, Pallas kernels, cross_blocks(): pl.pallas_call(body, out_shape=shapes, in_specs=specs, out_specs=out_spec...  12.4 us
    ppermute x5, starting transfers between devices, on_device(): flying.append(lax.ppermute(arrived, 'grp', ring))  8.09 us
    ppermute x5, waiting for transfers between devices, on_device(): flying.append(lax.ppermute(arrived, 'grp', ring))  5.13 us
    ppermute x16, starting transfers between devices, swap_pieces(): lax.ppermute(block[k * rows:(k + 1) * rows], 'grp', swap_by(1))  4.49 us
    ppermute x1, starting transfers between devices, on_device(): lax.ppermute(power, 'freq', from_freq(shift))  3.03 us
    unnamed x8, local copies, waits for them, and re-layouts  2.87 us
    ppermute x1, waiting for transfers between devices, on_device(): flying = [None, lax.ppermute(jnp.concatenate(swapped, axis=0), 'grp', ring)]  2.44 us
    ppermute x1, waiting for transfers between devices, on_device(): lax.ppermute(power, 'freq', from_freq(shift))  2.33 us
  transfers between devices with their start and end apart: 29, of which 12 were waited for; matrix products, arithmetic and copies ran while one was open for 2% of the time, Pallas kernels for 25%

profile of v7, /device:TPU:0, one launch (start us, length us, event | category | flops | bytes accessed | tf_op | source)
XLA Modules:
  0.0 57.4 jit_solution(17361007442993273244)
XLA Ops:
  0.6 1.0 %copy-done = bf16[1,256,1024]{2,1,0:T(8,128)(2,1)S(1)} copy-done((bf16[1,256,1024]{2,1,0:T(8,128)(2,1)S(1)}, bf16[1,256,1024]{2,1,0:T(8,128)(2,1)}, u32[]{:S(2)}) %copy-start) | copy-done | bytes 524312
  1.8 3.0 %collective-permute-start = (bf16[256,512]{1,0:T(8,128)(2,1)S(1)}, bf16[256,512]{1,0:T(8,128)(2,1)S(1)}, u32[]{:S(2)}, u32[]{:S(2)}) collective-permute-start(bf16[256,512]{1,0:T(8,128)(2,1)S(1)} %get-tuple-element.58), channel_id=1, source_target_pairs={{0,1},{1,0},{2,3},{3,2},{4,5},{5,4},{6,7},{7,6},{8,9},{9,8},{10,11... | collective-permute-start | bytes 786440 | tf_op jit(solution)/shard_map/ppermute | solution.py:357
  4.8 1.6 %collective-permute-start.1 = (bf16[256,1024]{1,0:T(8,128)(2,1)S(1)}, bf16[256,1024]{1,0:T(8,128)(2,1)S(1)}, u32[]{:S(2)}, u32[]{:S(2)}) collective-permute-start(bf16[256,1024]{1,0:T(8,128)(2,1)S(1)} %get-tuple-element.56._.raw_ref), channel_id=1, source_target_pairs={{0,8},{2,6},{4,0},{6,14},{8,16},{10,2},{12,4},{14,22},{16,24},{18,... | collective-permute-start | bytes 1572872 | tf_op jit(solution)/shard_map/ppermute | solution.py:358
  6.4 1.0 %copy-done.1 = s32[256,512]{1,0:T(8,128)S(1)} copy-done((s32[256,512]{1,0:T(8,128)S(1)}, s32[256,512]{1,0:T(8,128)}, u32[]{:S(2)}) %copy-start.1) | copy-done | bytes 524312
  7.4 0.7 %copy-done.2 = s32[16]{0:T(128)S(1)} copy-done((s32[16]{0:T(128)S(1)}, s32[16]{0:T(128)}, u32[]{:S(2)}) %copy-start.2) | copy-done | bytes 88
  8.1 0.6 %shard_map.51 = (bf16[256,512]{1,0:T(8,128)(2,1)S(1)}, s32[16,256]{1,0:T(8,128)S(1)}) custom-call(s32[16]{0:T(128)S(1)} %copy-done.2, s32[256,512]{1,0:T(8,128)S(1)} %copy-done.1, bf16[256,1024]{1,0:T(8,128)(2,1)S(1)} %get-tuple-element.56._.raw_ref), custom_call_target="tpu_custom_call" | custom-call | flops 345000000 | tf_op jit(solution)/shard_map/pallas_call | solution.py:98
  8.8 2.3 %collective-permute-done.refs_0_ = bf16[256,512]{1,0:T(8,128)(2,1)S(1)} collective-permute-done((bf16[256,512]{1,0:T(8,128)(2,1)S(1)}, bf16[256,512]{1,0:T(8,128)(2,1)S(1)}, u32[]{:S(2)}, u32[]{:S(2)}) %collective-permute-start) | collective-permute-done | bytes 262176 | tf_op jit(solution)/shard_map/ppermute | solution.py:357
  11.5 1.8 %collective-permute-start.2 = (bf16[256,512]{1,0:T(8,128)(2,1)S(1)}, bf16[256,512]{1,0:T(8,128)(2,1)S(1)}, u32[]{:S(2)}, u32[]{:S(2)}) collective-permute-start(bf16[256,512]{1,0:T(8,128)(2,1)S(1)} %get-tuple-element.60), channel_id=1, source_target_pairs={{0,8},{2,6},{4,0},{6,14},{8,16},{10,2},{12,4},{14,22},{16,24},{18,... | collective-permute-start | bytes 786440 | tf_op jit(solution)/shard_map/ppermute | solution.py:360
  14.1 0.9 %collective-permute-done.4.refs_2_ = bf16[128,1024]{1,0:T(8,128)(2,1)S(1)} collective-permute-done((bf16[128,1024]{1,0:T(8,128)(2,1)S(1)}, bf16[128,1024]{1,0:T(8,128)(2,1)S(1)}, u32[]{:S(2)}, u32[]{:S(2)}) %collective-permute-start.4) | collective-permute-done | bytes 262176 | tf_op jit(solution)/shard_map/ppermute | solution.py:328
  15.4 1.6 %collective-permute-start.6 = (bf16[256,1024]{1,0:T(8,128)(2,1)S(1)}, bf16[256,1024]{1,0:T(8,128)(2,1)S(1)}, u32[]{:S(2)}, u32[]{:S(2)}) collective-permute-start(bf16[256,1024]{1,0:T(8,128)(2,1)S(1)} %pad_maximum_fusion.1), channel_id=1, source_target_pairs={{0,8},{2,6},{4,0},{6,14},{8,16},{10,2},{12,4},{14,22},{16,24},{18,... | collective-permute-start | bytes 1572872 | tf_op jit(solution)/shard_map/ppermute | solution.py:362
  17.0 0.9 %collective-permute-done.2.others_ref = bf16[256,512]{1,0:T(8,128)(2,1)S(1)} collective-permute-done((bf16[256,512]{1,0:T(8,128)(2,1)S(1)}, bf16[256,512]{1,0:T(8,128)(2,1)S(1)}, u32[]{:S(2)}, u32[]{:S(2)}) %collective-permute-start.2) | collective-permute-done | bytes 262176 | tf_op jit(solution)/shard_map/ppermute | solution.py:360
  18.2 1.8 %collective-permute-start.5 = (bf16[256,1024]{1,0:T(8,128)(2,1)S(1)}, bf16[256,1024]{1,0:T(8,128)(2,1)S(1)}, u32[]{:S(2)}, u32[]{:S(2)}) collective-permute-start(bf16[256,1024]{1,0:T(8,128)(2,1)S(1)} %shard_map.53.refs_0_), channel_id=1, source_target_pairs={{0,8},{2,6},{4,0},{6,14},{8,16},{10,2},{12,4},{14,22},{16,24},{18,... | collective-permute-start | bytes 1572872 | tf_op jit(solution)/shard_map/ppermute | solution.py:376
  20.1 0.5 collective-permute-start.7
  20.6 1.5 %shard_map.54 = (bf16[2,256,4096]{2,1,0:T(8,128)(2,1)}, bf16[16,1024]{1,0:T(8,128)(2,1)S(1)}) custom-call(bf16[512,1024]{1,0:T(8,128)(2,1)S(1)} %maximum_maximum_fusion.left_ref, bf16[256,1024]{1,0:T(8,128)(2,1)S(1)} %get-tuple-element.59.refs_0_, bf16[128,1024]{1,0:T(8,128)(2,1)S(1)} %collective-permute-done.3.refs_1_, ...), custom_call_target="tpu_custom_call" | custom-call | flops 4600000000 | tf_op jit(solution)/shard_map/pallas_call | solution.py:231
  22.2 2.4 %collective-permute-done.6.refs_0_ = bf16[256,1024]{1,0:T(8,128)(2,1)S(1)} collective-permute-done((bf16[256,1024]{1,0:T(8,128)(2,1)S(1)}, bf16[256,1024]{1,0:T(8,128)(2,1)S(1)}, u32[]{:S(2)}, u32[]{:S(2)}) %collective-permute-start.6) | collective-permute-done | bytes 524320 | tf_op jit(solution)/shard_map/ppermute | solution.py:362
  25.3 1.6 %collective-permute-start.12 = (bf16[256,1024]{1,0:T(8,128)(2,1)S(1)}, bf16[256,1024]{1,0:T(8,128)(2,1)S(1)}, u32[]{:S(2)}, u32[]{:S(2)}) collective-permute-start(bf16[256,1024]{1,0:T(8,128)(2,1)S(1)} %collective-permute-done.6.refs_0_), channel_id=1, source_target_pairs={{0,8},{2,6},{4,0},{6,14},{8,16},{10,2},{12,4},{14,22},{16,24},{18,... | collective-permute-start | bytes 1572872 | tf_op jit(solution)/shard_map/ppermute | solution.py:376
  26.9 1.6 %shard_map.55 = (bf16[2,256,4096]{2,1,0:T(8,128)(2,1)}, bf16[16,1024]{1,0:T(8,128)(2,1)S(1)}) custom-call(bf16[512,1024]{1,0:T(8,128)(2,1)S(1)} %maximum_maximum_fusion.left_ref, bf16[256,1024]{1,0:T(8,128)(2,1)S(1)} %shard_map.53.refs_0_, bf16[128,1024]{1,0:T(8,128)(2,1)S(1)} %collective-permute-done.7.refs_1_, ...), custom_call_target="tpu_custom_call", output_to_operand_aliasing={{0}: (6, {})} | custom-call | tf_op jit(solution)/shard_map/pallas_call | solution.py:231
  28.5 1.7 %collective-permute-done.5.refs_0_ = bf16[256,1024]{1,0:T(8,128)(2,1)S(1)} collective-permute-done((bf16[256,1024]{1,0:T(8,128)(2,1)S(1)}, bf16[256,1024]{1,0:T(8,128)(2,1)S(1)}, u32[]{:S(2)}, u32[]{:S(2)}) %collective-permute-start.5) | collective-permute-done | bytes 524320 | tf_op jit(solution)/shard_map/ppermute | solution.py:376
  31.2 1.6 %collective-permute-start.11 = (bf16[256,1024]{1,0:T(8,128)(2,1)S(1)}, bf16[256,1024]{1,0:T(8,128)(2,1)S(1)}, u32[]{:S(2)}, u32[]{:S(2)}) collective-permute-start(bf16[256,1024]{1,0:T(8,128)(2,1)S(1)} %collective-permute-done.5.refs_0_), channel_id=1, source_target_pairs={{0,8},{2,6},{4,0},{6,14},{8,16},{10,2},{12,4},{14,22},{16,24},{18,... | collective-permute-start | bytes 1572872 | tf_op jit(solution)/shard_map/ppermute | solution.py:376
  32.9 1.6 %shard_map.56 = (bf16[2,256,4096]{2,1,0:T(8,128)(2,1)}, bf16[16,1024]{1,0:T(8,128)(2,1)S(1)}) custom-call(bf16[512,1024]{1,0:T(8,128)(2,1)S(1)} %maximum_maximum_fusion.left_ref, bf16[256,1024]{1,0:T(8,128)(2,1)S(1)} %collective-permute-done.6.refs_0_, bf16[128,1024]{1,0:T(8,128)(2,1)S(1)} %collective-permute-done.9.refs_1_, ...), custom_call_target="tpu_custom_call", output_to_operand_aliasing={{0}: (6, {})} | custom-call | tf_op jit(solution)/shard_map/pallas_call | solution.py:231
  34.4 1.4 %collective-permute-done.12.refs_0_ = bf16[256,1024]{1,0:T(8,128)(2,1)S(1)} collective-permute-done((bf16[256,1024]{1,0:T(8,128)(2,1)S(1)}, bf16[256,1024]{1,0:T(8,128)(2,1)S(1)}, u32[]{:S(2)}, u32[]{:S(2)}) %collective-permute-start.12) | collective-permute-done | bytes 524320 | tf_op jit(solution)/shard_map/ppermute | solution.py:376
  36.5 1.6 %collective-permute-start.18 = (bf16[256,1024]{1,0:T(8,128)(2,1)S(1)}, bf16[256,1024]{1,0:T(8,128)(2,1)S(1)}, u32[]{:S(2)}, u32[]{:S(2)}) collective-permute-start(bf16[256,1024]{1,0:T(8,128)(2,1)S(1)} %collective-permute-done.12.refs_0_), channel_id=1, source_target_pairs={{0,8},{2,6},{4,0},{6,14},{8,16},{10,2},{12,4},{14,22},{16,24},{18,... | collective-permute-start | bytes 1572872 | tf_op jit(solution)/shard_map/ppermute | solution.py:376
  38.0 1.5 %shard_map.57 = (bf16[2,256,4096]{2,1,0:T(8,128)(2,1)}, bf16[16,1024]{1,0:T(8,128)(2,1)S(1)}) custom-call(bf16[512,1024]{1,0:T(8,128)(2,1)S(1)} %maximum_maximum_fusion.left_ref, bf16[256,1024]{1,0:T(8,128)(2,1)S(1)} %collective-permute-done.5.refs_0_, bf16[128,1024]{1,0:T(8,128)(2,1)S(1)} %collective-permute-done.13.refs_1_, ...), custom_call_target="tpu_custom_call", output_to_operand_aliasing={{0}: (6, {})} | custom-call | tf_op jit(solution)/shard_map/pallas_call | solution.py:231
  39.6 1.9 %collective-permute-done.11.refs_0_ = bf16[256,1024]{1,0:T(8,128)(2,1)S(1)} collective-permute-done((bf16[256,1024]{1,0:T(8,128)(2,1)S(1)}, bf16[256,1024]{1,0:T(8,128)(2,1)S(1)}, u32[]{:S(2)}, u32[]{:S(2)}) %collective-permute-start.11) | collective-permute-done | bytes 524320 | tf_op jit(solution)/shard_map/ppermute | solution.py:376
  42.3 1.2 %collective-permute-done.21 = bf16[16,1024]{1,0:T(8,128)(2,1)S(1)} collective-permute-done((bf16[16,1024]{1,0:T(8,128)(2,1)S(1)}, bf16[16,1024]{1,0:T(8,128)(2,1)S(1)}, u32[]{:S(2)}, u32[]{:S(2)}) %collective-permute-start.21) | collective-permute-done | bytes 32800 | tf_op jit(solution)/shard_map/ppermute | solution.py:379
  43.9 1.4 %collective-permute-start.17 = (bf16[256,1024]{1,0:T(8,128)(2,1)S(1)}, bf16[256,1024]{1,0:T(8,128)(2,1)S(1)}, u32[]{:S(2)}, u32[]{:S(2)}) collective-permute-start(bf16[256,1024]{1,0:T(8,128)(2,1)S(1)} %collective-permute-done.11.refs_0_), channel_id=1, source_target_pairs={{0,8},{2,6},{4,0},{6,14},{8,16},{10,2},{12,4},{14,22},{16,24},{18,... | collective-permute-start | bytes 1572872 | tf_op jit(solution)/shard_map/ppermute | solution.py:376
  45.3 1.6 %shard_map.58 = (bf16[2,256,4096]{2,1,0:T(8,128)(2,1)}, bf16[16,1024]{1,0:T(8,128)(2,1)S(1)}) custom-call(bf16[512,1024]{1,0:T(8,128)(2,1)S(1)} %maximum_maximum_fusion.left_ref, bf16[256,1024]{1,0:T(8,128)(2,1)S(1)} %collective-permute-done.12.refs_0_, bf16[128,1024]{1,0:T(8,128)(2,1)S(1)} %collective-permute-done.15.refs_1_, ...), custom_call_target="tpu_custom_call", output_to_operand_aliasing={{0}: (6, {})} | custom-call | tf_op jit(solution)/shard_map/pallas_call | solution.py:231
  48.1 1.5 %shard_map.60 = (bf16[2,256,4096]{2,1,0:T(8,128)(2,1)}, bf16[16,1024]{1,0:T(8,128)(2,1)S(1)}) custom-call(bf16[512,1024]{1,0:T(8,128)(2,1)S(1)} %maximum_maximum_fusion.left_ref, bf16[256,1024]{1,0:T(8,128)(2,1)S(1)} %collective-permute-done.11.refs_0_, bf16[128,1024]{1,0:T(8,128)(2,1)S(1)} %collective-permute-done.19.refs_1_, ...), custom_call_target="tpu_custom_call", output_to_operand_aliasing={{0}: (6, {})} | custom-call | tf_op jit(solution)/shard_map/pallas_call | solution.py:231
  50.2 1.6 %collective-permute-start.28 = (f32[32,256]{1,0:T(8,128)S(1)}, f32[32,256]{1,0:T(8,128)S(1)}, u32[]{:S(2)}, u32[]{:S(2)}) collective-permute-start(f32[32,256]{1,0:T(8,128)S(1)} %shard_map.62.refs_0_), channel_id=1, source_target_pairs={{0,1},{1,0},{2,3},{3,2},{4,5},{5,4},{6,7},{7,6},{8,9},{9,8},{10,11... | collective-permute-start | bytes 98312 | tf_op jit(solution)/shard_map/ppermute | solution.py:395
  51.8 1.5 %shard_map.63.refs_3_ = bf16[2,256,4096]{2,1,0:T(8,128)(2,1)} custom-call(bf16[512,1024]{1,0:T(8,128)(2,1)S(1)} %maximum_maximum_fusion.left_ref, bf16[256,1024]{1,0:T(8,128)(2,1)S(1)} %collective-permute-done.18.refs_0_, bf16[128,1024]{1,0:T(8,128)(2,1)S(1)} %collective-permute-done.23.refs_1_, ...), custom_call_target="tpu_custom_call", output_to_operand_aliasing={{}: (4, {})} | custom-call | tf_op jit(solution)/shard_map/pallas_call | solution.py:231
  54.2 1.6 %shard_map.65 = f32[16,256,128]{2,1,0:T(8,128)} custom-call(bf16[192,2048]{1,0:T(8,128)(2,1)S(1)} %pad_maximum_fusion.table_ref, f32[32,256]{1,0:T(8,128)S(1)} %shard_map.62.refs_0_, f32[32,256]{1,0:T(8,128)S(1)} %collective-permute-done.28.refs_1_), custom_call_target="tpu_custom_call" | custom-call | flops 9200000000 | tf_op jit(solution)/shard_map/pallas_call | solution.py:305
  55.8 1.6 %shard_map.64 = bf16[2,256,4096]{2,1,0:T(8,128)(2,1)} custom-call(bf16[512,1024]{1,0:T(8,128)(2,1)S(1)} %maximum_maximum_fusion.left_ref, bf16[256,1024]{1,0:T(8,128)(2,1)S(1)} %collective-permute-done.17.refs_0_, bf16[128,1024]{1,0:T(8,128)(2,1)S(1)} %collective-permute-done.26.refs_1_, ...), custom_call_target="tpu_custom_call", output_to_operand_aliasing={{}: (4, {})} | custom-call | tf_op jit(solution)/shard_map/pallas_call | solution.py:231
  (67 shorter events, 8.1 us)
Async XLA Ops:
  0.6 1.0 %copy-start = (bf16[1,256,1024]{2,1,0:T(8,128)(2,1)S(1)}, bf16[1,256,1024]{2,1,0:T(8,128)(2,1)}, u32[]{:S(2)}) copy-start(bf16[1,256,1024]{2,1,0:T(8,128)(2,1)} %param.3) | copy-start | bytes 1572868
  1.8 9.3 %collective-permute-start = (bf16[256,512]{1,0:T(8,128)(2,1)S(1)}, bf16[256,512]{1,0:T(8,128)(2,1)S(1)}, u32[]{:S(2)}, u32[]{:S(2)}) collective-permute-start(bf16[256,512]{1,0:T(8,128)(2,1)S(1)} %get-tuple-element.58), channel_id=1, source_target_pairs={{0,1},{1,0},{2,3},{3,2},{4,5},{5,4},{6,7},{7,6},{8,9},{9,8},{10,11... | collective-permute-start | bytes 786440 | tf_op jit(solution)/shard_map/ppermute | solution.py:357
  4.8 13.1 %collective-permute-start.1 = (bf16[256,1024]{1,0:T(8,128)(2,1)S(1)}, bf16[256,1024]{1,0:T(8,128)(2,1)S(1)}, u32[]{:S(2)}, u32[]{:S(2)}) collective-permute-start(bf16[256,1024]{1,0:T(8,128)(2,1)S(1)} %get-tuple-element.56._.raw_ref), channel_id=1, source_target_pairs={{0,8},{2,6},{4,0},{6,14},{8,16},{10,2},{12,4},{14,22},{16,24},{18,... | collective-permute-start | bytes 1572872 | tf_op jit(solution)/shard_map/ppermute | solution.py:358
  6.4 1.0 %copy-start.1 = (s32[256,512]{1,0:T(8,128)S(1)}, s32[256,512]{1,0:T(8,128)}, u32[]{:S(2)}) copy-start(s32[256,512]{1,0:T(8,128)} %valid_ref.1) | copy-start | bytes 1572868
  7.4 0.7 %copy-start.2 = (s32[16]{0:T(128)S(1)}, s32[16]{0:T(128)}, u32[]{:S(2)}) copy-start(s32[16]{0:T(128)} %index_ref.1) | copy-start | bytes 196
  11.5 6.4 %collective-permute-start.2 = (bf16[256,512]{1,0:T(8,128)(2,1)S(1)}, bf16[256,512]{1,0:T(8,128)(2,1)S(1)}, u32[]{:S(2)}, u32[]{:S(2)}) collective-permute-start(bf16[256,512]{1,0:T(8,128)(2,1)S(1)} %get-tuple-element.60), channel_id=1, source_target_pairs={{0,8},{2,6},{4,0},{6,14},{8,16},{10,2},{12,4},{14,22},{16,24},{18,... | collective-permute-start | bytes 786440 | tf_op jit(solution)/shard_map/ppermute | solution.py:360
  13.4 1.6 %collective-permute-start.4 = (bf16[128,1024]{1,0:T(8,128)(2,1)S(1)}, bf16[128,1024]{1,0:T(8,128)(2,1)S(1)}, u32[]{:S(2)}, u32[]{:S(2)}) collective-permute-start(bf16[128,1024]{1,0:T(8,128)(2,1)S(1)} %get-tuple-element.124), channel_id=1, source_target_pairs={{0,2},{2,0},{4,6},{6,4},{8,10},{10,8},{12,14},{14,12},{16,18},{18,... | collective-permute-start | bytes 786440 | tf_op jit(solution)/shard_map/ppermute | solution.py:328
  13.4 1.9 %collective-permute-start.3 = (bf16[128,1024]{1,0:T(8,128)(2,1)S(1)}, bf16[128,1024]{1,0:T(8,128)(2,1)S(1)}, u32[]{:S(2)}, u32[]{:S(2)}) collective-permute-start(bf16[128,1024]{1,0:T(8,128)(2,1)S(1)} %get-tuple-element.125), channel_id=1, source_target_pairs={{0,2},{2,0},{4,6},{6,4},{8,10},{10,8},{12,14},{14,12},{16,18},{18,... | collective-permute-start | bytes 786440 | tf_op jit(solution)/shard_map/ppermute | solution.py:328
  15.4 9.2 %collective-permute-start.6 = (bf16[256,1024]{1,0:T(8,128)(2,1)S(1)}, bf16[256,1024]{1,0:T(8,128)(2,1)S(1)}, u32[]{:S(2)}, u32[]{:S(2)}) collective-permute-start(bf16[256,1024]{1,0:T(8,128)(2,1)S(1)} %pad_maximum_fusion.1), channel_id=1, source_target_pairs={{0,8},{2,6},{4,0},{6,14},{8,16},{10,2},{12,4},{14,22},{16,24},{18,... | collective-permute-start | bytes 1572872 | tf_op jit(solution)/shard_map/ppermute | solution.py:362
  18.2 12.0 %collective-permute-start.5 = (bf16[256,1024]{1,0:T(8,128)(2,1)S(1)}, bf16[256,1024]{1,0:T(8,128)(2,1)S(1)}, u32[]{:S(2)}, u32[]{:S(2)}) collective-permute-start(bf16[256,1024]{1,0:T(8,128)(2,1)S(1)} %shard_map.53.refs_0_), channel_id=1, source_target_pairs={{0,8},{2,6},{4,0},{6,14},{8,16},{10,2},{12,4},{14,22},{16,24},{18,... | collective-permute-start | bytes 1572872 | tf_op jit(solution)/shard_map/ppermute | solution.py:376
  20.1 2.1 %collective-permute-start.8 = (bf16[128,1024]{1,0:T(8,128)(2,1)S(1)}, bf16[128,1024]{1,0:T(8,128)(2,1)S(1)}, u32[]{:S(2)}, u32[]{:S(2)}) collective-permute-start(bf16[128,1024]{1,0:T(8,128)(2,1)S(1)} %get-tuple-element.122), channel_id=1, source_target_pairs={{0,2},{2,0},{4,6},{6,4},{8,10},{10,8},{12,14},{14,12},{16,18},{18,... | collective-permute-start | bytes 786440 | tf_op jit(solution)/shard_map/ppermute | solution.py:328
  20.1 2.1 %collective-permute-start.7 = (bf16[128,1024]{1,0:T(8,128)(2,1)S(1)}, bf16[128,1024]{1,0:T(8,128)(2,1)S(1)}, u32[]{:S(2)}, u32[]{:S(2)}) collective-permute-start(bf16[128,1024]{1,0:T(8,128)(2,1)S(1)} %get-tuple-element.123), channel_id=1, source_target_pairs={{0,2},{2,0},{4,6},{6,4},{8,10},{10,8},{12,14},{14,12},{16,18},{18,... | collective-permute-start | bytes 786440 | tf_op jit(solution)/shard_map/ppermute | solution.py:328
  24.6 5.6 %collective-permute-start.10 = (bf16[128,1024]{1,0:T(8,128)(2,1)S(1)}, bf16[128,1024]{1,0:T(8,128)(2,1)S(1)}, u32[]{:S(2)}, u32[]{:S(2)}) collective-permute-start(bf16[128,1024]{1,0:T(8,128)(2,1)S(1)} %get-tuple-element.120), channel_id=1, source_target_pairs={{0,2},{2,0},{4,6},{6,4},{8,10},{10,8},{12,14},{14,12},{16,18},{18,... | collective-permute-start | bytes 786440 | tf_op jit(solution)/shard_map/ppermute | solution.py:328
  24.7 5.5 %collective-permute-start.9 = (bf16[128,1024]{1,0:T(8,128)(2,1)S(1)}, bf16[128,1024]{1,0:T(8,128)(2,1)S(1)}, u32[]{:S(2)}, u32[]{:S(2)}) collective-permute-start(bf16[128,1024]{1,0:T(8,128)(2,1)S(1)} %get-tuple-element.121), channel_id=1, source_target_pairs={{0,2},{2,0},{4,6},{6,4},{8,10},{10,8},{12,14},{14,12},{16,18},{18,... | collective-permute-start | bytes 786440 | tf_op jit(solution)/shard_map/ppermute | solution.py:328
  25.3 10.5 %collective-permute-start.12 = (bf16[256,1024]{1,0:T(8,128)(2,1)S(1)}, bf16[256,1024]{1,0:T(8,128)(2,1)S(1)}, u32[]{:S(2)}, u32[]{:S(2)}) collective-permute-start(bf16[256,1024]{1,0:T(8,128)(2,1)S(1)} %collective-permute-done.6.refs_0_), channel_id=1, source_target_pairs={{0,8},{2,6},{4,0},{6,14},{8,16},{10,2},{12,4},{14,22},{16,24},{18,... | collective-permute-start | bytes 1572872 | tf_op jit(solution)/shard_map/ppermute | solution.py:376
  30.3 5.6 %collective-permute-start.14 = (bf16[128,1024]{1,0:T(8,128)(2,1)S(1)}, bf16[128,1024]{1,0:T(8,128)(2,1)S(1)}, u32[]{:S(2)}, u32[]{:S(2)}) collective-permute-start(bf16[128,1024]{1,0:T(8,128)(2,1)S(1)} %get-tuple-element.118), channel_id=1, source_target_pairs={{0,2},{2,0},{4,6},{6,4},{8,10},{10,8},{12,14},{14,12},{16,18},{18,... | collective-permute-start | bytes 786440 | tf_op jit(solution)/shard_map/ppermute | solution.py:328
  30.3 5.5 %collective-permute-start.13 = (bf16[128,1024]{1,0:T(8,128)(2,1)S(1)}, bf16[128,1024]{1,0:T(8,128)(2,1)S(1)}, u32[]{:S(2)}, u32[]{:S(2)}) collective-permute-start(bf16[128,1024]{1,0:T(8,128)(2,1)S(1)} %get-tuple-element.119), channel_id=1, source_target_pairs={{0,2},{2,0},{4,6},{6,4},{8,10},{10,8},{12,14},{14,12},{16,18},{18,... | collective-permute-start | bytes 786440 | tf_op jit(solution)/shard_map/ppermute | solution.py:328
  31.2 10.3 %collective-permute-start.11 = (bf16[256,1024]{1,0:T(8,128)(2,1)S(1)}, bf16[256,1024]{1,0:T(8,128)(2,1)S(1)}, u32[]{:S(2)}, u32[]{:S(2)}) collective-permute-start(bf16[256,1024]{1,0:T(8,128)(2,1)S(1)} %collective-permute-done.5.refs_0_), channel_id=1, source_target_pairs={{0,8},{2,6},{4,0},{6,14},{8,16},{10,2},{12,4},{14,22},{16,24},{18,... | collective-permute-start | bytes 1572872 | tf_op jit(solution)/shard_map/ppermute | solution.py:376
  35.9 5.6 %collective-permute-start.16 = (bf16[128,1024]{1,0:T(8,128)(2,1)S(1)}, bf16[128,1024]{1,0:T(8,128)(2,1)S(1)}, u32[]{:S(2)}, u32[]{:S(2)}) collective-permute-start(bf16[128,1024]{1,0:T(8,128)(2,1)S(1)} %get-tuple-element.116), channel_id=1, source_target_pairs={{0,2},{2,0},{4,6},{6,4},{8,10},{10,8},{12,14},{14,12},{16,18},{18,... | collective-permute-start | bytes 786440 | tf_op jit(solution)/shard_map/ppermute | solution.py:328
  36.0 5.5 %collective-permute-start.15 = (bf16[128,1024]{1,0:T(8,128)(2,1)S(1)}, bf16[128,1024]{1,0:T(8,128)(2,1)S(1)}, u32[]{:S(2)}, u32[]{:S(2)}) collective-permute-start(bf16[128,1024]{1,0:T(8,128)(2,1)S(1)} %get-tuple-element.117), channel_id=1, source_target_pairs={{0,2},{2,0},{4,6},{6,4},{8,10},{10,8},{12,14},{14,12},{16,18},{18,... | collective-permute-start | bytes 786440 | tf_op jit(solution)/shard_map/ppermute | solution.py:328
  36.5 11.0 %collective-permute-start.18 = (bf16[256,1024]{1,0:T(8,128)(2,1)S(1)}, bf16[256,1024]{1,0:T(8,128)(2,1)S(1)}, u32[]{:S(2)}, u32[]{:S(2)}) collective-permute-start(bf16[256,1024]{1,0:T(8,128)(2,1)S(1)} %collective-permute-done.12.refs_0_), channel_id=1, source_target_pairs={{0,8},{2,6},{4,0},{6,14},{8,16},{10,2},{12,4},{14,22},{16,24},{18,... | collective-permute-start | bytes 1572872 | tf_op jit(solution)/shard_map/ppermute | solution.py:376
  41.5 5.8 %collective-permute-start.20 = (bf16[128,1024]{1,0:T(8,128)(2,1)S(1)}, bf16[128,1024]{1,0:T(8,128)(2,1)S(1)}, u32[]{:S(2)}, u32[]{:S(2)}) collective-permute-start(bf16[128,1024]{1,0:T(8,128)(2,1)S(1)} %get-tuple-element.114), channel_id=1, source_target_pairs={{0,2},{2,0},{4,6},{6,4},{8,10},{10,8},{12,14},{14,12},{16,18},{18,... | collective-permute-start | bytes 786440 | tf_op jit(solution)/shard_map/ppermute | solution.py:328
  41.6 5.7 %collective-permute-start.19 = (bf16[128,1024]{1,0:T(8,128)(2,1)S(1)}, bf16[128,1024]{1,0:T(8,128)(2,1)S(1)}, u32[]{:S(2)}, u32[]{:S(2)}) collective-permute-start(bf16[128,1024]{1,0:T(8,128)(2,1)S(1)} %get-tuple-element.115), channel_id=1, source_target_pairs={{0,2},{2,0},{4,6},{6,4},{8,10},{10,8},{12,14},{14,12},{16,18},{18,... | collective-permute-start | bytes 786440 | tf_op jit(solution)/shard_map/ppermute | solution.py:328
  42.2 1.3 %collective-permute-start.21 = (bf16[16,1024]{1,0:T(8,128)(2,1)S(1)}, bf16[16,1024]{1,0:T(8,128)(2,1)S(1)}, u32[]{:S(2)}, u32[]{:S(2)}) collective-permute-start(bf16[16,1024]{1,0:T(8,128)(2,1)S(1)} %shard_map.59), channel_id=1, source_target_pairs={{0,2},{2,0},{4,6},{6,4},{8,10},{10,8},{12,14},{14,12},{16,18},{18,... | collective-permute-start | bytes 98312 | tf_op jit(solution)/shard_map/ppermute | solution.py:379
  43.5 3.8 %collective-permute-start.22 = (bf16[16,1024]{1,0:T(8,128)(2,1)S(1)}, bf16[16,1024]{1,0:T(8,128)(2,1)S(1)}, u32[]{:S(2)}, u32[]{:S(2)}) collective-permute-start(bf16[16,1024]{1,0:T(8,128)(2,1)S(1)} %collective-permute-done.21), channel_id=1, source_target_pairs={{0,6},{2,8},{4,14},{6,0},{8,2},{10,16},{12,22},{14,4},{16,10},{18,... | collective-permute-start | bytes 98312 | tf_op jit(solution)/shard_map/ppermute | solution.py:379
  43.9 9.4 %collective-permute-start.17 = (bf16[256,1024]{1,0:T(8,128)(2,1)S(1)}, bf16[256,1024]{1,0:T(8,128)(2,1)S(1)}, u32[]{:S(2)}, u32[]{:S(2)}) collective-permute-start(bf16[256,1024]{1,0:T(8,128)(2,1)S(1)} %collective-permute-done.11.refs_0_), channel_id=1, source_target_pairs={{0,8},{2,6},{4,0},{6,14},{8,16},{10,2},{12,4},{14,22},{16,24},{18,... | collective-permute-start | bytes 1572872 | tf_op jit(solution)/shard_map/ppermute | solution.py:376
  47.5 2.2 %collective-permute-start.24 = (bf16[128,1024]{1,0:T(8,128)(2,1)S(1)}, bf16[128,1024]{1,0:T(8,128)(2,1)S(1)}, u32[]{:S(2)}, u32[]{:S(2)}) collective-permute-start(bf16[128,1024]{1,0:T(8,128)(2,1)S(1)} %get-tuple-element.112), channel_id=1, source_target_pairs={{0,2},{2,0},{4,6},{6,4},{8,10},{10,8},{12,14},{14,12},{16,18},{18,... | collective-permute-start | bytes 786440 | tf_op jit(solution)/shard_map/ppermute | solution.py:328
  47.5 2.1 %collective-permute-start.23 = (bf16[128,1024]{1,0:T(8,128)(2,1)S(1)}, bf16[128,1024]{1,0:T(8,128)(2,1)S(1)}, u32[]{:S(2)}, u32[]{:S(2)}) collective-permute-start(bf16[128,1024]{1,0:T(8,128)(2,1)S(1)} %get-tuple-element.113), channel_id=1, source_target_pairs={{0,2},{2,0},{4,6},{6,4},{8,10},{10,8},{12,14},{14,12},{16,18},{18,... | collective-permute-start | bytes 786440 | tf_op jit(solution)/shard_map/ppermute | solution.py:328
  48.0 1.9 %collective-permute-start.25 = (bf16[16,1024]{1,0:T(8,128)(2,1)S(1)}, bf16[16,1024]{1,0:T(8,128)(2,1)S(1)}, u32[]{:S(2)}, u32[]{:S(2)}) collective-permute-start(bf16[16,1024]{1,0:T(8,128)(2,1)S(1)} %collective-permute-done.22.refs_2_), channel_id=1, source_target_pairs={{0,2},{2,0},{4,6},{6,4},{8,10},{10,8},{12,14},{14,12},{16,18},{18,... | collective-permute-start | bytes 98312 | tf_op jit(solution)/shard_map/ppermute | solution.py:383
  50.2 4.0 %collective-permute-start.28 = (f32[32,256]{1,0:T(8,128)S(1)}, f32[32,256]{1,0:T(8,128)S(1)}, u32[]{:S(2)}, u32[]{:S(2)}) collective-permute-start(f32[32,256]{1,0:T(8,128)S(1)} %shard_map.62.refs_0_), channel_id=1, source_target_pairs={{0,1},{1,0},{2,3},{3,2},{4,5},{5,4},{6,7},{7,6},{8,9},{9,8},{10,11... | collective-permute-start | bytes 98312 | tf_op jit(solution)/shard_map/ppermute | solution.py:395
  53.4 2.4 %collective-permute-start.27 = (bf16[128,1024]{1,0:T(8,128)(2,1)S(1)}, bf16[128,1024]{1,0:T(8,128)(2,1)S(1)}, u32[]{:S(2)}, u32[]{:S(2)}) collective-permute-start(bf16[128,1024]{1,0:T(8,128)(2,1)S(1)} %get-tuple-element.110), channel_id=1, source_target_pairs={{0,2},{2,0},{4,6},{6,4},{8,10},{10,8},{12,14},{14,12},{16,18},{18,... | collective-permute-start | bytes 786440 | tf_op jit(solution)/shard_map/ppermute | solution.py:328
  53.6 2.2 %collective-permute-start.26 = (bf16[128,1024]{1,0:T(8,128)(2,1)S(1)}, bf16[128,1024]{1,0:T(8,128)(2,1)S(1)}, u32[]{:S(2)}, u32[]{:S(2)}) collective-permute-start(bf16[128,1024]{1,0:T(8,128)(2,1)S(1)} %get-tuple-element.111), channel_id=1, source_target_pairs={{0,2},{2,0},{4,6},{6,4},{8,10},{10,8},{12,14},{14,12},{16,18},{18,... | collective-permute-start | bytes 786440 | tf_op jit(solution)/shard_map/ppermute | solution.py:328

commit v8 on v7

--- a/solution.py
+++ b/solution.py
@@ -356,9 +356,11 @@
         valid, numbers = prepare(valid, station_index, raw)
         received = [lax.ppermute(power, "freq", from_freq(shift)) for shift in range(1, freq_size)]
         raw_flying = lax.ppermute(raw, "grp", ring)
+        raw_sibling = lax.ppermute(raw, "grp", swap_by(1))
         whitened, others = whiten_own(raw, valid, received, total_bins)
         others_flying = lax.ppermute(others, "grp", ring)
-        swapped = swap(whitened)
+        others_sibling = lax.ppermute(others, "grp", swap_by(1))
+        swapped = [whiten_passed(raw_sibling, others_sibling, total_bins)]
         flying = [None, lax.ppermute(jnp.concatenate(swapped, axis=0), "grp", ring)]
         left = jnp.concatenate(
             [whitened, jnp.concatenate([whitened[:, window_count:], -whitened[:, :window_count]], axis=1)], axis=0

time: 57.6 us -> 57.2 us (level)
  waiting for transfers between devices: 13.9 us -> 12.8 us
    ppermute x1, waiting for transfers between devices: 0.89 us -> 2.48 us  [on_device(): others_flying = lax.ppermute(others, 'grp', ring)]
    ppermute x16 -> x14, waiting for transfers between devices: 1.28 us -> 0.04 us  [swap_pieces(): lax.ppermute(block[k * rows:(k + 1) * rows], 'grp', swap_by(1))]
    ppermute x1, waiting for transfers between devices: 2.44 us -> 1.34 us  [on_device(): flying = [None, lax.ppermute(jnp.concatenate(swapped, axis=0), 'grp', ring)]]
    ppermute x1, starting transfers between devices: 0.36 us -> 1.45 us  [on_device(): lax.ppermute(lax.ppermute(found, 'grp', swap_by(1)), 'grp', across)]
    ppermute x16 -> x14, starting transfers between devices: 4.49 us -> 3.92 us  [swap_pieces(): lax.ppermute(block[k * rows:(k + 1) * rows], 'grp', swap_by(1))]
  transfers between devices with their start and end apart: 29 -> 29, of which waited for: 12 -> 10; matrix products, arithmetic and copies ran while one was open for 2% -> 2% of each run, Pallas kernels for 25% -> 26%
where the time goes in v8:
time: 57.2 us; the launch traced here: 57 us
  starting transfers between devices  23.2 us (41%)
  Pallas kernels  16.3 us (28%)
  waiting for transfers between devices  12.8 us (22%)
  local copies, waits for them, and re-layouts  3.12 us (5%)
  between operations  0.98 us (2%)
    pallas_call x8, Pallas kernels, cross_blocks(): pl.pallas_call(body, out_shape=shapes, in_specs=specs, out_specs=out_spec...  12.4 us
    ppermute x5, starting transfers between devices, on_device(): flying.append(lax.ppermute(arrived, 'grp', ring))  7.72 us
    ppermute x5, waiting for transfers between devices, on_device(): flying.append(lax.ppermute(arrived, 'grp', ring))  5.06 us
    ppermute x14, starting transfers between devices, swap_pieces(): lax.ppermute(block[k * rows:(k + 1) * rows], 'grp', swap_by(1))  3.92 us
    ppermute x1, starting transfers between devices, on_device(): lax.ppermute(power, 'freq', from_freq(shift))  3.03 us
    unnamed x8, local copies, waits for them, and re-layouts  2.87 us
    ppermute x1, waiting for transfers between devices, on_device(): others_flying = lax.ppermute(others, 'grp', ring)  2.48 us
    ppermute x1, waiting for transfers between devices, on_device(): lax.ppermute(power, 'freq', from_freq(shift))  2.32 us
  transfers between devices with their start and end apart: 29, of which 10 were waited for; matrix products, arithmetic and copies ran while one was open for 2% of the time, Pallas kernels for 26%

profile of v8, /device:TPU:0, one launch (start us, length us, event | category | flops | bytes accessed | tf_op | source)
XLA Modules:
  0.0 57.0 jit_solution(16585085875679414330)
XLA Ops:
  0.6 1.0 %copy-done = bf16[1,256,1024]{2,1,0:T(8,128)(2,1)S(1)} copy-done((bf16[1,256,1024]{2,1,0:T(8,128)(2,1)S(1)}, bf16[1,256,1024]{2,1,0:T(8,128)(2,1)}, u32[]{:S(2)}) %copy-start) | copy-done | bytes 524312
  1.8 3.0 %collective-permute-start = (bf16[256,512]{1,0:T(8,128)(2,1)S(1)}, bf16[256,512]{1,0:T(8,128)(2,1)S(1)}, u32[]{:S(2)}, u32[]{:S(2)}) collective-permute-start(bf16[256,512]{1,0:T(8,128)(2,1)S(1)} %get-tuple-element.57), channel_id=1, source_target_pairs={{0,1},{1,0},{2,3},{3,2},{4,5},{5,4},{6,7},{7,6},{8,9},{9,8},{10,11... | collective-permute-start | bytes 786440 | tf_op jit(solution)/shard_map/ppermute | solution.py:357
  4.8 1.6 %collective-permute-start.1 = (bf16[256,1024]{1,0:T(8,128)(2,1)S(1)}, bf16[256,1024]{1,0:T(8,128)(2,1)S(1)}, u32[]{:S(2)}, u32[]{:S(2)}) collective-permute-start(bf16[256,1024]{1,0:T(8,128)(2,1)S(1)} %get-tuple-element.55._.raw_ref), channel_id=1, source_target_pairs={{0,8},{2,6},{4,0},{6,14},{8,16},{10,2},{12,4},{14,22},{16,24},{18,... | collective-permute-start | bytes 1572872 | tf_op jit(solution)/shard_map/ppermute | solution.py:358
  6.4 1.0 %copy-done.1 = s32[256,512]{1,0:T(8,128)S(1)} copy-done((s32[256,512]{1,0:T(8,128)S(1)}, s32[256,512]{1,0:T(8,128)}, u32[]{:S(2)}) %copy-start.1) | copy-done | bytes 524312
  7.4 0.7 %copy-done.2 = s32[16]{0:T(128)S(1)} copy-done((s32[16]{0:T(128)S(1)}, s32[16]{0:T(128)}, u32[]{:S(2)}) %copy-start.2) | copy-done | bytes 88
  8.1 0.6 %shard_map.51 = (bf16[256,512]{1,0:T(8,128)(2,1)S(1)}, s32[16,256]{1,0:T(8,128)S(1)}) custom-call(s32[16]{0:T(128)S(1)} %copy-done.2, s32[256,512]{1,0:T(8,128)S(1)} %copy-done.1, bf16[256,1024]{1,0:T(8,128)(2,1)S(1)} %get-tuple-element.55._.raw_ref), custom_call_target="tpu_custom_call" | custom-call | flops 345000000 | tf_op jit(solution)/shard_map/pallas_call | solution.py:98
  8.8 2.3 %collective-permute-done.refs_0_ = bf16[256,512]{1,0:T(8,128)(2,1)S(1)} collective-permute-done((bf16[256,512]{1,0:T(8,128)(2,1)S(1)}, bf16[256,512]{1,0:T(8,128)(2,1)S(1)}, u32[]{:S(2)}, u32[]{:S(2)}) %collective-permute-start) | collective-permute-done | bytes 262176 | tf_op jit(solution)/shard_map/ppermute | solution.py:357
  11.5 1.8 %collective-permute-start.2 = (bf16[256,512]{1,0:T(8,128)(2,1)S(1)}, bf16[256,512]{1,0:T(8,128)(2,1)S(1)}, u32[]{:S(2)}, u32[]{:S(2)}) collective-permute-start(bf16[256,512]{1,0:T(8,128)(2,1)S(1)} %get-tuple-element.59), channel_id=1, source_target_pairs={{0,8},{2,6},{4,0},{6,14},{8,16},{10,2},{12,4},{14,22},{16,24},{18,... | collective-permute-start | bytes 786440 | tf_op jit(solution)/shard_map/ppermute | solution.py:361
  13.8 1.6 %collective-permute-start.6 = (bf16[256,1024]{1,0:T(8,128)(2,1)S(1)}, bf16[256,1024]{1,0:T(8,128)(2,1)S(1)}, u32[]{:S(2)}, u32[]{:S(2)}) collective-permute-start(bf16[256,1024]{1,0:T(8,128)(2,1)S(1)} %shard_map.54.refs_1_), channel_id=1, source_target_pairs={{0,8},{2,6},{4,0},{6,14},{8,16},{10,2},{12,4},{14,22},{16,24},{18,... | collective-permute-start | bytes 1572872 | tf_op jit(solution)/shard_map/ppermute | solution.py:364
  15.5 2.5 %collective-permute-done.2.others_ref = bf16[256,512]{1,0:T(8,128)(2,1)S(1)} collective-permute-done((bf16[256,512]{1,0:T(8,128)(2,1)S(1)}, bf16[256,512]{1,0:T(8,128)(2,1)S(1)}, u32[]{:S(2)}, u32[]{:S(2)}) %collective-permute-start.2) | collective-permute-done | bytes 262176 | tf_op jit(solution)/shard_map/ppermute | solution.py:361
  18.3 1.8 %collective-permute-start.5 = (bf16[256,1024]{1,0:T(8,128)(2,1)S(1)}, bf16[256,1024]{1,0:T(8,128)(2,1)S(1)}, u32[]{:S(2)}, u32[]{:S(2)}) collective-permute-start(bf16[256,1024]{1,0:T(8,128)(2,1)S(1)} %shard_map.53.refs_0_), channel_id=1, source_target_pairs={{0,8},{2,6},{4,0},{6,14},{8,16},{10,2},{12,4},{14,22},{16,24},{18,... | collective-permute-start | bytes 1572872 | tf_op jit(solution)/shard_map/ppermute | solution.py:378
  20.1 0.5 collective-permute-start.7
  20.7 1.6 %shard_map.55 = (bf16[2,256,4096]{2,1,0:T(8,128)(2,1)}, bf16[16,1024]{1,0:T(8,128)(2,1)S(1)}) custom-call(bf16[512,1024]{1,0:T(8,128)(2,1)S(1)} %maximum_maximum_fusion.left_ref, bf16[256,1024]{1,0:T(8,128)(2,1)S(1)} %get-tuple-element.58.refs_0_, bf16[256,1024]{1,0:T(8,128)(2,1)S(1)} %shard_map.54.refs_1_, ...), custom_call_target="tpu_custom_call" | custom-call | flops 4600000000 | tf_op jit(solution)/shard_map/pallas_call | solution.py:231
  22.2 1.3 %collective-permute-done.6.refs_0_ = bf16[256,1024]{1,0:T(8,128)(2,1)S(1)} collective-permute-done((bf16[256,1024]{1,0:T(8,128)(2,1)S(1)}, bf16[256,1024]{1,0:T(8,128)(2,1)S(1)}, u32[]{:S(2)}, u32[]{:S(2)}) %collective-permute-start.6) | collective-permute-done | bytes 524320 | tf_op jit(solution)/shard_map/ppermute | solution.py:364
  24.3 1.8 %collective-permute-start.12 = (bf16[256,1024]{1,0:T(8,128)(2,1)S(1)}, bf16[256,1024]{1,0:T(8,128)(2,1)S(1)}, u32[]{:S(2)}, u32[]{:S(2)}) collective-permute-start(bf16[256,1024]{1,0:T(8,128)(2,1)S(1)} %collective-permute-done.6.refs_0_), channel_id=1, source_target_pairs={{0,8},{2,6},{4,0},{6,14},{8,16},{10,2},{12,4},{14,22},{16,24},{18,... | collective-permute-start | bytes 1572872 | tf_op jit(solution)/shard_map/ppermute | solution.py:378
  26.1 1.5 %shard_map.56 = (bf16[2,256,4096]{2,1,0:T(8,128)(2,1)}, bf16[16,1024]{1,0:T(8,128)(2,1)S(1)}) custom-call(bf16[512,1024]{1,0:T(8,128)(2,1)S(1)} %maximum_maximum_fusion.left_ref, bf16[256,1024]{1,0:T(8,128)(2,1)S(1)} %shard_map.53.refs_0_, bf16[128,1024]{1,0:T(8,128)(2,1)S(1)} %collective-permute-done.7.refs_1_, ...), custom_call_target="tpu_custom_call", output_to_operand_aliasing={{0}: (6, {})} | custom-call | tf_op jit(solution)/shard_map/pallas_call | solution.py:231
  27.7 1.5 %collective-permute-done.5.refs_0_ = bf16[256,1024]{1,0:T(8,128)(2,1)S(1)} collective-permute-done((bf16[256,1024]{1,0:T(8,128)(2,1)S(1)}, bf16[256,1024]{1,0:T(8,128)(2,1)S(1)}, u32[]{:S(2)}, u32[]{:S(2)}) %collective-permute-start.5) | collective-permute-done | bytes 524320 | tf_op jit(solution)/shard_map/ppermute | solution.py:378
  30.1 1.8 %collective-permute-start.11 = (bf16[256,1024]{1,0:T(8,128)(2,1)S(1)}, bf16[256,1024]{1,0:T(8,128)(2,1)S(1)}, u32[]{:S(2)}, u32[]{:S(2)}) collective-permute-start(bf16[256,1024]{1,0:T(8,128)(2,1)S(1)} %collective-permute-done.5.refs_0_), channel_id=1, source_target_pairs={{0,8},{2,6},{4,0},{6,14},{8,16},{10,2},{12,4},{14,22},{16,24},{18,... | collective-permute-start | bytes 1572872 | tf_op jit(solution)/shard_map/ppermute | solution.py:378
  32.1 1.6 %shard_map.57 = (bf16[2,256,4096]{2,1,0:T(8,128)(2,1)}, bf16[16,1024]{1,0:T(8,128)(2,1)S(1)}) custom-call(bf16[512,1024]{1,0:T(8,128)(2,1)S(1)} %maximum_maximum_fusion.left_ref, bf16[256,1024]{1,0:T(8,128)(2,1)S(1)} %collective-permute-done.6.refs_0_, bf16[128,1024]{1,0:T(8,128)(2,1)S(1)} %collective-permute-done.9.refs_1_, ...), custom_call_target="tpu_custom_call", output_to_operand_aliasing={{0}: (6, {})} | custom-call | tf_op jit(solution)/shard_map/pallas_call | solution.py:231
  33.6 1.2 %collective-permute-done.12.refs_0_ = bf16[256,1024]{1,0:T(8,128)(2,1)S(1)} collective-permute-done((bf16[256,1024]{1,0:T(8,128)(2,1)S(1)}, bf16[256,1024]{1,0:T(8,128)(2,1)S(1)}, u32[]{:S(2)}, u32[]{:S(2)}) %collective-permute-start.12) | collective-permute-done | bytes 524320 | tf_op jit(solution)/shard_map/ppermute | solution.py:378
  35.4 1.8 %collective-permute-start.18 = (bf16[256,1024]{1,0:T(8,128)(2,1)S(1)}, bf16[256,1024]{1,0:T(8,128)(2,1)S(1)}, u32[]{:S(2)}, u32[]{:S(2)}) collective-permute-start(bf16[256,1024]{1,0:T(8,128)(2,1)S(1)} %collective-permute-done.12.refs_0_), channel_id=1, source_target_pairs={{0,8},{2,6},{4,0},{6,14},{8,16},{10,2},{12,4},{14,22},{16,24},{18,... | collective-permute-start | bytes 1572872 | tf_op jit(solution)/shard_map/ppermute | solution.py:378
  37.2 1.6 %shard_map.58 = (bf16[2,256,4096]{2,1,0:T(8,128)(2,1)}, bf16[16,1024]{1,0:T(8,128)(2,1)S(1)}) custom-call(bf16[512,1024]{1,0:T(8,128)(2,1)S(1)} %maximum_maximum_fusion.left_ref, bf16[256,1024]{1,0:T(8,128)(2,1)S(1)} %collective-permute-done.5.refs_0_, bf16[128,1024]{1,0:T(8,128)(2,1)S(1)} %collective-permute-done.13.refs_1_, ...), custom_call_target="tpu_custom_call", output_to_operand_aliasing={{0}: (6, {})} | custom-call | tf_op jit(solution)/shard_map/pallas_call | solution.py:231
  38.8 1.6 %collective-permute-done.11.refs_0_ = bf16[256,1024]{1,0:T(8,128)(2,1)S(1)} collective-permute-done((bf16[256,1024]{1,0:T(8,128)(2,1)S(1)}, bf16[256,1024]{1,0:T(8,128)(2,1)S(1)}, u32[]{:S(2)}, u32[]{:S(2)}) %collective-permute-start.11) | collective-permute-done | bytes 524320 | tf_op jit(solution)/shard_map/ppermute | solution.py:378
  41.3 1.2 %collective-permute-done.21 = bf16[16,1024]{1,0:T(8,128)(2,1)S(1)} collective-permute-done((bf16[16,1024]{1,0:T(8,128)(2,1)S(1)}, bf16[16,1024]{1,0:T(8,128)(2,1)S(1)}, u32[]{:S(2)}, u32[]{:S(2)}) %collective-permute-start.21) | collective-permute-done | bytes 32800 | tf_op jit(solution)/shard_map/ppermute | solution.py:381
  42.5 1.5 %collective-permute-start.22 = (bf16[16,1024]{1,0:T(8,128)(2,1)S(1)}, bf16[16,1024]{1,0:T(8,128)(2,1)S(1)}, u32[]{:S(2)}, u32[]{:S(2)}) collective-permute-start(bf16[16,1024]{1,0:T(8,128)(2,1)S(1)} %collective-permute-done.21), channel_id=1, source_target_pairs={{0,6},{2,8},{4,14},{6,0},{8,2},{10,16},{12,22},{14,4},{16,10},{18,... | collective-permute-start | bytes 98312 | tf_op jit(solution)/shard_map/ppermute | solution.py:381
  44.3 1.6 %shard_map.59 = (bf16[2,256,4096]{2,1,0:T(8,128)(2,1)}, bf16[16,1024]{1,0:T(8,128)(2,1)S(1)}) custom-call(bf16[512,1024]{1,0:T(8,128)(2,1)S(1)} %maximum_maximum_fusion.left_ref, bf16[256,1024]{1,0:T(8,128)(2,1)S(1)} %collective-permute-done.12.refs_0_, bf16[128,1024]{1,0:T(8,128)(2,1)S(1)} %collective-permute-done.15.refs_1_, ...), custom_call_target="tpu_custom_call", output_to_operand_aliasing={{0}: (6, {})} | custom-call | tf_op jit(solution)/shard_map/pallas_call | solution.py:231
  47.1 1.5 %shard_map.61 = (bf16[2,256,4096]{2,1,0:T(8,128)(2,1)}, bf16[16,1024]{1,0:T(8,128)(2,1)S(1)}) custom-call(bf16[512,1024]{1,0:T(8,128)(2,1)S(1)} %maximum_maximum_fusion.left_ref, bf16[256,1024]{1,0:T(8,128)(2,1)S(1)} %collective-permute-done.11.refs_0_, bf16[128,1024]{1,0:T(8,128)(2,1)S(1)} %collective-permute-done.19.refs_1_, ...), custom_call_target="tpu_custom_call", output_to_operand_aliasing={{0}: (6, {})} | custom-call | tf_op jit(solution)/shard_map/pallas_call | solution.py:231
  49.2 1.8 %collective-permute-start.28 = (f32[32,256]{1,0:T(8,128)S(1)}, f32[32,256]{1,0:T(8,128)S(1)}, u32[]{:S(2)}, u32[]{:S(2)}) collective-permute-start(f32[32,256]{1,0:T(8,128)S(1)} %shard_map.63.refs_0_), channel_id=1, source_target_pairs={{0,1},{1,0},{2,3},{3,2},{4,5},{5,4},{6,7},{7,6},{8,9},{9,8},{10,11... | collective-permute-start | bytes 98312 | tf_op jit(solution)/shard_map/ppermute | solution.py:397
  51.0 1.5 %shard_map.64.refs_3_ = bf16[2,256,4096]{2,1,0:T(8,128)(2,1)} custom-call(bf16[512,1024]{1,0:T(8,128)(2,1)S(1)} %maximum_maximum_fusion.left_ref, bf16[256,1024]{1,0:T(8,128)(2,1)S(1)} %collective-permute-done.18.refs_0_, bf16[128,1024]{1,0:T(8,128)(2,1)S(1)} %collective-permute-done.23.refs_1_, ...), custom_call_target="tpu_custom_call", output_to_operand_aliasing={{}: (4, {})} | custom-call | tf_op jit(solution)/shard_map/pallas_call | solution.py:231
  52.5 0.6 %collective-permute-done.17.refs_0_ = bf16[256,1024]{1,0:T(8,128)(2,1)S(1)} collective-permute-done((bf16[256,1024]{1,0:T(8,128)(2,1)S(1)}, bf16[256,1024]{1,0:T(8,128)(2,1)S(1)}, u32[]{:S(2)}, u32[]{:S(2)}) %collective-permute-start.17) | collective-permute-done | bytes 524320 | tf_op jit(solution)/shard_map/ppermute | solution.py:378
  53.8 1.6 %shard_map.66 = f32[16,256,128]{2,1,0:T(8,128)} custom-call(bf16[192,2048]{1,0:T(8,128)(2,1)S(1)} %pad_maximum_fusion.table_ref, f32[32,256]{1,0:T(8,128)S(1)} %shard_map.63.refs_0_, f32[32,256]{1,0:T(8,128)S(1)} %collective-permute-done.28.refs_1_), custom_call_target="tpu_custom_call" | custom-call | flops 9200000000 | tf_op jit(solution)/shard_map/pallas_call | solution.py:305
  55.4 1.6 %shard_map.65 = bf16[2,256,4096]{2,1,0:T(8,128)(2,1)} custom-call(bf16[512,1024]{1,0:T(8,128)(2,1)S(1)} %maximum_maximum_fusion.left_ref, bf16[256,1024]{1,0:T(8,128)(2,1)S(1)} %collective-permute-done.17.refs_0_, bf16[128,1024]{1,0:T(8,128)(2,1)S(1)} %collective-permute-done.26.refs_1_, ...), custom_call_target="tpu_custom_call", output_to_operand_aliasing={{}: (4, {})} | custom-call | tf_op jit(solution)/shard_map/pallas_call | solution.py:231
  (66 shorter events, 7.1 us)
Async XLA Ops:
  0.6 1.0 %copy-start = (bf16[1,256,1024]{2,1,0:T(8,128)(2,1)S(1)}, bf16[1,256,1024]{2,1,0:T(8,128)(2,1)}, u32[]{:S(2)}) copy-start(bf16[1,256,1024]{2,1,0:T(8,128)(2,1)} %param.3) | copy-start | bytes 1572868
  1.8 9.3 %collective-permute-start = (bf16[256,512]{1,0:T(8,128)(2,1)S(1)}, bf16[256,512]{1,0:T(8,128)(2,1)S(1)}, u32[]{:S(2)}, u32[]{:S(2)}) collective-permute-start(bf16[256,512]{1,0:T(8,128)(2,1)S(1)} %get-tuple-element.57), channel_id=1, source_target_pairs={{0,1},{1,0},{2,3},{3,2},{4,5},{5,4},{6,7},{7,6},{8,9},{9,8},{10,11... | collective-permute-start | bytes 786440 | tf_op jit(solution)/shard_map/ppermute | solution.py:357
  4.8 8.7 %collective-permute-start.3 = (bf16[256,1024]{1,0:T(8,128)(2,1)S(1)}, bf16[256,1024]{1,0:T(8,128)(2,1)S(1)}, u32[]{:S(2)}, u32[]{:S(2)}) collective-permute-start(bf16[256,1024]{1,0:T(8,128)(2,1)S(1)} %get-tuple-element.55._.raw_ref), channel_id=1, source_target_pairs={{0,2},{2,0},{4,6},{6,4},{8,10},{10,8},{12,14},{14,12},{16,18},{18,... | collective-permute-start | bytes 1572872 | tf_op jit(solution)/shard_map/ppermute | solution.py:359
  4.8 13.1 %collective-permute-start.1 = (bf16[256,1024]{1,0:T(8,128)(2,1)S(1)}, bf16[256,1024]{1,0:T(8,128)(2,1)S(1)}, u32[]{:S(2)}, u32[]{:S(2)}) collective-permute-start(bf16[256,1024]{1,0:T(8,128)(2,1)S(1)} %get-tuple-element.55._.raw_ref), channel_id=1, source_target_pairs={{0,8},{2,6},{4,0},{6,14},{8,16},{10,2},{12,4},{14,22},{16,24},{18,... | collective-permute-start | bytes 1572872 | tf_op jit(solution)/shard_map/ppermute | solution.py:358
  6.4 1.0 %copy-start.1 = (s32[256,512]{1,0:T(8,128)S(1)}, s32[256,512]{1,0:T(8,128)}, u32[]{:S(2)}) copy-start(s32[256,512]{1,0:T(8,128)} %valid_ref.1) | copy-start | bytes 1572868
  7.4 0.7 %copy-start.2 = (s32[16]{0:T(128)S(1)}, s32[16]{0:T(128)}, u32[]{:S(2)}) copy-start(s32[16]{0:T(128)} %index_ref.1) | copy-start | bytes 196
  11.5 2.1 %collective-permute-start.4 = (bf16[256,512]{1,0:T(8,128)(2,1)S(1)}, bf16[256,512]{1,0:T(8,128)(2,1)S(1)}, u32[]{:S(2)}, u32[]{:S(2)}) collective-permute-start(bf16[256,512]{1,0:T(8,128)(2,1)S(1)} %get-tuple-element.59), channel_id=1, source_target_pairs={{0,2},{2,0},{4,6},{6,4},{8,10},{10,8},{12,14},{14,12},{16,18},{18,... | collective-permute-start | bytes 786440 | tf_op jit(solution)/shard_map/ppermute | solution.py:362
  11.5 6.4 %collective-permute-start.2 = (bf16[256,512]{1,0:T(8,128)(2,1)S(1)}, bf16[256,512]{1,0:T(8,128)(2,1)S(1)}, u32[]{:S(2)}, u32[]{:S(2)}) collective-permute-start(bf16[256,512]{1,0:T(8,128)(2,1)S(1)} %get-tuple-element.59), channel_id=1, source_target_pairs={{0,8},{2,6},{4,0},{6,14},{8,16},{10,2},{12,4},{14,22},{16,24},{18,... | collective-permute-start | bytes 786440 | tf_op jit(solution)/shard_map/ppermute | solution.py:361
  13.8 9.7 %collective-permute-start.6 = (bf16[256,1024]{1,0:T(8,128)(2,1)S(1)}, bf16[256,1024]{1,0:T(8,128)(2,1)S(1)}, u32[]{:S(2)}, u32[]{:S(2)}) collective-permute-start(bf16[256,1024]{1,0:T(8,128)(2,1)S(1)} %shard_map.54.refs_1_), channel_id=1, source_target_pairs={{0,8},{2,6},{4,0},{6,14},{8,16},{10,2},{12,4},{14,22},{16,24},{18,... | collective-permute-start | bytes 1572872 | tf_op jit(solution)/shard_map/ppermute | solution.py:364
  18.3 10.9 %collective-permute-start.5 = (bf16[256,1024]{1,0:T(8,128)(2,1)S(1)}, bf16[256,1024]{1,0:T(8,128)(2,1)S(1)}, u32[]{:S(2)}, u32[]{:S(2)}) collective-permute-start(bf16[256,1024]{1,0:T(8,128)(2,1)S(1)} %shard_map.53.refs_0_), channel_id=1, source_target_pairs={{0,8},{2,6},{4,0},{6,14},{8,16},{10,2},{12,4},{14,22},{16,24},{18,... | collective-permute-start | bytes 1572872 | tf_op jit(solution)/shard_map/ppermute | solution.py:378
  20.1 2.1 %collective-permute-start.8 = (bf16[128,1024]{1,0:T(8,128)(2,1)S(1)}, bf16[128,1024]{1,0:T(8,128)(2,1)S(1)}, u32[]{:S(2)}, u32[]{:S(2)}) collective-permute-start(bf16[128,1024]{1,0:T(8,128)(2,1)S(1)} %get-tuple-element.120), channel_id=1, source_target_pairs={{0,2},{2,0},{4,6},{6,4},{8,10},{10,8},{12,14},{14,12},{16,18},{18,... | collective-permute-start | bytes 786440 | tf_op jit(solution)/shard_map/ppermute | solution.py:328
  20.1 2.1 %collective-permute-start.7 = (bf16[128,1024]{1,0:T(8,128)(2,1)S(1)}, bf16[128,1024]{1,0:T(8,128)(2,1)S(1)}, u32[]{:S(2)}, u32[]{:S(2)}) collective-permute-start(bf16[128,1024]{1,0:T(8,128)(2,1)S(1)} %get-tuple-element.121), channel_id=1, source_target_pairs={{0,2},{2,0},{4,6},{6,4},{8,10},{10,8},{12,14},{14,12},{16,18},{18,... | collective-permute-start | bytes 786440 | tf_op jit(solution)/shard_map/ppermute | solution.py:328
  23.6 5.6 %collective-permute-start.10 = (bf16[128,1024]{1,0:T(8,128)(2,1)S(1)}, bf16[128,1024]{1,0:T(8,128)(2,1)S(1)}, u32[]{:S(2)}, u32[]{:S(2)}) collective-permute-start(bf16[128,1024]{1,0:T(8,128)(2,1)S(1)} %get-tuple-element.118), channel_id=1, source_target_pairs={{0,2},{2,0},{4,6},{6,4},{8,10},{10,8},{12,14},{14,12},{16,18},{18,... | collective-permute-start | bytes 786440 | tf_op jit(solution)/shard_map/ppermute | solution.py:328
  23.7 5.5 %collective-permute-start.9 = (bf16[128,1024]{1,0:T(8,128)(2,1)S(1)}, bf16[128,1024]{1,0:T(8,128)(2,1)S(1)}, u32[]{:S(2)}, u32[]{:S(2)}) collective-permute-start(bf16[128,1024]{1,0:T(8,128)(2,1)S(1)} %get-tuple-element.119), channel_id=1, source_target_pairs={{0,2},{2,0},{4,6},{6,4},{8,10},{10,8},{12,14},{14,12},{16,18},{18,... | collective-permute-start | bytes 786440 | tf_op jit(solution)/shard_map/ppermute | solution.py:328
  24.3 10.5 %collective-permute-start.12 = (bf16[256,1024]{1,0:T(8,128)(2,1)S(1)}, bf16[256,1024]{1,0:T(8,128)(2,1)S(1)}, u32[]{:S(2)}, u32[]{:S(2)}) collective-permute-start(bf16[256,1024]{1,0:T(8,128)(2,1)S(1)} %collective-permute-done.6.refs_0_), channel_id=1, source_target_pairs={{0,8},{2,6},{4,0},{6,14},{8,16},{10,2},{12,4},{14,22},{16,24},{18,... | collective-permute-start | bytes 1572872 | tf_op jit(solution)/shard_map/ppermute | solution.py:378
  29.2 5.6 %collective-permute-start.14 = (bf16[128,1024]{1,0:T(8,128)(2,1)S(1)}, bf16[128,1024]{1,0:T(8,128)(2,1)S(1)}, u32[]{:S(2)}, u32[]{:S(2)}) collective-permute-start(bf16[128,1024]{1,0:T(8,128)(2,1)S(1)} %get-tuple-element.116), channel_id=1, source_target_pairs={{0,2},{2,0},{4,6},{6,4},{8,10},{10,8},{12,14},{14,12},{16,18},{18,... | collective-permute-start | bytes 786440 | tf_op jit(solution)/shard_map/ppermute | solution.py:328
  29.3 5.5 %collective-permute-start.13 = (bf16[128,1024]{1,0:T(8,128)(2,1)S(1)}, bf16[128,1024]{1,0:T(8,128)(2,1)S(1)}, u32[]{:S(2)}, u32[]{:S(2)}) collective-permute-start(bf16[128,1024]{1,0:T(8,128)(2,1)S(1)} %get-tuple-element.117), channel_id=1, source_target_pairs={{0,2},{2,0},{4,6},{6,4},{8,10},{10,8},{12,14},{14,12},{16,18},{18,... | collective-permute-start | bytes 786440 | tf_op jit(solution)/shard_map/ppermute | solution.py:328
  30.1 10.3 %collective-permute-start.11 = (bf16[256,1024]{1,0:T(8,128)(2,1)S(1)}, bf16[256,1024]{1,0:T(8,128)(2,1)S(1)}, u32[]{:S(2)}, u32[]{:S(2)}) collective-permute-start(bf16[256,1024]{1,0:T(8,128)(2,1)S(1)} %collective-permute-done.5.refs_0_), channel_id=1, source_target_pairs={{0,8},{2,6},{4,0},{6,14},{8,16},{10,2},{12,4},{14,22},{16,24},{18,... | collective-permute-start | bytes 1572872 | tf_op jit(solution)/shard_map/ppermute | solution.py:378
  34.9 5.6 %collective-permute-start.16 = (bf16[128,1024]{1,0:T(8,128)(2,1)S(1)}, bf16[128,1024]{1,0:T(8,128)(2,1)S(1)}, u32[]{:S(2)}, u32[]{:S(2)}) collective-permute-start(bf16[128,1024]{1,0:T(8,128)(2,1)S(1)} %get-tuple-element.114), channel_id=1, source_target_pairs={{0,2},{2,0},{4,6},{6,4},{8,10},{10,8},{12,14},{14,12},{16,18},{18,... | collective-permute-start | bytes 786440 | tf_op jit(solution)/shard_map/ppermute | solution.py:328
  34.9 5.5 %collective-permute-start.15 = (bf16[128,1024]{1,0:T(8,128)(2,1)S(1)}, bf16[128,1024]{1,0:T(8,128)(2,1)S(1)}, u32[]{:S(2)}, u32[]{:S(2)}) collective-permute-start(bf16[128,1024]{1,0:T(8,128)(2,1)S(1)} %get-tuple-element.115), channel_id=1, source_target_pairs={{0,2},{2,0},{4,6},{6,4},{8,10},{10,8},{12,14},{14,12},{16,18},{18,... | collective-permute-start | bytes 786440 | tf_op jit(solution)/shard_map/ppermute | solution.py:328
  35.4 11.0 %collective-permute-start.18 = (bf16[256,1024]{1,0:T(8,128)(2,1)S(1)}, bf16[256,1024]{1,0:T(8,128)(2,1)S(1)}, u32[]{:S(2)}, u32[]{:S(2)}) collective-permute-start(bf16[256,1024]{1,0:T(8,128)(2,1)S(1)} %collective-permute-done.12.refs_0_), channel_id=1, source_target_pairs={{0,8},{2,6},{4,0},{6,14},{8,16},{10,2},{12,4},{14,22},{16,24},{18,... | collective-permute-start | bytes 1572872 | tf_op jit(solution)/shard_map/ppermute | solution.py:378
  40.5 5.8 %collective-permute-start.20 = (bf16[128,1024]{1,0:T(8,128)(2,1)S(1)}, bf16[128,1024]{1,0:T(8,128)(2,1)S(1)}, u32[]{:S(2)}, u32[]{:S(2)}) collective-permute-start(bf16[128,1024]{1,0:T(8,128)(2,1)S(1)} %get-tuple-element.112), channel_id=1, source_target_pairs={{0,2},{2,0},{4,6},{6,4},{8,10},{10,8},{12,14},{14,12},{16,18},{18,... | collective-permute-start | bytes 786440 | tf_op jit(solution)/shard_map/ppermute | solution.py:328
  40.6 5.7 %collective-permute-start.19 = (bf16[128,1024]{1,0:T(8,128)(2,1)S(1)}, bf16[128,1024]{1,0:T(8,128)(2,1)S(1)}, u32[]{:S(2)}, u32[]{:S(2)}) collective-permute-start(bf16[128,1024]{1,0:T(8,128)(2,1)S(1)} %get-tuple-element.113), channel_id=1, source_target_pairs={{0,2},{2,0},{4,6},{6,4},{8,10},{10,8},{12,14},{14,12},{16,18},{18,... | collective-permute-start | bytes 786440 | tf_op jit(solution)/shard_map/ppermute | solution.py:328
  41.2 1.3 %collective-permute-start.21 = (bf16[16,1024]{1,0:T(8,128)(2,1)S(1)}, bf16[16,1024]{1,0:T(8,128)(2,1)S(1)}, u32[]{:S(2)}, u32[]{:S(2)}) collective-permute-start(bf16[16,1024]{1,0:T(8,128)(2,1)S(1)} %shard_map.60), channel_id=1, source_target_pairs={{0,2},{2,0},{4,6},{6,4},{8,10},{10,8},{12,14},{14,12},{16,18},{18,... | collective-permute-start | bytes 98312 | tf_op jit(solution)/shard_map/ppermute | solution.py:381
  42.5 3.8 %collective-permute-start.22 = (bf16[16,1024]{1,0:T(8,128)(2,1)S(1)}, bf16[16,1024]{1,0:T(8,128)(2,1)S(1)}, u32[]{:S(2)}, u32[]{:S(2)}) collective-permute-start(bf16[16,1024]{1,0:T(8,128)(2,1)S(1)} %collective-permute-done.21), channel_id=1, source_target_pairs={{0,6},{2,8},{4,14},{6,0},{8,2},{10,16},{12,22},{14,4},{16,10},{18,... | collective-permute-start | bytes 98312 | tf_op jit(solution)/shard_map/ppermute | solution.py:381
  44.0 9.2 %collective-permute-start.17 = (bf16[256,1024]{1,0:T(8,128)(2,1)S(1)}, bf16[256,1024]{1,0:T(8,128)(2,1)S(1)}, u32[]{:S(2)}, u32[]{:S(2)}) collective-permute-start(bf16[256,1024]{1,0:T(8,128)(2,1)S(1)} %collective-permute-done.11.refs_0_), channel_id=1, source_target_pairs={{0,8},{2,6},{4,0},{6,14},{8,16},{10,2},{12,4},{14,22},{16,24},{18,... | collective-permute-start | bytes 1572872 | tf_op jit(solution)/shard_map/ppermute | solution.py:378
  46.4 2.2 %collective-permute-start.24 = (bf16[128,1024]{1,0:T(8,128)(2,1)S(1)}, bf16[128,1024]{1,0:T(8,128)(2,1)S(1)}, u32[]{:S(2)}, u32[]{:S(2)}) collective-permute-start(bf16[128,1024]{1,0:T(8,128)(2,1)S(1)} %get-tuple-element.110), channel_id=1, source_target_pairs={{0,2},{2,0},{4,6},{6,4},{8,10},{10,8},{12,14},{14,12},{16,18},{18,... | collective-permute-start | bytes 786440 | tf_op jit(solution)/shard_map/ppermute | solution.py:328
  46.5 2.1 %collective-permute-start.23 = (bf16[128,1024]{1,0:T(8,128)(2,1)S(1)}, bf16[128,1024]{1,0:T(8,128)(2,1)S(1)}, u32[]{:S(2)}, u32[]{:S(2)}) collective-permute-start(bf16[128,1024]{1,0:T(8,128)(2,1)S(1)} %get-tuple-element.111), channel_id=1, source_target_pairs={{0,2},{2,0},{4,6},{6,4},{8,10},{10,8},{12,14},{14,12},{16,18},{18,... | collective-permute-start | bytes 786440 | tf_op jit(solution)/shard_map/ppermute | solution.py:328
  47.0 1.9 %collective-permute-start.25 = (bf16[16,1024]{1,0:T(8,128)(2,1)S(1)}, bf16[16,1024]{1,0:T(8,128)(2,1)S(1)}, u32[]{:S(2)}, u32[]{:S(2)}) collective-permute-start(bf16[16,1024]{1,0:T(8,128)(2,1)S(1)} %collective-permute-done.22.refs_2_), channel_id=1, source_target_pairs={{0,2},{2,0},{4,6},{6,4},{8,10},{10,8},{12,14},{14,12},{16,18},{18,... | collective-permute-start | bytes 98312 | tf_op jit(solution)/shard_map/ppermute | solution.py:385
  49.2 4.6 %collective-permute-start.28 = (f32[32,256]{1,0:T(8,128)S(1)}, f32[32,256]{1,0:T(8,128)S(1)}, u32[]{:S(2)}, u32[]{:S(2)}) collective-permute-start(f32[32,256]{1,0:T(8,128)S(1)} %shard_map.63.refs_0_), channel_id=1, source_target_pairs={{0,1},{1,0},{2,3},{3,2},{4,5},{5,4},{6,7},{7,6},{8,9},{9,8},{10,11... | collective-permute-start | bytes 98312 | tf_op jit(solution)/shard_map/ppermute | solution.py:397
  53.2 2.2 %collective-permute-start.27 = (bf16[128,1024]{1,0:T(8,128)(2,1)S(1)}, bf16[128,1024]{1,0:T(8,128)(2,1)S(1)}, u32[]{:S(2)}, u32[]{:S(2)}) collective-permute-start(bf16[128,1024]{1,0:T(8,128)(2,1)S(1)} %get-tuple-element.108), channel_id=1, source_target_pairs={{0,2},{2,0},{4,6},{6,4},{8,10},{10,8},{12,14},{14,12},{16,18},{18,... | collective-permute-start | bytes 786440 | tf_op jit(solution)/shard_map/ppermute | solution.py:328
  53.3 2.2 %collective-permute-start.26 = (bf16[128,1024]{1,0:T(8,128)(2,1)S(1)}, bf16[128,1024]{1,0:T(8,128)(2,1)S(1)}, u32[]{:S(2)}, u32[]{:S(2)}) collective-permute-start(bf16[128,1024]{1,0:T(8,128)(2,1)S(1)} %get-tuple-element.109), channel_id=1, source_target_pairs={{0,2},{2,0},{4,6},{6,4},{8,10},{10,8},{12,14},{14,12},{16,18},{18,... | collective-permute-start | bytes 786440 | tf_op jit(solution)/shard_map/ppermute | solution.py:328

commit v9 on v6

--- a/solution.py
+++ b/solution.py
@@ -356,9 +356,11 @@
         valid, numbers = prepare(valid, station_index, raw)
         received = [lax.ppermute(power, "freq", from_freq(shift)) for shift in range(1, freq_size)]
         raw_flying = lax.ppermute(raw, "grp", ring)
+        raw_sibling = lax.ppermute(raw, "grp", swap_by(1))
         whitened, others = whiten_own(raw, valid, received, total_bins)
         others_flying = lax.ppermute(others, "grp", ring)
-        swapped = swap(whitened)
+        others_sibling = lax.ppermute(others, "grp", swap_by(1))
+        swapped = [whiten_passed(raw_sibling, others_sibling, total_bins)]
         flying = [None, lax.ppermute(jnp.concatenate(swapped, axis=0), "grp", ring)]
         left = jnp.concatenate(
             [whitened, jnp.concatenate([whitened[:, window_count:], -whitened[:, :window_count]], axis=1)], axis=0

time: 57.6 us -> 57.2 us (level)
  waiting for transfers between devices: 13.4 us -> 12.1 us
  starting transfers between devices: 22.6 us -> 23.2 us
    ppermute x16 -> x14, waiting for transfers between devices: 1.28 us -> 0.04 us  [swap_pieces(): lax.ppermute(block[k * rows:(k + 1) * rows], 'grp', swap_by(1))]
    ppermute x1, starting transfers between devices: 0.36 us -> 1.45 us  [on_device(): lax.ppermute(lax.ppermute(found, 'grp', swap_by(1)), 'grp', across)]
    ppermute x1, waiting for transfers between devices: 0.01 us -> 0.93 us  [on_device(): others_flying = lax.ppermute(others, 'grp', ring)]
    ppermute x1, waiting for transfers between devices: 2.77 us -> 2.17 us  [on_device(): flying = [None, lax.ppermute(jnp.concatenate(swapped, axis=0), 'grp', ring)]]
    ppermute x16 -> x14, starting transfers between devices: 4.49 us -> 3.92 us  [swap_pieces(): lax.ppermute(block[k * rows:(k + 1) * rows], 'grp', swap_by(1))]
  transfers between devices with their start and end apart: 29 -> 29, of which waited for: 11 -> 10; matrix products, arithmetic and copies ran while one was open for 3% -> 3% of each run, Pallas kernels for 25% -> 26%
where the time goes in v9:
time: 57.2 us; the launch traced here: 57 us
  starting transfers between devices  23.2 us (41%)
  Pallas kernels  16.3 us (28%)
  waiting for transfers between devices  12.1 us (21%)
  local copies, waits for them, and re-layouts  3.82 us (7%)
  between operations  0.96 us (2%)
    pallas_call x8, Pallas kernels, cross_blocks(): pl.pallas_call(body, out_shape=shapes, in_specs=specs, out_specs=out_spec...  12.4 us
    ppermute x5, starting transfers between devices, on_device(): flying.append(lax.ppermute(arrived, 'grp', ring))  7.72 us
    ppermute x5, waiting for transfers between devices, on_device(): flying.append(lax.ppermute(arrived, 'grp', ring))  5.06 us
    ppermute x14, starting transfers between devices, swap_pieces(): lax.ppermute(block[k * rows:(k + 1) * rows], 'grp', swap_by(1))  3.92 us
    ppermute x1, starting transfers between devices, on_device(): lax.ppermute(power, 'freq', from_freq(shift))  3.03 us
    unnamed x8, local copies, waits for them, and re-layouts  2.87 us
    ppermute x1, waiting for transfers between devices, on_device(): lax.ppermute(power, 'freq', from_freq(shift))  2.39 us
    ppermute x1, waiting for transfers between devices, on_device(): flying = [None, lax.ppermute(jnp.concatenate(swapped, axis=0), 'grp', ring)]  2.17 us
  transfers between devices with their start and end apart: 29, of which 10 were waited for; matrix products, arithmetic and copies ran while one was open for 3% of the time, Pallas kernels for 26%

profile of v9, /device:TPU:0, one launch (start us, length us, event | category | flops | bytes accessed | tf_op | source)
XLA Modules:
  0.0 57.0 jit_solution(11286040329401043379)
XLA Ops:
  0.6 1.0 %copy-done = bf16[1,256,1024]{2,1,0:T(8,128)(2,1)S(1)} copy-done((bf16[1,256,1024]{2,1,0:T(8,128)(2,1)S(1)}, bf16[1,256,1024]{2,1,0:T(8,128)(2,1)}, u32[]{:S(2)}) %copy-start) | copy-done | bytes 524312
  1.8 3.0 %collective-permute-start = (bf16[256,512]{1,0:T(8,128)(2,1)S(1)}, bf16[256,512]{1,0:T(8,128)(2,1)S(1)}, u32[]{:S(2)}, u32[]{:S(2)}) collective-permute-start(bf16[256,512]{1,0:T(8,128)(2,1)S(1)} %get-tuple-element.58), channel_id=1, source_target_pairs={{0,1},{1,0},{2,3},{3,2},{4,5},{5,4},{6,7},{7,6},{8,9},{9,8},{10,11... | collective-permute-start | bytes 786440 | tf_op jit(solution)/shard_map/ppermute | solution.py:357
  4.8 1.6 %collective-permute-start.1 = (bf16[256,1024]{1,0:T(8,128)(2,1)S(1)}, bf16[256,1024]{1,0:T(8,128)(2,1)S(1)}, u32[]{:S(2)}, u32[]{:S(2)}) collective-permute-start(bf16[256,1024]{1,0:T(8,128)(2,1)S(1)} %get-tuple-element.56._.raw_ref), channel_id=1, source_target_pairs={{0,8},{2,6},{4,0},{6,14},{8,16},{10,2},{12,4},{14,22},{16,24},{18,... | collective-permute-start | bytes 1572872 | tf_op jit(solution)/shard_map/ppermute | solution.py:358
  6.4 1.0 %copy-done.1 = s32[256,512]{1,0:T(8,128)S(1)} copy-done((s32[256,512]{1,0:T(8,128)S(1)}, s32[256,512]{1,0:T(8,128)}, u32[]{:S(2)}) %copy-start.1) | copy-done | bytes 524312
  7.4 0.7 %copy-done.2 = s32[16]{0:T(128)S(1)} copy-done((s32[16]{0:T(128)S(1)}, s32[16]{0:T(128)}, u32[]{:S(2)}) %copy-start.2) | copy-done | bytes 88
  8.1 0.6 %shard_map.51 = (bf16[256,512]{1,0:T(8,128)(2,1)S(1)}, s32[16,256]{1,0:T(8,128)S(1)}) custom-call(s32[16]{0:T(128)S(1)} %copy-done.2, s32[256,512]{1,0:T(8,128)S(1)} %copy-done.1, bf16[256,1024]{1,0:T(8,128)(2,1)S(1)} %get-tuple-element.56._.raw_ref), custom_call_target="tpu_custom_call" | custom-call | flops 345000000 | tf_op jit(solution)/shard_map/pallas_call | solution.py:98
  8.7 2.4 %collective-permute-done.refs_0_ = bf16[256,512]{1,0:T(8,128)(2,1)S(1)} collective-permute-done((bf16[256,512]{1,0:T(8,128)(2,1)S(1)}, bf16[256,512]{1,0:T(8,128)(2,1)S(1)}, u32[]{:S(2)}, u32[]{:S(2)}) %collective-permute-start) | collective-permute-done | bytes 262176 | tf_op jit(solution)/shard_map/ppermute | solution.py:357
  11.5 1.8 %collective-permute-start.2 = (bf16[256,512]{1,0:T(8,128)(2,1)S(1)}, bf16[256,512]{1,0:T(8,128)(2,1)S(1)}, u32[]{:S(2)}, u32[]{:S(2)}) collective-permute-start(bf16[256,512]{1,0:T(8,128)(2,1)S(1)} %get-tuple-element.60), channel_id=1, source_target_pairs={{0,8},{2,6},{4,0},{6,14},{8,16},{10,2},{12,4},{14,22},{16,24},{18,... | collective-permute-start | bytes 786440 | tf_op jit(solution)/shard_map/ppermute | solution.py:361
  13.8 1.6 %collective-permute-start.6 = (bf16[256,1024]{1,0:T(8,128)(2,1)S(1)}, bf16[256,1024]{1,0:T(8,128)(2,1)S(1)}, u32[]{:S(2)}, u32[]{:S(2)}) collective-permute-start(bf16[256,1024]{1,0:T(8,128)(2,1)S(1)} %shard_map.54.refs_1_), channel_id=1, source_target_pairs={{0,8},{2,6},{4,0},{6,14},{8,16},{10,2},{12,4},{14,22},{16,24},{18,... | collective-permute-start | bytes 1572872 | tf_op jit(solution)/shard_map/ppermute | solution.py:364
  15.5 1.5 %shard_map.55 = (bf16[2,256,4096]{2,1,0:T(8,128)(2,1)}, bf16[16,1024]{1,0:T(8,128)(2,1)S(1)}) custom-call(bf16[512,1024]{1,0:T(8,128)(2,1)S(1)} %maximum_maximum_fusion.left_ref, bf16[256,1024]{1,0:T(8,128)(2,1)S(1)} %get-tuple-element.59.refs_0_, bf16[256,1024]{1,0:T(8,128)(2,1)S(1)} %shard_map.54.refs_1_, ...), custom_call_target="tpu_custom_call" | custom-call | flops 4600000000 | tf_op jit(solution)/shard_map/pallas_call | solution.py:231
  17.0 0.9 %collective-permute-done.2.others_ref = bf16[256,512]{1,0:T(8,128)(2,1)S(1)} collective-permute-done((bf16[256,512]{1,0:T(8,128)(2,1)S(1)}, bf16[256,512]{1,0:T(8,128)(2,1)S(1)}, u32[]{:S(2)}, u32[]{:S(2)}) %collective-permute-start.2) | collective-permute-done | bytes 262176 | tf_op jit(solution)/shard_map/ppermute | solution.py:361
  18.2 0.7 %fusion.10 = (bf16[128,1024]{1,0:T(8,128)(2,1)}, bf16[128,1024]{1,0:T(8,128)(2,1)S(1)}) fusion(bf16[256,1024]{1,0:T(8,128)(2,1)S(1)} %shard_map.53.refs_0_), kind=kLoop, calls=%fused_computation.25 | loop fusion | bytes 1048576 | tf_op jit(solution)/shard_map/slice | solution.py:328
  19.6 1.8 %collective-permute-start.5 = (bf16[256,1024]{1,0:T(8,128)(2,1)S(1)}, bf16[256,1024]{1,0:T(8,128)(2,1)S(1)}, u32[]{:S(2)}, u32[]{:S(2)}) collective-permute-start(bf16[256,1024]{1,0:T(8,128)(2,1)S(1)} %shard_map.53.refs_0_), channel_id=1, source_target_pairs={{0,8},{2,6},{4,0},{6,14},{8,16},{10,2},{12,4},{14,22},{16,24},{18,... | collective-permute-start | bytes 1572872 | tf_op jit(solution)/shard_map/ppermute | solution.py:380
  21.4 2.2 %collective-permute-done.6.refs_0_ = bf16[256,1024]{1,0:T(8,128)(2,1)S(1)} collective-permute-done((bf16[256,1024]{1,0:T(8,128)(2,1)S(1)}, bf16[256,1024]{1,0:T(8,128)(2,1)S(1)}, u32[]{:S(2)}, u32[]{:S(2)}) %collective-permute-start.6) | collective-permute-done | bytes 524320 | tf_op jit(solution)/shard_map/ppermute | solution.py:364
  24.3 1.8 %collective-permute-start.12 = (bf16[256,1024]{1,0:T(8,128)(2,1)S(1)}, bf16[256,1024]{1,0:T(8,128)(2,1)S(1)}, u32[]{:S(2)}, u32[]{:S(2)}) collective-permute-start(bf16[256,1024]{1,0:T(8,128)(2,1)S(1)} %collective-permute-done.6.refs_0_), channel_id=1, source_target_pairs={{0,8},{2,6},{4,0},{6,14},{8,16},{10,2},{12,4},{14,22},{16,24},{18,... | collective-permute-start | bytes 1572872 | tf_op jit(solution)/shard_map/ppermute | solution.py:380
  26.1 1.5 %shard_map.56 = (bf16[2,256,4096]{2,1,0:T(8,128)(2,1)}, bf16[16,1024]{1,0:T(8,128)(2,1)S(1)}) custom-call(bf16[512,1024]{1,0:T(8,128)(2,1)S(1)} %maximum_maximum_fusion.left_ref, bf16[256,1024]{1,0:T(8,128)(2,1)S(1)} %shard_map.53.refs_0_, bf16[128,1024]{1,0:T(8,128)(2,1)S(1)} %collective-permute-done.7.refs_1_, ...), custom_call_target="tpu_custom_call", output_to_operand_aliasing={{0}: (6, {})} | custom-call | tf_op jit(solution)/shard_map/pallas_call | solution.py:231
  27.7 1.5 %collective-permute-done.5.refs_0_ = bf16[256,1024]{1,0:T(8,128)(2,1)S(1)} collective-permute-done((bf16[256,1024]{1,0:T(8,128)(2,1)S(1)}, bf16[256,1024]{1,0:T(8,128)(2,1)S(1)}, u32[]{:S(2)}, u32[]{:S(2)}) %collective-permute-start.5) | collective-permute-done | bytes 524320 | tf_op jit(solution)/shard_map/ppermute | solution.py:380
  30.1 1.8 %collective-permute-start.11 = (bf16[256,1024]{1,0:T(8,128)(2,1)S(1)}, bf16[256,1024]{1,0:T(8,128)(2,1)S(1)}, u32[]{:S(2)}, u32[]{:S(2)}) collective-permute-start(bf16[256,1024]{1,0:T(8,128)(2,1)S(1)} %collective-permute-done.5.refs_0_), channel_id=1, source_target_pairs={{0,8},{2,6},{4,0},{6,14},{8,16},{10,2},{12,4},{14,22},{16,24},{18,... | collective-permute-start | bytes 1572872 | tf_op jit(solution)/shard_map/ppermute | solution.py:380
  32.1 1.6 %shard_map.57 = (bf16[2,256,4096]{2,1,0:T(8,128)(2,1)}, bf16[16,1024]{1,0:T(8,128)(2,1)S(1)}) custom-call(bf16[512,1024]{1,0:T(8,128)(2,1)S(1)} %maximum_maximum_fusion.left_ref, bf16[256,1024]{1,0:T(8,128)(2,1)S(1)} %collective-permute-done.6.refs_0_, bf16[128,1024]{1,0:T(8,128)(2,1)S(1)} %collective-permute-done.9.refs_1_, ...), custom_call_target="tpu_custom_call", output_to_operand_aliasing={{0}: (6, {})} | custom-call | tf_op jit(solution)/shard_map/pallas_call | solution.py:231
  33.6 1.2 %collective-permute-done.12.refs_0_ = bf16[256,1024]{1,0:T(8,128)(2,1)S(1)} collective-permute-done((bf16[256,1024]{1,0:T(8,128)(2,1)S(1)}, bf16[256,1024]{1,0:T(8,128)(2,1)S(1)}, u32[]{:S(2)}, u32[]{:S(2)}) %collective-permute-start.12) | collective-permute-done | bytes 524320 | tf_op jit(solution)/shard_map/ppermute | solution.py:380
  35.4 1.8 %collective-permute-start.18 = (bf16[256,1024]{1,0:T(8,128)(2,1)S(1)}, bf16[256,1024]{1,0:T(8,128)(2,1)S(1)}, u32[]{:S(2)}, u32[]{:S(2)}) collective-permute-start(bf16[256,1024]{1,0:T(8,128)(2,1)S(1)} %collective-permute-done.12.refs_0_), channel_id=1, source_target_pairs={{0,8},{2,6},{4,0},{6,14},{8,16},{10,2},{12,4},{14,22},{16,24},{18,... | collective-permute-start | bytes 1572872 | tf_op jit(solution)/shard_map/ppermute | solution.py:380
  37.2 1.6 %shard_map.58 = (bf16[2,256,4096]{2,1,0:T(8,128)(2,1)}, bf16[16,1024]{1,0:T(8,128)(2,1)S(1)}) custom-call(bf16[512,1024]{1,0:T(8,128)(2,1)S(1)} %maximum_maximum_fusion.left_ref, bf16[256,1024]{1,0:T(8,128)(2,1)S(1)} %collective-permute-done.5.refs_0_, bf16[128,1024]{1,0:T(8,128)(2,1)S(1)} %collective-permute-done.13.refs_1_, ...), custom_call_target="tpu_custom_call", output_to_operand_aliasing={{0}: (6, {})} | custom-call | tf_op jit(solution)/shard_map/pallas_call | solution.py:231
  38.8 1.6 %collective-permute-done.11.refs_0_ = bf16[256,1024]{1,0:T(8,128)(2,1)S(1)} collective-permute-done((bf16[256,1024]{1,0:T(8,128)(2,1)S(1)}, bf16[256,1024]{1,0:T(8,128)(2,1)S(1)}, u32[]{:S(2)}, u32[]{:S(2)}) %collective-permute-start.11) | collective-permute-done | bytes 524320 | tf_op jit(solution)/shard_map/ppermute | solution.py:380
  41.3 1.2 %collective-permute-done.21 = bf16[16,1024]{1,0:T(8,128)(2,1)S(1)} collective-permute-done((bf16[16,1024]{1,0:T(8,128)(2,1)S(1)}, bf16[16,1024]{1,0:T(8,128)(2,1)S(1)}, u32[]{:S(2)}, u32[]{:S(2)}) %collective-permute-start.21) | collective-permute-done | bytes 32800 | tf_op jit(solution)/shard_map/ppermute | solution.py:383
  42.5 1.5 %collective-permute-start.22 = (bf16[16,1024]{1,0:T(8,128)(2,1)S(1)}, bf16[16,1024]{1,0:T(8,128)(2,1)S(1)}, u32[]{:S(2)}, u32[]{:S(2)}) collective-permute-start(bf16[16,1024]{1,0:T(8,128)(2,1)S(1)} %collective-permute-done.21), channel_id=1, source_target_pairs={{0,6},{2,8},{4,14},{6,0},{8,2},{10,16},{12,22},{14,4},{16,10},{18,... | collective-permute-start | bytes 98312 | tf_op jit(solution)/shard_map/ppermute | solution.py:383
  44.3 1.6 %shard_map.59 = (bf16[2,256,4096]{2,1,0:T(8,128)(2,1)}, bf16[16,1024]{1,0:T(8,128)(2,1)S(1)}) custom-call(bf16[512,1024]{1,0:T(8,128)(2,1)S(1)} %maximum_maximum_fusion.left_ref, bf16[256,1024]{1,0:T(8,128)(2,1)S(1)} %collective-permute-done.12.refs_0_, bf16[128,1024]{1,0:T(8,128)(2,1)S(1)} %collective-permute-done.15.refs_1_, ...), custom_call_target="tpu_custom_call", output_to_operand_aliasing={{0}: (6, {})} | custom-call | tf_op jit(solution)/shard_map/pallas_call | solution.py:231
  47.1 1.5 %shard_map.61 = (bf16[2,256,4096]{2,1,0:T(8,128)(2,1)}, bf16[16,1024]{1,0:T(8,128)(2,1)S(1)}) custom-call(bf16[512,1024]{1,0:T(8,128)(2,1)S(1)} %maximum_maximum_fusion.left_ref, bf16[256,1024]{1,0:T(8,128)(2,1)S(1)} %collective-permute-done.11.refs_0_, bf16[128,1024]{1,0:T(8,128)(2,1)S(1)} %collective-permute-done.19.refs_1_, ...), custom_call_target="tpu_custom_call", output_to_operand_aliasing={{0}: (6, {})} | custom-call | tf_op jit(solution)/shard_map/pallas_call | solution.py:231
  49.2 1.8 %collective-permute-start.28 = (f32[32,256]{1,0:T(8,128)S(1)}, f32[32,256]{1,0:T(8,128)S(1)}, u32[]{:S(2)}, u32[]{:S(2)}) collective-permute-start(f32[32,256]{1,0:T(8,128)S(1)} %shard_map.63.refs_0_), channel_id=1, source_target_pairs={{0,1},{1,0},{2,3},{3,2},{4,5},{5,4},{6,7},{7,6},{8,9},{9,8},{10,11... | collective-permute-start | bytes 98312 | tf_op jit(solution)/shard_map/ppermute | solution.py:395
  51.0 1.5 %shard_map.64.refs_3_ = bf16[2,256,4096]{2,1,0:T(8,128)(2,1)} custom-call(bf16[512,1024]{1,0:T(8,128)(2,1)S(1)} %maximum_maximum_fusion.left_ref, bf16[256,1024]{1,0:T(8,128)(2,1)S(1)} %collective-permute-done.18.refs_0_, bf16[128,1024]{1,0:T(8,128)(2,1)S(1)} %collective-permute-done.23.refs_1_, ...), custom_call_target="tpu_custom_call", output_to_operand_aliasing={{}: (4, {})} | custom-call | tf_op jit(solution)/shard_map/pallas_call | solution.py:231
  52.5 0.6 %collective-permute-done.17.refs_0_ = bf16[256,1024]{1,0:T(8,128)(2,1)S(1)} collective-permute-done((bf16[256,1024]{1,0:T(8,128)(2,1)S(1)}, bf16[256,1024]{1,0:T(8,128)(2,1)S(1)}, u32[]{:S(2)}, u32[]{:S(2)}) %collective-permute-start.17) | collective-permute-done | bytes 524320 | tf_op jit(solution)/shard_map/ppermute | solution.py:380
  53.7 1.6 %shard_map.66 = f32[16,256,128]{2,1,0:T(8,128)} custom-call(bf16[192,2048]{1,0:T(8,128)(2,1)S(1)} %pad_maximum_fusion.table_ref, f32[32,256]{1,0:T(8,128)S(1)} %shard_map.63.refs_0_, f32[32,256]{1,0:T(8,128)S(1)} %collective-permute-done.28.refs_1_), custom_call_target="tpu_custom_call" | custom-call | flops 9200000000 | tf_op jit(solution)/shard_map/pallas_call | solution.py:305
  55.4 1.6 %shard_map.65 = bf16[2,256,4096]{2,1,0:T(8,128)(2,1)} custom-call(bf16[512,1024]{1,0:T(8,128)(2,1)S(1)} %maximum_maximum_fusion.left_ref, bf16[256,1024]{1,0:T(8,128)(2,1)S(1)} %collective-permute-done.17.refs_0_, bf16[128,1024]{1,0:T(8,128)(2,1)S(1)} %collective-permute-done.26.refs_1_, ...), custom_call_target="tpu_custom_call", output_to_operand_aliasing={{}: (4, {})} | custom-call | tf_op jit(solution)/shard_map/pallas_call | solution.py:231
  (66 shorter events, 7.6 us)
Async XLA Ops:
  0.6 1.0 %copy-start = (bf16[1,256,1024]{2,1,0:T(8,128)(2,1)S(1)}, bf16[1,256,1024]{2,1,0:T(8,128)(2,1)}, u32[]{:S(2)}) copy-start(bf16[1,256,1024]{2,1,0:T(8,128)(2,1)} %param.3) | copy-start | bytes 1572868
  1.8 9.3 %collective-permute-start = (bf16[256,512]{1,0:T(8,128)(2,1)S(1)}, bf16[256,512]{1,0:T(8,128)(2,1)S(1)}, u32[]{:S(2)}, u32[]{:S(2)}) collective-permute-start(bf16[256,512]{1,0:T(8,128)(2,1)S(1)} %get-tuple-element.58), channel_id=1, source_target_pairs={{0,1},{1,0},{2,3},{3,2},{4,5},{5,4},{6,7},{7,6},{8,9},{9,8},{10,11... | collective-permute-start | bytes 786440 | tf_op jit(solution)/shard_map/ppermute | solution.py:357
  4.8 8.7 %collective-permute-start.3 = (bf16[256,1024]{1,0:T(8,128)(2,1)S(1)}, bf16[256,1024]{1,0:T(8,128)(2,1)S(1)}, u32[]{:S(2)}, u32[]{:S(2)}) collective-permute-start(bf16[256,1024]{1,0:T(8,128)(2,1)S(1)} %get-tuple-element.56._.raw_ref), channel_id=1, source_target_pairs={{0,2},{2,0},{4,6},{6,4},{8,10},{10,8},{12,14},{14,12},{16,18},{18,... | collective-permute-start | bytes 1572872 | tf_op jit(solution)/shard_map/ppermute | solution.py:359
  4.8 13.1 %collective-permute-start.1 = (bf16[256,1024]{1,0:T(8,128)(2,1)S(1)}, bf16[256,1024]{1,0:T(8,128)(2,1)S(1)}, u32[]{:S(2)}, u32[]{:S(2)}) collective-permute-start(bf16[256,1024]{1,0:T(8,128)(2,1)S(1)} %get-tuple-element.56._.raw_ref), channel_id=1, source_target_pairs={{0,8},{2,6},{4,0},{6,14},{8,16},{10,2},{12,4},{14,22},{16,24},{18,... | collective-permute-start | bytes 1572872 | tf_op jit(solution)/shard_map/ppermute | solution.py:358
  6.4 1.0 %copy-start.1 = (s32[256,512]{1,0:T(8,128)S(1)}, s32[256,512]{1,0:T(8,128)}, u32[]{:S(2)}) copy-start(s32[256,512]{1,0:T(8,128)} %valid_ref.1) | copy-start | bytes 1572868
  7.4 0.7 %copy-start.2 = (s32[16]{0:T(128)S(1)}, s32[16]{0:T(128)}, u32[]{:S(2)}) copy-start(s32[16]{0:T(128)} %index_ref.1) | copy-start | bytes 196
  11.5 2.1 %collective-permute-start.4 = (bf16[256,512]{1,0:T(8,128)(2,1)S(1)}, bf16[256,512]{1,0:T(8,128)(2,1)S(1)}, u32[]{:S(2)}, u32[]{:S(2)}) collective-permute-start(bf16[256,512]{1,0:T(8,128)(2,1)S(1)} %get-tuple-element.60), channel_id=1, source_target_pairs={{0,2},{2,0},{4,6},{6,4},{8,10},{10,8},{12,14},{14,12},{16,18},{18,... | collective-permute-start | bytes 786440 | tf_op jit(solution)/shard_map/ppermute | solution.py:362
  11.5 6.4 %collective-permute-start.2 = (bf16[256,512]{1,0:T(8,128)(2,1)S(1)}, bf16[256,512]{1,0:T(8,128)(2,1)S(1)}, u32[]{:S(2)}, u32[]{:S(2)}) collective-permute-start(bf16[256,512]{1,0:T(8,128)(2,1)S(1)} %get-tuple-element.60), channel_id=1, source_target_pairs={{0,8},{2,6},{4,0},{6,14},{8,16},{10,2},{12,4},{14,22},{16,24},{18,... | collective-permute-start | bytes 786440 | tf_op jit(solution)/shard_map/ppermute | solution.py:361
  13.8 9.7 %collective-permute-start.6 = (bf16[256,1024]{1,0:T(8,128)(2,1)S(1)}, bf16[256,1024]{1,0:T(8,128)(2,1)S(1)}, u32[]{:S(2)}, u32[]{:S(2)}) collective-permute-start(bf16[256,1024]{1,0:T(8,128)(2,1)S(1)} %shard_map.54.refs_1_), channel_id=1, source_target_pairs={{0,8},{2,6},{4,0},{6,14},{8,16},{10,2},{12,4},{14,22},{16,24},{18,... | collective-permute-start | bytes 1572872 | tf_op jit(solution)/shard_map/ppermute | solution.py:364
  19.0 2.4 %collective-permute-start.8 = (bf16[128,1024]{1,0:T(8,128)(2,1)}, bf16[128,1024]{1,0:T(8,128)(2,1)S(1)}, u32[]{:S(2)}, u32[]{:S(2)}) collective-permute-start(bf16[128,1024]{1,0:T(8,128)(2,1)} %get-tuple-element.122), channel_id=1, source_target_pairs={{0,2},{2,0},{4,6},{6,4},{8,10},{10,8},{12,14},{14,12},{16,18},{18,... | collective-permute-start | bytes 786440 | tf_op jit(solution)/shard_map/ppermute | solution.py:328
  19.0 2.4 %collective-permute-start.7 = (bf16[128,1024]{1,0:T(8,128)(2,1)S(1)}, bf16[128,1024]{1,0:T(8,128)(2,1)S(1)}, u32[]{:S(2)}, u32[]{:S(2)}) collective-permute-start(bf16[128,1024]{1,0:T(8,128)(2,1)S(1)} %get-tuple-element.123), channel_id=1, source_target_pairs={{0,2},{2,0},{4,6},{6,4},{8,10},{10,8},{12,14},{14,12},{16,18},{18,... | collective-permute-start | bytes 786440 | tf_op jit(solution)/shard_map/ppermute | solution.py:328
  19.6 9.6 %collective-permute-start.5 = (bf16[256,1024]{1,0:T(8,128)(2,1)S(1)}, bf16[256,1024]{1,0:T(8,128)(2,1)S(1)}, u32[]{:S(2)}, u32[]{:S(2)}) collective-permute-start(bf16[256,1024]{1,0:T(8,128)(2,1)S(1)} %shard_map.53.refs_0_), channel_id=1, source_target_pairs={{0,8},{2,6},{4,0},{6,14},{8,16},{10,2},{12,4},{14,22},{16,24},{18,... | collective-permute-start | bytes 1572872 | tf_op jit(solution)/shard_map/ppermute | solution.py:380
  23.6 5.6 %collective-permute-start.10 = (bf16[128,1024]{1,0:T(8,128)(2,1)S(1)}, bf16[128,1024]{1,0:T(8,128)(2,1)S(1)}, u32[]{:S(2)}, u32[]{:S(2)}) collective-permute-start(bf16[128,1024]{1,0:T(8,128)(2,1)S(1)} %get-tuple-element.120), channel_id=1, source_target_pairs={{0,2},{2,0},{4,6},{6,4},{8,10},{10,8},{12,14},{14,12},{16,18},{18,... | collective-permute-start | bytes 786440 | tf_op jit(solution)/shard_map/ppermute | solution.py:328
  23.7 5.5 %collective-permute-start.9 = (bf16[128,1024]{1,0:T(8,128)(2,1)S(1)}, bf16[128,1024]{1,0:T(8,128)(2,1)S(1)}, u32[]{:S(2)}, u32[]{:S(2)}) collective-permute-start(bf16[128,1024]{1,0:T(8,128)(2,1)S(1)} %get-tuple-element.121), channel_id=1, source_target_pairs={{0,2},{2,0},{4,6},{6,4},{8,10},{10,8},{12,14},{14,12},{16,18},{18,... | collective-permute-start | bytes 786440 | tf_op jit(solution)/shard_map/ppermute | solution.py:328
  24.3 10.5 %collective-permute-start.12 = (bf16[256,1024]{1,0:T(8,128)(2,1)S(1)}, bf16[256,1024]{1,0:T(8,128)(2,1)S(1)}, u32[]{:S(2)}, u32[]{:S(2)}) collective-permute-start(bf16[256,1024]{1,0:T(8,128)(2,1)S(1)} %collective-permute-done.6.refs_0_), channel_id=1, source_target_pairs={{0,8},{2,6},{4,0},{6,14},{8,16},{10,2},{12,4},{14,22},{16,24},{18,... | collective-permute-start | bytes 1572872 | tf_op jit(solution)/shard_map/ppermute | solution.py:380
  29.2 5.6 %collective-permute-start.14 = (bf16[128,1024]{1,0:T(8,128)(2,1)S(1)}, bf16[128,1024]{1,0:T(8,128)(2,1)S(1)}, u32[]{:S(2)}, u32[]{:S(2)}) collective-permute-start(bf16[128,1024]{1,0:T(8,128)(2,1)S(1)} %get-tuple-element.118), channel_id=1, source_target_pairs={{0,2},{2,0},{4,6},{6,4},{8,10},{10,8},{12,14},{14,12},{16,18},{18,... | collective-permute-start | bytes 786440 | tf_op jit(solution)/shard_map/ppermute | solution.py:328
  29.3 5.5 %collective-permute-start.13 = (bf16[128,1024]{1,0:T(8,128)(2,1)S(1)}, bf16[128,1024]{1,0:T(8,128)(2,1)S(1)}, u32[]{:S(2)}, u32[]{:S(2)}) collective-permute-start(bf16[128,1024]{1,0:T(8,128)(2,1)S(1)} %get-tuple-element.119), channel_id=1, source_target_pairs={{0,2},{2,0},{4,6},{6,4},{8,10},{10,8},{12,14},{14,12},{16,18},{18,... | collective-permute-start | bytes 786440 | tf_op jit(solution)/shard_map/ppermute | solution.py:328
  30.1 10.3 %collective-permute-start.11 = (bf16[256,1024]{1,0:T(8,128)(2,1)S(1)}, bf16[256,1024]{1,0:T(8,128)(2,1)S(1)}, u32[]{:S(2)}, u32[]{:S(2)}) collective-permute-start(bf16[256,1024]{1,0:T(8,128)(2,1)S(1)} %collective-permute-done.5.refs_0_), channel_id=1, source_target_pairs={{0,8},{2,6},{4,0},{6,14},{8,16},{10,2},{12,4},{14,22},{16,24},{18,... | collective-permute-start | bytes 1572872 | tf_op jit(solution)/shard_map/ppermute | solution.py:380
  34.9 3.9 %collective-permute-start.16 = (bf16[128,1024]{1,0:T(8,128)(2,1)S(1)}, bf16[128,1024]{1,0:T(8,128)(2,1)S(1)}, u32[]{:S(2)}, u32[]{:S(2)}) collective-permute-start(bf16[128,1024]{1,0:T(8,128)(2,1)S(1)} %get-tuple-element.116), channel_id=1, source_target_pairs={{0,2},{2,0},{4,6},{6,4},{8,10},{10,8},{12,14},{14,12},{16,18},{18,... | collective-permute-start | bytes 786440 | tf_op jit(solution)/shard_map/ppermute | solution.py:328
  34.9 3.9 %collective-permute-start.15 = (bf16[128,1024]{1,0:T(8,128)(2,1)S(1)}, bf16[128,1024]{1,0:T(8,128)(2,1)S(1)}, u32[]{:S(2)}, u32[]{:S(2)}) collective-permute-start(bf16[128,1024]{1,0:T(8,128)(2,1)S(1)} %get-tuple-element.117), channel_id=1, source_target_pairs={{0,2},{2,0},{4,6},{6,4},{8,10},{10,8},{12,14},{14,12},{16,18},{18,... | collective-permute-start | bytes 786440 | tf_op jit(solution)/shard_map/ppermute | solution.py:328
  35.4 11.0 %collective-permute-start.18 = (bf16[256,1024]{1,0:T(8,128)(2,1)S(1)}, bf16[256,1024]{1,0:T(8,128)(2,1)S(1)}, u32[]{:S(2)}, u32[]{:S(2)}) collective-permute-start(bf16[256,1024]{1,0:T(8,128)(2,1)S(1)} %collective-permute-done.12.refs_0_), channel_id=1, source_target_pairs={{0,8},{2,6},{4,0},{6,14},{8,16},{10,2},{12,4},{14,22},{16,24},{18,... | collective-permute-start | bytes 1572872 | tf_op jit(solution)/shard_map/ppermute | solution.py:380
  40.5 5.9 %collective-permute-start.20 = (bf16[128,1024]{1,0:T(8,128)(2,1)S(1)}, bf16[128,1024]{1,0:T(8,128)(2,1)S(1)}, u32[]{:S(2)}, u32[]{:S(2)}) collective-permute-start(bf16[128,1024]{1,0:T(8,128)(2,1)S(1)} %get-tuple-element.114), channel_id=1, source_target_pairs={{0,2},{2,0},{4,6},{6,4},{8,10},{10,8},{12,14},{14,12},{16,18},{18,... | collective-permute-start | bytes 786440 | tf_op jit(solution)/shard_map/ppermute | solution.py:328
  40.5 5.9 %collective-permute-start.19 = (bf16[128,1024]{1,0:T(8,128)(2,1)S(1)}, bf16[128,1024]{1,0:T(8,128)(2,1)S(1)}, u32[]{:S(2)}, u32[]{:S(2)}) collective-permute-start(bf16[128,1024]{1,0:T(8,128)(2,1)S(1)} %get-tuple-element.115), channel_id=1, source_target_pairs={{0,2},{2,0},{4,6},{6,4},{8,10},{10,8},{12,14},{14,12},{16,18},{18,... | collective-permute-start | bytes 786440 | tf_op jit(solution)/shard_map/ppermute | solution.py:328
  41.2 1.3 %collective-permute-start.21 = (bf16[16,1024]{1,0:T(8,128)(2,1)S(1)}, bf16[16,1024]{1,0:T(8,128)(2,1)S(1)}, u32[]{:S(2)}, u32[]{:S(2)}) collective-permute-start(bf16[16,1024]{1,0:T(8,128)(2,1)S(1)} %shard_map.60), channel_id=1, source_target_pairs={{0,2},{2,0},{4,6},{6,4},{8,10},{10,8},{12,14},{14,12},{16,18},{18,... | collective-permute-start | bytes 98312 | tf_op jit(solution)/shard_map/ppermute | solution.py:383
  42.5 3.8 %collective-permute-start.22 = (bf16[16,1024]{1,0:T(8,128)(2,1)S(1)}, bf16[16,1024]{1,0:T(8,128)(2,1)S(1)}, u32[]{:S(2)}, u32[]{:S(2)}) collective-permute-start(bf16[16,1024]{1,0:T(8,128)(2,1)S(1)} %collective-permute-done.21), channel_id=1, source_target_pairs={{0,6},{2,8},{4,14},{6,0},{8,2},{10,16},{12,22},{14,4},{16,10},{18,... | collective-permute-start | bytes 98312 | tf_op jit(solution)/shard_map/ppermute | solution.py:383
  43.9 9.2 %collective-permute-start.17 = (bf16[256,1024]{1,0:T(8,128)(2,1)S(1)}, bf16[256,1024]{1,0:T(8,128)(2,1)S(1)}, u32[]{:S(2)}, u32[]{:S(2)}) collective-permute-start(bf16[256,1024]{1,0:T(8,128)(2,1)S(1)} %collective-permute-done.11.refs_0_), channel_id=1, source_target_pairs={{0,8},{2,6},{4,0},{6,14},{8,16},{10,2},{12,4},{14,22},{16,24},{18,... | collective-permute-start | bytes 1572872 | tf_op jit(solution)/shard_map/ppermute | solution.py:380
  46.4 2.2 %collective-permute-start.24 = (bf16[128,1024]{1,0:T(8,128)(2,1)S(1)}, bf16[128,1024]{1,0:T(8,128)(2,1)S(1)}, u32[]{:S(2)}, u32[]{:S(2)}) collective-permute-start(bf16[128,1024]{1,0:T(8,128)(2,1)S(1)} %get-tuple-element.112), channel_id=1, source_target_pairs={{0,2},{2,0},{4,6},{6,4},{8,10},{10,8},{12,14},{14,12},{16,18},{18,... | collective-permute-start | bytes 786440 | tf_op jit(solution)/shard_map/ppermute | solution.py:328
  46.5 2.1 %collective-permute-start.23 = (bf16[128,1024]{1,0:T(8,128)(2,1)S(1)}, bf16[128,1024]{1,0:T(8,128)(2,1)S(1)}, u32[]{:S(2)}, u32[]{:S(2)}) collective-permute-start(bf16[128,1024]{1,0:T(8,128)(2,1)S(1)} %get-tuple-element.113), channel_id=1, source_target_pairs={{0,2},{2,0},{4,6},{6,4},{8,10},{10,8},{12,14},{14,12},{16,18},{18,... | collective-permute-start | bytes 786440 | tf_op jit(solution)/shard_map/ppermute | solution.py:328
  47.0 1.9 %collective-permute-start.25 = (bf16[16,1024]{1,0:T(8,128)(2,1)S(1)}, bf16[16,1024]{1,0:T(8,128)(2,1)S(1)}, u32[]{:S(2)}, u32[]{:S(2)}) collective-permute-start(bf16[16,1024]{1,0:T(8,128)(2,1)S(1)} %collective-permute-done.22.refs_2_), channel_id=1, source_target_pairs={{0,2},{2,0},{4,6},{6,4},{8,10},{10,8},{12,14},{14,12},{16,18},{18,... | collective-permute-start | bytes 98312 | tf_op jit(solution)/shard_map/ppermute | solution.py:387
  49.2 4.6 %collective-permute-start.28 = (f32[32,256]{1,0:T(8,128)S(1)}, f32[32,256]{1,0:T(8,128)S(1)}, u32[]{:S(2)}, u32[]{:S(2)}) collective-permute-start(f32[32,256]{1,0:T(8,128)S(1)} %shard_map.63.refs_0_), channel_id=1, source_target_pairs={{0,1},{1,0},{2,3},{3,2},{4,5},{5,4},{6,7},{7,6},{8,9},{9,8},{10,11... | collective-permute-start | bytes 98312 | tf_op jit(solution)/shard_map/ppermute | solution.py:395
  53.2 2.2 %collective-permute-start.27 = (bf16[128,1024]{1,0:T(8,128)(2,1)S(1)}, bf16[128,1024]{1,0:T(8,128)(2,1)S(1)}, u32[]{:S(2)}, u32[]{:S(2)}) collective-permute-start(bf16[128,1024]{1,0:T(8,128)(2,1)S(1)} %get-tuple-element.110), channel_id=1, source_target_pairs={{0,2},{2,0},{4,6},{6,4},{8,10},{10,8},{12,14},{14,12},{16,18},{18,... | collective-permute-start | bytes 786440 | tf_op jit(solution)/shard_map/ppermute | solution.py:328
  53.2 2.2 %collective-permute-start.26 = (bf16[128,1024]{1,0:T(8,128)(2,1)S(1)}, bf16[128,1024]{1,0:T(8,128)(2,1)S(1)}, u32[]{:S(2)}, u32[]{:S(2)}) collective-permute-start(bf16[128,1024]{1,0:T(8,128)(2,1)S(1)} %get-tuple-element.111), channel_id=1, source_target_pairs={{0,2},{2,0},{4,6},{6,4},{8,10},{10,8},{12,14},{14,12},{16,18},{18,... | collective-permute-start | bytes 786440 | tf_op jit(solution)/shard_map/ppermute | solution.py:328
